TPU v7x, 32 devices: a whole 2x2x4 slice. The times are simulated.
32 devices in a mesh: gx: 8 (over z, x), gy: 4 (over y, core).
Axes of the slice: x: 2, y: 2, z: 4, core: 2. Of those that a mesh axis runs over, the one named last changes fastest.
Arguments:
- velocity: float32 [256, 512, 256], P('gx', 'gy'), may hold values from -6 to 6
- threshold_table: float32 [16], replicated, may hold values from 0.05 to 1.5
- band_index: int32 [3, 7], replicated, may hold values from 0 to 15
Outputs:
- updated: float32 [256, 512, 256], P('gx', 'gy')
All inputs are finite; a program needn't handle non-finite values.
Results may differ from a plain program's by a relative error of at most 0.0003.
Values sent between devices are 32-bit elements; how exact they have to be, the bound alone decides.
No kernel may reach another device: no remote copies, remote signals or barrier semaphores. Data moves between devices by JAX's collectives and lax.ppermute only.
A program may use at most 128 MiB of HBM per device.

v0:
```python
import functools

import jax
import jax.numpy as jnp
import ml_dtypes
import numpy as np
from jax import lax
from jax.experimental import pallas as pl
from jax.experimental.pallas import tpu as pltpu
from jax.sharding import PartitionSpec as P

H = [
    0.23037781330885523,
    0.7148465705525415,
    0.6308807679295904,
    -0.02798376941698385,
    -0.18703481171888114,
    0.030841381835986965,
    0.032883011666982945,
    -0.010597401784997278,
]
G = [(-1.0) ** j * H[7 - j] for j in range(8)]
F32 = jnp.float32
BF16 = jnp.bfloat16
NOTHING = 3.0e38
VMEM_BYTES = 56 * 1024 * 1024


def tap(filt, j):
    return filt[j] if 0 <= j < 8 else 0.0


def analysis_rows(cells, ks):
    matrix = np.zeros((2 * len(ks), len(cells)))
    for row, k in enumerate(ks):
        for col, cell in enumerate(cells):
            if k is not None and cell is not None:
                matrix[row, col] = tap(H, cell - 2 * k + 3)
                matrix[len(ks) + row, col] = tap(G, cell - 2 * k + 3)
    return matrix


def synthesis_rows(cells, ks):
    return analysis_rows(cells, ks).T


def periodic(length, padded_to):
    matrix = np.zeros((padded_to, padded_to))
    for k in range(length // 2):
        for j in range(8):
            matrix[(2 * k + j - 3) % length, k] += H[j]
            matrix[(2 * k + j - 3) % length, length // 2 + k] += G[j]
    return matrix


def fill(items, length):
    return items + [None] * (length - len(items))


def up_to(count, step):
    return -(-count // step) * step


def pieces(matrix):
    rows, cols = matrix.shape
    matrix = np.pad(matrix, ((0, up_to(rows, 16) - rows), (0, up_to(cols, 16) - cols))).astype(np.float32)
    high = matrix.astype(ml_dtypes.bfloat16)
    low = (matrix - high.astype(np.float32)).astype(ml_dtypes.bfloat16)
    return [high, low]


def halves(values):
    high = values.astype(BF16)
    return high, (values - high.astype(F32)).astype(BF16)


def dot(left, right):
    return jnp.dot(left, right, preferred_element_type=F32)


def times(values, matrix):
    high, low = halves(values)
    return dot(high, matrix[0][...]) + (dot(low, matrix[0][...]) + dot(high, matrix[1][...]))


def left_times(matrix, values):
    missing = matrix[0].shape[1] - values.shape[0]
    if missing:
        values = jnp.concatenate([values, jnp.zeros((missing, values.shape[1]), F32)], axis=0)
    high, low = halves(values)
    return dot(matrix[0][...], high) + (dot(matrix[0][...], low) + dot(matrix[1][...], high))


def added(terms):
    total = None
    for coef, value in terms:
        part = value if coef == 1.0 else coef * value
        total = part if total is None else total + part
    return total


def x_terms(k, n):
    terms = []
    for j in range(8):
        cell = 2 * k + j - 3
        if 0 <= cell < n:
            terms.append((cell, H[j], G[j]))
        elif cell == -1:
            terms.append(("l1", H[j], G[j]))
        elif cell == n:
            terms.append(("r1", H[j], G[j]))
    if k == 0:
        terms.append(("l2", 1.0, G[0] / H[0]))
    if k == n // 2 - 1:
        terms.append(("r2", 1.0, G[6] / H[6]))
    return terms


def x_low(get, k, n):
    return added([(low, get(key)) for key, low, _ in x_terms(k, n)])


def x_high(get, k, n):
    return added([(high, get(key)) for key, _, high in x_terms(k, n)])


def x_synth(m, lows, highs):
    terms = [(H[m + 3 - 2 * k], v) for k, v in lows.items() if 0 <= m + 3 - 2 * k < 8]
    terms += [(G[m + 3 - 2 * k], v) for k, v in highs.items() if 0 <= m + 3 - 2 * k < 8]
    return added(terms)


def spill_up(low, high, n):
    first = added([(H[5], low[n - 1]), (G[5], high[n - 1]), (H[7], low[n - 2]), (G[7], high[n - 2])])
    return first, added([(H[6], low[n - 1]), (G[6], high[n - 1])])


def spill_down(low, high):
    first = added([(H[2], low[0]), (G[2], high[0]), (H[0], low[1]), (G[0], high[1])])
    return first, added([(H[1], low[0]), (G[1], high[0])])


THIRD_UP = H[7] / H[6]
THIRD_DOWN = H[0] / H[1]


def shrink(values, thresh):
    return values - jnp.minimum(jnp.maximum(values, -thresh), thresh)


def call(kernel, grid, in_specs, out_specs, out_shapes, args, flops, moved, scratch=(), name=None):
    return pl.pallas_call(
        kernel,
        grid=grid,
        in_specs=in_specs,
        out_specs=out_specs,
        out_shape=out_shapes,
        scratch_shapes=list(scratch),
        name=name,
        cost_estimate=pl.CostEstimate(flops=int(flops), bytes_accessed=int(moved), transcendentals=0),
        compiler_params=pltpu.CompilerParams(vmem_limit_bytes=VMEM_BYTES),
    )(*args)


def shape(*dims):
    return jax.ShapeDtypeStruct(dims, F32)


def whole(array):
    dims = array.shape
    return pl.BlockSpec(dims, lambda *_: (0,) * len(dims))


def whole_out(*dims):
    return pl.BlockSpec(dims, lambda *_: (0,) * len(dims))


SMEM = pl.BlockSpec(memory_space=pltpu.SMEM)


def x_messages(last, first, up, down):
    up[0] = last[3]
    up[1] = H[0] * last[1] + H[1] * last[2]
    down[0] = first[0]
    down[1] = H[6] * first[1] + H[7] * first[2]


def first_messages(v):
    nx, ny, nz = v.shape

    def kernel(last, first, y_last, y_first, up, down, y_up, y_down):
        x_messages(last, first, up, down)
        y_up[...] = y_last[...]
        y_down[...] = y_first[...]

    return call(
        kernel,
        (1,),
        [
            pl.BlockSpec((4, ny, nz), lambda i: (nx // 4 - 1, 0, 0)),
            pl.BlockSpec((4, ny, nz), lambda i: (0, 0, 0)),
            pl.BlockSpec((nx, 8, nz), lambda i: (0, ny // 8 - 1, 0)),
            pl.BlockSpec((nx, 8, nz), lambda i: (0, 0, 0)),
        ],
        [whole_out(2, ny, nz)] * 2 + [whole_out(nx, 8, nz)] * 2,
        [shape(2, ny, nz)] * 2 + [shape(nx, 8, nz)] * 2,
        [v] * 4,
        1e6,
        3e6,
        name="first_messages",
    )


def corner_messages(y_left, y_right):
    nx, rows, nz = y_left.shape

    def kernel(last_l, first_l, last_r, first_r, up, down):
        for part, last, first in ((0, last_l, first_l), (1, last_r, first_r)):
            at = pl.ds(8 * part, 8)
            up[0, at] = last[3]
            up[1, at] = H[0] * last[1] + H[1] * last[2]
            down[0, at] = first[0]
            down[1, at] = H[6] * first[1] + H[7] * first[2]

    last = pl.BlockSpec((4, rows, nz), lambda i: (nx // 4 - 1, 0, 0))
    first = pl.BlockSpec((4, rows, nz), lambda i: (0, 0, 0))
    return call(
        kernel,
        (1,),
        [last, first, last, first],
        [whole_out(2, 16, nz)] * 2,
        [shape(2, 16, nz)] * 2,
        [y_left, y_left, y_right, y_right],
        1e5,
        2e5,
        name="corner_messages",
    )


def depth_analysis(v, z_matrix):
    nx, ny, nz = v.shape

    def kernel(v_ref, z0, z1, out):
        out[...] = times(v_ref[...].reshape(4 * ny, nz), (z0, z1)).reshape(4, ny, nz)

    block = pl.BlockSpec((4, ny, nz), lambda i: (i, 0, 0))
    return call(
        kernel,
        (nx // 4,),
        [block, whole(z_matrix[0]), whole(z_matrix[1])],
        block,
        shape(nx, ny, nz),
        [v, *z_matrix],
        6 * nx * ny * nz * nz,
        8 * nx * ny * nz,
        name="depth_analysis",
    )


def y_analysis(zed, y_left, y_right, z_matrix, y_matrix):
    nx, ny, nz = zed.shape
    rows = y_matrix[0].shape[0]

    def kernel(zed_ref, left, right, z0, z1, y0, y1, out):
        sides = jnp.concatenate([left[...].reshape(32, nz), right[...].reshape(32, nz)], axis=0)
        sides = times(sides, (z0, z1))
        for i in range(4):
            plane = jnp.concatenate(
                [sides[8 * i : 8 * i + 8], zed_ref[i], sides[32 + 8 * i : 40 + 8 * i]], axis=0
            )
            out[i] = left_times((y0, y1), plane)

    return call(
        kernel,
        (nx // 4,),
        [
            pl.BlockSpec((4, ny, nz), lambda i: (i, 0, 0)),
            pl.BlockSpec((4, 8, nz), lambda i: (i, 0, 0)),
            pl.BlockSpec((4, 8, nz), lambda i: (i, 0, 0)),
        ]
        + [whole(m) for m in z_matrix + y_matrix],
        pl.BlockSpec((4, rows, nz), lambda i: (i, 0, 0)),
        shape(nx, rows, nz),
        [zed, y_left, y_right, *z_matrix, *y_matrix],
        6 * nx * rows * (ny + 16) * nz,
        4 * nx * nz * (ny + rows + 16),
        name="y_analysis",
    )


def first_approx(bands, x_left, x_right, c_left, c_right, z_matrix, y_matrix, own, ghost_rows):
    nx, rows, nz = bands.shape
    ny = x_left.shape[1]
    half_rows = rows // 2
    half_z = nz // 2
    n1 = nx // 2

    def kernel(b_ref, xl, xr, cl, cr, z0, z1, y0, y1, halo, approx, up, down):
        for side, (main, corner) in enumerate(((xl, cl), (xr, cr))):
            for i in range(2):
                plane = jnp.concatenate([corner[i, :8], main[i], corner[i, 8:]], axis=0)
                halo[2 * side + i] = left_times((y0, y1), times(plane, (z0, z1)))
        place = {"l1": 0, "l2": 1, "r1": 2, "r2": 3}

        def tile(t, carry):
            at = pl.ds(pl.multiple_of(t * 8, 8), 8)

            def get(key):
                if isinstance(key, str):
                    return halo[place[key], at, :half_z]
                return b_ref[key, at]

            for k in range(n1):
                approx[k, at] = x_low(get, k, nx)
            return carry

        lax.fori_loop(0, own // 8, tile, 0)
        up[...] = approx[:, own - ghost_rows :]
        down[...] = approx[:, :ghost_rows]

    return call(
        kernel,
        (1,),
        [pl.BlockSpec((nx, half_rows, half_z), lambda i: (0, 0, 0))]
        + [whole(a) for a in (x_left, x_right, c_left, c_right, *z_matrix, *y_matrix)],
        [
            whole_out(4, rows, nz),
            whole_out(n1, own, half_z),
            whole_out(n1, ghost_rows, half_z),
            whole_out(n1, ghost_rows, half_z),
        ],
        [
            shape(4, rows, nz),
            shape(n1, own, half_z),
            shape(n1, ghost_rows, half_z),
            shape(n1, ghost_rows, half_z),
        ],
        [bands, x_left, x_right, c_left, c_right, *z_matrix, *y_matrix],
        24 * rows * (ny + 16) * nz + 24 * (ny + 16) * nz * nz,
        6e6,
        name="first_approx",
    )


def detail_bands(bands, halo, table, index):
    nx, rows, nz = bands.shape
    n1 = nx // 2
    step_rows = 24 if (rows // 2) % 24 == 0 else 8
    steps = rows // step_rows
    half_z = nz // 2

    def kernel(table_ref, index_ref, b_ref, h_ref, out):
        by = (pl.program_id(0) >= steps // 2).astype(jnp.int32)
        place = {"l1": 0, "l2": 1, "r1": 2, "r2": 3}
        limits = {}
        for bx in range(2):
            for bz in range(2):
                band = 4 * bx + 2 * by + bz
                found = table_ref[index_ref[0, jnp.maximum(band - 1, 0)]]
                limits[bx, bz] = jnp.where(band == 0, NOTHING, found)

        def tile(t, carry):
            at = pl.ds(pl.multiple_of(t * 8, 8), 8)
            for bz in range(2):
                lanes = pl.ds(bz * half_z, half_z)

                def get(key):
                    if isinstance(key, str):
                        return h_ref[place[key], at, lanes]
                    return b_ref[key, at, lanes]

                for k in range(n1):
                    out[k, at, lanes] = shrink(x_low(get, k, nx), limits[0, bz])
                    out[n1 + k, at, lanes] = shrink(x_high(get, k, nx), limits[1, bz])
            return carry

        lax.fori_loop(0, step_rows // 8, tile, 0)

    block = pl.BlockSpec((nx, step_rows, nz), lambda i: (0, i, 0))
    return call(
        kernel,
        (steps,),
        [SMEM, SMEM, block, pl.BlockSpec((4, step_rows, nz), lambda i: (0, i, 0))],
        block,
        shape(nx, rows, nz),
        [table, index, bands, halo],
        40 * nx * rows * nz,
        8 * nx * rows * nz,
        name="detail_bands",
    )


def detail_yz(coeffs, z_matrix, y_matrix):
    nx, rows, nz = coeffs.shape
    ny = y_matrix[0].shape[0]
    blocks = nx // 8

    def kernel(c_ref, z0, z1, y0, y1, out, up, down):
        step = pl.program_id(0)
        zed = times(c_ref[...].reshape(4 * rows, nz), (z0, z1))
        for i in range(4):
            out[i] = left_times((y0, y1), zed[i * rows : (i + 1) * rows])

        @pl.when(step == 0)
        def _():
            down[0] = H[2] * out[0] + H[0] * out[1]
            down[1] = H[1] * out[0]

        @pl.when(step == blocks)
        def _():
            down[0] += G[2] * out[0] + G[0] * out[1]
            down[1] += G[1] * out[0]

        @pl.when(step == blocks - 1)
        def _():
            up[0] = H[5] * out[3] + H[7] * out[2]
            up[1] = H[6] * out[3]

        @pl.when(step == 2 * blocks - 1)
        def _():
            up[0] += G[5] * out[3] + G[7] * out[2]
            up[1] += G[6] * out[3]

    return call(
        kernel,
        (2 * blocks,),
        [pl.BlockSpec((4, rows, nz), lambda i: (i, 0, 0))] + [whole(m) for m in z_matrix + y_matrix],
        [pl.BlockSpec((4, ny, nz), lambda i: (i, 0, 0)), whole_out(2, ny, nz), whole_out(2, ny, nz)],
        [shape(nx, ny, nz), shape(2, ny, nz), shape(2, ny, nz)],
        [coeffs, *z_matrix, *y_matrix],
        6 * nx * rows * nz * nz + 6 * nx * rows * ny * nz,
        4 * nx * nz * (rows + ny),
        name="detail_yz",
    )


def detail_x(parts):
    nx, ny, nz = parts.shape
    n1 = nx // 2
    step_rows = 16

    def kernel(p_ref, out):
        def tile(t, carry):
            at = pl.ds(pl.multiple_of(t * 8, 8), 8)
            for lane in range(0, nz, 128):
                lanes = pl.ds(lane, 128)
                for m in range(nx):
                    ks = [k for k in range(n1) if 0 <= m + 3 - 2 * k < 8]
                    lows = {k: p_ref[k, at, lanes] for k in ks}
                    highs = {k: p_ref[n1 + k, at, lanes] for k in ks}
                    out[m, at, lanes] = x_synth(m, lows, highs)
            return carry

        lax.fori_loop(0, step_rows // 8, tile, 0)

    block = pl.BlockSpec((nx, step_rows, nz), lambda i: (0, i, 0))
    return call(
        kernel,
        (ny // step_rows,),
        [block],
        block,
        shape(nx, ny, nz),
        [parts],
        16 * nx * ny * nz,
        8 * nx * ny * nz,
        name="detail_x",
    )


def second_bands(own, left, right, z_matrix, y_matrix, low_rows):
    n1, own_rows, nz = own.shape
    ghost_rows = left.shape[1]
    in_rows = own_rows + 2 * ghost_rows
    rows = 2 * low_rows
    lane_half = nz // 2

    def kernel(o_ref, l_ref, r_ref, z0, z1, y0, y1, out, up, down):
        for i in range(0, n1, 4):
            stack = jnp.concatenate(
                [part[j] for j in range(i, i + 4) for part in (o_ref, l_ref, r_ref)], axis=0
            )
            zed = times(stack, (z0, z1))
            for j in range(4):
                out[i + j] = left_times((y0, y1), zed[j * in_rows : (j + 1) * in_rows])
        low = lambda c: out[c, :low_rows]
        up[0:rows] = out[n1 - 1]
        up[rows : 2 * rows] = H[0] * out[n1 - 3] + H[1] * out[n1 - 2]
        first = added([(H[j], low(n1 - 5 + j)) for j in range(5)])
        second = added([(H[0] * H[j], low(n1 - 9 + j)) for j in range(8)])
        second += added([(H[1] * H[j], low(n1 - 7 + j)) for j in range(7)])
        lane = lax.broadcasted_iota(jnp.int32, first.shape, 1)
        up[2 * rows :] = jnp.where(lane < lane_half, first, pltpu.roll(second, lane_half, 1))
        down[0:rows] = out[0]
        down[rows : 2 * rows] = H[6] * out[1] + H[7] * out[2]
        first = added([(H[j], low(j - 3)) for j in range(3, 8)])
        second = added([(H[6] * H[j], low(j - 1)) for j in range(1, 8)])
        second += added([(H[7] * H[j], low(j + 1)) for j in range(8)])
        down[2 * rows :] = jnp.where(lane < lane_half, first, pltpu.roll(second, lane_half, 1))

    message = 2 * rows + low_rows
    return call(
        kernel,
        (1,),
        [whole(a) for a in (own, left, right, *z_matrix, *y_matrix)],
        [whole_out(n1, rows, nz), whole_out(message, nz), whole_out(message, nz)],
        [shape(n1, rows, nz), shape(message, nz), shape(message, nz)],
        [own, left, right, *z_matrix, *y_matrix],
        6 * n1 * in_rows * nz * (nz + rows),
        4 * n1 * nz * (in_rows + rows),
        name="second_bands",
    )


def limits_plane(table_ref, index_ref, level, bx, dims, row_split, lane_split, zeroth):
    row_high = lax.broadcasted_iota(jnp.int32, dims, 0) >= row_split
    lane_high = lax.broadcasted_iota(jnp.int32, dims, 1) >= lane_split

    def limit(by, bz):
        band = 4 * bx + 2 * by + bz
        return zeroth if band == 0 else table_ref[index_ref[level, band - 1]]

    low_y = jnp.where(lane_high, limit(0, 1), limit(0, 0))
    return jnp.where(row_high, jnp.where(lane_high, limit(1, 1), limit(1, 0)), low_y)


def coarse(bands, left, right, table, index, z1_mats, z2_mats, ya2, ys2, ys1, low_rows, z1_len):
    n1, rows, nz = bands.shape
    n2, n3 = n1 // 2, n1 // 4
    rows2 = ya2[0].shape[0]
    out_rows = up_to(ys1[0].shape[0], 8)
    out_rows = ys1[2]
    mats = [*z1_mats, *z2_mats, *ya2[:2], *ys2[:2], *ys1[:2]]
    lane_half = z1_len // 2

    def kernel(table_ref, index_ref, b_ref, l_ref, r_ref, *refs):
        z1s, z2a, z2s, a2, s2, s1 = [refs[2 * i : 2 * i + 2] for i in range(6)]
        approx, up, down, c1, p1 = refs[12:]
        sides = {
            "l1": lambda: l_ref[0:rows],
            "l2": lambda: l_ref[rows : 2 * rows],
            "r1": lambda: r_ref[0:rows],
            "r2": lambda: r_ref[rows : 2 * rows],
        }
        get = lambda key: sides[key]() if isinstance(key, str) else b_ref[key]
        lowpart = lambda c: b_ref[c, :low_rows]
        dims = (rows, nz)
        quiet = limits_plane(table_ref, index_ref, 1, 0, dims, low_rows, lane_half, NOTHING)
        loud = limits_plane(table_ref, index_ref, 1, 1, dims, low_rows, lane_half, NOTHING)
        planes = []
        for k in range(n2):
            low = x_low(get, k, n1)
            planes.append(low[:low_rows])
            c1[k] = shrink(low, quiet)
            c1[n2 + k] = shrink(x_high(get, k, n1), loud)
        packed = l_ref[2 * rows :]
        planes.append(packed + added([(H[5 + i], lowpart(i)) for i in range(3)]))
        planes.append(pltpu.roll(packed, lane_half, 1) + H[1] * H[7] * lowpart(0))
        packed = r_ref[2 * rows :]
        planes.append(packed + added([(H[i], lowpart(n1 - 3 + i)) for i in range(3)]))
        planes.append(pltpu.roll(packed, lane_half, 1) + H[6] * H[0] * lowpart(n1 - 1))
        zed = times(jnp.concatenate(planes, axis=0), z2a)
        third = [left_times(a2, zed[i * low_rows : (i + 1) * low_rows]) for i in range(len(planes))]
        keys = {"l1": n2, "l2": n2 + 1, "r1": n2 + 2, "r2": n2 + 3}
        get2 = lambda key: third[keys.get(key, key)]
        dims = (rows2, nz)
        quiet = limits_plane(table_ref, index_ref, 2, 0, dims, rows2 // 2, lane_half // 2, 0.0)
        loud = limits_plane(table_ref, index_ref, 2, 1, dims, rows2 // 2, lane_half // 2, 0.0)
        kept = [shrink(x_low(get2, k, n2), quiet) for k in range(n3)]
        kept += [shrink(x_high(get2, k, n2), loud) for k in range(n3)]
        zed = times(jnp.concatenate(kept, axis=0), z2s)
        parts = [left_times(s2, zed[i * rows2 : (i + 1) * rows2])[:low_rows] for i in range(2 * n3)]
        lows = dict(enumerate(parts[:n3]))
        highs = dict(enumerate(parts[n3:]))
        ghosts = [-3, -2, -1, n2, n2 + 1, n2 + 2]
        for k in range(n2):
            c1[k, :low_rows] += x_synth(k, lows, highs)
        stack = [x_synth(k, lows, highs) for k in ghosts]
        pad = jnp.zeros((rows - low_rows, nz), F32)
        stack_zed = times(jnp.concatenate(stack, axis=0), z1s)
        for i in range(6):
            plane = jnp.concatenate([stack_zed[i * low_rows : (i + 1) * low_rows], pad], axis=0)
            p1[2 * n2 + i] = left_times(s1, plane)[:out_rows]
        for i in range(0, 2 * n2, 4):
            zed = times(c1[i : i + 4].reshape(4 * rows, nz), z1s)
            for j in range(4):
                p1[i + j] = left_times(s1, zed[j * rows : (j + 1) * rows])[:out_rows]
        lows = {k: p1.at[k] for k in range(n2)}
        highs = {k: p1.at[n2 + k] for k in range(n2)}
        for i, k in enumerate(ghosts):
            lows[k] = p1.at[2 * n2 + i]

        def cell(m):
            near = lambda part: {k: ref[...] for k, ref in part.items() if 0 <= m + 3 - 2 * k < 8}
            return x_synth(m, near(lows), near(highs))

        for m in range(-2, n1 + 2):
            approx[m + 2] = cell(m)
        value = lambda part, ks: {k: part[k][...] for k in ks}
        ends = (n2 - 2, n2 - 1)
        up[0], up[1] = approx[n1], approx[n1 + 1]
        up[2], up[3] = spill_up(value(lows, ends), value(highs, ends), n2)
        up[4], up[5] = lows[n2][...], lows[n2 + 1][...]
        down[0], down[1] = approx[2], approx[3]
        down[2], down[3] = spill_down(value(lows, (0, 1)), value(highs, (0, 1)))
        down[4], down[5] = lows[-1][...], lows[-2][...]

    return call(
        kernel,
        (1,),
        [SMEM, SMEM] + [whole(a) for a in (bands, left, right, *mats)],
        [whole_out(n1 + 4, out_rows, nz), whole_out(6, out_rows, nz), whole_out(6, out_rows, nz)],
        [shape(n1 + 4, out_rows, nz), shape(6, out_rows, nz), shape(6, out_rows, nz)],
        [table, index, bands, left, right, *mats],
        1.5e9,
        8 * n1 * rows * nz,
        scratch=[pltpu.VMEM((2 * n2, rows, nz), F32), pltpu.VMEM((2 * n2 + 6, out_rows, nz), F32)],
        name="coarse",
    )


def final(approx, left, right, detail, e_left, e_right, z_matrix, y_matrix):
    planes, rows, half_z = approx.shape
    nx, ny, nz = detail.shape
    n1 = nx // 2
    n2 = n1 // 2
    step_rows = 16

    def kernel(a_ref, l_ref, r_ref, d_ref, el, er, z0, z1, y0, y1, out, total, parts):
        @pl.when(pl.program_id(0) == 0)
        def _():
            for m in range(n1):
                terms = [(1.0, a_ref[m + 2])]
                for k, coef, source in ((0, 1.0, 4), (1, 1.0, 5), (2, THIRD_UP, 5)):
                    if 0 <= m + 3 - 2 * k < 8:
                        terms.append((coef * H[m + 3 - 2 * k], l_ref[source]))
                for k, coef, source in ((n2 - 1, 1.0, 4), (n2 - 2, 1.0, 5), (n2 - 3, THIRD_DOWN, 5)):
                    if 0 <= m + 3 - 2 * k < 8:
                        terms.append((coef * H[m + 3 - 2 * k], r_ref[source]))
                if m < 3:
                    terms.append(((1.0, 1.0, THIRD_UP)[m], l_ref[(2, 3, 3)[m]]))
                if m >= n1 - 3:
                    terms.append(((1.0, 1.0, THIRD_DOWN)[n1 - 1 - m], r_ref[(2, 3, 3)[n1 - 1 - m]]))
                total[m + 2] = added(terms)
            total[0] = a_ref[0] + l_ref[0]
            total[1] = a_ref[1] + l_ref[1]
            total[n1 + 2] = a_ref[n1 + 2] + r_ref[0]
            total[n1 + 3] = a_ref[n1 + 3] + r_ref[1]
            for i in range(0, planes, 4):
                zed = times(total[i : i + 4].reshape(4 * rows, half_z), (z0, z1))
                for j in range(4):
                    parts[i + j] = left_times((y0, y1), zed[j * rows : (j + 1) * rows])

        start = pl.program_id(0) * step_rows

        def tile(t, carry):
            at = pl.ds(pl.multiple_of(t * 8, 8), 8)
            within = pl.ds(pl.multiple_of(start + t * 8, 8), 8)
            for lane in range(0, nz, 128):
                lanes = pl.ds(lane, 128)
                for m in range(nx):
                    ks = [k for k in range(-2, n1 + 2) if 0 <= m + 3 - 2 * k < 8]
                    value = d_ref[m, at, lanes] + x_synth(m, {k: parts[k + 2, within, lanes] for k in ks}, {})
                    if m < 3:
                        extra = el[(0, 1, 1)[m], at, lanes]
                        value += extra if m < 2 else THIRD_UP * extra
                    if m >= nx - 3:
                        extra = er[(0, 1, 1)[nx - 1 - m], at, lanes]
                        value += extra if m > nx - 3 else THIRD_DOWN * extra
                    out[m, at, lanes] = value
            return carry

        lax.fori_loop(0, step_rows // 8, tile, 0)

    block = pl.BlockSpec((nx, step_rows, nz), lambda i: (0, i, 0))
    side = pl.BlockSpec((2, step_rows, nz), lambda i: (0, i, 0))
    return call(
        kernel,
        (ny // step_rows,),
        [whole(approx), whole(left), whole(right), block, side, side]
        + [whole(m) for m in z_matrix + y_matrix],
        block,
        shape(nx, ny, nz),
        [approx, left, right, detail, e_left, e_right, *z_matrix, *y_matrix],
        8 * nx * ny * nz,
        8 * nx * ny * nz,
        scratch=[pltpu.VMEM((planes, rows, half_z), F32), pltpu.VMEM((planes, ny, nz), F32)],
        name="final",
    )


def to_next(array, axis):
    size = lax.axis_size(axis)
    return lax.ppermute(array, axis, [(i, (i + 1) % size) for i in range(size)])


def to_previous(array, axis):
    size = lax.axis_size(axis)
    return lax.ppermute(array, axis, [((i + 1) % size, i) for i in range(size)])


def local(velocity, table, index):
    nx, ny, nz = velocity.shape
    y1, y2, y3 = ny // 2, ny // 4, ny // 8
    ghost = 24
    cells0 = list(range(-8, ny + 8))
    rows0 = up_to(y1 + 4, 8)
    ks0 = fill(list(range(y1)) + [-2, -1, y1, y1 + 1], rows0)
    cells1 = list(range(y1)) + list(range(-ghost, 0)) + list(range(y1, y1 + ghost))
    rows1 = up_to(y2 + 18, 8)
    ks1 = fill(list(range(-9, y2 + 9)), rows1)
    rows2 = up_to(y3 + 6, 8)
    ks2 = fill(list(range(-3, y3 + 3)), rows2)
    ya0 = pieces(analysis_rows(cells0, ks0))
    ys0_matrix = synthesis_rows(list(range(ny)), ks0)
    ys0 = pieces(ys0_matrix)
    ys0_low = pieces(ys0_matrix[:, :rows0])
    ya1 = pieces(analysis_rows(cells1, ks1))
    ys1 = pieces(synthesis_rows(ks0, ks1)) + [rows0]
    ya2 = pieces(analysis_rows(ks1, ks2))
    ys2 = pieces(synthesis_rows(ks1, ks2))
    z0 = periodic(nz, nz)
    z1 = periodic(nz // 2, nz // 2)
    z2 = periodic(nz // 4, nz // 2)
    za0, zs0, zs0_low = pieces(z0), pieces(z0.T), pieces(z0.T[: nz // 2])
    za1, zs1 = pieces(z1), pieces(z1.T)
    za2, zs2 = pieces(z2), pieces(z2.T)

    x_up, x_down, y_up, y_down = first_messages(velocity)
    x_left = to_next(x_up, "gx")
    x_right = to_previous(x_down, "gx")
    y_left = to_next(y_up, "gy")
    y_right = to_previous(y_down, "gy")
    zed = depth_analysis(velocity, za0)
    c_up, c_down = corner_messages(y_left, y_right)
    c_left = to_next(c_up, "gx")
    c_right = to_previous(c_down, "gx")
    bands = y_analysis(zed, y_left, y_right, za0, ya0)
    halo, approx, a_up, a_down = first_approx(
        bands, x_left, x_right, c_left, c_right, za0, ya0, y1, ghost
    )
    a_left = to_next(a_up, "gy")
    a_right = to_previous(a_down, "gy")
    coeffs = detail_bands(bands, halo, table, index)
    bands1, b_up, b_down = second_bands(approx, a_left, a_right, za1, ya1, rows1)
    b_left = to_next(b_up, "gx")
    b_right = to_previous(b_down, "gx")
    parts, e_up, e_down = detail_yz(coeffs, zs0, ys0)
    e_left = to_next(e_up, "gx")
    e_right = to_previous(e_down, "gx")
    approx1, s_up, s_down = coarse(
        bands1, b_left, b_right, table, index, zs1, za2 + zs2, ya2, ys2, ys1, rows1, nz // 2
    )
    s_left = to_next(s_up, "gx")
    s_right = to_previous(s_down, "gx")
    detail = detail_x(parts)
    return final(approx1, s_left, s_right, detail, e_left, e_right, zs0_low, ys0_low)


def solution(mesh):
    return jax.shard_map(
        local,
        mesh=mesh,
        in_specs=(P("gx", "gy", None), P(), P()),
        out_specs=P("gx", "gy", None),
        check_vma=False,
    )
```

profile of v0, /device:TPU:0, one launch (start us, length us, event | category | flops | bytes accessed | tf_op | source)
XLA Modules:
  0.0 105.7 jit_solution(15427826268640664222)
XLA Ops:
  0.0 2.4 %first_messages.1 = (f32[2,128,256]{2,1,0:T(8,128)}, f32[2,128,256]{2,1,0:T(8,128)}, f32[32,8,256]{2,1,0:T(8,128)}, f32[32,8,256]{2,1,0:T(8,128)}) custom-call(f32[32,128,256]{2,1,0:T(8,128)} %y_first.1, f32[32,128,256]{2,1,0:T(8,128)} %y_first.1, f32[32,128,256]{2,1,0:T(8,128)} %y_first.1, f32[32,128,256]{2,1,0:T(8,128)} %y_first.1), custom_call_target="tpu_custom_call" | custom-call | flops 1000000 | bytes 3000000 | tf_op jit(solution)/shard_map/first_messages/pallas_call | solution.py:152
  2.4 0.5 collective-permute-start
  2.8 2.0 %collective-permute-start.1 = (f32[32,8,256]{2,1,0:T(8,128)}, f32[32,8,256]{2,1,0:T(8,128)S(1)}, u32[]{:S(2)}, u32[]{:S(2)}) collective-permute-start(f32[32,8,256]{2,1,0:T(8,128)} %get-tuple-element.25), channel_id=1, source_target_pairs={{1,0},{2,1},{3,2},{0,3},{5,4},{6,5},{7,6},{4,7},{9,8},{10,9},{11,1... | collective-permute-start | bytes 786440 | tf_op jit(solution)/shard_map/ppermute | solution.py:698
  4.8 2.3 %collective-permute-start.2 = (f32[2,128,256]{2,1,0:T(8,128)}, f32[2,128,256]{2,1,0:T(8,128)S(1)}, u32[]{:S(2)}, u32[]{:S(2)}) collective-permute-start(f32[2,128,256]{2,1,0:T(8,128)} %get-tuple-element.26), channel_id=1, source_target_pairs={{0,4},{4,8},{8,12},{12,16},{16,20},{20,24},{24,28},{28,0},{1,5},{5... | collective-permute-start | bytes 786440 | tf_op jit(solution)/shard_map/ppermute | solution.py:693
  7.1 3.0 %collective-permute-start.3 = (f32[2,128,256]{2,1,0:T(8,128)}, f32[2,128,256]{2,1,0:T(8,128)S(1)}, u32[]{:S(2)}, u32[]{:S(2)}) collective-permute-start(f32[2,128,256]{2,1,0:T(8,128)} %get-tuple-element.27), channel_id=1, source_target_pairs={{4,0},{8,4},{12,8},{16,12},{20,16},{24,20},{28,24},{0,28},{5,1},{9... | collective-permute-start | bytes 786440 | tf_op jit(solution)/shard_map/ppermute | solution.py:698
  10.1 7.8 %depth_analysis.1.zed_ref = f32[32,128,256]{2,1,0:T(8,128)} custom-call(f32[32,128,256]{2,1,0:T(8,128)} %y_first.1, bf16[256,256]{1,0:T(8,128)(2,1)} %constant.56.clone.z0, bf16[256,256]{1,0:T(8,128)(2,1)} %constant.57.clone.z1), custom_call_target="tpu_custom_call" | custom-call | flops 1610612736 | bytes 8388608 | tf_op jit(solution)/shard_map/depth_analysis/pallas_call | solution.py:152
  17.9 0.0 collective-permute-done.left.last_l.first_l
  17.9 0.0 collective-permute-done.1.right.last_r.first_r
  17.9 0.7 copy-done
  18.6 0.7 copy-done.1
  19.3 1.4 %corner_messages.1 = (f32[2,16,256]{2,1,0:T(8,128)}, f32[2,16,256]{2,1,0:T(8,128)}) custom-call(f32[32,8,256]{2,1,0:T(8,128)} %copy-done, f32[32,8,256]{2,1,0:T(8,128)} %copy-done, f32[32,8,256]{2,1,0:T(8,128)} %copy-done.1, f32[32,8,256]{2,1,0:T(8,128)} %copy-done.1), custom_call_target="tpu_custom_call" | custom-call | flops 100000 | bytes 200000 | tf_op jit(solution)/shard_map/corner_messages/pallas_call | solution.py:152
  20.8 0.0 collective-permute-start.4
  20.8 4.7 %collective-permute-start.5 = (f32[2,16,256]{2,1,0:T(8,128)}, f32[2,16,256]{2,1,0:T(8,128)S(1)}, u32[]{:S(2)}, u32[]{:S(2)}) collective-permute-start(f32[2,16,256]{2,1,0:T(8,128)} %get-tuple-element.29), channel_id=1, source_target_pairs={{4,0},{8,4},{12,8},{16,12},{20,16},{24,20},{28,24},{0,28},{5,1},{9... | collective-permute-start | bytes 98312 | tf_op jit(solution)/shard_map/ppermute | solution.py:698
  25.5 9.3 %y_analysis.1.b_ref = f32[32,144,256]{2,1,0:T(8,128)} custom-call(f32[32,128,256]{2,1,0:T(8,128)} %depth_analysis.1.zed_ref, f32[32,8,256]{2,1,0:T(8,128)} %copy-done, f32[32,8,256]{2,1,0:T(8,128)} %copy-done.1, bf16[256,256]{1,0:T(8,128)(2,1)} %constant.56.clone.z0, bf16[256,256]{1,0:T(8,128)(2,1)} %constant.57.clone.z1, ...), custom_call_target="tpu_custom_call" | custom-call | flops 1019215872 | bytes 9437184 | tf_op jit(solution)/shard_map/y_analysis/pallas_call | solution.py:152
  34.8 0.0 collective-permute-done.2.xl
  34.8 0.0 collective-permute-done.3.xr
  34.9 0.0 collective-permute-done.4.cl
  34.9 0.0 collective-permute-done.5.cr
  34.9 0.7 copy-done.4
  35.6 0.1 copy-done.5
  35.6 0.0 copy-done.8
  35.6 0.6 copy-done.9
  36.2 4.0 %first_approx.1 = (f32[4,144,256]{2,1,0:T(8,128)}, f32[16,64,128]{2,1,0:T(8,128)}, f32[16,24,128]{2,1,0:T(8,128)}, f32[16,24,128]{2,1,0:T(8,128)}) custom-call(f32[32,144,256]{2,1,0:T(8,128)} %y_analysis.1.b_ref, f32[2,128,256]{2,1,0:T(8,128)} %copy-done.4, f32[2,128,256]{2,1,0:T(8,128)} %copy-done.5, f32[2,16,256]{2,1,0:T(8,128)} %copy-done.8, ...), custom_call_target="tpu_custom_call" | custom-call | flops 353894400 | bytes 6000000 | tf_op jit(solution)/shard_map/first_approx/pallas_call | solution.py:152
  40.2 0.0 collective-permute-start.6
  40.3 1.8 %collective-permute-start.7 = (f32[16,24,128]{2,1,0:T(8,128)}, f32[16,24,128]{2,1,0:T(8,128)S(1)}, u32[]{:S(2)}, u32[]{:S(2)}) collective-permute-start(f32[16,24,128]{2,1,0:T(8,128)} %get-tuple-element.32), channel_id=1, source_target_pairs={{1,0},{2,1},{3,2},{0,3},{5,4},{6,5},{7,6},{4,7},{9,8},{10,9},{11,1... | collective-permute-start | bytes 589832 | tf_op jit(solution)/shard_map/ppermute | solution.py:698
  42.0 7.2 %detail_bands.1.c_ref = f32[32,144,256]{2,1,0:T(8,128)} custom-call(f32[16]{0:T(128)} %table_ref.3, s32[3,7]{1,0:T(4,128)} %index_ref.3, f32[32,144,256]{2,1,0:T(8,128)} %y_analysis.1.b_ref, f32[4,144,256]{2,1,0:T(8,128)} %get-tuple-element.39.h_ref), custom_call_target="tpu_custom_call" | custom-call | flops 47185920 | bytes 9437184 | tf_op jit(solution)/shard_map/detail_bands/pallas_call | solution.py:152
  49.2 0.0 collective-permute-done.6.l_ref
  49.2 0.0 collective-permute-done.7.r_ref
  49.2 0.7 copy-done.10
  49.9 0.1 copy-done.11
  49.9 4.2 %second_bands.1 = (f32[16,112,128]{2,1,0:T(8,128)}, f32[280,128]{1,0:T(8,128)}, f32[280,128]{1,0:T(8,128)}) custom-call(f32[16,64,128]{2,1,0:T(8,128)} %get-tuple-element.30.o_ref, f32[16,24,128]{2,1,0:T(8,128)} %copy-done.10, f32[16,24,128]{2,1,0:T(8,128)} %copy-done.11, bf16[128,128]{1,0:T(8,128)(2,1)} %constant.60.clone.z0, ...), custom_call_target="tpu_custom_call" | custom-call | flops 330301440 | bytes 1835008 | tf_op jit(solution)/shard_map/second_bands/pallas_call | solution.py:152
  54.2 4.7 %collective-permute-start.9 = (f32[280,128]{1,0:T(8,128)}, f32[280,128]{1,0:T(8,128)S(1)}, u32[]{:S(2)}, u32[]{:S(2)}) collective-permute-start(f32[280,128]{1,0:T(8,128)} %get-tuple-element.35), channel_id=1, source_target_pairs={{4,0},{8,4},{12,8},{16,12},{20,16},{24,20},{28,24},{0,28},{5,1},{9... | collective-permute-start | bytes 430088 | tf_op jit(solution)/shard_map/ppermute | solution.py:698
  58.9 11.2 %detail_yz.1 = (f32[32,128,256]{2,1,0:T(8,128)}, f32[2,128,256]{2,1,0:T(8,128)}, f32[2,128,256]{2,1,0:T(8,128)}) custom-call(f32[32,144,256]{2,1,0:T(8,128)} %detail_bands.1.c_ref, bf16[256,256]{1,0:T(8,128)(2,1)} %constant.64.clone.z0, bf16[256,256]{1,0:T(8,128)(2,1)} %constant.65.clone.z1, bf16[128,144]{1,0:T(8,128)(2,1)} %constant.66.clone.y0, ...), custom_call_target="tpu_custom_call" | custom-call | flops 2717908992 | bytes 8912896 | tf_op jit(solution)/shard_map/detail_yz/pallas_call | solution.py:152
  70.1 4.7 %collective-permute-start.13 = (f32[2,128,256]{2,1,0:T(8,128)}, f32[2,128,256]{2,1,0:T(8,128)S(1)}, u32[]{:S(2)}, u32[]{:S(2)}) collective-permute-start(f32[2,128,256]{2,1,0:T(8,128)} %get-tuple-element.42), channel_id=1, source_target_pairs={{4,0},{8,4},{12,8},{16,12},{20,16},{24,20},{28,24},{0,28},{5,1},{9... | collective-permute-start | bytes 786440 | tf_op jit(solution)/shard_map/ppermute | solution.py:698
  74.8 0.0 collective-permute-done.8.l_ref
  74.8 0.6 copy-done.12
  75.4 0.1 copy-done.13
  75.5 6.4 %coarse.1 = (f32[20,72,128]{2,1,0:T(8,128)}, f32[6,72,128]{2,1,0:T(8,128)}, f32[6,72,128]{2,1,0:T(8,128)}) custom-call(f32[16]{0:T(128)} %table_ref.3, s32[3,7]{1,0:T(4,128)} %index_ref.3, f32[16,112,128]{2,1,0:T(8,128)} %get-tuple-element.33.b_ref, f32[280,128]{1,0:T(8,128)} %copy-done.12, f32[280,128]{1,0:T(8,128)} %copy-done.13, ...), custom_call_target="tpu_custom_call" | custom-call | flops 1500000000 | bytes 1835008 | tf_op jit(solution)/shard_map/coarse/pallas_call | solution.py:152
  81.9 0.0 collective-permute-start.10
  81.9 4.7 %collective-permute-start.11 = (f32[6,72,128]{2,1,0:T(8,128)}, f32[6,72,128]{2,1,0:T(8,128)S(1)}, u32[]{:S(2)}, u32[]{:S(2)}) collective-permute-start(f32[6,72,128]{2,1,0:T(8,128)} %get-tuple-element.38), channel_id=1, source_target_pairs={{4,0},{8,4},{12,8},{16,12},{20,16},{24,20},{28,24},{0,28},{5,1},{9... | collective-permute-start | bytes 663560 | tf_op jit(solution)/shard_map/ppermute | solution.py:698
  86.6 7.6 %detail_x.1.d_ref = f32[32,128,256]{2,1,0:T(8,128)} custom-call(f32[32,128,256]{2,1,0:T(8,128)} %get-tuple-element.40.p_ref), custom_call_target="tpu_custom_call" | custom-call | flops 16777216 | bytes 8388608 | tf_op jit(solution)/shard_map/detail_x/pallas_call | solution.py:152
  94.2 0.0 collective-permute-done.10.l_ref
  94.2 0.0 collective-permute-done.11.r_ref
  94.2 0.7 copy-done.2
  94.9 0.1 copy-done.3
  95.0 0.1 copy-done.6
  95.1 0.1 copy-done.7
  95.1 10.5 %final.1 = f32[32,128,256]{2,1,0:T(8,128)} custom-call(f32[20,72,128]{2,1,0:T(8,128)} %get-tuple-element.36.a_ref, f32[6,72,128]{2,1,0:T(8,128)} %copy-done.6, f32[6,72,128]{2,1,0:T(8,128)} %copy-done.7, f32[32,128,256]{2,1,0:T(8,128)} %detail_x.1.d_ref, f32[2,128,256]{2,1,0:T(8,128)} %copy-done.2, f32[2,128,256]{2,1,0:T(8,128)} %copy-done.3, ...), custom_call_target="tpu_custom_call" | custom-call | flops 8388608 | bytes 8388608 | tf_op jit(solution)/shard_map/final/pallas_call | solution.py:152
  (19 shorter events, 0.0 us)
Async XLA Ops:
  2.4 15.5 %collective-permute-start = (f32[32,8,256]{2,1,0:T(8,128)}, f32[32,8,256]{2,1,0:T(8,128)S(1)}, u32[]{:S(2)}, u32[]{:S(2)}) collective-permute-start(f32[32,8,256]{2,1,0:T(8,128)} %get-tuple-element.24), channel_id=1, source_target_pairs={{0,1},{1,2},{2,3},{3,0},{4,5},{5,6},{6,7},{7,4},{8,9},{9,10},{10,1... | collective-permute-start | bytes 786440 | tf_op jit(solution)/shard_map/ppermute | solution.py:693
  2.8 15.1 %collective-permute-start.1 = (f32[32,8,256]{2,1,0:T(8,128)}, f32[32,8,256]{2,1,0:T(8,128)S(1)}, u32[]{:S(2)}, u32[]{:S(2)}) collective-permute-start(f32[32,8,256]{2,1,0:T(8,128)} %get-tuple-element.25), channel_id=1, source_target_pairs={{1,0},{2,1},{3,2},{0,3},{5,4},{6,5},{7,6},{4,7},{9,8},{10,9},{11,1... | collective-permute-start | bytes 786440 | tf_op jit(solution)/shard_map/ppermute | solution.py:698
  4.8 30.1 %collective-permute-start.2 = (f32[2,128,256]{2,1,0:T(8,128)}, f32[2,128,256]{2,1,0:T(8,128)S(1)}, u32[]{:S(2)}, u32[]{:S(2)}) collective-permute-start(f32[2,128,256]{2,1,0:T(8,128)} %get-tuple-element.26), channel_id=1, source_target_pairs={{0,4},{4,8},{8,12},{12,16},{16,20},{20,24},{24,28},{28,0},{1,5},{5... | collective-permute-start | bytes 786440 | tf_op jit(solution)/shard_map/ppermute | solution.py:693
  7.1 27.8 %collective-permute-start.3 = (f32[2,128,256]{2,1,0:T(8,128)}, f32[2,128,256]{2,1,0:T(8,128)S(1)}, u32[]{:S(2)}, u32[]{:S(2)}) collective-permute-start(f32[2,128,256]{2,1,0:T(8,128)} %get-tuple-element.27), channel_id=1, source_target_pairs={{4,0},{8,4},{12,8},{16,12},{20,16},{24,20},{28,24},{0,28},{5,1},{9... | collective-permute-start | bytes 786440 | tf_op jit(solution)/shard_map/ppermute | solution.py:698
  17.9 0.7 copy-start
  18.6 0.7 copy-start.1
  20.8 14.1 %collective-permute-start.4 = (f32[2,16,256]{2,1,0:T(8,128)}, f32[2,16,256]{2,1,0:T(8,128)S(1)}, u32[]{:S(2)}, u32[]{:S(2)}) collective-permute-start(f32[2,16,256]{2,1,0:T(8,128)} %get-tuple-element.28), channel_id=1, source_target_pairs={{0,4},{4,8},{8,12},{12,16},{16,20},{20,24},{24,28},{28,0},{1,5},{5... | collective-permute-start | bytes 98312 | tf_op jit(solution)/shard_map/ppermute | solution.py:693
  20.8 14.1 %collective-permute-start.5 = (f32[2,16,256]{2,1,0:T(8,128)}, f32[2,16,256]{2,1,0:T(8,128)S(1)}, u32[]{:S(2)}, u32[]{:S(2)}) collective-permute-start(f32[2,16,256]{2,1,0:T(8,128)} %get-tuple-element.29), channel_id=1, source_target_pairs={{4,0},{8,4},{12,8},{16,12},{20,16},{24,20},{28,24},{0,28},{5,1},{9... | collective-permute-start | bytes 98312 | tf_op jit(solution)/shard_map/ppermute | solution.py:698
  34.8 0.7 copy-start.4
  34.8 0.8 copy-start.5
  34.9 0.8 copy-start.8
  35.6 0.6 copy-start.9
  40.2 9.0 %collective-permute-start.6 = (f32[16,24,128]{2,1,0:T(8,128)}, f32[16,24,128]{2,1,0:T(8,128)S(1)}, u32[]{:S(2)}, u32[]{:S(2)}) collective-permute-start(f32[16,24,128]{2,1,0:T(8,128)} %get-tuple-element.31), channel_id=1, source_target_pairs={{0,1},{1,2},{2,3},{3,0},{4,5},{5,6},{6,7},{7,4},{8,9},{9,10},{10,1... | collective-permute-start | bytes 589832 | tf_op jit(solution)/shard_map/ppermute | solution.py:693
  40.3 9.0 %collective-permute-start.7 = (f32[16,24,128]{2,1,0:T(8,128)}, f32[16,24,128]{2,1,0:T(8,128)S(1)}, u32[]{:S(2)}, u32[]{:S(2)}) collective-permute-start(f32[16,24,128]{2,1,0:T(8,128)} %get-tuple-element.32), channel_id=1, source_target_pairs={{1,0},{2,1},{3,2},{0,3},{5,4},{6,5},{7,6},{4,7},{9,8},{10,9},{11,1... | collective-permute-start | bytes 589832 | tf_op jit(solution)/shard_map/ppermute | solution.py:698
  49.2 0.7 copy-start.10
  49.2 0.7 copy-start.11
  54.2 20.6 %collective-permute-start.8 = (f32[280,128]{1,0:T(8,128)}, f32[280,128]{1,0:T(8,128)S(1)}, u32[]{:S(2)}, u32[]{:S(2)}) collective-permute-start(f32[280,128]{1,0:T(8,128)} %get-tuple-element.34), channel_id=1, source_target_pairs={{0,4},{4,8},{8,12},{12,16},{16,20},{20,24},{24,28},{28,0},{1,5},{5... | collective-permute-start | bytes 430088 | tf_op jit(solution)/shard_map/ppermute | solution.py:693
  54.2 20.6 %collective-permute-start.9 = (f32[280,128]{1,0:T(8,128)}, f32[280,128]{1,0:T(8,128)S(1)}, u32[]{:S(2)}, u32[]{:S(2)}) collective-permute-start(f32[280,128]{1,0:T(8,128)} %get-tuple-element.35), channel_id=1, source_target_pairs={{4,0},{8,4},{12,8},{16,12},{20,16},{24,20},{28,24},{0,28},{5,1},{9... | collective-permute-start | bytes 430088 | tf_op jit(solution)/shard_map/ppermute | solution.py:698
  70.0 24.1 %collective-permute-start.12 = (f32[2,128,256]{2,1,0:T(8,128)}, f32[2,128,256]{2,1,0:T(8,128)S(1)}, u32[]{:S(2)}, u32[]{:S(2)}) collective-permute-start(f32[2,128,256]{2,1,0:T(8,128)} %get-tuple-element.41), channel_id=1, source_target_pairs={{0,4},{4,8},{8,12},{12,16},{16,20},{20,24},{24,28},{28,0},{1,5},{5... | collective-permute-start | bytes 786440 | tf_op jit(solution)/shard_map/ppermute | solution.py:693
  70.1 24.1 %collective-permute-start.13 = (f32[2,128,256]{2,1,0:T(8,128)}, f32[2,128,256]{2,1,0:T(8,128)S(1)}, u32[]{:S(2)}, u32[]{:S(2)}) collective-permute-start(f32[2,128,256]{2,1,0:T(8,128)} %get-tuple-element.42), channel_id=1, source_target_pairs={{4,0},{8,4},{12,8},{16,12},{20,16},{24,20},{28,24},{0,28},{5,1},{9... | collective-permute-start | bytes 786440 | tf_op jit(solution)/shard_map/ppermute | solution.py:698
  74.8 0.6 copy-start.12
  74.8 0.7 copy-start.13
  81.9 12.3 %collective-permute-start.10 = (f32[6,72,128]{2,1,0:T(8,128)}, f32[6,72,128]{2,1,0:T(8,128)S(1)}, u32[]{:S(2)}, u32[]{:S(2)}) collective-permute-start(f32[6,72,128]{2,1,0:T(8,128)} %get-tuple-element.37), channel_id=1, source_target_pairs={{0,4},{4,8},{8,12},{12,16},{16,20},{20,24},{24,28},{28,0},{1,5},{5... | collective-permute-start | bytes 663560 | tf_op jit(solution)/shard_map/ppermute | solution.py:693
  81.9 12.3 %collective-permute-start.11 = (f32[6,72,128]{2,1,0:T(8,128)}, f32[6,72,128]{2,1,0:T(8,128)S(1)}, u32[]{:S(2)}, u32[]{:S(2)}) collective-permute-start(f32[6,72,128]{2,1,0:T(8,128)} %get-tuple-element.38), channel_id=1, source_target_pairs={{4,0},{8,4},{12,8},{16,12},{20,16},{24,20},{28,24},{0,28},{5,1},{9... | collective-permute-start | bytes 663560 | tf_op jit(solution)/shard_map/ppermute | solution.py:698
  94.2 0.7 copy-start.2
  94.2 0.8 copy-start.3
  94.2 0.9 copy-start.6
  94.2 0.9 copy-start.7
where the time goes:
time: 107 us; the launch traced here: 106 us
  Pallas kernels  72 us (67%)
  starting transfers between devices  28.4 us (27%)
  local copies, waits for them, and re-layouts  5.1 us (5%)
    pallas_call x11, Pallas kernels, call(): pl.pallas_call(kernel, grid=grid, in_specs=in_specs, out_specs=out_specs,...  72 us
    ppermute x7, starting transfers between devices, to_previous(): return lax.ppermute(array, axis, [((i + 1) % size, i) for i in range(size)])  25.6 us
    unnamed x28, local copies, waits for them, and re-layouts  5.1 us
    ppermute x7, starting transfers between devices, to_next(): return lax.ppermute(array, axis, [(i, (i + 1) % size) for i in range(size)])  2.74 us
  transfers between devices with their start and end apart: 14, of which 0 were waited for; matrix products, arithmetic and copies ran while one was open for 0% of the time, Pallas kernels for 48%

commit v1 on v0

--- a/solution.py
+++ b/solution.py
@@ -23,7 +23,7 @@
 F32 = jnp.float32
 BF16 = jnp.bfloat16
 NOTHING = 3.0e38
-VMEM_BYTES = 56 * 1024 * 1024
+VMEM_BYTES = 16 * 1024 * 1024
 
 
 def tap(filt, j):

time: 107 us -> 77.5 us (0.72); the launches traced: 106 us -> 77.4 us
  Pallas kernels: 72 us -> 39.3 us
  waiting for transfers between devices: 0.04 us -> 6.63 us
  local copies, waits for them, and re-layouts: 5.1 us -> 2.36 us
    pallas_call x11, Pallas kernels: 72 us -> 39.3 us  [call(): pl.pallas_call(kernel, grid=grid, in_specs=in_specs, out_specs=out_specs,...]
    ppermute x7, waiting for transfers between devices: 0.02 us -> 5.25 us  [to_previous(): return lax.ppermute(array, axis, [((i + 1) % size, i) for i in range(size)])]
    unnamed x28 -> x62, local copies, waits for them, and re-layouts: 5.1 us -> 2.36 us
    ppermute x7, waiting for transfers between devices: 0.02 us -> 1.38 us  [to_next(): return lax.ppermute(array, axis, [(i, (i + 1) % size) for i in range(size)])]
  transfers between devices with their start and end apart: 14 -> 14, of which waited for: 0 -> 4; matrix products, arithmetic and copies ran while one was open for 0% -> 0% of each run, Pallas kernels for 48% -> 37%
where the time goes in v1:
time: 77.5 us; the launch traced here: 77.4 us
  Pallas kernels  39.3 us (51%)
  starting transfers between devices  28.7 us (37%)
  waiting for transfers between devices  6.63 us (9%)
  local copies, waits for them, and re-layouts  2.36 us (3%)
    pallas_call x11, Pallas kernels, call(): pl.pallas_call(kernel, grid=grid, in_specs=in_specs, out_specs=out_specs,...  39.3 us
    ppermute x7, starting transfers between devices, to_previous(): return lax.ppermute(array, axis, [((i + 1) % size, i) for i in range(size)])  25.6 us
    ppermute x7, waiting for transfers between devices, to_previous(): return lax.ppermute(array, axis, [((i + 1) % size, i) for i in range(size)])  5.25 us
    ppermute x7, starting transfers between devices, to_next(): return lax.ppermute(array, axis, [(i, (i + 1) % size) for i in range(size)])  3.01 us
    unnamed x62, local copies, waits for them, and re-layouts  2.36 us
  transfers between devices with their start and end apart: 14, of which 4 were waited for; matrix products, arithmetic and copies ran while one was open for 0% of the time, Pallas kernels for 37%

profile of v1, /device:TPU:0, one launch (start us, length us, event | category | flops | bytes accessed | tf_op | source)
XLA Modules:
  0.0 77.4 jit_solution(368504622829334885)
XLA Ops:
  0.0 2.2 %copy-done = f32[32,128,256]{2,1,0:T(8,128)S(1)} copy-done((f32[32,128,256]{2,1,0:T(8,128)S(1)}, f32[32,128,256]{2,1,0:T(8,128)}, u32[]{:S(2)}) %copy-start) | copy-done | bytes 4194328
  2.2 0.1 first_messages.1
  2.3 0.5 collective-permute-start
  2.8 2.0 %collective-permute-start.1 = (f32[32,8,256]{2,1,0:T(8,128)S(1)}, f32[32,8,256]{2,1,0:T(8,128)S(1)}, u32[]{:S(2)}, u32[]{:S(2)}) collective-permute-start(f32[32,8,256]{2,1,0:T(8,128)S(1)} %get-tuple-element.25), channel_id=1, source_target_pairs={{1,0},{2,1},{3,2},{0,3},{5,4},{6,5},{7,6},{4,7},{9,8},{10,9},{11,1... | collective-permute-start | bytes 786440 | tf_op jit(solution)/shard_map/ppermute | solution.py:698
  4.8 2.2 %collective-permute-start.2 = (f32[2,128,256]{2,1,0:T(8,128)S(1)}, f32[2,128,256]{2,1,0:T(8,128)S(1)}, u32[]{:S(2)}, u32[]{:S(2)}) collective-permute-start(f32[2,128,256]{2,1,0:T(8,128)S(1)} %get-tuple-element.26), channel_id=1, source_target_pairs={{0,4},{4,8},{8,12},{12,16},{16,20},{20,24},{24,28},{28,0},{1,5},{5... | collective-permute-start | bytes 786440 | tf_op jit(solution)/shard_map/ppermute | solution.py:693
  7.0 3.0 %collective-permute-start.3 = (f32[2,128,256]{2,1,0:T(8,128)S(1)}, f32[2,128,256]{2,1,0:T(8,128)S(1)}, u32[]{:S(2)}, u32[]{:S(2)}) collective-permute-start(f32[2,128,256]{2,1,0:T(8,128)S(1)} %get-tuple-element.27), channel_id=1, source_target_pairs={{4,0},{8,4},{12,8},{16,12},{20,16},{24,20},{28,24},{0,28},{5,1},{9... | collective-permute-start | bytes 786440 | tf_op jit(solution)/shard_map/ppermute | solution.py:698
  10.1 3.0 %depth_analysis.1.zed_ref = f32[32,128,256]{2,1,0:T(8,128)S(1)} custom-call(f32[32,128,256]{2,1,0:T(8,128)S(1)} %copy-done, bf16[256,256]{1,0:T(8,128)(2,1)S(1)} %copy-done.2, bf16[256,256]{1,0:T(8,128)(2,1)S(1)} %copy-done.1), custom_call_target="tpu_custom_call" | custom-call | flops 1610612736 | bytes 8388608 | tf_op jit(solution)/shard_map/depth_analysis/pallas_call | solution.py:152
  13.2 0.1 collective-permute-start.4
  13.2 4.7 %collective-permute-start.5 = (f32[2,16,256]{2,1,0:T(8,128)S(1)}, f32[2,16,256]{2,1,0:T(8,128)S(1)}, u32[]{:S(2)}, u32[]{:S(2)}) collective-permute-start(f32[2,16,256]{2,1,0:T(8,128)S(1)} %get-tuple-element.29), channel_id=1, source_target_pairs={{4,0},{8,4},{12,8},{16,12},{20,16},{24,20},{28,24},{0,28},{5,1},{9... | collective-permute-start | bytes 98312 | tf_op jit(solution)/shard_map/ppermute | solution.py:698
  17.9 5.3 %y_analysis.1.b_ref = f32[32,144,256]{2,1,0:T(8,128)S(1)} custom-call(f32[32,128,256]{2,1,0:T(8,128)S(1)} %depth_analysis.1.zed_ref, f32[32,8,256]{2,1,0:T(8,128)S(1)} %collective-permute-done.left.last_l.first_l, f32[32,8,256]{2,1,0:T(8,128)S(1)} %collective-permute-done.1.right.last_r.first_r, bf16[256,256]{1,0:T(8,128)(2,1)S(1)} %copy-done.2, ...), custom_call_target="tpu_custom_call" | custom-call | flops 1019215872 | bytes 9437184 | tf_op jit(solution)/shard_map/y_analysis/pallas_call | solution.py:152
  23.3 0.0 copy-start.9
  23.3 1.5 %first_approx.1 = (f32[4,144,256]{2,1,0:T(8,128)S(1)}, f32[16,64,128]{2,1,0:T(8,128)S(1)}, f32[16,24,128]{2,1,0:T(8,128)S(1)}, f32[16,24,128]{2,1,0:T(8,128)S(1)}) custom-call(f32[32,144,256]{2,1,0:T(8,128)S(1)} %y_analysis.1.b_ref, f32[2,128,256]{2,1,0:T(8,128)S(1)} %collective-permute-done.2.xl, f32[2,128,256]{2,1,0:T(8,128)S(1)} %collective-permute-done.3.xr, ...), custom_call_target="tpu_custom_call" | custom-call | flops 353894400 | bytes 6000000 | tf_op jit(solution)/shard_map/first_approx/pallas_call | solution.py:152
  24.9 0.1 collective-permute-start.6
  24.9 1.7 %collective-permute-start.7 = (f32[16,24,128]{2,1,0:T(8,128)S(1)}, f32[16,24,128]{2,1,0:T(8,128)S(1)}, u32[]{:S(2)}, u32[]{:S(2)}) collective-permute-start(f32[16,24,128]{2,1,0:T(8,128)S(1)} %get-tuple-element.32), channel_id=1, source_target_pairs={{1,0},{2,1},{3,2},{0,3},{5,4},{6,5},{7,6},{4,7},{9,8},{10,9},{11,1... | collective-permute-start | bytes 589832 | tf_op jit(solution)/shard_map/ppermute | solution.py:698
  26.7 0.0 copy-start.23
  26.7 0.0 copy-start.24
  26.7 0.0 copy-start.11
  26.7 0.0 copy-start.12
  26.7 0.0 copy-start.13
  26.7 0.0 copy-start.14
  26.7 4.3 %detail_bands.1.c_ref = f32[32,144,256]{2,1,0:T(8,128)S(1)} custom-call(f32[16]{0:T(128)S(1)} %copy-done.10, s32[3,7]{1,0:T(4,128)S(1)} %copy-done.9, f32[32,144,256]{2,1,0:T(8,128)S(1)} %y_analysis.1.b_ref, f32[4,144,256]{2,1,0:T(8,128)S(1)} %get-tuple-element.39.h_ref), custom_call_target="tpu_custom_call" | custom-call | flops 47185920 | bytes 9437184 | tf_op jit(solution)/shard_map/detail_bands/pallas_call | solution.py:152
  31.1 0.2 collective-permute-done.7.r_ref
  31.3 2.0 %second_bands.1 = (f32[16,112,128]{2,1,0:T(8,128)S(1)}, f32[280,128]{1,0:T(8,128)S(1)}, f32[280,128]{1,0:T(8,128)S(1)}) custom-call(f32[16,64,128]{2,1,0:T(8,128)S(1)} %get-tuple-element.30.o_ref, f32[16,24,128]{2,1,0:T(8,128)S(1)} %collective-permute-done.6.l_ref, f32[16,24,128]{2,1,0:T(8,128)S(1)} %collective-permute-done.7.r_ref, ...), custom_call_target="tpu_custom_call" | custom-call | flops 330301440 | bytes 1835008 | tf_op jit(solution)/shard_map/second_bands/pallas_call | solution.py:152
  33.4 0.1 collective-permute-start.8
  33.4 0.0 copy-start.15
  33.5 0.0 copy-start.16
  33.5 0.0 copy-start.17
  33.5 0.0 copy-start.18
  33.5 0.0 copy-start.19
  33.5 0.0 copy-start.20
  33.5 0.0 copy-start.25
  33.5 0.0 copy-start.26
  33.5 0.0 copy-start.27
  33.6 0.0 copy-start.28
  33.6 0.0 copy-start.29
  33.6 0.0 copy-start.30
  33.6 4.7 %collective-permute-start.9 = (f32[280,128]{1,0:T(8,128)S(1)}, f32[280,128]{1,0:T(8,128)S(1)}, u32[]{:S(2)}, u32[]{:S(2)}) collective-permute-start(f32[280,128]{1,0:T(8,128)S(1)} %get-tuple-element.35), channel_id=1, source_target_pairs={{4,0},{8,4},{12,8},{16,12},{20,16},{24,20},{28,24},{0,28},{5,1},{9... | collective-permute-start | bytes 430088 | tf_op jit(solution)/shard_map/ppermute | solution.py:698
  38.3 8.2 %detail_yz.1 = (f32[32,128,256]{2,1,0:T(8,128)S(1)}, f32[2,128,256]{2,1,0:T(8,128)S(1)}, f32[2,128,256]{2,1,0:T(8,128)S(1)}) custom-call(f32[32,144,256]{2,1,0:T(8,128)S(1)} %detail_bands.1.c_ref, bf16[256,256]{1,0:T(8,128)(2,1)S(1)} %copy-done.12, bf16[256,256]{1,0:T(8,128)(2,1)S(1)} %copy-done.11, bf16[128,144]{1,0:T(8,128)(2,1)S(1)} %copy-done.14, ...), custom_call_target="tpu_custom_call" | custom-call | flops 2717908992 | bytes 8912896 | tf_op jit(solution)/shard_map/detail_yz/pallas_call | solution.py:152
  46.5 0.1 collective-permute-start.12
  46.6 4.7 %collective-permute-start.13 = (f32[2,128,256]{2,1,0:T(8,128)S(1)}, f32[2,128,256]{2,1,0:T(8,128)S(1)}, u32[]{:S(2)}, u32[]{:S(2)}) collective-permute-start(f32[2,128,256]{2,1,0:T(8,128)S(1)} %get-tuple-element.42), channel_id=1, source_target_pairs={{4,0},{8,4},{12,8},{16,12},{20,16},{24,20},{28,24},{0,28},{5,1},{9... | collective-permute-start | bytes 786440 | tf_op jit(solution)/shard_map/ppermute | solution.py:698
  51.4 4.6 %coarse.1 = (f32[20,72,128]{2,1,0:T(8,128)S(1)}, f32[6,72,128]{2,1,0:T(8,128)S(1)}, f32[6,72,128]{2,1,0:T(8,128)S(1)}) custom-call(f32[16]{0:T(128)S(1)} %copy-done.10, s32[3,7]{1,0:T(4,128)S(1)} %copy-done.9, f32[16,112,128]{2,1,0:T(8,128)S(1)} %get-tuple-element.33.b_ref, f32[280,128]{1,0:T(8,128)S(1)} %collective-permute-done.8.l_ref, ...), custom_call_target="tpu_custom_call" | custom-call | flops 1500000000 | bytes 1835008 | tf_op jit(solution)/shard_map/coarse/pallas_call | solution.py:152
  56.0 0.1 collective-permute-start.10
  56.1 4.7 %collective-permute-start.11 = (f32[6,72,128]{2,1,0:T(8,128)S(1)}, f32[6,72,128]{2,1,0:T(8,128)S(1)}, u32[]{:S(2)}, u32[]{:S(2)}) collective-permute-start(f32[6,72,128]{2,1,0:T(8,128)S(1)} %get-tuple-element.38), channel_id=1, source_target_pairs={{4,0},{8,4},{12,8},{16,12},{20,16},{24,20},{28,24},{0,28},{5,1},{9... | collective-permute-start | bytes 663560 | tf_op jit(solution)/shard_map/ppermute | solution.py:698
  60.8 2.8 %detail_x.1.d_ref = f32[32,128,256]{2,1,0:T(8,128)S(1)} custom-call(f32[32,128,256]{2,1,0:T(8,128)S(1)} %get-tuple-element.40.p_ref), custom_call_target="tpu_custom_call" | custom-call | flops 16777216 | bytes 8388608 | tf_op jit(solution)/shard_map/detail_x/pallas_call | solution.py:152
  63.7 2.5 %collective-permute-done.13.er = f32[2,128,256]{2,1,0:T(8,128)S(1)} collective-permute-done((f32[2,128,256]{2,1,0:T(8,128)S(1)}, f32[2,128,256]{2,1,0:T(8,128)S(1)}, u32[]{:S(2)}, u32[]{:S(2)}) %collective-permute-start.13) | collective-permute-done | bytes 262176 | tf_op jit(solution)/shard_map/ppermute | solution.py:698
  66.2 1.4 %collective-permute-done.10.l_ref = f32[6,72,128]{2,1,0:T(8,128)S(1)} collective-permute-done((f32[6,72,128]{2,1,0:T(8,128)S(1)}, f32[6,72,128]{2,1,0:T(8,128)S(1)}, u32[]{:S(2)}, u32[]{:S(2)}) %collective-permute-start.10) | collective-permute-done | bytes 221216 | tf_op jit(solution)/shard_map/ppermute | solution.py:693
  67.6 2.5 %collective-permute-done.11.r_ref = f32[6,72,128]{2,1,0:T(8,128)S(1)} collective-permute-done((f32[6,72,128]{2,1,0:T(8,128)S(1)}, f32[6,72,128]{2,1,0:T(8,128)S(1)}, u32[]{:S(2)}, u32[]{:S(2)}) %collective-permute-start.11) | collective-permute-done | bytes 221216 | tf_op jit(solution)/shard_map/ppermute | solution.py:698
  70.0 7.4 %final.1 = f32[32,128,256]{2,1,0:T(8,128)} custom-call(f32[20,72,128]{2,1,0:T(8,128)S(1)} %get-tuple-element.36.a_ref, f32[6,72,128]{2,1,0:T(8,128)S(1)} %collective-permute-done.10.l_ref, f32[6,72,128]{2,1,0:T(8,128)S(1)} %collective-permute-done.11.r_ref, f32[32,128,256]{2,1,0:T(8,128)S(1)} %detail_x.1.d_ref, ...), custom_call_target="tpu_custom_call" | custom-call | flops 8388608 | bytes 8388608 | tf_op jit(solution)/shard_map/final/pallas_call | solution.py:152
  (53 shorter events, 0.1 us)
Async XLA Ops:
  0.0 2.2 %copy-start = (f32[32,128,256]{2,1,0:T(8,128)S(1)}, f32[32,128,256]{2,1,0:T(8,128)}, u32[]{:S(2)}) copy-start(f32[32,128,256]{2,1,0:T(8,128)} %y_first.1) | copy-start | bytes 12582916
  2.2 7.9 %copy-start.1 = (bf16[256,256]{1,0:T(8,128)(2,1)S(1)}, bf16[256,256]{1,0:T(8,128)(2,1)}, u32[]{:S(2)}) copy-start(bf16[256,256]{1,0:T(8,128)(2,1)} %constant.57.clone.z1) | copy-start | bytes 393220
  2.2 7.9 %copy-start.2 = (bf16[256,256]{1,0:T(8,128)(2,1)S(1)}, bf16[256,256]{1,0:T(8,128)(2,1)}, u32[]{:S(2)}) copy-start(bf16[256,256]{1,0:T(8,128)(2,1)} %constant.56.clone.z0) | copy-start | bytes 393220
  2.3 10.8 %collective-permute-start = (f32[32,8,256]{2,1,0:T(8,128)S(1)}, f32[32,8,256]{2,1,0:T(8,128)S(1)}, u32[]{:S(2)}, u32[]{:S(2)}) collective-permute-start(f32[32,8,256]{2,1,0:T(8,128)S(1)} %get-tuple-element.24), channel_id=1, source_target_pairs={{0,1},{1,2},{2,3},{3,0},{4,5},{5,6},{6,7},{7,4},{8,9},{9,10},{10,1... | collective-permute-start | bytes 786440 | tf_op jit(solution)/shard_map/ppermute | solution.py:693
  2.8 10.3 %collective-permute-start.1 = (f32[32,8,256]{2,1,0:T(8,128)S(1)}, f32[32,8,256]{2,1,0:T(8,128)S(1)}, u32[]{:S(2)}, u32[]{:S(2)}) collective-permute-start(f32[32,8,256]{2,1,0:T(8,128)S(1)} %get-tuple-element.25), channel_id=1, source_target_pairs={{1,0},{2,1},{3,2},{0,3},{5,4},{6,5},{7,6},{4,7},{9,8},{10,9},{11,1... | collective-permute-start | bytes 786440 | tf_op jit(solution)/shard_map/ppermute | solution.py:698
  4.8 18.5 %collective-permute-start.2 = (f32[2,128,256]{2,1,0:T(8,128)S(1)}, f32[2,128,256]{2,1,0:T(8,128)S(1)}, u32[]{:S(2)}, u32[]{:S(2)}) collective-permute-start(f32[2,128,256]{2,1,0:T(8,128)S(1)} %get-tuple-element.26), channel_id=1, source_target_pairs={{0,4},{4,8},{8,12},{12,16},{16,20},{20,24},{24,28},{28,0},{1,5},{5... | collective-permute-start | bytes 786440 | tf_op jit(solution)/shard_map/ppermute | solution.py:693
  7.0 10.9 %copy-start.3 = (bf16[144,144]{1,0:T(8,128)(2,1)S(1)}, bf16[144,144]{1,0:T(8,128)(2,1)}, u32[]{:S(2)}) copy-start(bf16[144,144]{1,0:T(8,128)(2,1)} %constant.59.clone.y1) | copy-start | bytes 124420
  7.0 10.9 %copy-start.4 = (bf16[144,144]{1,0:T(8,128)(2,1)S(1)}, bf16[144,144]{1,0:T(8,128)(2,1)}, u32[]{:S(2)}) copy-start(bf16[144,144]{1,0:T(8,128)(2,1)} %constant.58.clone.y0) | copy-start | bytes 124420
  7.0 16.3 %collective-permute-start.3 = (f32[2,128,256]{2,1,0:T(8,128)S(1)}, f32[2,128,256]{2,1,0:T(8,128)S(1)}, u32[]{:S(2)}, u32[]{:S(2)}) collective-permute-start(f32[2,128,256]{2,1,0:T(8,128)S(1)} %get-tuple-element.27), channel_id=1, source_target_pairs={{4,0},{8,4},{12,8},{16,12},{20,16},{24,20},{28,24},{0,28},{5,1},{9... | collective-permute-start | bytes 786440 | tf_op jit(solution)/shard_map/ppermute | solution.py:698
  13.2 10.2 %collective-permute-start.4 = (f32[2,16,256]{2,1,0:T(8,128)S(1)}, f32[2,16,256]{2,1,0:T(8,128)S(1)}, u32[]{:S(2)}, u32[]{:S(2)}) collective-permute-start(f32[2,16,256]{2,1,0:T(8,128)S(1)} %get-tuple-element.28), channel_id=1, source_target_pairs={{0,4},{4,8},{8,12},{12,16},{16,20},{20,24},{24,28},{28,0},{1,5},{5... | collective-permute-start | bytes 98312 | tf_op jit(solution)/shard_map/ppermute | solution.py:693
  13.2 10.1 %collective-permute-start.5 = (f32[2,16,256]{2,1,0:T(8,128)S(1)}, f32[2,16,256]{2,1,0:T(8,128)S(1)}, u32[]{:S(2)}, u32[]{:S(2)}) collective-permute-start(f32[2,16,256]{2,1,0:T(8,128)S(1)} %get-tuple-element.29), channel_id=1, source_target_pairs={{4,0},{8,4},{12,8},{16,12},{20,16},{24,20},{28,24},{0,28},{5,1},{9... | collective-permute-start | bytes 98312 | tf_op jit(solution)/shard_map/ppermute | solution.py:698
  23.3 3.4 %copy-start.9 = (s32[3,7]{1,0:T(4,128)S(1)}, s32[3,7]{1,0:T(4,128)}, u32[]{:S(2)}) copy-start(s32[3,7]{1,0:T(4,128)} %index_ref.3) | copy-start | bytes 256
  23.3 3.4 %copy-start.10 = (f32[16]{0:T(128)S(1)}, f32[16]{0:T(128)}, u32[]{:S(2)}) copy-start(f32[16]{0:T(128)} %table_ref.3) | copy-start | bytes 196
  24.9 6.2 %collective-permute-start.6 = (f32[16,24,128]{2,1,0:T(8,128)S(1)}, f32[16,24,128]{2,1,0:T(8,128)S(1)}, u32[]{:S(2)}, u32[]{:S(2)}) collective-permute-start(f32[16,24,128]{2,1,0:T(8,128)S(1)} %get-tuple-element.31), channel_id=1, source_target_pairs={{0,1},{1,2},{2,3},{3,0},{4,5},{5,6},{6,7},{7,4},{8,9},{9,10},{10,1... | collective-permute-start | bytes 589832 | tf_op jit(solution)/shard_map/ppermute | solution.py:693
  24.9 6.4 %collective-permute-start.7 = (f32[16,24,128]{2,1,0:T(8,128)S(1)}, f32[16,24,128]{2,1,0:T(8,128)S(1)}, u32[]{:S(2)}, u32[]{:S(2)}) collective-permute-start(f32[16,24,128]{2,1,0:T(8,128)S(1)} %get-tuple-element.32), channel_id=1, source_target_pairs={{1,0},{2,1},{3,2},{0,3},{5,4},{6,5},{7,6},{4,7},{9,8},{10,9},{11,1... | collective-permute-start | bytes 589832 | tf_op jit(solution)/shard_map/ppermute | solution.py:698
  26.7 4.7 %copy-start.21 = (bf16[128,128]{1,0:T(8,128)(2,1)S(1)}, bf16[128,128]{1,0:T(8,128)(2,1)}, u32[]{:S(2)}) copy-start(bf16[128,128]{1,0:T(8,128)(2,1)} %constant.61.clone.z1) | copy-start | bytes 98308
  26.7 4.7 %copy-start.22 = (bf16[128,128]{1,0:T(8,128)(2,1)S(1)}, bf16[128,128]{1,0:T(8,128)(2,1)}, u32[]{:S(2)}) copy-start(bf16[128,128]{1,0:T(8,128)(2,1)} %constant.60.clone.z0) | copy-start | bytes 98308
  26.7 4.7 %copy-start.23 = (bf16[112,112]{1,0:T(8,128)(2,1)S(1)}, bf16[112,112]{1,0:T(8,128)(2,1)}, u32[]{:S(2)}) copy-start(bf16[112,112]{1,0:T(8,128)(2,1)} %constant.63.clone.y1) | copy-start | bytes 75268
  26.7 4.7 %copy-start.24 = (bf16[112,112]{1,0:T(8,128)(2,1)S(1)}, bf16[112,112]{1,0:T(8,128)(2,1)}, u32[]{:S(2)}) copy-start(bf16[112,112]{1,0:T(8,128)(2,1)} %constant.62.clone.y0) | copy-start | bytes 75268
  26.7 11.6 %copy-start.11 = (bf16[256,256]{1,0:T(8,128)(2,1)S(1)}, bf16[256,256]{1,0:T(8,128)(2,1)}, u32[]{:S(2)}) copy-start(bf16[256,256]{1,0:T(8,128)(2,1)} %constant.65.clone.z1) | copy-start | bytes 393220
  26.7 11.6 %copy-start.12 = (bf16[256,256]{1,0:T(8,128)(2,1)S(1)}, bf16[256,256]{1,0:T(8,128)(2,1)}, u32[]{:S(2)}) copy-start(bf16[256,256]{1,0:T(8,128)(2,1)} %constant.64.clone.z0) | copy-start | bytes 393220
  26.7 11.6 %copy-start.13 = (bf16[128,144]{1,0:T(8,128)(2,1)S(1)}, bf16[128,144]{1,0:T(8,128)(2,1)}, u32[]{:S(2)}) copy-start(bf16[128,144]{1,0:T(8,128)(2,1)} %constant.67.clone.y1) | copy-start | bytes 110596
  26.7 11.6 %copy-start.14 = (bf16[128,144]{1,0:T(8,128)(2,1)S(1)}, bf16[128,144]{1,0:T(8,128)(2,1)}, u32[]{:S(2)}) copy-start(bf16[128,144]{1,0:T(8,128)(2,1)} %constant.66.clone.y0) | copy-start | bytes 110596
  33.4 17.9 %collective-permute-start.8 = (f32[280,128]{1,0:T(8,128)S(1)}, f32[280,128]{1,0:T(8,128)S(1)}, u32[]{:S(2)}, u32[]{:S(2)}) collective-permute-start(f32[280,128]{1,0:T(8,128)S(1)} %get-tuple-element.34), channel_id=1, source_target_pairs={{0,4},{4,8},{8,12},{12,16},{16,20},{20,24},{24,28},{28,0},{1,5},{5... | collective-permute-start | bytes 430088 | tf_op jit(solution)/shard_map/ppermute | solution.py:693
  33.4 17.9 %copy-start.15 = (bf16[128,128]{1,0:T(8,128)(2,1)S(1)}, bf16[128,128]{1,0:T(8,128)(2,1)}, u32[]{:S(2)}) copy-start(bf16[128,128]{1,0:T(8,128)(2,1)} %constant.73.clone.refs_5_) | copy-start | bytes 98308
  33.5 17.9 %copy-start.16 = (bf16[128,128]{1,0:T(8,128)(2,1)S(1)}, bf16[128,128]{1,0:T(8,128)(2,1)}, u32[]{:S(2)}) copy-start(bf16[128,128]{1,0:T(8,128)(2,1)} %constant.72.clone.refs_4_) | copy-start | bytes 98308
  33.5 17.9 %copy-start.17 = (bf16[128,128]{1,0:T(8,128)(2,1)S(1)}, bf16[128,128]{1,0:T(8,128)(2,1)}, u32[]{:S(2)}) copy-start(bf16[128,128]{1,0:T(8,128)(2,1)} %constant.71.clone.refs_3_) | copy-start | bytes 98308
  33.5 17.9 %copy-start.18 = (bf16[128,128]{1,0:T(8,128)(2,1)S(1)}, bf16[128,128]{1,0:T(8,128)(2,1)}, u32[]{:S(2)}) copy-start(bf16[128,128]{1,0:T(8,128)(2,1)} %constant.70.clone.refs_2_) | copy-start | bytes 98308
  33.5 17.9 %copy-start.19 = (bf16[128,128]{1,0:T(8,128)(2,1)S(1)}, bf16[128,128]{1,0:T(8,128)(2,1)}, u32[]{:S(2)}) copy-start(bf16[128,128]{1,0:T(8,128)(2,1)} %constant.69.clone.refs_1_) | copy-start | bytes 98308
  33.5 17.9 %copy-start.20 = (bf16[128,128]{1,0:T(8,128)(2,1)S(1)}, bf16[128,128]{1,0:T(8,128)(2,1)}, u32[]{:S(2)}) copy-start(bf16[128,128]{1,0:T(8,128)(2,1)} %constant.68.clone.refs_0_) | copy-start | bytes 98308
  33.5 17.9 %copy-start.25 = (bf16[80,112]{1,0:T(8,128)(2,1)S(1)}, bf16[80,112]{1,0:T(8,128)(2,1)}, u32[]{:S(2)}) copy-start(bf16[80,112]{1,0:T(8,128)(2,1)} %constant.79.clone.refs_11_) | copy-start | bytes 53764
  33.5 17.9 %copy-start.26 = (bf16[80,112]{1,0:T(8,128)(2,1)S(1)}, bf16[80,112]{1,0:T(8,128)(2,1)}, u32[]{:S(2)}) copy-start(bf16[80,112]{1,0:T(8,128)(2,1)} %constant.78.clone.refs_10_) | copy-start | bytes 53764
  33.5 17.9 %copy-start.27 = (bf16[64,48]{1,0:T(8,128)(2,1)S(1)}, bf16[64,48]{1,0:T(8,128)(2,1)}, u32[]{:S(2)}) copy-start(bf16[64,48]{1,0:T(8,128)(2,1)} %constant.77.clone.refs_9_) | copy-start | bytes 18436
  33.6 17.9 %copy-start.28 = (bf16[64,48]{1,0:T(8,128)(2,1)S(1)}, bf16[64,48]{1,0:T(8,128)(2,1)}, u32[]{:S(2)}) copy-start(bf16[64,48]{1,0:T(8,128)(2,1)} %constant.76.clone.refs_8_) | copy-start | bytes 18436
  33.6 17.9 %copy-start.29 = (bf16[48,64]{1,0:T(8,128)(2,1)S(1)}, bf16[48,64]{1,0:T(8,128)(2,1)}, u32[]{:S(2)}) copy-start(bf16[48,64]{1,0:T(8,128)(2,1)} %constant.75.clone.refs_7_) | copy-start | bytes 18436
  33.6 17.8 %copy-start.30 = (bf16[48,64]{1,0:T(8,128)(2,1)S(1)}, bf16[48,64]{1,0:T(8,128)(2,1)}, u32[]{:S(2)}) copy-start(bf16[48,64]{1,0:T(8,128)(2,1)} %constant.74.clone.refs_6_) | copy-start | bytes 18436
  33.6 17.7 %collective-permute-start.9 = (f32[280,128]{1,0:T(8,128)S(1)}, f32[280,128]{1,0:T(8,128)S(1)}, u32[]{:S(2)}, u32[]{:S(2)}) collective-permute-start(f32[280,128]{1,0:T(8,128)S(1)} %get-tuple-element.35), channel_id=1, source_target_pairs={{4,0},{8,4},{12,8},{16,12},{20,16},{24,20},{28,24},{0,28},{5,1},{9... | collective-permute-start | bytes 430088 | tf_op jit(solution)/shard_map/ppermute | solution.py:698
  46.5 17.1 %collective-permute-start.12 = (f32[2,128,256]{2,1,0:T(8,128)S(1)}, f32[2,128,256]{2,1,0:T(8,128)S(1)}, u32[]{:S(2)}, u32[]{:S(2)}) collective-permute-start(f32[2,128,256]{2,1,0:T(8,128)S(1)} %get-tuple-element.41), channel_id=1, source_target_pairs={{0,4},{4,8},{8,12},{12,16},{16,20},{20,24},{24,28},{28,0},{1,5},{5... | collective-permute-start | bytes 786440 | tf_op jit(solution)/shard_map/ppermute | solution.py:693
  46.6 19.6 %collective-permute-start.13 = (f32[2,128,256]{2,1,0:T(8,128)S(1)}, f32[2,128,256]{2,1,0:T(8,128)S(1)}, u32[]{:S(2)}, u32[]{:S(2)}) collective-permute-start(f32[2,128,256]{2,1,0:T(8,128)S(1)} %get-tuple-element.42), channel_id=1, source_target_pairs={{4,0},{8,4},{12,8},{16,12},{20,16},{24,20},{28,24},{0,28},{5,1},{9... | collective-permute-start | bytes 786440 | tf_op jit(solution)/shard_map/ppermute | solution.py:698
  56.0 11.6 %collective-permute-start.10 = (f32[6,72,128]{2,1,0:T(8,128)S(1)}, f32[6,72,128]{2,1,0:T(8,128)S(1)}, u32[]{:S(2)}, u32[]{:S(2)}) collective-permute-start(f32[6,72,128]{2,1,0:T(8,128)S(1)} %get-tuple-element.37), channel_id=1, source_target_pairs={{0,4},{4,8},{8,12},{12,16},{16,20},{20,24},{24,28},{28,0},{1,5},{5... | collective-permute-start | bytes 663560 | tf_op jit(solution)/shard_map/ppermute | solution.py:693
  56.1 13.9 %collective-permute-start.11 = (f32[6,72,128]{2,1,0:T(8,128)S(1)}, f32[6,72,128]{2,1,0:T(8,128)S(1)}, u32[]{:S(2)}, u32[]{:S(2)}) collective-permute-start(f32[6,72,128]{2,1,0:T(8,128)S(1)} %get-tuple-element.38), channel_id=1, source_target_pairs={{4,0},{8,4},{12,8},{16,12},{20,16},{24,20},{28,24},{0,28},{5,1},{9... | collective-permute-start | bytes 663560 | tf_op jit(solution)/shard_map/ppermute | solution.py:698
  60.8 9.2 %copy-start.5 = (bf16[128,256]{1,0:T(8,128)(2,1)S(1)}, bf16[128,256]{1,0:T(8,128)(2,1)}, u32[]{:S(2)}) copy-start(bf16[128,256]{1,0:T(8,128)(2,1)} %constant.81.clone.z1) | copy-start | bytes 196612
  60.8 9.2 %copy-start.6 = (bf16[128,256]{1,0:T(8,128)(2,1)S(1)}, bf16[128,256]{1,0:T(8,128)(2,1)}, u32[]{:S(2)}) copy-start(bf16[128,256]{1,0:T(8,128)(2,1)} %constant.80.clone.z0) | copy-start | bytes 196612
  60.8 9.2 %copy-start.7 = (bf16[128,80]{1,0:T(8,128)(2,1)S(1)}, bf16[128,80]{1,0:T(8,128)(2,1)}, u32[]{:S(2)}) copy-start(bf16[128,80]{1,0:T(8,128)(2,1)} %constant.83.clone.y1) | copy-start | bytes 61444
  60.8 9.2 %copy-start.8 = (bf16[128,80]{1,0:T(8,128)(2,1)S(1)}, bf16[128,80]{1,0:T(8,128)(2,1)}, u32[]{:S(2)}) copy-start(bf16[128,80]{1,0:T(8,128)(2,1)} %constant.82.clone.y0) | copy-start | bytes 61444

commit v2 on v1

v2 whole, which is shorter than its diff:
```python
import functools

import jax
import jax.numpy as jnp
import ml_dtypes
import numpy as np
from jax import lax
from jax.experimental import pallas as pl
from jax.experimental.pallas import tpu as pltpu
from jax.sharding import PartitionSpec as P

H = [
    0.23037781330885523,
    0.7148465705525415,
    0.6308807679295904,
    -0.02798376941698385,
    -0.18703481171888114,
    0.030841381835986965,
    0.032883011666982945,
    -0.010597401784997278,
]
G = [(-1.0) ** j * H[7 - j] for j in range(8)]
F32 = jnp.float32
BF16 = jnp.bfloat16
NOTHING = 3.0e38
VMEM_BYTES = 16 * 1024 * 1024


def tap(filt, j):
    return filt[j] if 0 <= j < 8 else 0.0


def analysis_rows(cells, low_ks, high_ks):
    matrix = np.zeros((len(low_ks) + len(high_ks), len(cells)))
    rows = [(H, k) for k in low_ks] + [(G, k) for k in high_ks]
    for row, (filt, k) in enumerate(rows):
        for col, cell in enumerate(cells):
            if k is not None and cell is not None:
                matrix[row, col] = tap(filt, cell - 2 * k + 3)
    return matrix


def synthesis_rows(cells, low_ks, high_ks):
    return analysis_rows(cells, low_ks, high_ks).T


def periodic(length, padded_to):
    matrix = np.zeros((padded_to, padded_to))
    for k in range(length // 2):
        for j in range(8):
            matrix[(2 * k + j - 3) % length, k] += H[j]
            matrix[(2 * k + j - 3) % length, length // 2 + k] += G[j]
    return matrix


def fill(items, length):
    return items + [None] * (length - len(items))


def up_to(count, step):
    return -(-count // step) * step


def pieces(matrix, axis):
    rows, cols = matrix.shape
    matrix = np.pad(matrix, ((0, up_to(rows, 16) - rows), (0, up_to(cols, 16) - cols))).astype(np.float32)
    high = matrix.astype(ml_dtypes.bfloat16)
    low = (matrix - high.astype(np.float32)).astype(ml_dtypes.bfloat16)
    return np.concatenate([high, high, low], axis=axis)


def from_left(matrix):
    return pieces(matrix, 1)


def from_right(matrix):
    return pieces(matrix, 0)


def halves(values):
    high = values.astype(BF16)
    return high, (values - high.astype(F32)).astype(BF16)


def times(values, matrix):
    high, low = halves(values)
    return jnp.dot(jnp.concatenate([high, low, high], axis=1), matrix[...], preferred_element_type=F32)


def left_times(matrix, values):
    missing = matrix.shape[1] // 3 - values.shape[0]
    if missing:
        values = jnp.concatenate([values, jnp.zeros((missing, values.shape[1]), F32)], axis=0)
    high, low = halves(values)
    return jnp.dot(matrix[...], jnp.concatenate([high, low, high], axis=0), preferred_element_type=F32)


def added(terms):
    total = None
    for coef, value in terms:
        part = value if coef == 1.0 else coef * value
        total = part if total is None else total + part
    return total


def x_terms(k, n):
    terms = []
    for j in range(8):
        cell = 2 * k + j - 3
        if 0 <= cell < n:
            terms.append((cell, H[j], G[j]))
        elif cell == -1:
            terms.append(("l1", H[j], G[j]))
        elif cell == n:
            terms.append(("r1", H[j], G[j]))
    if k == 0:
        terms.append(("l2", 1.0, G[0] / H[0]))
    if k == n // 2 - 1:
        terms.append(("r2", 1.0, G[6] / H[6]))
    return terms


def lattice():
    low = np.array(H).reshape(4, 2)
    high = np.array(G).reshape(4, 2)
    tangents = []
    for _ in range(3):
        t = (low[0] @ high[0]) / (high[0] @ high[0])
        tangents.append(float(t))
        low, high = (low - t * high)[1:] / (1 + t * t), (high + t * low)[:-1] / (1 + t * t)
    return low[0].tolist(), high[0].tolist(), tangents[::-1]


def x_interior(get, n):
    first, second, tangents = lattice()
    a, b = {}, {}
    for i in range(1, n // 2):
        x, y = get(2 * i - 1), get(2 * i)
        a[i] = first[0] * x + first[1] * y
        b[i] = second[0] * x + second[1] * y
    for t in tangents:
        shared = [i for i in a if i + 1 in a]
        a, b = {i: a[i + 1] + t * b[i] for i in shared}, {i: b[i] - t * a[i + 1] for i in shared}
    return {i + 1: (a[i], b[i]) for i in a}


def x_low(get, k, n):
    return added([(low, get(key)) for key, low, _ in x_terms(k, n)])


def x_high(get, k, n):
    return added([(high, get(key)) for key, _, high in x_terms(k, n)])


def x_synth(m, lows, highs):
    terms = [(H[m + 3 - 2 * k], v) for k, v in lows.items() if 0 <= m + 3 - 2 * k < 8]
    terms += [(G[m + 3 - 2 * k], v) for k, v in highs.items() if 0 <= m + 3 - 2 * k < 8]
    return added(terms)


def spill_up(low, high, n):
    first = added([(H[5], low[n - 1]), (G[5], high[n - 1]), (H[7], low[n - 2]), (G[7], high[n - 2])])
    return first, added([(H[6], low[n - 1]), (G[6], high[n - 1])])


def spill_down(low, high):
    first = added([(H[2], low[0]), (G[2], high[0]), (H[0], low[1]), (G[0], high[1])])
    return first, added([(H[1], low[0]), (G[1], high[0])])


THIRD_UP = H[7] / H[6]
THIRD_DOWN = H[0] / H[1]


def shrink(values, thresh):
    return values - jnp.minimum(jnp.maximum(values, -thresh), thresh)


def whole_call(kernel, out_shapes, args, flops, moved, scratch=(), name=None):
    specs = [SMEM if a.ndim == 1 or a.dtype == jnp.int32 else VMEM for a in args]
    outs = [VMEM] * len(out_shapes) if isinstance(out_shapes, list) else VMEM
    return pl.pallas_call(
        kernel,
        in_specs=specs,
        out_specs=outs,
        out_shape=out_shapes,
        scratch_shapes=list(scratch),
        name=name,
        cost_estimate=pl.CostEstimate(flops=int(flops), bytes_accessed=int(moved), transcendentals=0),
        compiler_params=pltpu.CompilerParams(vmem_limit_bytes=VMEM_BYTES),
    )(*args)


def call(kernel, grid, in_specs, out_specs, out_shapes, args, flops, moved, scratch=(), name=None):
    return pl.pallas_call(
        kernel,
        grid=grid,
        in_specs=in_specs,
        out_specs=out_specs,
        out_shape=out_shapes,
        scratch_shapes=list(scratch),
        name=name,
        cost_estimate=pl.CostEstimate(flops=int(flops), bytes_accessed=int(moved), transcendentals=0),
        compiler_params=pltpu.CompilerParams(vmem_limit_bytes=VMEM_BYTES),
    )(*args)


def shape(*dims):
    return jax.ShapeDtypeStruct(dims, F32)


def whole(array):
    dims = array.shape
    return pl.BlockSpec(dims, lambda *_: (0,) * len(dims))


def whole_out(*dims):
    return pl.BlockSpec(dims, lambda *_: (0,) * len(dims))


SMEM = pl.BlockSpec(memory_space=pltpu.SMEM)
VMEM = pl.BlockSpec(memory_space=pltpu.VMEM)


def x_messages(last, first, up, down):
    up[0] = last[3]
    up[1] = H[0] * last[1] + H[1] * last[2]
    down[0] = first[0]
    down[1] = H[6] * first[1] + H[7] * first[2]


def first_messages(v):
    nx, ny, nz = v.shape

    def kernel(last, first, y_last, y_first, up, down, y_up, y_down):
        x_messages(last, first, up, down)
        y_up[...] = y_last[...]
        y_down[...] = y_first[...]

    return call(
        kernel,
        (1,),
        [
            pl.BlockSpec((4, ny, nz), lambda i: (nx // 4 - 1, 0, 0)),
            pl.BlockSpec((4, ny, nz), lambda i: (0, 0, 0)),
            pl.BlockSpec((nx, 8, nz), lambda i: (0, ny // 8 - 1, 0)),
            pl.BlockSpec((nx, 8, nz), lambda i: (0, 0, 0)),
        ],
        [whole_out(2, ny, nz)] * 2 + [whole_out(nx, 8, nz)] * 2,
        [shape(2, ny, nz)] * 2 + [shape(nx, 8, nz)] * 2,
        [v] * 4,
        1e6,
        3e6,
        name="first_messages",
    )


def corner_messages(y_left, y_right):
    nx, rows, nz = y_left.shape

    def kernel(last_l, first_l, last_r, first_r, up, down):
        for part, last, first in ((0, last_l, first_l), (1, last_r, first_r)):
            at = pl.ds(8 * part, 8)
            up[0, at] = last[3]
            up[1, at] = H[0] * last[1] + H[1] * last[2]
            down[0, at] = first[0]
            down[1, at] = H[6] * first[1] + H[7] * first[2]

    last = pl.BlockSpec((4, rows, nz), lambda i: (nx // 4 - 1, 0, 0))
    first = pl.BlockSpec((4, rows, nz), lambda i: (0, 0, 0))
    return call(
        kernel,
        (1,),
        [last, first, last, first],
        [whole_out(2, 16, nz)] * 2,
        [shape(2, 16, nz)] * 2,
        [y_left, y_left, y_right, y_right],
        1e5,
        2e5,
        name="corner_messages",
    )


def over_planes(count, group, body):
    def step(i, carry):
        body(i * group)
        return carry

    lax.fori_loop(0, count // group, step, 0)


def depth(v, z_matrix, group, name):
    nx, rows, nz = v.shape

    def kernel(v_ref, z, out):
        def body(first):
            at = pl.ds(first, group)
            out[at] = times(v_ref[at].reshape(group * rows, nz), z).reshape(group, rows, nz)

        over_planes(nx, group, body)

    return whole_call(
        kernel, shape(nx, rows, nz), [v, z_matrix], 6 * nx * rows * nz * nz, 8 * nx * rows * nz, name=name
    )


def y_analysis(zed, y_left, y_right, z_matrix, y_matrix):
    nx, ny, nz = zed.shape
    rows = y_matrix.shape[0]
    group = 8

    def kernel(zed_ref, left, right, z, y, out, left_z, right_z):
        left_z[...] = times(left[...].reshape(8 * nx, nz), z).reshape(nx, 8, nz)
        right_z[...] = times(right[...].reshape(8 * nx, nz), z).reshape(nx, 8, nz)

        def body(first):
            for j in range(group):
                i = first + j
                out[i] = left_times(y, jnp.concatenate([left_z[i], zed_ref[i], right_z[i]], axis=0))

        over_planes(nx, group, body)

    return whole_call(
        kernel,
        shape(nx, rows, nz),
        [zed, y_left, y_right, z_matrix, y_matrix],
        6 * nx * rows * (ny + 16) * nz,
        4 * nx * nz * (ny + rows + 16),
        scratch=[pltpu.VMEM((nx, 8, nz), F32)] * 2,
        name="y_analysis",
    )


def first_approx(bands, x_left, x_right, c_left, c_right, z_matrix, y_matrix, own, ghost_rows):
    nx, rows, nz = bands.shape
    ny = x_left.shape[1]
    half_z = nz // 2
    n1 = nx // 2

    def kernel(b_ref, xl, xr, cl, cr, z, y, halo, approx, up, down):
        planes = [
            jnp.concatenate([corner[i, :8], main[i], corner[i, 8:]], axis=0)
            for main, corner in ((xl, cl), (xr, cr))
            for i in range(2)
        ]
        zed = times(jnp.concatenate(planes, axis=0), z)
        for i in range(4):
            halo[i] = left_times(y, zed[i * (ny + 16) : (i + 1) * (ny + 16)])
        place = {"l1": 0, "l2": 1, "r1": 2, "r2": 3}

        def tile(t, carry):
            at = pl.ds(pl.multiple_of(t * 8, 8), 8)
            values = {key: halo[i, at, :half_z] for key, i in place.items()}
            values.update({i: b_ref[i, at, :half_z] for i in range(nx)})
            for k in range(n1):
                approx[k, at] = x_low(values.get, k, nx)
            return carry

        lax.fori_loop(0, own // 8, tile, 0)
        up[...] = approx[:, own - ghost_rows :]
        down[...] = approx[:, :ghost_rows]

    return whole_call(
        kernel,
        [
            shape(4, rows, nz),
            shape(n1, own, half_z),
            shape(n1, ghost_rows, half_z),
            shape(n1, ghost_rows, half_z),
        ],
        [bands, x_left, x_right, c_left, c_right, z_matrix, y_matrix],
        24 * rows * (ny + 16) * nz + 24 * (ny + 16) * nz * nz,
        3e6,
        name="first_approx",
    )


def detail_bands(bands, halo, table, index):
    nx, rows, nz = bands.shape
    n1 = nx // 2
    half_z = nz // 2
    half_tiles = rows // 16

    def kernel(table_ref, index_ref, b_ref, h_ref, out):
        place = {"l1": 0, "l2": 1, "r1": 2, "r2": 3}

        def tiles(by):
            def tile(t, carry):
                at = pl.ds(pl.multiple_of((t + by * half_tiles) * 8, 8), 8)
                for bz in range(2):
                    lanes = pl.ds(bz * half_z, half_z)
                    band = 2 * by + bz
                    quiet = table_ref[index_ref[0, band - 1]] if band else NOTHING
                    loud = table_ref[index_ref[0, band + 3]]
                    values = {key: h_ref[i, at, lanes] for key, i in place.items()}
                    values.update({i: b_ref[i, at, lanes] for i in range(nx)})
                    coeffs = x_interior(values.get, nx)
                    for k in (0, 1, n1 - 2, n1 - 1):
                        coeffs[k] = (x_low(values.get, k, nx), x_high(values.get, k, nx))
                    for k, (low, high) in coeffs.items():
                        out[k, at, lanes] = shrink(low, quiet) if band else jnp.zeros_like(low)
                        out[n1 + k, at, lanes] = shrink(high, loud)
                return carry

            return tile

        lax.fori_loop(0, half_tiles, tiles(0), 0)
        lax.fori_loop(0, half_tiles, tiles(1), 0)

    return whole_call(
        kernel,
        shape(nx, rows, nz),
        [table, index, bands, halo],
        40 * nx * rows * nz,
        8 * nx * rows * nz,
        name="detail_bands",
    )


def detail_yz(coeffs, z_matrix, y_matrix):
    nx, rows, nz = coeffs.shape
    ny = y_matrix.shape[0]
    n1 = nx // 2

    def kernel(c_ref, z, y, out, up, down, zed):
        def z_body(first):
            at = pl.ds(first, 8)
            zed[at] = times(c_ref[at].reshape(8 * rows, nz), z).reshape(8, rows, nz)

        def y_body(first):
            for j in range(8):
                out[first + j] = left_times(y, zed[first + j])

        over_planes(nx, 8, z_body)
        over_planes(nx, 8, y_body)
        lows = {k: out.at[k] for k in range(n1)}
        highs = {k: out.at[n1 + k] for k in range(n1)}
        value = lambda part, ks: {k: part[k][...] for k in ks}
        ends = (n1 - 2, n1 - 1)
        up[0], up[1] = spill_up(value(lows, ends), value(highs, ends), n1)
        down[0], down[1] = spill_down(value(lows, (0, 1)), value(highs, (0, 1)))

    return whole_call(
        kernel,
        [shape(nx, ny, nz), shape(2, ny, nz), shape(2, ny, nz)],
        [coeffs, z_matrix, y_matrix],
        6 * nx * rows * nz * nz + 6 * nx * rows * ny * nz,
        4 * nx * nz * (rows + ny),
        scratch=[pltpu.VMEM((nx, rows, nz), F32)],
        name="detail_yz",
    )


def detail_x(parts):
    nx, ny, nz = parts.shape
    n1 = nx // 2

    def kernel(p_ref, out):
        def tile(t, carry):
            at = pl.ds(pl.multiple_of(t * 8, 8), 8)
            for lane in range(0, nz, 128):
                lanes = pl.ds(lane, 128)
                lows = {k: p_ref[k, at, lanes] for k in range(n1)}
                highs = {k: p_ref[n1 + k, at, lanes] for k in range(n1)}
                for m in range(nx):
                    out[m, at, lanes] = x_synth(m, lows, highs)
            return carry

        lax.fori_loop(0, ny // 8, tile, 0)

    return whole_call(
        kernel, shape(nx, ny, nz), [parts], 16 * nx * ny * nz, 8 * nx * ny * nz, name="detail_x"
    )


def in_pairs(matrix, planes):
    results = []
    for i in range(0, len(planes), 2):
        both = left_times(matrix, jnp.concatenate(planes[i : i + 2], axis=1))
        width = both.shape[1] // 2
        results += [both[:, :width], both[:, width:]]
    return results


def cut(values, rows):
    return [values[i : i + rows] for i in range(0, values.shape[0], rows)]


def packed(first, second):
    half = first.shape[1] // 2
    lane = lax.broadcasted_iota(jnp.int32, first.shape, 1)
    return jnp.where(lane < half, first, pltpu.roll(second, half, 1))


def unpacked(both):
    half = both.shape[1] // 2
    lane = lax.broadcasted_iota(jnp.int32, both.shape, 1)
    return [jnp.where(lane < half, part, 0.0) for part in (both, pltpu.roll(both, half, 1))]


def second_bands(own, left, right, z_matrix, y_matrix, low_rows):
    n1, own_rows, nz = own.shape
    in_rows = own_rows + 2 * left.shape[1]
    rows = y_matrix.shape[0]

    def kernel(o_ref, l_ref, r_ref, z, y, out, up, down):
        for i in range(0, n1, 8):
            stack = [part[j] for j in range(i, i + 8) for part in (o_ref, l_ref, r_ref)]
            zed = times(jnp.concatenate(stack, axis=0), z)
            for j, plane in enumerate(in_pairs(y, cut(zed, in_rows))):
                out[i + j] = plane
        low = lambda c: out[c, :low_rows]
        up[0:rows] = out[n1 - 1]
        up[rows : 2 * rows] = H[0] * out[n1 - 3] + H[1] * out[n1 - 2]
        first = added([(H[j], low(n1 - 5 + j)) for j in range(5)])
        second = added([(H[0] * H[j], low(n1 - 9 + j)) for j in range(8)])
        second += added([(H[1] * H[j], low(n1 - 7 + j)) for j in range(7)])
        up[2 * rows :] = packed(first, second)
        down[0:rows] = out[0]
        down[rows : 2 * rows] = H[6] * out[1] + H[7] * out[2]
        first = added([(H[j], low(j - 3)) for j in range(3, 8)])
        second = added([(H[6] * H[j], low(j - 1)) for j in range(1, 8)])
        second += added([(H[7] * H[j], low(j + 1)) for j in range(8)])
        down[2 * rows :] = packed(first, second)

    message = 2 * rows + low_rows
    return whole_call(
        kernel,
        [shape(n1, rows, nz), shape(message, nz), shape(message, nz)],
        [own, left, right, z_matrix, y_matrix],
        6 * n1 * in_rows * nz * (nz + rows),
        4 * n1 * nz * (in_rows + rows),
        name="second_bands",
    )


def limits_plane(table_ref, index_ref, level, bx, dims, row_split, lane_split, zeroth):
    row_high = lax.broadcasted_iota(jnp.int32, dims, 0) >= row_split
    lane_high = lax.broadcasted_iota(jnp.int32, dims, 1) >= lane_split

    def limit(by, bz):
        band = 4 * bx + 2 * by + bz
        return zeroth if band == 0 else table_ref[index_ref[level, band - 1]]

    low_y = jnp.where(lane_high, limit(0, 1), limit(0, 0))
    return jnp.where(row_high, jnp.where(lane_high, limit(1, 1), limit(1, 0)), low_y)


def coarse(bands, left, right, table, index, zs1, za2, zs2, ya2, ys2, ys1, low_rows, out_rows):
    n1, rows, nz = bands.shape
    n2, n3 = n1 // 2, n1 // 4
    rows2 = ya2.shape[0]
    lane_half = nz // 2

    def kernel(table_ref, index_ref, b_ref, l_ref, r_ref, z1, z2a, z2s, a2, s2, s1, approx, up, down, c1, p1):
        sides = {
            "l1": lambda: l_ref[0:rows],
            "l2": lambda: l_ref[rows : 2 * rows],
            "r1": lambda: r_ref[0:rows],
            "r2": lambda: r_ref[rows : 2 * rows],
        }
        get = lambda key: sides[key]() if isinstance(key, str) else b_ref[key]
        low_part = lambda c: b_ref[c, :low_rows]
        dims = (rows, nz)
        quiet = limits_plane(table_ref, index_ref, 1, 0, dims, low_rows, lane_half, NOTHING)
        loud = limits_plane(table_ref, index_ref, 1, 1, dims, low_rows, lane_half, NOTHING)
        planes = []
        for k in range(n2):
            low = x_low(get, k, n1)
            planes.append(low[:low_rows])
            c1[k] = shrink(low, quiet)
            c1[n2 + k] = shrink(x_high(get, k, n1), loud)
        first, second = unpacked(l_ref[2 * rows :])
        planes.append(first + added([(H[5 + i], low_part(i)) for i in range(3)]))
        planes.append(second + H[1] * H[7] * low_part(0))
        first, second = unpacked(r_ref[2 * rows :])
        planes.append(first + added([(H[i], low_part(n1 - 3 + i)) for i in range(3)]))
        planes.append(second + H[6] * H[0] * low_part(n1 - 1))
        third = in_pairs(a2, cut(times(jnp.concatenate(planes, axis=0), z2a), low_rows))
        keys = {"l1": n2, "l2": n2 + 1, "r1": n2 + 2, "r2": n2 + 3}
        get2 = lambda key: third[keys.get(key, key)]
        dims = (rows2, nz)
        quiet = limits_plane(table_ref, index_ref, 2, 0, dims, rows2 // 2, lane_half // 2, 0.0)
        loud = limits_plane(table_ref, index_ref, 2, 1, dims, rows2 // 2, lane_half // 2, 0.0)
        kept = [shrink(x_low(get2, k, n2), quiet) for k in range(n3)]
        kept += [shrink(x_high(get2, k, n2), loud) for k in range(n3)]
        parts = in_pairs(s2, cut(times(jnp.concatenate(kept, axis=0), z2s), rows2))
        parts = [part[:low_rows] for part in parts]
        lows = dict(enumerate(parts[:n3]))
        highs = dict(enumerate(parts[n3:]))
        ghosts = [-3, -2, -1, n2, n2 + 1, n2 + 2]
        for k in range(n2):
            c1[k, :low_rows] += x_synth(k, lows, highs)
        stack = [x_synth(k, lows, highs) for k in ghosts]
        beyond = dict(zip(ghosts, stack))
        zed = times(jnp.concatenate(stack, axis=0), z1)
        for i, plane in enumerate(in_pairs(s1, cut(zed, low_rows))):
            p1[2 * n2 + i] = plane[:out_rows]
        for i in range(0, 2 * n2, 8):
            zed = times(c1[i : i + 8].reshape(8 * rows, nz), z1)
            for j, plane in enumerate(in_pairs(s1, cut(zed, rows))):
                p1[i + j] = plane[:out_rows]
        lows = {k: p1.at[k] for k in range(n2)}
        highs = {k: p1.at[n2 + k] for k in range(n2)}
        for i, k in enumerate(ghosts):
            lows[k] = p1.at[2 * n2 + i]

        def cell(m):
            near = lambda part: {k: ref[...] for k, ref in part.items() if 0 <= m + 3 - 2 * k < 8}
            return x_synth(m, near(lows), near(highs))

        for m in range(-2, n1 + 2):
            approx[m + 2] = cell(m)
        value = lambda part, ks: {k: part[k][...] for k in ks}
        ends = (n2 - 2, n2 - 1)
        slot = lambda i: pl.ds(i * out_rows, out_rows)
        up[slot(0)], up[slot(1)] = approx[n1], approx[n1 + 1]
        up[slot(2)], up[slot(3)] = spill_up(value(lows, ends), value(highs, ends), n2)
        up[4 * out_rows :] = packed(beyond[n2], beyond[n2 + 1])
        down[slot(0)], down[slot(1)] = approx[2], approx[3]
        down[slot(2)], down[slot(3)] = spill_down(value(lows, (0, 1)), value(highs, (0, 1)))
        down[4 * out_rows :] = packed(beyond[-1], beyond[-2])

    message = 4 * out_rows + low_rows
    return whole_call(
        kernel,
        [shape(n1 + 4, out_rows, nz), shape(message, nz), shape(message, nz)],
        [table, index, bands, left, right, zs1, za2, zs2, ya2, ys2, ys1],
        1.5e9,
        8 * n1 * rows * nz,
        scratch=[pltpu.VMEM((2 * n2, rows, nz), F32), pltpu.VMEM((2 * n2 + 6, out_rows, nz), F32)],
        name="coarse",
    )


def final(approx, left, right, detail, e_left, e_right, zs1, ys1, z_matrix, y_matrix, low_rows):
    planes, rows, half_z = approx.shape
    nx, ny, nz = detail.shape
    n1 = nx // 2
    n2 = n1 // 2
    step_rows = 16
    steps = ny // step_rows

    def kernel(a_ref, l_ref, r_ref, d_ref, el, er, z1, s1, z, y, out, total, parts, done, sems):
        stack = [p for ref in (l_ref, r_ref) for p in unpacked(ref[4 * rows :])]
        zed = times(jnp.concatenate(stack, axis=0), z1)
        spilled = [p[:rows] for p in in_pairs(s1, cut(zed, low_rows))]
        slot = lambda ref, i: ref[pl.ds(i * rows, rows)]
        for m in range(n1):
            terms = [(1.0, a_ref[m + 2])]
            for k, coef, source in (
                (0, 1.0, 0),
                (1, 1.0, 1),
                (2, THIRD_UP, 1),
                (n2 - 1, 1.0, 2),
                (n2 - 2, 1.0, 3),
                (n2 - 3, THIRD_DOWN, 3),
            ):
                if 0 <= m + 3 - 2 * k < 8:
                    terms.append((coef * H[m + 3 - 2 * k], spilled[source]))
            if m < 3:
                terms.append(((1.0, 1.0, THIRD_UP)[m], slot(l_ref, (2, 3, 3)[m])))
            if m >= n1 - 3:
                terms.append(((1.0, 1.0, THIRD_DOWN)[n1 - 1 - m], slot(r_ref, (2, 3, 3)[n1 - 1 - m])))
            total[m + 2] = added(terms)
        total[0] = a_ref[0] + slot(l_ref, 0)
        total[1] = a_ref[1] + slot(l_ref, 1)
        total[n1 + 2] = a_ref[n1 + 2] + slot(r_ref, 0)
        total[n1 + 3] = a_ref[n1 + 3] + slot(r_ref, 1)

        def body(first):
            zed = times(total[pl.ds(first, 4)].reshape(4 * rows, half_z), z)
            for j, plane in enumerate(cut(zed, rows)):
                parts[first + j] = left_times(y, plane)

        over_planes(planes, 4, body)

        def copy(i):
            at = pl.ds(pl.multiple_of(i * step_rows, step_rows), step_rows)
            return pltpu.make_async_copy(done.at[:, at], out.at[:, at], sems.at[i])

        def step(i, carry):
            for t in range(step_rows // 8):
                at = pl.ds(pl.multiple_of(i * step_rows + 8 * t, 8), 8)
                for lane in range(0, nz, 128):
                    lanes = pl.ds(lane, 128)
                    lows = {k: parts[k + 2, at, lanes] for k in range(-2, n1 + 2)}
                    for m in range(nx):
                        value = d_ref[m, at, lanes] + x_synth(m, lows, {})
                        if m < 3:
                            extra = el[(0, 1, 1)[m], at, lanes]
                            value += extra if m < 2 else THIRD_UP * extra
                        if m >= nx - 3:
                            extra = er[(0, 1, 1)[nx - 1 - m], at, lanes]
                            value += extra if m > nx - 3 else THIRD_DOWN * extra
                        done[m, at, lanes] = value
            copy(i).start()
            return carry

        lax.fori_loop(0, steps, step, 0)

        def finish(i, carry):
            copy(i).wait()
            return carry

        lax.fori_loop(0, steps, finish, 0)

    return pl.pallas_call(
        kernel,
        in_specs=[VMEM] * 10,
        out_specs=pl.BlockSpec(memory_space=pl.ANY),
        out_shape=shape(nx, ny, nz),
        scratch_shapes=[
            pltpu.VMEM((planes, rows, half_z), F32),
            pltpu.VMEM((planes, ny, nz), F32),
            pltpu.VMEM((nx, ny, nz), F32),
            pltpu.SemaphoreType.DMA((steps,)),
        ],
        name="final",
        cost_estimate=pl.CostEstimate(flops=8 * nx * ny * nz, bytes_accessed=8 * nx * ny * nz, transcendentals=0),
        compiler_params=pltpu.CompilerParams(vmem_limit_bytes=VMEM_BYTES),
    )(approx, left, right, detail, e_left, e_right, zs1, ys1, z_matrix, y_matrix)


def to_next(array, axis):
    size = lax.axis_size(axis)
    return lax.ppermute(array, axis, [(i, (i + 1) % size) for i in range(size)])


def to_previous(array, axis):
    size = lax.axis_size(axis)
    return lax.ppermute(array, axis, [((i + 1) % size, i) for i in range(size)])


def local(velocity, table, index):
    nx, ny, nz = velocity.shape
    y1, y2, y3 = ny // 2, ny // 4, ny // 8
    ghost = 24
    cells0 = list(range(-8, ny + 8))
    rows0 = up_to(y1 + 4, 8)
    ks0 = fill(list(range(y1)) + [-2, -1, y1, y1 + 1], rows0)
    cells1 = list(range(y1)) + list(range(-ghost, 0)) + list(range(y1, y1 + ghost))
    rows1 = up_to(y2 + 18, 8)
    low1 = fill(list(range(-9, y2 + 9)), rows1)
    high1 = fill(list(range(-3, y2 + 3)), up_to(y2 + 6, 8))
    ks2 = fill(list(range(-3, y3 + 3)), up_to(y3 + 6, 8))
    ya0 = from_left(analysis_rows(cells0, ks0, ks0))
    ys0_matrix = synthesis_rows(list(range(ny)), ks0, ks0)
    ys0 = from_left(ys0_matrix)
    ys0_low = from_left(ys0_matrix[:, :rows0])
    ya1 = from_left(analysis_rows(cells1, low1, high1))
    ys1 = from_left(synthesis_rows(ks0, low1, high1))
    ya2 = from_left(analysis_rows(low1, ks2, ks2))
    ys2 = from_left(synthesis_rows(low1, ks2, ks2))
    z0 = periodic(nz, nz)
    z1 = periodic(nz // 2, nz // 2)
    z2 = periodic(nz // 4, nz // 2)
    za0, zs0, zs0_low = from_right(z0), from_right(z0.T), from_right(z0.T[: nz // 2])
    za1, zs1 = from_right(z1), from_right(z1.T)
    za2, zs2 = from_right(z2), from_right(z2.T)

    x_up, x_down, y_up, y_down = first_messages(velocity)
    y_left = to_next(y_up, "gy")
    y_right = to_previous(y_down, "gy")
    x_left = to_next(x_up, "gx")
    x_right = to_previous(x_down, "gx")
    zed = depth(velocity, za0, 16, "depth_analysis")
    c_up, c_down = corner_messages(y_left, y_right)
    c_left = to_next(c_up, "gx")
    c_right = to_previous(c_down, "gx")
    bands = y_analysis(zed, y_left, y_right, za0, ya0)
    halo, approx, a_up, a_down = first_approx(
        bands, x_left, x_right, c_left, c_right, za0, ya0, y1, ghost
    )
    a_left = to_next(a_up, "gy")
    a_right = to_previous(a_down, "gy")
    coeffs = detail_bands(bands, halo, table, index)
    bands1, b_up, b_down = second_bands(approx, a_left, a_right, za1, ya1, rows1)
    b_left = to_next(b_up, "gx")
    b_right = to_previous(b_down, "gx")
    parts, e_up, e_down = detail_yz(coeffs, zs0, ys0)
    e_left = to_next(e_up, "gx")
    e_right = to_previous(e_down, "gx")
    approx1, s_up, s_down = coarse(
        bands1, b_left, b_right, table, index, zs1, za2, zs2, ya2, ys2, ys1, rows1, rows0
    )
    s_left = to_next(s_up, "gx")
    s_right = to_previous(s_down, "gx")
    detail = detail_x(parts)
    return final(
        approx1, s_left, s_right, detail, e_left, e_right, zs1, ys1, zs0_low, ys0_low, rows1
    )


def solution(mesh):
    return jax.shard_map(
        local,
        mesh=mesh,
        in_specs=(P("gx", "gy", None), P(), P()),
        out_specs=P("gx", "gy", None),
        check_vma=False,
    )
```

time: 77.5 us -> 67.2 us (0.87)
  Pallas kernels: 39.3 us -> 24.3 us
  waiting for transfers between devices: 6.63 us -> 11.5 us
    pallas_call x11 -> x2, Pallas kernels: 39.3 us -> 0.1 us  [call(): pl.pallas_call(kernel, grid=grid, in_specs=in_specs, out_specs=out_specs,...]
    pallas_call x0 -> x9, Pallas kernels: none -> 24.2 us  [the longest x8 18.7 us: whole_call(): pl.pallas_call(kernel, in_specs=specs, out_specs=outs, out_shape=out_shap...]
    ppermute x7, waiting for transfers between devices: 1.38 us -> 4.09 us  [to_next(): return lax.ppermute(array, axis, [(i, (i + 1) % size) for i in range(size)])]
    ppermute x7, waiting for transfers between devices: 5.25 us -> 7.4 us  [to_previous(): return lax.ppermute(array, axis, [((i + 1) % size, i) for i in range(size)])]
    ppermute x7, starting transfers between devices: 3.01 us -> 4.12 us  [to_next(): return lax.ppermute(array, axis, [(i, (i + 1) % size) for i in range(size)])]
    ppermute x7, starting transfers between devices: 25.6 us -> 24.6 us  [to_previous(): return lax.ppermute(array, axis, [((i + 1) % size, i) for i in range(size)])]
    unnamed x62 -> x34, local copies, waits for them, and re-layouts: 2.36 us -> 2.26 us
  transfers between devices with their start and end apart: 14 -> 14, of which waited for: 4 -> 8; matrix products, arithmetic and copies ran while one was open for 0% -> 0% of each run, Pallas kernels for 37% -> 25%
where the time goes in v2:
time: 67.2 us; the launch traced here: 67 us
  starting transfers between devices  28.7 us (43%)
  Pallas kernels  24.3 us (36%)
  waiting for transfers between devices  11.5 us (17%)
  local copies, waits for them, and re-layouts  2.26 us (3%)
    ppermute x7, starting transfers between devices, to_previous(): return lax.ppermute(array, axis, [((i + 1) % size, i) for i in range(size)])  24.6 us
    pallas_call x8, Pallas kernels, whole_call(): pl.pallas_call(kernel, in_specs=specs, out_specs=outs, out_shape=out_shap...  18.7 us
    ppermute x7, waiting for transfers between devices, to_previous(): return lax.ppermute(array, axis, [((i + 1) % size, i) for i in range(size)])  7.4 us
    pallas_call x1, Pallas kernels, final(): pl.pallas_call(kernel, in_specs=[VMEM] * 10, out_specs=pl.BlockSpec(memor...  5.48 us
    ppermute x7, starting transfers between devices, to_next(): return lax.ppermute(array, axis, [(i, (i + 1) % size) for i in range(size)])  4.12 us
    ppermute x7, waiting for transfers between devices, to_next(): return lax.ppermute(array, axis, [(i, (i + 1) % size) for i in range(size)])  4.09 us
    unnamed x34, local copies, waits for them, and re-layouts  2.26 us
  transfers between devices with their start and end apart: 14, of which 8 were waited for; matrix products, arithmetic and copies ran while one was open for 0% of the time, Pallas kernels for 25%

profile of v2, /device:TPU:0, one launch (start us, length us, event | category | flops | bytes accessed | tf_op | source)
XLA Modules:
  0.0 67.0 jit_solution(10560343018119286862)
XLA Ops:
  0.0 2.2 %copy-done = f32[32,128,256]{2,1,0:T(8,128)S(1)} copy-done((f32[32,128,256]{2,1,0:T(8,128)S(1)}, f32[32,128,256]{2,1,0:T(8,128)}, u32[]{:S(2)}) %copy-start) | copy-done | bytes 4194328
  2.2 0.1 first_messages.1
  2.3 0.5 collective-permute-start
  2.8 2.0 %collective-permute-start.1 = (f32[32,8,256]{2,1,0:T(8,128)S(1)}, f32[32,8,256]{2,1,0:T(8,128)S(1)}, u32[]{:S(2)}, u32[]{:S(2)}) collective-permute-start(f32[32,8,256]{2,1,0:T(8,128)S(1)} %get-tuple-element.25), channel_id=1, source_target_pairs={{1,0},{2,1},{3,2},{0,3},{5,4},{6,5},{7,6},{4,7},{9,8},{10,9},{11,1... | collective-permute-start | bytes 786440 | tf_op jit(solution)/shard_map/ppermute | solution.py:732
  4.8 2.2 %collective-permute-start.2 = (f32[2,128,256]{2,1,0:T(8,128)S(1)}, f32[2,128,256]{2,1,0:T(8,128)S(1)}, u32[]{:S(2)}, u32[]{:S(2)}) collective-permute-start(f32[2,128,256]{2,1,0:T(8,128)S(1)} %get-tuple-element.26), channel_id=1, source_target_pairs={{0,4},{4,8},{8,12},{12,16},{16,20},{20,24},{24,28},{28,0},{1,5},{5... | collective-permute-start | bytes 786440 | tf_op jit(solution)/shard_map/ppermute | solution.py:727
  7.0 3.0 %collective-permute-start.3 = (f32[2,128,256]{2,1,0:T(8,128)S(1)}, f32[2,128,256]{2,1,0:T(8,128)S(1)}, u32[]{:S(2)}, u32[]{:S(2)}) collective-permute-start(f32[2,128,256]{2,1,0:T(8,128)S(1)} %get-tuple-element.27), channel_id=1, source_target_pairs={{4,0},{8,4},{12,8},{16,12},{20,16},{24,20},{28,24},{0,28},{5,1},{9... | collective-permute-start | bytes 786440 | tf_op jit(solution)/shard_map/ppermute | solution.py:732
  10.1 2.0 %depth_analysis.1.zed_ref = f32[32,128,256]{2,1,0:T(8,128)S(1)} custom-call(f32[32,128,256]{2,1,0:T(8,128)S(1)} %copy-done, bf16[768,256]{1,0:T(8,128)(2,1)S(1)} %copy-done.1), custom_call_target="tpu_custom_call" | custom-call | flops 1610612736 | bytes 8388608 | tf_op jit(solution)/shard_map/depth_analysis/pallas_call | solution.py:182
  12.1 0.0 collective-permute-done.left.last_l.first_l
  12.1 0.0 collective-permute-done.1.right.last_r.first_r
  12.1 0.9 %collective-permute-start.4 = (f32[2,16,256]{2,1,0:T(8,128)S(1)}, f32[2,16,256]{2,1,0:T(8,128)S(1)}, u32[]{:S(2)}, u32[]{:S(2)}) collective-permute-start(f32[2,16,256]{2,1,0:T(8,128)S(1)} %get-tuple-element.28), channel_id=1, source_target_pairs={{0,4},{4,8},{8,12},{12,16},{16,20},{20,24},{24,28},{28,0},{1,5},{5... | collective-permute-start | bytes 98312 | tf_op jit(solution)/shard_map/ppermute | solution.py:727
  13.0 3.9 %collective-permute-start.5 = (f32[2,16,256]{2,1,0:T(8,128)S(1)}, f32[2,16,256]{2,1,0:T(8,128)S(1)}, u32[]{:S(2)}, u32[]{:S(2)}) collective-permute-start(f32[2,16,256]{2,1,0:T(8,128)S(1)} %get-tuple-element.29), channel_id=1, source_target_pairs={{4,0},{8,4},{12,8},{16,12},{20,16},{24,20},{28,24},{0,28},{5,1},{9... | collective-permute-start | bytes 98312 | tf_op jit(solution)/shard_map/ppermute | solution.py:732
  16.9 2.3 %y_analysis.1.b_ref = f32[32,144,256]{2,1,0:T(8,128)S(1)} custom-call(f32[32,128,256]{2,1,0:T(8,128)S(1)} %depth_analysis.1.zed_ref, f32[32,8,256]{2,1,0:T(8,128)S(1)} %collective-permute-done.left.last_l.first_l, f32[32,8,256]{2,1,0:T(8,128)S(1)} %collective-permute-done.1.right.last_r.first_r, bf16[768,256]{1,0:T(8,128)(2,1)S(1)} %copy-done.1, ...), custom_call_target="tpu_custom_call" | custom-call | flops 1019215872 | bytes 9437184 | tf_op jit(solution)/shard_map/y_analysis/pallas_call | solution.py:182
  19.2 0.0 copy-start.7
  19.2 0.0 copy-start.8
  19.2 0.1 collective-permute-done.2.xl
  19.3 2.2 %collective-permute-done.3.xr = f32[2,128,256]{2,1,0:T(8,128)S(1)} collective-permute-done((f32[2,128,256]{2,1,0:T(8,128)S(1)}, f32[2,128,256]{2,1,0:T(8,128)S(1)}, u32[]{:S(2)}, u32[]{:S(2)}) %collective-permute-start.3) | collective-permute-done | bytes 262176 | tf_op jit(solution)/shard_map/ppermute | solution.py:732
  21.5 0.0 collective-permute-done.4.cl
  21.5 0.3 collective-permute-done.5.cr
  21.9 1.2 %first_approx.1 = (f32[4,144,256]{2,1,0:T(8,128)S(1)}, f32[16,64,128]{2,1,0:T(8,128)S(1)}, f32[16,24,128]{2,1,0:T(8,128)S(1)}, f32[16,24,128]{2,1,0:T(8,128)S(1)}) custom-call(f32[32,144,256]{2,1,0:T(8,128)S(1)} %y_analysis.1.b_ref, f32[2,128,256]{2,1,0:T(8,128)S(1)} %collective-permute-done.2.xl, f32[2,128,256]{2,1,0:T(8,128)S(1)} %collective-permute-done.3.xr, ...), custom_call_target="tpu_custom_call" | custom-call | flops 353894400 | bytes 3000000 | tf_op jit(solution)/shard_map/first_approx/pallas_call | solution.py:182
  23.1 0.1 collective-permute-start.6
  23.1 1.7 %collective-permute-start.7 = (f32[16,24,128]{2,1,0:T(8,128)S(1)}, f32[16,24,128]{2,1,0:T(8,128)S(1)}, u32[]{:S(2)}, u32[]{:S(2)}) collective-permute-start(f32[16,24,128]{2,1,0:T(8,128)S(1)} %get-tuple-element.32), channel_id=1, source_target_pairs={{1,0},{2,1},{3,2},{0,3},{5,4},{6,5},{7,6},{4,7},{9,8},{10,9},{11,1... | collective-permute-start | bytes 589832 | tf_op jit(solution)/shard_map/ppermute | solution.py:732
  24.9 0.0 copy-done.7
  24.9 0.0 copy-start.9
  24.9 0.0 copy-start.10
  24.9 2.7 %detail_bands.1.c_ref = f32[32,144,256]{2,1,0:T(8,128)S(1)} custom-call(f32[16]{0:T(128)S(1)} %copy-done.8, s32[3,7]{1,0:T(4,128)S(1)} %copy-done.7, f32[32,144,256]{2,1,0:T(8,128)S(1)} %y_analysis.1.b_ref, f32[4,144,256]{2,1,0:T(8,128)S(1)} %get-tuple-element.39.h_ref), custom_call_target="tpu_custom_call" | custom-call | flops 47185920 | bytes 9437184 | tf_op jit(solution)/shard_map/detail_bands/pallas_call | solution.py:182
  27.6 1.9 %collective-permute-done.6.l_ref = f32[16,24,128]{2,1,0:T(8,128)S(1)} collective-permute-done((f32[16,24,128]{2,1,0:T(8,128)S(1)}, f32[16,24,128]{2,1,0:T(8,128)S(1)}, u32[]{:S(2)}, u32[]{:S(2)}) %collective-permute-start.6) | collective-permute-done | bytes 196640 | tf_op jit(solution)/shard_map/ppermute | solution.py:727
  29.6 0.0 collective-permute-done.7.r_ref
  29.6 0.0 copy-done.13
  29.6 1.0 %second_bands.1 = (f32[16,96,128]{2,1,0:T(8,128)S(1)}, f32[248,128]{1,0:T(8,128)S(1)}, f32[248,128]{1,0:T(8,128)S(1)}) custom-call(f32[16,64,128]{2,1,0:T(8,128)S(1)} %get-tuple-element.30.o_ref, f32[16,24,128]{2,1,0:T(8,128)S(1)} %collective-permute-done.6.l_ref, f32[16,24,128]{2,1,0:T(8,128)S(1)} %collective-permute-done.7.r_ref, ...), custom_call_target="tpu_custom_call" | custom-call | flops 308281344 | bytes 1703936 | tf_op jit(solution)/shard_map/second_bands/pallas_call | solution.py:182
  30.6 0.3 collective-permute-start.8
  31.0 0.0 copy-start.15
  31.0 0.0 copy-start.16
  31.0 4.5 %collective-permute-start.9 = (f32[248,128]{1,0:T(8,128)S(1)}, f32[248,128]{1,0:T(8,128)S(1)}, u32[]{:S(2)}, u32[]{:S(2)}) collective-permute-start(f32[248,128]{1,0:T(8,128)S(1)} %get-tuple-element.35), channel_id=1, source_target_pairs={{4,0},{8,4},{12,8},{16,12},{20,16},{24,20},{28,24},{0,28},{5,1},{9... | collective-permute-start | bytes 380936 | tf_op jit(solution)/shard_map/ppermute | solution.py:732
  35.5 0.0 copy-done.9
  35.5 4.5 %detail_yz.1 = (f32[32,128,256]{2,1,0:T(8,128)S(1)}, f32[2,128,256]{2,1,0:T(8,128)S(1)}, f32[2,128,256]{2,1,0:T(8,128)S(1)}) custom-call(f32[32,144,256]{2,1,0:T(8,128)S(1)} %detail_bands.1.c_ref, bf16[768,256]{1,0:T(8,128)(2,1)S(1)} %copy-done.9, bf16[128,432]{1,0:T(8,128)(2,1)S(1)} %copy-done.10), custom_call_target="tpu_custom_call" | custom-call | flops 2717908992 | bytes 8912896 | tf_op jit(solution)/shard_map/detail_yz/pallas_call | solution.py:182
  40.0 0.1 collective-permute-start.12
  40.1 4.7 %collective-permute-start.13 = (f32[2,128,256]{2,1,0:T(8,128)S(1)}, f32[2,128,256]{2,1,0:T(8,128)S(1)}, u32[]{:S(2)}, u32[]{:S(2)}) collective-permute-start(f32[2,128,256]{2,1,0:T(8,128)S(1)} %get-tuple-element.42), channel_id=1, source_target_pairs={{4,0},{8,4},{12,8},{16,12},{20,16},{24,20},{28,24},{0,28},{5,1},{9... | collective-permute-start | bytes 786440 | tf_op jit(solution)/shard_map/ppermute | solution.py:732
  44.8 0.0 collective-permute-done.8.l_ref
  44.8 0.0 collective-permute-done.9.r_ref
  44.9 2.9 %coarse.1 = (f32[20,72,128]{2,1,0:T(8,128)S(1)}, f32[344,128]{1,0:T(8,128)S(1)}, f32[344,128]{1,0:T(8,128)S(1)}) custom-call(f32[16]{0:T(128)S(1)} %copy-done.8, s32[3,7]{1,0:T(4,128)S(1)} %copy-done.7, f32[16,96,128]{2,1,0:T(8,128)S(1)} %get-tuple-element.33.b_ref, f32[248,128]{1,0:T(8,128)S(1)} %collective-permute-done.8.l_ref, ...), custom_call_target="tpu_custom_call" | custom-call | flops 1500000000 | bytes 1572864 | tf_op jit(solution)/shard_map/coarse/pallas_call | solution.py:182
  47.8 0.1 collective-permute-start.10
  47.9 4.7 %collective-permute-start.11 = (f32[344,128]{1,0:T(8,128)S(1)}, f32[344,128]{1,0:T(8,128)S(1)}, u32[]{:S(2)}, u32[]{:S(2)}) collective-permute-start(f32[344,128]{1,0:T(8,128)S(1)} %get-tuple-element.38), channel_id=1, source_target_pairs={{4,0},{8,4},{12,8},{16,12},{20,16},{24,20},{28,24},{0,28},{5,1},{9... | collective-permute-start | bytes 528392 | tf_op jit(solution)/shard_map/ppermute | solution.py:732
  52.6 2.1 %detail_x.1.d_ref = f32[32,128,256]{2,1,0:T(8,128)S(1)} custom-call(f32[32,128,256]{2,1,0:T(8,128)S(1)} %get-tuple-element.40.p_ref), custom_call_target="tpu_custom_call" | custom-call | flops 16777216 | bytes 8388608 | tf_op jit(solution)/shard_map/detail_x/pallas_call | solution.py:182
  54.7 1.4 %collective-permute-done.12.el = f32[2,128,256]{2,1,0:T(8,128)S(1)} collective-permute-done((f32[2,128,256]{2,1,0:T(8,128)S(1)}, f32[2,128,256]{2,1,0:T(8,128)S(1)}, u32[]{:S(2)}, u32[]{:S(2)}) %collective-permute-start.12) | collective-permute-done | bytes 262176 | tf_op jit(solution)/shard_map/ppermute | solution.py:727
  56.1 2.6 %collective-permute-done.13.er = f32[2,128,256]{2,1,0:T(8,128)S(1)} collective-permute-done((f32[2,128,256]{2,1,0:T(8,128)S(1)}, f32[2,128,256]{2,1,0:T(8,128)S(1)}, u32[]{:S(2)}, u32[]{:S(2)}) %collective-permute-start.13) | collective-permute-done | bytes 262176 | tf_op jit(solution)/shard_map/ppermute | solution.py:732
  58.7 0.6 collective-permute-done.10.l_ref
  59.3 2.3 %collective-permute-done.11.r_ref = f32[344,128]{1,0:T(8,128)S(1)} collective-permute-done((f32[344,128]{1,0:T(8,128)S(1)}, f32[344,128]{1,0:T(8,128)S(1)}, u32[]{:S(2)}, u32[]{:S(2)}) %collective-permute-start.11) | collective-permute-done | bytes 176160 | tf_op jit(solution)/shard_map/ppermute | solution.py:732
  61.6 5.5 %final.1 = f32[32,128,256]{2,1,0:T(8,128)} custom-call(f32[20,72,128]{2,1,0:T(8,128)S(1)} %get-tuple-element.36.a_ref, f32[344,128]{1,0:T(8,128)S(1)} %collective-permute-done.10.l_ref, f32[344,128]{1,0:T(8,128)S(1)} %collective-permute-done.11.r_ref, f32[32,128,256]{2,1,0:T(8,128)S(1)} %detail_x.1.d_ref, f32[2,128,256]{2,1,0:T(8,128)S(1)} %collective-permute-done.12.el, ...), custom_call_target="tpu_custom_call" | custom-call | flops 8388608 | bytes 8388608 | tf_op jit(solution)/shard_map/final/pallas_call | solution.py:708
  (25 shorter events, 0.1 us)
Async XLA Ops:
  0.0 2.2 %copy-start = (f32[32,128,256]{2,1,0:T(8,128)S(1)}, f32[32,128,256]{2,1,0:T(8,128)}, u32[]{:S(2)}) copy-start(f32[32,128,256]{2,1,0:T(8,128)} %y_first.1) | copy-start | bytes 12582916
  2.2 7.9 %copy-start.1 = (bf16[768,256]{1,0:T(8,128)(2,1)S(1)}, bf16[768,256]{1,0:T(8,128)(2,1)}, u32[]{:S(2)}) copy-start(bf16[768,256]{1,0:T(8,128)(2,1)} %constant.28.clone.z) | copy-start | bytes 1179652
  2.3 9.8 %collective-permute-start = (f32[32,8,256]{2,1,0:T(8,128)S(1)}, f32[32,8,256]{2,1,0:T(8,128)S(1)}, u32[]{:S(2)}, u32[]{:S(2)}) collective-permute-start(f32[32,8,256]{2,1,0:T(8,128)S(1)} %get-tuple-element.24), channel_id=1, source_target_pairs={{0,1},{1,2},{2,3},{3,0},{4,5},{5,6},{6,7},{7,4},{8,9},{9,10},{10,1... | collective-permute-start | bytes 786440 | tf_op jit(solution)/shard_map/ppermute | solution.py:727
  2.8 9.3 %collective-permute-start.1 = (f32[32,8,256]{2,1,0:T(8,128)S(1)}, f32[32,8,256]{2,1,0:T(8,128)S(1)}, u32[]{:S(2)}, u32[]{:S(2)}) collective-permute-start(f32[32,8,256]{2,1,0:T(8,128)S(1)} %get-tuple-element.25), channel_id=1, source_target_pairs={{1,0},{2,1},{3,2},{0,3},{5,4},{6,5},{7,6},{4,7},{9,8},{10,9},{11,1... | collective-permute-start | bytes 786440 | tf_op jit(solution)/shard_map/ppermute | solution.py:732
  4.8 14.5 %collective-permute-start.2 = (f32[2,128,256]{2,1,0:T(8,128)S(1)}, f32[2,128,256]{2,1,0:T(8,128)S(1)}, u32[]{:S(2)}, u32[]{:S(2)}) collective-permute-start(f32[2,128,256]{2,1,0:T(8,128)S(1)} %get-tuple-element.26), channel_id=1, source_target_pairs={{0,4},{4,8},{8,12},{12,16},{16,20},{20,24},{24,28},{28,0},{1,5},{5... | collective-permute-start | bytes 786440 | tf_op jit(solution)/shard_map/ppermute | solution.py:727
  7.0 9.9 %copy-start.2 = (bf16[144,432]{1,0:T(8,128)(2,1)S(1)}, bf16[144,432]{1,0:T(8,128)(2,1)}, u32[]{:S(2)}) copy-start(bf16[144,432]{1,0:T(8,128)(2,1)} %constant.29.clone.y) | copy-start | bytes 373252
  7.0 14.5 %collective-permute-start.3 = (f32[2,128,256]{2,1,0:T(8,128)S(1)}, f32[2,128,256]{2,1,0:T(8,128)S(1)}, u32[]{:S(2)}, u32[]{:S(2)}) collective-permute-start(f32[2,128,256]{2,1,0:T(8,128)S(1)} %get-tuple-element.27), channel_id=1, source_target_pairs={{4,0},{8,4},{12,8},{16,12},{20,16},{24,20},{28,24},{0,28},{5,1},{9... | collective-permute-start | bytes 786440 | tf_op jit(solution)/shard_map/ppermute | solution.py:732
  12.1 9.4 %collective-permute-start.4 = (f32[2,16,256]{2,1,0:T(8,128)S(1)}, f32[2,16,256]{2,1,0:T(8,128)S(1)}, u32[]{:S(2)}, u32[]{:S(2)}) collective-permute-start(f32[2,16,256]{2,1,0:T(8,128)S(1)} %get-tuple-element.28), channel_id=1, source_target_pairs={{0,4},{4,8},{8,12},{12,16},{16,20},{20,24},{24,28},{28,0},{1,5},{5... | collective-permute-start | bytes 98312 | tf_op jit(solution)/shard_map/ppermute | solution.py:727
  13.0 8.9 %collective-permute-start.5 = (f32[2,16,256]{2,1,0:T(8,128)S(1)}, f32[2,16,256]{2,1,0:T(8,128)S(1)}, u32[]{:S(2)}, u32[]{:S(2)}) collective-permute-start(f32[2,16,256]{2,1,0:T(8,128)S(1)} %get-tuple-element.29), channel_id=1, source_target_pairs={{4,0},{8,4},{12,8},{16,12},{20,16},{24,20},{28,24},{0,28},{5,1},{9... | collective-permute-start | bytes 98312 | tf_op jit(solution)/shard_map/ppermute | solution.py:732
  19.2 5.7 %copy-start.7 = (s32[3,7]{1,0:T(4,128)S(1)}, s32[3,7]{1,0:T(4,128)}, u32[]{:S(2)}) copy-start(s32[3,7]{1,0:T(4,128)} %index_ref.3) | copy-start | bytes 256
  19.2 5.7 %copy-start.8 = (f32[16]{0:T(128)S(1)}, f32[16]{0:T(128)}, u32[]{:S(2)}) copy-start(f32[16]{0:T(128)} %table_ref.3) | copy-start | bytes 196
  23.1 6.5 %collective-permute-start.6 = (f32[16,24,128]{2,1,0:T(8,128)S(1)}, f32[16,24,128]{2,1,0:T(8,128)S(1)}, u32[]{:S(2)}, u32[]{:S(2)}) collective-permute-start(f32[16,24,128]{2,1,0:T(8,128)S(1)} %get-tuple-element.31), channel_id=1, source_target_pairs={{0,1},{1,2},{2,3},{3,0},{4,5},{5,6},{6,7},{7,4},{8,9},{9,10},{10,1... | collective-permute-start | bytes 589832 | tf_op jit(solution)/shard_map/ppermute | solution.py:727
  23.1 6.4 %collective-permute-start.7 = (f32[16,24,128]{2,1,0:T(8,128)S(1)}, f32[16,24,128]{2,1,0:T(8,128)S(1)}, u32[]{:S(2)}, u32[]{:S(2)}) collective-permute-start(f32[16,24,128]{2,1,0:T(8,128)S(1)} %get-tuple-element.32), channel_id=1, source_target_pairs={{1,0},{2,1},{3,2},{0,3},{5,4},{6,5},{7,6},{4,7},{9,8},{10,9},{11,1... | collective-permute-start | bytes 589832 | tf_op jit(solution)/shard_map/ppermute | solution.py:732
  24.9 4.7 %copy-start.13 = (bf16[384,128]{1,0:T(8,128)(2,1)S(1)}, bf16[384,128]{1,0:T(8,128)(2,1)}, u32[]{:S(2)}) copy-start(bf16[384,128]{1,0:T(8,128)(2,1)} %constant.30.clone.z) | copy-start | bytes 294916
  24.9 4.7 %copy-start.14 = (bf16[96,336]{1,0:T(8,128)(2,1)S(1)}, bf16[96,336]{1,0:T(8,128)(2,1)}, u32[]{:S(2)}) copy-start(bf16[96,336]{1,0:T(8,128)(2,1)} %constant.31.clone.y) | copy-start | bytes 193540
  24.9 10.6 %copy-start.9 = (bf16[768,256]{1,0:T(8,128)(2,1)S(1)}, bf16[768,256]{1,0:T(8,128)(2,1)}, u32[]{:S(2)}) copy-start(bf16[768,256]{1,0:T(8,128)(2,1)} %constant.32.clone.z) | copy-start | bytes 1179652
  24.9 10.6 %copy-start.10 = (bf16[128,432]{1,0:T(8,128)(2,1)S(1)}, bf16[128,432]{1,0:T(8,128)(2,1)}, u32[]{:S(2)}) copy-start(bf16[128,432]{1,0:T(8,128)(2,1)} %constant.33.clone.y) | copy-start | bytes 331780
  30.6 14.2 %collective-permute-start.8 = (f32[248,128]{1,0:T(8,128)S(1)}, f32[248,128]{1,0:T(8,128)S(1)}, u32[]{:S(2)}, u32[]{:S(2)}) collective-permute-start(f32[248,128]{1,0:T(8,128)S(1)} %get-tuple-element.34), channel_id=1, source_target_pairs={{0,4},{4,8},{8,12},{12,16},{16,20},{20,24},{24,28},{28,0},{1,5},{5... | collective-permute-start | bytes 380936 | tf_op jit(solution)/shard_map/ppermute | solution.py:727
  30.9 13.8 %copy-start.4 = (bf16[384,128]{1,0:T(8,128)(2,1)S(1)}, bf16[384,128]{1,0:T(8,128)(2,1)}, u32[]{:S(2)}) copy-start(bf16[384,128]{1,0:T(8,128)(2,1)} %constant.34.clone.z1) | copy-start | bytes 294916
  31.0 13.9 %copy-start.6 = (bf16[80,288]{1,0:T(8,128)(2,1)S(1)}, bf16[80,288]{1,0:T(8,128)(2,1)}, u32[]{:S(2)}) copy-start(bf16[80,288]{1,0:T(8,128)(2,1)} %constant.39.clone.s1) | copy-start | bytes 138244
  31.0 13.9 %copy-start.11 = (bf16[384,128]{1,0:T(8,128)(2,1)S(1)}, bf16[384,128]{1,0:T(8,128)(2,1)}, u32[]{:S(2)}) copy-start(bf16[384,128]{1,0:T(8,128)(2,1)} %constant.36.clone.z2s) | copy-start | bytes 294916
  31.0 13.9 %copy-start.12 = (bf16[384,128]{1,0:T(8,128)(2,1)S(1)}, bf16[384,128]{1,0:T(8,128)(2,1)}, u32[]{:S(2)}) copy-start(bf16[384,128]{1,0:T(8,128)(2,1)} %constant.35.clone.z2a) | copy-start | bytes 294916
  31.0 13.9 %copy-start.15 = (bf16[64,144]{1,0:T(8,128)(2,1)S(1)}, bf16[64,144]{1,0:T(8,128)(2,1)}, u32[]{:S(2)}) copy-start(bf16[64,144]{1,0:T(8,128)(2,1)} %constant.38.clone.s2) | copy-start | bytes 55300
  31.0 13.9 %copy-start.16 = (bf16[48,192]{1,0:T(8,128)(2,1)S(1)}, bf16[48,192]{1,0:T(8,128)(2,1)}, u32[]{:S(2)}) copy-start(bf16[48,192]{1,0:T(8,128)(2,1)} %constant.37.clone.a2) | copy-start | bytes 55300
  31.0 13.8 %collective-permute-start.9 = (f32[248,128]{1,0:T(8,128)S(1)}, f32[248,128]{1,0:T(8,128)S(1)}, u32[]{:S(2)}, u32[]{:S(2)}) collective-permute-start(f32[248,128]{1,0:T(8,128)S(1)} %get-tuple-element.35), channel_id=1, source_target_pairs={{4,0},{8,4},{12,8},{16,12},{20,16},{24,20},{28,24},{0,28},{5,1},{9... | collective-permute-start | bytes 380936 | tf_op jit(solution)/shard_map/ppermute | solution.py:732
  40.0 16.1 %collective-permute-start.12 = (f32[2,128,256]{2,1,0:T(8,128)S(1)}, f32[2,128,256]{2,1,0:T(8,128)S(1)}, u32[]{:S(2)}, u32[]{:S(2)}) collective-permute-start(f32[2,128,256]{2,1,0:T(8,128)S(1)} %get-tuple-element.41), channel_id=1, source_target_pairs={{0,4},{4,8},{8,12},{12,16},{16,20},{20,24},{24,28},{28,0},{1,5},{5... | collective-permute-start | bytes 786440 | tf_op jit(solution)/shard_map/ppermute | solution.py:727
  40.1 18.6 %collective-permute-start.13 = (f32[2,128,256]{2,1,0:T(8,128)S(1)}, f32[2,128,256]{2,1,0:T(8,128)S(1)}, u32[]{:S(2)}, u32[]{:S(2)}) collective-permute-start(f32[2,128,256]{2,1,0:T(8,128)S(1)} %get-tuple-element.42), channel_id=1, source_target_pairs={{4,0},{8,4},{12,8},{16,12},{20,16},{24,20},{28,24},{0,28},{5,1},{9... | collective-permute-start | bytes 786440 | tf_op jit(solution)/shard_map/ppermute | solution.py:732
  47.8 11.5 %collective-permute-start.10 = (f32[344,128]{1,0:T(8,128)S(1)}, f32[344,128]{1,0:T(8,128)S(1)}, u32[]{:S(2)}, u32[]{:S(2)}) collective-permute-start(f32[344,128]{1,0:T(8,128)S(1)} %get-tuple-element.37), channel_id=1, source_target_pairs={{0,4},{4,8},{8,12},{12,16},{16,20},{20,24},{24,28},{28,0},{1,5},{5... | collective-permute-start | bytes 528392 | tf_op jit(solution)/shard_map/ppermute | solution.py:727
  47.9 13.7 %collective-permute-start.11 = (f32[344,128]{1,0:T(8,128)S(1)}, f32[344,128]{1,0:T(8,128)S(1)}, u32[]{:S(2)}, u32[]{:S(2)}) collective-permute-start(f32[344,128]{1,0:T(8,128)S(1)} %get-tuple-element.38), channel_id=1, source_target_pairs={{4,0},{8,4},{12,8},{16,12},{20,16},{24,20},{28,24},{0,28},{5,1},{9... | collective-permute-start | bytes 528392 | tf_op jit(solution)/shard_map/ppermute | solution.py:732
  52.6 9.0 %copy-start.3 = (bf16[384,256]{1,0:T(8,128)(2,1)S(1)}, bf16[384,256]{1,0:T(8,128)(2,1)}, u32[]{:S(2)}) copy-start(bf16[384,256]{1,0:T(8,128)(2,1)} %constant.40.clone.z) | copy-start | bytes 589828
  52.6 9.0 %copy-start.5 = (bf16[128,240]{1,0:T(8,128)(2,1)S(1)}, bf16[128,240]{1,0:T(8,128)(2,1)}, u32[]{:S(2)}) copy-start(bf16[128,240]{1,0:T(8,128)(2,1)} %constant.41.clone.y) | copy-start | bytes 184324

commit v3 on v2

--- a/solution.py
+++ b/solution.py
@@ -255,32 +255,6 @@
     )
 
 
-def corner_messages(y_left, y_right):
-    nx, rows, nz = y_left.shape
-
-    def kernel(last_l, first_l, last_r, first_r, up, down):
-        for part, last, first in ((0, last_l, first_l), (1, last_r, first_r)):
-            at = pl.ds(8 * part, 8)
-            up[0, at] = last[3]
-            up[1, at] = H[0] * last[1] + H[1] * last[2]
-            down[0, at] = first[0]
-            down[1, at] = H[6] * first[1] + H[7] * first[2]
-
-    last = pl.BlockSpec((4, rows, nz), lambda i: (nx // 4 - 1, 0, 0))
-    first = pl.BlockSpec((4, rows, nz), lambda i: (0, 0, 0))
-    return call(
-        kernel,
-        (1,),
-        [last, first, last, first],
-        [whole_out(2, 16, nz)] * 2,
-        [shape(2, 16, nz)] * 2,
-        [y_left, y_left, y_right, y_right],
-        1e5,
-        2e5,
-        name="corner_messages",
-    )
-
-
 def over_planes(count, group, body):
     def step(i, carry):
         body(i * group)
@@ -331,29 +305,17 @@
     )
 
 
-def first_approx(bands, x_left, x_right, c_left, c_right, z_matrix, y_matrix, own, ghost_rows):
+def own_approx(bands, own, ghost_rows):
     nx, rows, nz = bands.shape
-    ny = x_left.shape[1]
     half_z = nz // 2
     n1 = nx // 2
 
-    def kernel(b_ref, xl, xr, cl, cr, z, y, halo, approx, up, down):
-        planes = [
-            jnp.concatenate([corner[i, :8], main[i], corner[i, 8:]], axis=0)
-            for main, corner in ((xl, cl), (xr, cr))
-            for i in range(2)
-        ]
-        zed = times(jnp.concatenate(planes, axis=0), z)
-        for i in range(4):
-            halo[i] = left_times(y, zed[i * (ny + 16) : (i + 1) * (ny + 16)])
-        place = {"l1": 0, "l2": 1, "r1": 2, "r2": 3}
-
+    def kernel(b_ref, approx, up, down):
         def tile(t, carry):
             at = pl.ds(pl.multiple_of(t * 8, 8), 8)
-            values = {key: halo[i, at, :half_z] for key, i in place.items()}
-            values.update({i: b_ref[i, at, :half_z] for i in range(nx)})
+            values = {i: b_ref[i, at, :half_z] for i in range(nx)}
             for k in range(n1):
-                approx[k, at] = x_low(values.get, k, nx)
+                approx[k, at] = added([(c, values[i]) for i, c, _ in x_terms(k, nx) if i in values])
             return carry
 
         lax.fori_loop(0, own // 8, tile, 0)
@@ -362,26 +324,54 @@
 
     return whole_call(
         kernel,
-        [
-            shape(4, rows, nz),
-            shape(n1, own, half_z),
-            shape(n1, ghost_rows, half_z),
-            shape(n1, ghost_rows, half_z),
-        ],
-        [bands, x_left, x_right, c_left, c_right, z_matrix, y_matrix],
-        24 * rows * (ny + 16) * nz + 24 * (ny + 16) * nz * nz,
+        [shape(n1, own, half_z), shape(n1, ghost_rows, half_z), shape(n1, ghost_rows, half_z)],
+        [bands],
+        16 * n1 * own * half_z,
         3e6,
-        name="first_approx",
-    )
-
-
-def detail_bands(bands, halo, table, index):
+        name="own_approx",
+    )
+
+
+def x_halo_messages(x_left, x_right, z_matrix, wide):
+    _, ny, nz = x_left.shape
+    half_z = nz // 2
+
+    def kernel(xl, xr, z, out, up, down):
+        planes = jnp.concatenate([xl[0], xl[1], xr[0], xr[1]], axis=0)
+        out[...] = times(planes, z).reshape(4, ny, nz)
+        up[:, :wide] = out[:, ny - wide :, :half_z]
+        up[:, wide:] = out[:, ny - 8 :, half_z:]
+        down[:, :wide] = out[:, :wide, :half_z]
+        down[:, wide:] = out[:, :8, half_z:]
+
+    return whole_call(
+        kernel,
+        [shape(4, ny, nz), shape(4, wide + 8, half_z), shape(4, wide + 8, half_z)],
+        [x_left, x_right, z_matrix],
+        24 * ny * nz * nz,
+        3e6,
+        name="x_halo_messages",
+    )
+
+
+def edges_of(n):
+    return [0, 1, n - 2, n - 1]
+
+
+def detail_bands(bands, halo, h_left, h_right, table, index, y_matrix):
     nx, rows, nz = bands.shape
     n1 = nx // 2
     half_z = nz // 2
     half_tiles = rows // 16
-
-    def kernel(table_ref, index_ref, b_ref, h_ref, out):
+    wide = h_left.shape[1] - 8
+    ends = edges_of(n1)
+    inner = [k for k in range(n1) if k not in ends]
+
+    def kernel(table_ref, index_ref, b_ref, x_ref, hl, hr, y, edge, rest, h_ref):
+        for i in range(4):
+            low = jnp.concatenate([hl[i, wide - 8 : wide], x_ref[i, :, :half_z], hr[i, :8]], axis=0)
+            high = jnp.concatenate([hl[i, wide:], x_ref[i, :, half_z:], hr[i, wide:]], axis=0)
+            h_ref[i] = left_times(y, jnp.concatenate([low, high], axis=1))
         place = {"l1": 0, "l2": 1, "r1": 2, "r2": 3}
 
         def tiles(by):
@@ -395,11 +385,12 @@
                     values = {key: h_ref[i, at, lanes] for key, i in place.items()}
                     values.update({i: b_ref[i, at, lanes] for i in range(nx)})
                     coeffs = x_interior(values.get, nx)
-                    for k in (0, 1, n1 - 2, n1 - 1):
+                    for k in ends:
                         coeffs[k] = (x_low(values.get, k, nx), x_high(values.get, k, nx))
                     for k, (low, high) in coeffs.items():
-                        out[k, at, lanes] = shrink(low, quiet) if band else jnp.zeros_like(low)
-                        out[n1 + k, at, lanes] = shrink(high, loud)
+                        target, place_k, count = (edge, ends.index(k), 4) if k in ends else (rest, k - 2, n1 - 4)
+                        target[place_k, at, lanes] = shrink(low, quiet) if band else jnp.zeros_like(low)
+                        target[count + place_k, at, lanes] = shrink(high, loud)
                 return carry
 
             return tile
@@ -409,59 +400,84 @@
 
     return whole_call(
         kernel,
-        shape(nx, rows, nz),
-        [table, index, bands, halo],
+        [shape(8, rows, nz), shape(2 * len(inner), rows, nz)],
+        [table, index, bands, halo, h_left, h_right, y_matrix],
         40 * nx * rows * nz,
         8 * nx * rows * nz,
+        scratch=[pltpu.VMEM((4, rows, nz), F32)],
         name="detail_bands",
     )
 
 
-def detail_yz(coeffs, z_matrix, y_matrix):
-    nx, rows, nz = coeffs.shape
+def yz_synthesis(coeffs, z, y, out, zed):
+    count, rows, nz = coeffs.shape
+
+    def z_body(first):
+        at = pl.ds(first, 8)
+        zed[at] = times(coeffs[at].reshape(8 * rows, nz), z).reshape(8, rows, nz)
+
+    def y_body(first):
+        for j in range(8):
+            out[first + j] = left_times(y, zed[first + j])
+
+    over_planes(count, 8, z_body)
+    over_planes(count, 8, y_body)
+
+
+def detail_edges(coeffs, z_matrix, y_matrix):
+    count, rows, nz = coeffs.shape
     ny = y_matrix.shape[0]
-    n1 = nx // 2
 
     def kernel(c_ref, z, y, out, up, down, zed):
-        def z_body(first):
-            at = pl.ds(first, 8)
-            zed[at] = times(c_ref[at].reshape(8 * rows, nz), z).reshape(8, rows, nz)
-
-        def y_body(first):
-            for j in range(8):
-                out[first + j] = left_times(y, zed[first + j])
-
-        over_planes(nx, 8, z_body)
-        over_planes(nx, 8, y_body)
-        lows = {k: out.at[k] for k in range(n1)}
-        highs = {k: out.at[n1 + k] for k in range(n1)}
-        value = lambda part, ks: {k: part[k][...] for k in ks}
-        ends = (n1 - 2, n1 - 1)
-        up[0], up[1] = spill_up(value(lows, ends), value(highs, ends), n1)
-        down[0], down[1] = spill_down(value(lows, (0, 1)), value(highs, (0, 1)))
-
-    return whole_call(
-        kernel,
-        [shape(nx, ny, nz), shape(2, ny, nz), shape(2, ny, nz)],
+        yz_synthesis(c_ref, z, y, out, zed)
+        part = lambda ks, at: {k: out[i] for k, i in zip(ks, at)}
+        up[0], up[1] = spill_up(part((0, 1), (2, 3)), part((0, 1), (6, 7)), 2)
+        down[0], down[1] = spill_down(part((0, 1), (0, 1)), part((0, 1), (4, 5)))
+
+    return whole_call(
+        kernel,
+        [shape(count, ny, nz), shape(2, ny, nz), shape(2, ny, nz)],
         [coeffs, z_matrix, y_matrix],
-        6 * nx * rows * nz * nz + 6 * nx * rows * ny * nz,
-        4 * nx * nz * (rows + ny),
-        scratch=[pltpu.VMEM((nx, rows, nz), F32)],
-        name="detail_yz",
-    )
-
-
-def detail_x(parts):
-    nx, ny, nz = parts.shape
-    n1 = nx // 2
-
-    def kernel(p_ref, out):
+        6 * count * rows * nz * (nz + ny),
+        4 * count * nz * (rows + ny),
+        scratch=[pltpu.VMEM((count, rows, nz), F32)],
+        name="detail_edges",
+    )
+
+
+def detail_rest(coeffs, z_matrix, y_matrix):
+    count, rows, nz = coeffs.shape
+    ny = y_matrix.shape[0]
+    return whole_call(
+        yz_synthesis,
+        shape(count, ny, nz),
+        [coeffs, z_matrix, y_matrix],
+        6 * count * rows * nz * (nz + ny),
+        4 * count * nz * (rows + ny),
+        scratch=[pltpu.VMEM((count, rows, nz), F32)],
+        name="detail_rest",
+    )
+
+
+def detail_x(edge, rest):
+    count, ny, nz = rest.shape
+    n1 = (count + 8) // 2
+    nx = 2 * n1
+    ends = edges_of(n1)
+
+    def kernel(e_ref, r_ref, out):
         def tile(t, carry):
             at = pl.ds(pl.multiple_of(t * 8, 8), 8)
             for lane in range(0, nz, 128):
                 lanes = pl.ds(lane, 128)
-                lows = {k: p_ref[k, at, lanes] for k in range(n1)}
-                highs = {k: p_ref[n1 + k, at, lanes] for k in range(n1)}
+
+                def coeff(k, high):
+                    if k in ends:
+                        return e_ref[4 * high + ends.index(k), at, lanes]
+                    return r_ref[(n1 - 4) * high + k - 2, at, lanes]
+
+                lows = {k: coeff(k, 0) for k in range(n1)}
+                highs = {k: coeff(k, 1) for k in range(n1)}
                 for m in range(nx):
                     out[m, at, lanes] = x_synth(m, lows, highs)
             return carry
@@ -469,7 +485,7 @@
         lax.fori_loop(0, ny // 8, tile, 0)
 
     return whole_call(
-        kernel, shape(nx, ny, nz), [parts], 16 * nx * ny * nz, 8 * nx * ny * nz, name="detail_x"
+        kernel, shape(nx, ny, nz), [edge, rest], 16 * nx * ny * nz, 8 * nx * ny * nz, name="detail_x"
     )
 
 
@@ -498,14 +514,27 @@
     return [jnp.where(lane < half, part, 0.0) for part in (both, pltpu.roll(both, half, 1))]
 
 
-def second_bands(own, left, right, z_matrix, y_matrix, low_rows):
+def second_bands(own, left, right, halo, h_left, h_right, z_matrix, yx_matrix, y_matrix, low_rows):
     n1, own_rows, nz = own.shape
     in_rows = own_rows + 2 * left.shape[1]
     rows = y_matrix.shape[0]
 
-    def kernel(o_ref, l_ref, r_ref, z, y, out, up, down):
+    wide = h_left.shape[1] - 8
+
+    def kernel(o_ref, l_ref, r_ref, x_ref, hl, hr, z, yx, y, out, up, down):
+        planes = [jnp.concatenate([hl[i, :wide], x_ref[i, :, :nz], hr[i, :wide]], axis=0) for i in range(4)]
+        l1, l2, r1, r2 = [plane[:in_rows] for plane in in_pairs(yx, planes)]
+        beyond = {
+            0: l2 + H[2] * l1,
+            1: H[0] * l1,
+            n1 - 2: H[7] * r1,
+            n1 - 1: r2 + H[5] * r1,
+        }
         for i in range(0, n1, 8):
-            stack = [part[j] for j in range(i, i + 8) for part in (o_ref, l_ref, r_ref)]
+            stack = []
+            for j in range(i, i + 8):
+                plane = jnp.concatenate([o_ref[j], l_ref[j], r_ref[j]], axis=0)
+                stack.append(plane + beyond[j] if j in beyond else plane)
             zed = times(jnp.concatenate(stack, axis=0), z)
             for j, plane in enumerate(in_pairs(y, cut(zed, in_rows))):
                 out[i + j] = plane
@@ -527,7 +556,7 @@
     return whole_call(
         kernel,
         [shape(n1, rows, nz), shape(message, nz), shape(message, nz)],
-        [own, left, right, z_matrix, y_matrix],
+        [own, left, right, halo, h_left, h_right, z_matrix, yx_matrix, y_matrix],
         6 * n1 * in_rows * nz * (nz + rows),
         4 * n1 * nz * (in_rows + rows),
         name="second_bands",
@@ -735,7 +764,7 @@
 def local(velocity, table, index):
     nx, ny, nz = velocity.shape
     y1, y2, y3 = ny // 2, ny // 4, ny // 8
-    ghost = 24
+    ghost, wide = 24, 48
     cells0 = list(range(-8, ny + 8))
     rows0 = up_to(y1 + 4, 8)
     ks0 = fill(list(range(y1)) + [-2, -1, y1, y1 + 1], rows0)
@@ -748,6 +777,7 @@
     ys0_matrix = synthesis_rows(list(range(ny)), ks0, ks0)
     ys0 = from_left(ys0_matrix)
     ys0_low = from_left(ys0_matrix[:, :rows0])
+    yx0 = from_left(analysis_rows(list(range(-wide, ny + wide)), cells1, []))
     ya1 = from_left(analysis_rows(cells1, low1, high1))
     ys1 = from_left(synthesis_rows(ks0, low1, high1))
     ya2 = from_left(analysis_rows(low1, ks2, ks2))
@@ -760,33 +790,36 @@
     za2, zs2 = from_right(z2), from_right(z2.T)
 
     x_up, x_down, y_up, y_down = first_messages(velocity)
+    x_left = to_next(x_up, "gx")
+    x_right = to_previous(x_down, "gx")
     y_left = to_next(y_up, "gy")
     y_right = to_previous(y_down, "gy")
-    x_left = to_next(x_up, "gx")
-    x_right = to_previous(x_down, "gx")
     zed = depth(velocity, za0, 16, "depth_analysis")
-    c_up, c_down = corner_messages(y_left, y_right)
-    c_left = to_next(c_up, "gx")
-    c_right = to_previous(c_down, "gx")
     bands = y_analysis(zed, y_left, y_right, za0, ya0)
-    halo, approx, a_up, a_down = first_approx(
-        bands, x_left, x_right, c_left, c_right, za0, ya0, y1, ghost
-    )
+    approx, a_up, a_down = own_approx(bands, y1, ghost)
     a_left = to_next(a_up, "gy")
     a_right = to_previous(a_down, "gy")
-    coeffs = detail_bands(bands, halo, table, index)
-    bands1, b_up, b_down = second_bands(approx, a_left, a_right, za1, ya1, rows1)
+    halo, h_up, h_down = x_halo_messages(x_left, x_right, za0, wide)
+    h_left = to_next(h_up, "gy")
+    h_right = to_previous(h_down, "gy")
+    bands1, b_up, b_down = second_bands(
+        approx, a_left, a_right, halo, h_left, h_right, za1, yx0, ya1, rows1
+    )
     b_left = to_next(b_up, "gx")
     b_right = to_previous(b_down, "gx")
-    parts, e_up, e_down = detail_yz(coeffs, zs0, ys0)
+    h_left, h_right, bands1 = lax.optimization_barrier((h_left, h_right, bands1))
+    edge, rest = detail_bands(bands, halo, h_left, h_right, table, index, ya0)
+    edge, e_up, e_down = detail_edges(edge, zs0, ys0)
     e_left = to_next(e_up, "gx")
     e_right = to_previous(e_down, "gx")
+    bands1, edge = lax.optimization_barrier((bands1, edge))
     approx1, s_up, s_down = coarse(
         bands1, b_left, b_right, table, index, zs1, za2, zs2, ya2, ys2, ys1, rows1, rows0
     )
     s_left = to_next(s_up, "gx")
     s_right = to_previous(s_down, "gx")
-    detail = detail_x(parts)
+    rest, approx1 = lax.optimization_barrier((rest, approx1))
+    detail = detail_x(edge, detail_rest(rest, zs0, ys0))
     return final(
         approx1, s_left, s_right, detail, e_left, e_right, zs1, ys1, zs0_low, ys0_low, rows1
     )

time: 67.2 us -> 63.3 us (0.942)
  starting transfers between devices: 28.7 us -> 25.7 us
  waiting for transfers between devices: 11.5 us -> 10.3 us
    ppermute x7, waiting for transfers between devices: 7.4 us -> 5.15 us  [to_previous(): return lax.ppermute(array, axis, [((i + 1) % size, i) for i in range(size)])]
    ppermute x7, starting transfers between devices: 24.6 us -> 22.4 us  [to_previous(): return lax.ppermute(array, axis, [((i + 1) % size, i) for i in range(size)])]
    ppermute x7, waiting for transfers between devices: 4.09 us -> 5.17 us  [to_next(): return lax.ppermute(array, axis, [(i, (i + 1) % size) for i in range(size)])]
    ppermute x7, starting transfers between devices: 4.12 us -> 3.28 us  [to_next(): return lax.ppermute(array, axis, [(i, (i + 1) % size) for i in range(size)])]
    pallas_call x8 -> x10, Pallas kernels: 18.7 us -> 18.9 us  [whole_call(): pl.pallas_call(kernel, in_specs=specs, out_specs=outs, out_shape=out_shap...]
    unnamed x34 -> x36, local copies, waits for them, and re-layouts: 2.26 us -> 2.3 us
  transfers between devices with their start and end apart: 14 -> 14, of which waited for: 8 -> 6; matrix products, arithmetic and copies ran while one was open for 0% -> 0% of each run, Pallas kernels for 25% -> 28%
where the time goes in v3:
time: 63.3 us; the launch traced here: 63.1 us
  starting transfers between devices  25.7 us (41%)
  Pallas kernels  24.5 us (39%)
  waiting for transfers between devices  10.3 us (16%)
  local copies, waits for them, and re-layouts  2.3 us (4%)
    ppermute x7, starting transfers between devices, to_previous(): return lax.ppermute(array, axis, [((i + 1) % size, i) for i in range(size)])  22.4 us
    pallas_call x10, Pallas kernels, whole_call(): pl.pallas_call(kernel, in_specs=specs, out_specs=outs, out_shape=out_shap...  18.9 us
    pallas_call x1, Pallas kernels, final(): pl.pallas_call(kernel, in_specs=[VMEM] * 10, out_specs=pl.BlockSpec(memor...  5.48 us
    ppermute x7, waiting for transfers between devices, to_next(): return lax.ppermute(array, axis, [(i, (i + 1) % size) for i in range(size)])  5.17 us
    ppermute x7, waiting for transfers between devices, to_previous(): return lax.ppermute(array, axis, [((i + 1) % size, i) for i in range(size)])  5.15 us
    ppermute x7, starting transfers between devices, to_next(): return lax.ppermute(array, axis, [(i, (i + 1) % size) for i in range(size)])  3.28 us
    unnamed x36, local copies, waits for them, and re-layouts  2.3 us
  transfers between devices with their start and end apart: 14, of which 6 were waited for; matrix products, arithmetic and copies ran while one was open for 0% of the time, Pallas kernels for 28%

profile of v3, /device:TPU:0, one launch (start us, length us, event | category | flops | bytes accessed | tf_op | source)
XLA Modules:
  0.0 63.1 jit_solution(14059742159277022846)
XLA Ops:
  0.0 2.2 %copy-done = f32[32,128,256]{2,1,0:T(8,128)S(1)} copy-done((f32[32,128,256]{2,1,0:T(8,128)S(1)}, f32[32,128,256]{2,1,0:T(8,128)}, u32[]{:S(2)}) %copy-start) | copy-done | bytes 4194328
  2.2 0.1 first_messages.1
  2.3 0.5 collective-permute-start
  2.8 2.0 %collective-permute-start.1 = (f32[32,8,256]{2,1,0:T(8,128)S(1)}, f32[32,8,256]{2,1,0:T(8,128)S(1)}, u32[]{:S(2)}, u32[]{:S(2)}) collective-permute-start(f32[32,8,256]{2,1,0:T(8,128)S(1)} %get-tuple-element.34), channel_id=1, source_target_pairs={{1,0},{2,1},{3,2},{0,3},{5,4},{6,5},{7,6},{4,7},{9,8},{10,9},{11,1... | collective-permute-start | bytes 786440 | tf_op jit(solution)/shard_map/ppermute | solution.py:761
  4.8 2.2 %collective-permute-start.2 = (f32[2,128,256]{2,1,0:T(8,128)S(1)}, f32[2,128,256]{2,1,0:T(8,128)S(1)}, u32[]{:S(2)}, u32[]{:S(2)}) collective-permute-start(f32[2,128,256]{2,1,0:T(8,128)S(1)} %get-tuple-element.35), channel_id=1, source_target_pairs={{0,4},{4,8},{8,12},{12,16},{16,20},{20,24},{24,28},{28,0},{1,5},{5... | collective-permute-start | bytes 786440 | tf_op jit(solution)/shard_map/ppermute | solution.py:756
  7.0 3.0 %collective-permute-start.3 = (f32[2,128,256]{2,1,0:T(8,128)S(1)}, f32[2,128,256]{2,1,0:T(8,128)S(1)}, u32[]{:S(2)}, u32[]{:S(2)}) collective-permute-start(f32[2,128,256]{2,1,0:T(8,128)S(1)} %get-tuple-element.36), channel_id=1, source_target_pairs={{4,0},{8,4},{12,8},{16,12},{20,16},{24,20},{28,24},{0,28},{5,1},{9... | collective-permute-start | bytes 786440 | tf_op jit(solution)/shard_map/ppermute | solution.py:761
  10.1 2.0 %depth_analysis.1.zed_ref = f32[32,128,256]{2,1,0:T(8,128)S(1)} custom-call(f32[32,128,256]{2,1,0:T(8,128)S(1)} %copy-done, bf16[768,256]{1,0:T(8,128)(2,1)S(1)} %copy-done.1), custom_call_target="tpu_custom_call" | custom-call | flops 1610612736 | bytes 8388608 | tf_op jit(solution)/shard_map/depth_analysis/pallas_call | solution.py:182
  12.1 2.3 %y_analysis.1.b_ref = f32[32,144,256]{2,1,0:T(8,128)S(1)} custom-call(f32[32,128,256]{2,1,0:T(8,128)S(1)} %depth_analysis.1.zed_ref, f32[32,8,256]{2,1,0:T(8,128)S(1)} %collective-permute-done.left, f32[32,8,256]{2,1,0:T(8,128)S(1)} %collective-permute-done.1.right, bf16[768,256]{1,0:T(8,128)(2,1)S(1)} %copy-done.1, bf16[144,432]{1,0:T(8,128)(2,1)S(1)} %copy-done.2), custom_call_target="tpu_custom_call" | custom-call | flops 1019215872 | bytes 9437184 | tf_op jit(solution)/shard_map/y_analysis/pallas_call | solution.py:182
  14.4 0.0 copy-start.4
  14.4 0.0 copy-start.6
  14.4 0.0 copy-start.7
  14.4 0.0 copy-start.10
  14.4 0.0 copy-start.11
  14.5 0.3 own_approx.1
  14.8 0.1 collective-permute-start.6
  14.9 0.0 copy-start.12
  14.9 0.0 copy-start.13
  14.9 1.7 %collective-permute-start.7 = (f32[16,24,128]{2,1,0:T(8,128)S(1)}, f32[16,24,128]{2,1,0:T(8,128)S(1)}, u32[]{:S(2)}, u32[]{:S(2)}) collective-permute-start(f32[16,24,128]{2,1,0:T(8,128)S(1)} %get-tuple-element.42), channel_id=1, source_target_pairs={{1,0},{2,1},{3,2},{0,3},{5,4},{6,5},{7,6},{4,7},{9,8},{10,9},{11,1... | collective-permute-start | bytes 589832 | tf_op jit(solution)/shard_map/ppermute | solution.py:761
  16.6 1.7 %collective-permute-done.2.xl = f32[2,128,256]{2,1,0:T(8,128)S(1)} collective-permute-done((f32[2,128,256]{2,1,0:T(8,128)S(1)}, f32[2,128,256]{2,1,0:T(8,128)S(1)}, u32[]{:S(2)}, u32[]{:S(2)}) %collective-permute-start.2) | collective-permute-done | bytes 262176 | tf_op jit(solution)/shard_map/ppermute | solution.py:756
  18.3 2.2 %collective-permute-done.3.xr = f32[2,128,256]{2,1,0:T(8,128)S(1)} collective-permute-done((f32[2,128,256]{2,1,0:T(8,128)S(1)}, f32[2,128,256]{2,1,0:T(8,128)S(1)}, u32[]{:S(2)}, u32[]{:S(2)}) %collective-permute-start.3) | collective-permute-done | bytes 262176 | tf_op jit(solution)/shard_map/ppermute | solution.py:761
  20.5 0.4 x_halo_messages.1
  20.8 0.1 collective-permute-start.4
  20.9 1.7 %collective-permute-start.5 = (f32[4,56,128]{2,1,0:T(8,128)S(1)}, f32[4,56,128]{2,1,0:T(8,128)S(1)}, u32[]{:S(2)}, u32[]{:S(2)}) collective-permute-start(f32[4,56,128]{2,1,0:T(8,128)S(1)} %get-tuple-element.39), channel_id=1, source_target_pairs={{1,0},{2,1},{3,2},{0,3},{5,4},{6,5},{7,6},{4,7},{9,8},{10,9},{11,1... | collective-permute-start | bytes 344072 | tf_op jit(solution)/shard_map/ppermute | solution.py:761
  22.6 2.9 %collective-permute-done.4.hl = f32[4,56,128]{2,1,0:T(8,128)S(1)} collective-permute-done((f32[4,56,128]{2,1,0:T(8,128)S(1)}, f32[4,56,128]{2,1,0:T(8,128)S(1)}, u32[]{:S(2)}, u32[]{:S(2)}) %collective-permute-start.4) | collective-permute-done | bytes 114720 | tf_op jit(solution)/shard_map/ppermute | solution.py:756
  25.6 1.3 %second_bands.1 = (f32[16,96,128]{2,1,0:T(8,128)S(1)}, f32[248,128]{1,0:T(8,128)S(1)}, f32[248,128]{1,0:T(8,128)S(1)}) custom-call(f32[16,64,128]{2,1,0:T(8,128)S(1)} %get-tuple-element.40.o_ref, f32[16,24,128]{2,1,0:T(8,128)S(1)} %collective-permute-done.6.l_ref, f32[16,24,128]{2,1,0:T(8,128)S(1)} %collective-permute-done.7.r_ref, ...), custom_call_target="tpu_custom_call" | custom-call | flops 308281344 | bytes 1703936 | tf_op jit(solution)/shard_map/second_bands/pallas_call | solution.py:182
  26.9 0.0 copy-start.5
  26.9 0.0 copy-start.9
  26.9 0.0 copy-start.14
  26.9 0.0 copy-start.15
  26.9 0.0 copy-start.16
  27.0 0.0 copy-start.17
  27.0 0.3 collective-permute-start.8
  27.3 4.4 %collective-permute-start.9 = (f32[248,128]{1,0:T(8,128)S(1)}, f32[248,128]{1,0:T(8,128)S(1)}, u32[]{:S(2)}, u32[]{:S(2)}) collective-permute-start(f32[248,128]{1,0:T(8,128)S(1)} %get-tuple-element.52), channel_id=1, source_target_pairs={{4,0},{8,4},{12,8},{16,12},{20,16},{24,20},{28,24},{0,28},{5,1},{9... | collective-permute-start | bytes 380936 | tf_op jit(solution)/shard_map/ppermute | solution.py:761
  31.7 3.0 %detail_bands.1 = (f32[8,144,256]{2,1,0:T(8,128)S(1)}, f32[24,144,256]{2,1,0:T(8,128)S(1)}) custom-call(f32[16]{0:T(128)S(1)} %copy-done.11, s32[3,7]{1,0:T(4,128)S(1)} %copy-done.10, f32[32,144,256]{2,1,0:T(8,128)S(1)} %y_analysis.1.b_ref, f32[4,128,256]{2,1,0:T(8,128)S(1)} %get-tuple-element.37.x_ref, f32[4,56,128]{2,1,0:T(8,128)S(1)} %collective-permute-done.4.hl, ...), custom_call_target="tpu_custom_call" | custom-call | flops 47185920 | bytes 9437184 | tf_op jit(solution)/shard_map/detail_bands/pallas_call | solution.py:182
  34.8 1.3 %detail_edges.1 = (f32[8,128,256]{2,1,0:T(8,128)S(1)}, f32[2,128,256]{2,1,0:T(8,128)S(1)}, f32[2,128,256]{2,1,0:T(8,128)S(1)}) custom-call(f32[8,144,256]{2,1,0:T(8,128)S(1)} %get-tuple-element.48.c_ref, bf16[768,256]{1,0:T(8,128)(2,1)S(1)} %copy-done.12, bf16[128,432]{1,0:T(8,128)(2,1)S(1)} %copy-done.13), custom_call_target="tpu_custom_call" | custom-call | flops 679477248 | bytes 2228224 | tf_op jit(solution)/shard_map/detail_edges/pallas_call | solution.py:182
  36.1 0.1 collective-permute-start.12
  36.2 4.7 %collective-permute-start.13 = (f32[2,128,256]{2,1,0:T(8,128)S(1)}, f32[2,128,256]{2,1,0:T(8,128)S(1)}, u32[]{:S(2)}, u32[]{:S(2)}) collective-permute-start(f32[2,128,256]{2,1,0:T(8,128)S(1)} %get-tuple-element.60), channel_id=1, source_target_pairs={{4,0},{8,4},{12,8},{16,12},{20,16},{24,20},{28,24},{0,28},{5,1},{9... | collective-permute-start | bytes 786440 | tf_op jit(solution)/shard_map/ppermute | solution.py:761
  41.0 2.9 %coarse.1 = (f32[20,72,128]{2,1,0:T(8,128)S(1)}, f32[344,128]{1,0:T(8,128)S(1)}, f32[344,128]{1,0:T(8,128)S(1)}) custom-call(f32[16]{0:T(128)S(1)} %copy-done.11, s32[3,7]{1,0:T(4,128)S(1)} %copy-done.10, f32[16,96,128]{2,1,0:T(8,128)S(1)} %get-tuple-element.50.b_ref, f32[248,128]{1,0:T(8,128)S(1)} %collective-permute-done.8.l_ref, ...), custom_call_target="tpu_custom_call" | custom-call | flops 1500000000 | bytes 1572864 | tf_op jit(solution)/shard_map/coarse/pallas_call | solution.py:182
  43.9 0.1 collective-permute-start.10
  43.9 4.7 %collective-permute-start.11 = (f32[344,128]{1,0:T(8,128)S(1)}, f32[344,128]{1,0:T(8,128)S(1)}, u32[]{:S(2)}, u32[]{:S(2)}) collective-permute-start(f32[344,128]{1,0:T(8,128)S(1)} %get-tuple-element.56), channel_id=1, source_target_pairs={{4,0},{8,4},{12,8},{16,12},{20,16},{24,20},{28,24},{0,28},{5,1},{9... | collective-permute-start | bytes 528392 | tf_op jit(solution)/shard_map/ppermute | solution.py:761
  48.6 3.3 %detail_rest.1.r_ref = f32[24,128,256]{2,1,0:T(8,128)S(1)} custom-call(f32[24,144,256]{2,1,0:T(8,128)S(1)} %get-tuple-element.58.coeffs, bf16[768,256]{1,0:T(8,128)(2,1)S(1)} %copy-done.12, bf16[128,432]{1,0:T(8,128)(2,1)S(1)} %copy-done.13), custom_call_target="tpu_custom_call" | custom-call | flops 2038431744 | bytes 6684672 | tf_op jit(solution)/shard_map/detail_rest/pallas_call | solution.py:182
  52.0 0.0 copy-start.3
  52.0 0.0 copy-start.8
  52.0 2.1 %detail_x.1.d_ref = f32[32,128,256]{2,1,0:T(8,128)S(1)} custom-call(f32[8,128,256]{2,1,0:T(8,128)S(1)} %get-tuple-element.57.e_ref, f32[24,128,256]{2,1,0:T(8,128)S(1)} %detail_rest.1.r_ref), custom_call_target="tpu_custom_call" | custom-call | flops 16777216 | bytes 8388608 | tf_op jit(solution)/shard_map/detail_x/pallas_call | solution.py:182
  54.1 0.7 %collective-permute-done.13.er = f32[2,128,256]{2,1,0:T(8,128)S(1)} collective-permute-done((f32[2,128,256]{2,1,0:T(8,128)S(1)}, f32[2,128,256]{2,1,0:T(8,128)S(1)}, u32[]{:S(2)}, u32[]{:S(2)}) %collective-permute-start.13) | collective-permute-done | bytes 262176 | tf_op jit(solution)/shard_map/ppermute | solution.py:761
  54.8 0.6 collective-permute-done.10.l_ref
  55.4 2.3 %collective-permute-done.11.r_ref = f32[344,128]{1,0:T(8,128)S(1)} collective-permute-done((f32[344,128]{1,0:T(8,128)S(1)}, f32[344,128]{1,0:T(8,128)S(1)}, u32[]{:S(2)}, u32[]{:S(2)}) %collective-permute-start.11) | collective-permute-done | bytes 176160 | tf_op jit(solution)/shard_map/ppermute | solution.py:761
  57.6 5.5 %final.1 = f32[32,128,256]{2,1,0:T(8,128)} custom-call(f32[20,72,128]{2,1,0:T(8,128)S(1)} %get-tuple-element.54.a_ref, f32[344,128]{1,0:T(8,128)S(1)} %collective-permute-done.10.l_ref, f32[344,128]{1,0:T(8,128)S(1)} %collective-permute-done.11.r_ref, f32[32,128,256]{2,1,0:T(8,128)S(1)} %detail_x.1.d_ref, f32[2,128,256]{2,1,0:T(8,128)S(1)} %collective-permute-done.12.el, ...), custom_call_target="tpu_custom_call" | custom-call | flops 8388608 | bytes 8388608 | tf_op jit(solution)/shard_map/final/pallas_call | solution.py:737
  (28 shorter events, 0.1 us)
Async XLA Ops:
  0.0 2.2 %copy-start = (f32[32,128,256]{2,1,0:T(8,128)S(1)}, f32[32,128,256]{2,1,0:T(8,128)}, u32[]{:S(2)}) copy-start(f32[32,128,256]{2,1,0:T(8,128)} %y_first.1) | copy-start | bytes 12582916
  2.2 7.9 %copy-start.1 = (bf16[768,256]{1,0:T(8,128)(2,1)S(1)}, bf16[768,256]{1,0:T(8,128)(2,1)}, u32[]{:S(2)}) copy-start(bf16[768,256]{1,0:T(8,128)(2,1)} %constant.30.clone.z) | copy-start | bytes 1179652
  2.3 9.8 %collective-permute-start = (f32[32,8,256]{2,1,0:T(8,128)S(1)}, f32[32,8,256]{2,1,0:T(8,128)S(1)}, u32[]{:S(2)}, u32[]{:S(2)}) collective-permute-start(f32[32,8,256]{2,1,0:T(8,128)S(1)} %get-tuple-element.33), channel_id=1, source_target_pairs={{0,1},{1,2},{2,3},{3,0},{4,5},{5,6},{6,7},{7,4},{8,9},{9,10},{10,1... | collective-permute-start | bytes 786440 | tf_op jit(solution)/shard_map/ppermute | solution.py:756
  2.8 9.3 %collective-permute-start.1 = (f32[32,8,256]{2,1,0:T(8,128)S(1)}, f32[32,8,256]{2,1,0:T(8,128)S(1)}, u32[]{:S(2)}, u32[]{:S(2)}) collective-permute-start(f32[32,8,256]{2,1,0:T(8,128)S(1)} %get-tuple-element.34), channel_id=1, source_target_pairs={{1,0},{2,1},{3,2},{0,3},{5,4},{6,5},{7,6},{4,7},{9,8},{10,9},{11,1... | collective-permute-start | bytes 786440 | tf_op jit(solution)/shard_map/ppermute | solution.py:761
  4.8 13.5 %collective-permute-start.2 = (f32[2,128,256]{2,1,0:T(8,128)S(1)}, f32[2,128,256]{2,1,0:T(8,128)S(1)}, u32[]{:S(2)}, u32[]{:S(2)}) collective-permute-start(f32[2,128,256]{2,1,0:T(8,128)S(1)} %get-tuple-element.35), channel_id=1, source_target_pairs={{0,4},{4,8},{8,12},{12,16},{16,20},{20,24},{24,28},{28,0},{1,5},{5... | collective-permute-start | bytes 786440 | tf_op jit(solution)/shard_map/ppermute | solution.py:756
  7.0 5.1 %copy-start.2 = (bf16[144,432]{1,0:T(8,128)(2,1)S(1)}, bf16[144,432]{1,0:T(8,128)(2,1)}, u32[]{:S(2)}) copy-start(bf16[144,432]{1,0:T(8,128)(2,1)} %constant.31.clone.y) | copy-start | bytes 373252
  7.0 13.4 %collective-permute-start.3 = (f32[2,128,256]{2,1,0:T(8,128)S(1)}, f32[2,128,256]{2,1,0:T(8,128)S(1)}, u32[]{:S(2)}, u32[]{:S(2)}) collective-permute-start(f32[2,128,256]{2,1,0:T(8,128)S(1)} %get-tuple-element.36), channel_id=1, source_target_pairs={{4,0},{8,4},{12,8},{16,12},{20,16},{24,20},{28,24},{0,28},{5,1},{9... | collective-permute-start | bytes 786440 | tf_op jit(solution)/shard_map/ppermute | solution.py:761
  14.4 11.2 %copy-start.4 = (bf16[112,672]{1,0:T(8,128)(2,1)S(1)}, bf16[112,672]{1,0:T(8,128)(2,1)}, u32[]{:S(2)}) copy-start(bf16[112,672]{1,0:T(8,128)(2,1)} %constant.33.clone.yx) | copy-start | bytes 451588
  14.4 11.2 %copy-start.6 = (bf16[384,128]{1,0:T(8,128)(2,1)S(1)}, bf16[384,128]{1,0:T(8,128)(2,1)}, u32[]{:S(2)}) copy-start(bf16[384,128]{1,0:T(8,128)(2,1)} %constant.32.clone.z) | copy-start | bytes 294916
  14.4 11.2 %copy-start.7 = (bf16[96,336]{1,0:T(8,128)(2,1)S(1)}, bf16[96,336]{1,0:T(8,128)(2,1)}, u32[]{:S(2)}) copy-start(bf16[96,336]{1,0:T(8,128)(2,1)} %constant.34.clone.y) | copy-start | bytes 193540
  14.4 17.3 %copy-start.10 = (s32[3,7]{1,0:T(4,128)S(1)}, s32[3,7]{1,0:T(4,128)}, u32[]{:S(2)}) copy-start(s32[3,7]{1,0:T(4,128)} %index_ref.3) | copy-start | bytes 256
  14.4 17.3 %copy-start.11 = (f32[16]{0:T(128)S(1)}, f32[16]{0:T(128)}, u32[]{:S(2)}) copy-start(f32[16]{0:T(128)} %table_ref.3) | copy-start | bytes 196
  14.8 10.8 %collective-permute-start.6 = (f32[16,24,128]{2,1,0:T(8,128)S(1)}, f32[16,24,128]{2,1,0:T(8,128)S(1)}, u32[]{:S(2)}, u32[]{:S(2)}) collective-permute-start(f32[16,24,128]{2,1,0:T(8,128)S(1)} %get-tuple-element.41), channel_id=1, source_target_pairs={{0,1},{1,2},{2,3},{3,0},{4,5},{5,6},{6,7},{7,4},{8,9},{9,10},{10,1... | collective-permute-start | bytes 589832 | tf_op jit(solution)/shard_map/ppermute | solution.py:756
  14.9 19.9 %copy-start.12 = (bf16[768,256]{1,0:T(8,128)(2,1)S(1)}, bf16[768,256]{1,0:T(8,128)(2,1)}, u32[]{:S(2)}) copy-start(bf16[768,256]{1,0:T(8,128)(2,1)} %constant.35.clone.z) | copy-start | bytes 1179652
  14.9 19.9 %copy-start.13 = (bf16[128,432]{1,0:T(8,128)(2,1)S(1)}, bf16[128,432]{1,0:T(8,128)(2,1)}, u32[]{:S(2)}) copy-start(bf16[128,432]{1,0:T(8,128)(2,1)} %constant.36.clone.y) | copy-start | bytes 331780
  14.9 10.7 %collective-permute-start.7 = (f32[16,24,128]{2,1,0:T(8,128)S(1)}, f32[16,24,128]{2,1,0:T(8,128)S(1)}, u32[]{:S(2)}, u32[]{:S(2)}) collective-permute-start(f32[16,24,128]{2,1,0:T(8,128)S(1)} %get-tuple-element.42), channel_id=1, source_target_pairs={{1,0},{2,1},{3,2},{0,3},{5,4},{6,5},{7,6},{4,7},{9,8},{10,9},{11,1... | collective-permute-start | bytes 589832 | tf_op jit(solution)/shard_map/ppermute | solution.py:761
  20.8 4.7 %collective-permute-start.4 = (f32[4,56,128]{2,1,0:T(8,128)S(1)}, f32[4,56,128]{2,1,0:T(8,128)S(1)}, u32[]{:S(2)}, u32[]{:S(2)}) collective-permute-start(f32[4,56,128]{2,1,0:T(8,128)S(1)} %get-tuple-element.38), channel_id=1, source_target_pairs={{0,1},{1,2},{2,3},{3,0},{4,5},{5,6},{6,7},{7,4},{8,9},{9,10},{10,1... | collective-permute-start | bytes 344072 | tf_op jit(solution)/shard_map/ppermute | solution.py:756
  20.9 4.7 %collective-permute-start.5 = (f32[4,56,128]{2,1,0:T(8,128)S(1)}, f32[4,56,128]{2,1,0:T(8,128)S(1)}, u32[]{:S(2)}, u32[]{:S(2)}) collective-permute-start(f32[4,56,128]{2,1,0:T(8,128)S(1)} %get-tuple-element.39), channel_id=1, source_target_pairs={{1,0},{2,1},{3,2},{0,3},{5,4},{6,5},{7,6},{4,7},{9,8},{10,9},{11,1... | collective-permute-start | bytes 344072 | tf_op jit(solution)/shard_map/ppermute | solution.py:761
  26.9 14.0 %copy-start.5 = (bf16[384,128]{1,0:T(8,128)(2,1)S(1)}, bf16[384,128]{1,0:T(8,128)(2,1)}, u32[]{:S(2)}) copy-start(bf16[384,128]{1,0:T(8,128)(2,1)} %constant.37.clone.z1) | copy-start | bytes 294916
  26.9 14.0 %copy-start.9 = (bf16[80,288]{1,0:T(8,128)(2,1)S(1)}, bf16[80,288]{1,0:T(8,128)(2,1)}, u32[]{:S(2)}) copy-start(bf16[80,288]{1,0:T(8,128)(2,1)} %constant.42.clone.s1) | copy-start | bytes 138244
  26.9 14.0 %copy-start.14 = (bf16[384,128]{1,0:T(8,128)(2,1)S(1)}, bf16[384,128]{1,0:T(8,128)(2,1)}, u32[]{:S(2)}) copy-start(bf16[384,128]{1,0:T(8,128)(2,1)} %constant.39.clone.z2s) | copy-start | bytes 294916
  26.9 14.0 %copy-start.15 = (bf16[384,128]{1,0:T(8,128)(2,1)S(1)}, bf16[384,128]{1,0:T(8,128)(2,1)}, u32[]{:S(2)}) copy-start(bf16[384,128]{1,0:T(8,128)(2,1)} %constant.38.clone.z2a) | copy-start | bytes 294916
  26.9 14.0 %copy-start.16 = (bf16[64,144]{1,0:T(8,128)(2,1)S(1)}, bf16[64,144]{1,0:T(8,128)(2,1)}, u32[]{:S(2)}) copy-start(bf16[64,144]{1,0:T(8,128)(2,1)} %constant.41.clone.s2) | copy-start | bytes 55300
  27.0 14.0 %copy-start.17 = (bf16[48,192]{1,0:T(8,128)(2,1)S(1)}, bf16[48,192]{1,0:T(8,128)(2,1)}, u32[]{:S(2)}) copy-start(bf16[48,192]{1,0:T(8,128)(2,1)} %constant.40.clone.a2) | copy-start | bytes 55300
  27.0 13.9 %collective-permute-start.8 = (f32[248,128]{1,0:T(8,128)S(1)}, f32[248,128]{1,0:T(8,128)S(1)}, u32[]{:S(2)}, u32[]{:S(2)}) collective-permute-start(f32[248,128]{1,0:T(8,128)S(1)} %get-tuple-element.51), channel_id=1, source_target_pairs={{0,4},{4,8},{8,12},{12,16},{16,20},{20,24},{24,28},{28,0},{1,5},{5... | collective-permute-start | bytes 380936 | tf_op jit(solution)/shard_map/ppermute | solution.py:756
  27.3 13.6 %collective-permute-start.9 = (f32[248,128]{1,0:T(8,128)S(1)}, f32[248,128]{1,0:T(8,128)S(1)}, u32[]{:S(2)}, u32[]{:S(2)}) collective-permute-start(f32[248,128]{1,0:T(8,128)S(1)} %get-tuple-element.52), channel_id=1, source_target_pairs={{4,0},{8,4},{12,8},{16,12},{20,16},{24,20},{28,24},{0,28},{5,1},{9... | collective-permute-start | bytes 380936 | tf_op jit(solution)/shard_map/ppermute | solution.py:761
  36.1 18.0 %collective-permute-start.12 = (f32[2,128,256]{2,1,0:T(8,128)S(1)}, f32[2,128,256]{2,1,0:T(8,128)S(1)}, u32[]{:S(2)}, u32[]{:S(2)}) collective-permute-start(f32[2,128,256]{2,1,0:T(8,128)S(1)} %get-tuple-element.59), channel_id=1, source_target_pairs={{0,4},{4,8},{8,12},{12,16},{16,20},{20,24},{24,28},{28,0},{1,5},{5... | collective-permute-start | bytes 786440 | tf_op jit(solution)/shard_map/ppermute | solution.py:756
  36.2 18.6 %collective-permute-start.13 = (f32[2,128,256]{2,1,0:T(8,128)S(1)}, f32[2,128,256]{2,1,0:T(8,128)S(1)}, u32[]{:S(2)}, u32[]{:S(2)}) collective-permute-start(f32[2,128,256]{2,1,0:T(8,128)S(1)} %get-tuple-element.60), channel_id=1, source_target_pairs={{4,0},{8,4},{12,8},{16,12},{20,16},{24,20},{28,24},{0,28},{5,1},{9... | collective-permute-start | bytes 786440 | tf_op jit(solution)/shard_map/ppermute | solution.py:761
  43.9 11.5 %collective-permute-start.10 = (f32[344,128]{1,0:T(8,128)S(1)}, f32[344,128]{1,0:T(8,128)S(1)}, u32[]{:S(2)}, u32[]{:S(2)}) collective-permute-start(f32[344,128]{1,0:T(8,128)S(1)} %get-tuple-element.55), channel_id=1, source_target_pairs={{0,4},{4,8},{8,12},{12,16},{16,20},{20,24},{24,28},{28,0},{1,5},{5... | collective-permute-start | bytes 528392 | tf_op jit(solution)/shard_map/ppermute | solution.py:756
  43.9 13.7 %collective-permute-start.11 = (f32[344,128]{1,0:T(8,128)S(1)}, f32[344,128]{1,0:T(8,128)S(1)}, u32[]{:S(2)}, u32[]{:S(2)}) collective-permute-start(f32[344,128]{1,0:T(8,128)S(1)} %get-tuple-element.56), channel_id=1, source_target_pairs={{4,0},{8,4},{12,8},{16,12},{20,16},{24,20},{28,24},{0,28},{5,1},{9... | collective-permute-start | bytes 528392 | tf_op jit(solution)/shard_map/ppermute | solution.py:761
  52.0 5.7 %copy-start.3 = (bf16[384,256]{1,0:T(8,128)(2,1)S(1)}, bf16[384,256]{1,0:T(8,128)(2,1)}, u32[]{:S(2)}) copy-start(bf16[384,256]{1,0:T(8,128)(2,1)} %constant.43.clone.z) | copy-start | bytes 589828
  52.0 5.7 %copy-start.8 = (bf16[128,240]{1,0:T(8,128)(2,1)S(1)}, bf16[128,240]{1,0:T(8,128)(2,1)}, u32[]{:S(2)}) copy-start(bf16[128,240]{1,0:T(8,128)(2,1)} %constant.44.clone.y) | copy-start | bytes 184324

commit v4 on v3

--- a/solution.py
+++ b/solution.py
@@ -191,68 +191,48 @@
     )(*args)
 
 
-def call(kernel, grid, in_specs, out_specs, out_shapes, args, flops, moved, scratch=(), name=None):
-    return pl.pallas_call(
-        kernel,
-        grid=grid,
-        in_specs=in_specs,
-        out_specs=out_specs,
-        out_shape=out_shapes,
-        scratch_shapes=list(scratch),
-        name=name,
-        cost_estimate=pl.CostEstimate(flops=int(flops), bytes_accessed=int(moved), transcendentals=0),
-        compiler_params=pltpu.CompilerParams(vmem_limit_bytes=VMEM_BYTES),
-    )(*args)
-
-
 def shape(*dims):
     return jax.ShapeDtypeStruct(dims, F32)
 
 
-def whole(array):
-    dims = array.shape
-    return pl.BlockSpec(dims, lambda *_: (0,) * len(dims))
-
-
-def whole_out(*dims):
-    return pl.BlockSpec(dims, lambda *_: (0,) * len(dims))
-
-
 SMEM = pl.BlockSpec(memory_space=pltpu.SMEM)
 VMEM = pl.BlockSpec(memory_space=pltpu.VMEM)
 
 
-def x_messages(last, first, up, down):
-    up[0] = last[3]
-    up[1] = H[0] * last[1] + H[1] * last[2]
-    down[0] = first[0]
-    down[1] = H[6] * first[1] + H[7] * first[2]
-
-
 def first_messages(v):
     nx, ny, nz = v.shape
 
-    def kernel(last, first, y_last, y_first, up, down, y_up, y_down):
-        x_messages(last, first, up, down)
-        y_up[...] = y_last[...]
-        y_down[...] = y_first[...]
-
-    return call(
-        kernel,
-        (1,),
-        [
-            pl.BlockSpec((4, ny, nz), lambda i: (nx // 4 - 1, 0, 0)),
-            pl.BlockSpec((4, ny, nz), lambda i: (0, 0, 0)),
-            pl.BlockSpec((nx, 8, nz), lambda i: (0, ny // 8 - 1, 0)),
-            pl.BlockSpec((nx, 8, nz), lambda i: (0, 0, 0)),
-        ],
-        [whole_out(2, ny, nz)] * 2 + [whole_out(nx, 8, nz)] * 2,
-        [shape(2, ny, nz)] * 2 + [shape(nx, 8, nz)] * 2,
-        [v] * 4,
-        1e6,
-        3e6,
+    def kernel(v_ref, up, down, y_up, y_down, last, first, sems):
+        copies = [
+            pltpu.make_async_copy(source, target, sems.at[i])
+            for i, (source, target) in enumerate(
+                (
+                    (v_ref.at[pl.ds(nx - 3, 3)], last),
+                    (v_ref.at[pl.ds(0, 3)], first),
+                    (v_ref.at[:, pl.ds(ny - 8, 8)], y_up),
+                    (v_ref.at[:, pl.ds(0, 8)], y_down),
+                )
+            )
+        ]
+        for copy in copies:
+            copy.start()
+        for copy in copies:
+            copy.wait()
+        up[0] = last[2]
+        up[1] = H[0] * last[0] + H[1] * last[1]
+        down[0] = first[0]
+        down[1] = H[6] * first[1] + H[7] * first[2]
+
+    return pl.pallas_call(
+        kernel,
+        in_specs=[pl.BlockSpec(memory_space=pltpu.HBM)],
+        out_specs=[VMEM] * 4,
+        out_shape=[shape(2, ny, nz)] * 2 + [shape(nx, 8, nz)] * 2,
+        scratch_shapes=[pltpu.VMEM((3, ny, nz), F32)] * 2 + [pltpu.SemaphoreType.DMA((4,))],
         name="first_messages",
-    )
+        cost_estimate=pl.CostEstimate(flops=1000000, bytes_accessed=3000000, transcendentals=0),
+        compiler_params=pltpu.CompilerParams(vmem_limit_bytes=50 * 1024 * 1024),
+    )(v)
 
 
 def over_planes(count, group, body):
@@ -358,54 +338,82 @@
     return [0, 1, n - 2, n - 1]
 
 
-def detail_bands(bands, halo, h_left, h_right, table, index, y_matrix):
+def band_limits(table_ref, index_ref, by, bz):
+    band = 2 * by + bz
+    quiet = table_ref[index_ref[0, band - 1]] if band else NOTHING
+    return quiet, table_ref[index_ref[0, band + 3]]
+
+
+def over_tiles(rows, nz, body):
+    half_z, half_tiles = nz // 2, rows // 16
+    for by in range(2):
+
+        def tile(t, carry, by=by):
+            at = pl.ds(pl.multiple_of((t + by * half_tiles) * 8, 8), 8)
+            for bz in range(2):
+                body(at, pl.ds(bz * half_z, half_z), by, bz)
+            return carry
+
+        lax.fori_loop(0, half_tiles, tile, 0)
+
+
+def inner_bands(bands, table, index):
+    nx, rows, nz = bands.shape
+    count = nx // 2 - 4
+
+    def kernel(table_ref, index_ref, b_ref, out):
+        def body(at, lanes, by, bz):
+            quiet, loud = band_limits(table_ref, index_ref, by, bz)
+            values = {i: b_ref[i, at, lanes] for i in range(nx)}
+            for k, (low, high) in x_interior(values.get, nx).items():
+                out[k - 2, at, lanes] = shrink(low, quiet) if by + bz else jnp.zeros_like(low)
+                out[count + k - 2, at, lanes] = shrink(high, loud)
+
+        over_tiles(rows, nz, body)
+
+    return whole_call(
+        kernel,
+        shape(2 * count, rows, nz),
+        [table, index, bands],
+        30 * nx * rows * nz,
+        8 * nx * rows * nz,
+        name="inner_bands",
+    )
+
+
+def edge_bands(bands, halo, h_left, h_right, table, index, y_matrix):
     nx, rows, nz = bands.shape
     n1 = nx // 2
     half_z = nz // 2
-    half_tiles = rows // 16
     wide = h_left.shape[1] - 8
     ends = edges_of(n1)
-    inner = [k for k in range(n1) if k not in ends]
-
-    def kernel(table_ref, index_ref, b_ref, x_ref, hl, hr, y, edge, rest, h_ref):
+
+    def kernel(table_ref, index_ref, b_ref, x_ref, hl, hr, y, out, h_ref):
         for i in range(4):
             low = jnp.concatenate([hl[i, wide - 8 : wide], x_ref[i, :, :half_z], hr[i, :8]], axis=0)
             high = jnp.concatenate([hl[i, wide:], x_ref[i, :, half_z:], hr[i, wide:]], axis=0)
             h_ref[i] = left_times(y, jnp.concatenate([low, high], axis=1))
         place = {"l1": 0, "l2": 1, "r1": 2, "r2": 3}
 
-        def tiles(by):
-            def tile(t, carry):
-                at = pl.ds(pl.multiple_of((t + by * half_tiles) * 8, 8), 8)
-                for bz in range(2):
-                    lanes = pl.ds(bz * half_z, half_z)
-                    band = 2 * by + bz
-                    quiet = table_ref[index_ref[0, band - 1]] if band else NOTHING
-                    loud = table_ref[index_ref[0, band + 3]]
-                    values = {key: h_ref[i, at, lanes] for key, i in place.items()}
-                    values.update({i: b_ref[i, at, lanes] for i in range(nx)})
-                    coeffs = x_interior(values.get, nx)
-                    for k in ends:
-                        coeffs[k] = (x_low(values.get, k, nx), x_high(values.get, k, nx))
-                    for k, (low, high) in coeffs.items():
-                        target, place_k, count = (edge, ends.index(k), 4) if k in ends else (rest, k - 2, n1 - 4)
-                        target[place_k, at, lanes] = shrink(low, quiet) if band else jnp.zeros_like(low)
-                        target[count + place_k, at, lanes] = shrink(high, loud)
-                return carry
-
-            return tile
-
-        lax.fori_loop(0, half_tiles, tiles(0), 0)
-        lax.fori_loop(0, half_tiles, tiles(1), 0)
-
-    return whole_call(
-        kernel,
-        [shape(8, rows, nz), shape(2 * len(inner), rows, nz)],
+        def body(at, lanes, by, bz):
+            quiet, loud = band_limits(table_ref, index_ref, by, bz)
+            values = {key: h_ref[i, at, lanes] for key, i in place.items()}
+            values.update({i: b_ref[i, at, lanes] for i in [*range(7), *range(nx - 7, nx)]})
+            for i, k in enumerate(ends):
+                low, high = x_low(values.get, k, nx), x_high(values.get, k, nx)
+                out[i, at, lanes] = shrink(low, quiet) if by + bz else jnp.zeros_like(low)
+                out[4 + i, at, lanes] = shrink(high, loud)
+
+        over_tiles(rows, nz, body)
+
+    return whole_call(
+        kernel,
+        shape(8, rows, nz),
         [table, index, bands, halo, h_left, h_right, y_matrix],
-        40 * nx * rows * nz,
-        8 * nx * rows * nz,
+        20 * nx * rows * nz,
+        4 * nx * rows * nz,
         scratch=[pltpu.VMEM((4, rows, nz), F32)],
-        name="detail_bands",
+        name="edge_bands",
     )
 
 
@@ -459,13 +467,21 @@
     )
 
 
-def detail_x(edge, rest):
+def own_result(edge, rest, approx, z_matrix, y_matrix):
     count, ny, nz = rest.shape
     n1 = (count + 8) // 2
     nx = 2 * n1
     ends = edges_of(n1)
-
-    def kernel(e_ref, r_ref, out):
+    planes, rows, half_z = approx.shape
+
+    def kernel(e_ref, r_ref, a_ref, z, y, out, parts):
+        def body(first):
+            zed = times(a_ref[pl.ds(first, 4)].reshape(4 * rows, half_z), z)
+            for j, plane in enumerate(cut(zed, rows)):
+                parts[first + j] = left_times(y, plane)
+
+        over_planes(planes, 4, body)
+
         def tile(t, carry):
             at = pl.ds(pl.multiple_of(t * 8, 8), 8)
             for lane in range(0, nz, 128):
@@ -476,7 +492,9 @@
                         return e_ref[4 * high + ends.index(k), at, lanes]
                     return r_ref[(n1 - 4) * high + k - 2, at, lanes]
 
-                lows = {k: coeff(k, 0) for k in range(n1)}
+                lows = {k: parts[k + 2, at, lanes] for k in range(-2, n1 + 2)}
+                for k in range(n1):
+                    lows[k] = lows[k] + coeff(k, 0)
                 highs = {k: coeff(k, 1) for k in range(n1)}
                 for m in range(nx):
                     out[m, at, lanes] = x_synth(m, lows, highs)
@@ -485,7 +503,13 @@
         lax.fori_loop(0, ny // 8, tile, 0)
 
     return whole_call(
-        kernel, shape(nx, ny, nz), [edge, rest], 16 * nx * ny * nz, 8 * nx * ny * nz, name="detail_x"
+        kernel,
+        shape(nx, ny, nz),
+        [edge, rest, approx, z_matrix, y_matrix],
+        16 * nx * ny * nz,
+        8 * nx * ny * nz,
+        scratch=[pltpu.VMEM((planes, ny, nz), F32)],
+        name="own_result",
     )
 
 
@@ -662,47 +686,42 @@
     )
 
 
-def final(approx, left, right, detail, e_left, e_right, zs1, ys1, z_matrix, y_matrix, low_rows):
-    planes, rows, half_z = approx.shape
-    nx, ny, nz = detail.shape
-    n1 = nx // 2
-    n2 = n1 // 2
+def received_taps(n1):
+    n2, nx = n1 // 2, 2 * n1
+    from_approx = np.zeros((nx, n1 + 4))
+    for m in range(nx):
+        for k in range(-2, n1 + 2):
+            from_approx[m, k + 2] = tap(H, m + 3 - 2 * k)
+    approx = np.zeros((n1 + 4, 12))
+    third = {0: THIRD_UP, 6: THIRD_DOWN}
+    for first, cell, second in ((0, lambda i: i, lambda i: i), (6, lambda i: n1 - 1 - i, lambda i: n2 - 1 - i)):
+        ghost = (-2, -1) if first == 0 else (n1, n1 + 1)
+        for i in range(2):
+            approx[ghost[i] + 2, first + i] = 1.0
+        for place, source, coef in ((0, 0, 1.0), (1, 1, 1.0), (2, 1, third[first])):
+            approx[cell(place) + 2, first + 2 + source] += coef
+            for m in range(n1):
+                approx[m + 2, first + 4 + source] += coef * tap(H, m + 3 - 2 * second(place))
+    return from_approx @ approx
+
+
+def final(left, right, own, e_left, e_right, zs1, ys1, z_matrix, y_matrix, low_rows):
+    nx, ny, nz = own.shape
+    half_z = nz // 2
+    rows = (left.shape[0] - low_rows) // 4
     step_rows = 16
     steps = ny // step_rows
-
-    def kernel(a_ref, l_ref, r_ref, d_ref, el, er, z1, s1, z, y, out, total, parts, done, sems):
+    taps = received_taps(nx // 2)
+
+    def kernel(l_ref, r_ref, d_ref, el, er, z1, s1, z, y, out, parts, done, sems):
         stack = [p for ref in (l_ref, r_ref) for p in unpacked(ref[4 * rows :])]
         zed = times(jnp.concatenate(stack, axis=0), z1)
         spilled = [p[:rows] for p in in_pairs(s1, cut(zed, low_rows))]
-        slot = lambda ref, i: ref[pl.ds(i * rows, rows)]
-        for m in range(n1):
-            terms = [(1.0, a_ref[m + 2])]
-            for k, coef, source in (
-                (0, 1.0, 0),
-                (1, 1.0, 1),
-                (2, THIRD_UP, 1),
-                (n2 - 1, 1.0, 2),
-                (n2 - 2, 1.0, 3),
-                (n2 - 3, THIRD_DOWN, 3),
-            ):
-                if 0 <= m + 3 - 2 * k < 8:
-                    terms.append((coef * H[m + 3 - 2 * k], spilled[source]))
-            if m < 3:
-                terms.append(((1.0, 1.0, THIRD_UP)[m], slot(l_ref, (2, 3, 3)[m])))
-            if m >= n1 - 3:
-                terms.append(((1.0, 1.0, THIRD_DOWN)[n1 - 1 - m], slot(r_ref, (2, 3, 3)[n1 - 1 - m])))
-            total[m + 2] = added(terms)
-        total[0] = a_ref[0] + slot(l_ref, 0)
-        total[1] = a_ref[1] + slot(l_ref, 1)
-        total[n1 + 2] = a_ref[n1 + 2] + slot(r_ref, 0)
-        total[n1 + 3] = a_ref[n1 + 3] + slot(r_ref, 1)
-
-        def body(first):
-            zed = times(total[pl.ds(first, 4)].reshape(4 * rows, half_z), z)
-            for j, plane in enumerate(cut(zed, rows)):
-                parts[first + j] = left_times(y, plane)
-
-        over_planes(planes, 4, body)
+        planes = []
+        for side, ref in enumerate((l_ref, r_ref)):
+            planes += [ref[pl.ds(i * rows, rows)] for i in range(4)] + spilled[2 * side : 2 * side + 2]
+        for i, plane in enumerate(cut(times(jnp.concatenate(planes, axis=0), z), rows)):
+            parts[i] = left_times(y, plane)
 
         def copy(i):
             at = pl.ds(pl.multiple_of(i * step_rows, step_rows), step_rows)
@@ -713,9 +732,10 @@
                 at = pl.ds(pl.multiple_of(i * step_rows + 8 * t, 8), 8)
                 for lane in range(0, nz, 128):
                     lanes = pl.ds(lane, 128)
-                    lows = {k: parts[k + 2, at, lanes] for k in range(-2, n1 + 2)}
+                    values = [parts[i, at, lanes] for i in range(12)]
                     for m in range(nx):
-                        value = d_ref[m, at, lanes] + x_synth(m, lows, {})
+                        value = d_ref[m, at, lanes]
+                        value += added([(float(c), v) for c, v in zip(taps[m], values) if c != 0.0])
                         if m < 3:
                             extra = el[(0, 1, 1)[m], at, lanes]
                             value += extra if m < 2 else THIRD_UP * extra
@@ -736,19 +756,18 @@
 
     return pl.pallas_call(
         kernel,
-        in_specs=[VMEM] * 10,
+        in_specs=[VMEM] * 9,
         out_specs=pl.BlockSpec(memory_space=pl.ANY),
         out_shape=shape(nx, ny, nz),
         scratch_shapes=[
-            pltpu.VMEM((planes, rows, half_z), F32),
-            pltpu.VMEM((planes, ny, nz), F32),
+            pltpu.VMEM((12, ny, nz), F32),
             pltpu.VMEM((nx, ny, nz), F32),
             pltpu.SemaphoreType.DMA((steps,)),
         ],
         name="final",
         cost_estimate=pl.CostEstimate(flops=8 * nx * ny * nz, bytes_accessed=8 * nx * ny * nz, transcendentals=0),
         compiler_params=pltpu.CompilerParams(vmem_limit_bytes=VMEM_BYTES),
-    )(approx, left, right, detail, e_left, e_right, zs1, ys1, z_matrix, y_matrix)
+    )(left, right, own, e_left, e_right, zs1, ys1, z_matrix, y_matrix)
 
 
 def to_next(array, axis):
@@ -802,13 +821,16 @@
     halo, h_up, h_down = x_halo_messages(x_left, x_right, za0, wide)
     h_left = to_next(h_up, "gy")
     h_right = to_previous(h_down, "gy")
+    bands, halo = lax.optimization_barrier((bands, halo))
+    rest = inner_bands(bands, table, index)
+    rest, approx = lax.optimization_barrier((rest, approx))
     bands1, b_up, b_down = second_bands(
         approx, a_left, a_right, halo, h_left, h_right, za1, yx0, ya1, rows1
     )
     b_left = to_next(b_up, "gx")
     b_right = to_previous(b_down, "gx")
     h_left, h_right, bands1 = lax.optimization_barrier((h_left, h_right, bands1))
-    edge, rest = detail_bands(bands, halo, h_left, h_right, table, index, ya0)
+    edge = edge_bands(bands, halo, h_left, h_right, table, index, ya0)
     edge, e_up, e_down = detail_edges(edge, zs0, ys0)
     e_left = to_next(e_up, "gx")
     e_right = to_previous(e_down, "gx")
@@ -819,10 +841,8 @@
     s_left = to_next(s_up, "gx")
     s_right = to_previous(s_down, "gx")
     rest, approx1 = lax.optimization_barrier((rest, approx1))
-    detail = detail_x(edge, detail_rest(rest, zs0, ys0))
-    return final(
-        approx1, s_left, s_right, detail, e_left, e_right, zs1, ys1, zs0_low, ys0_low, rows1
-    )
+    own = own_result(edge, detail_rest(rest, zs0, ys0), approx1, zs0_low, ys0_low)
+    return final(s_left, s_right, own, e_left, e_right, zs1, ys1, zs0_low, ys0_low, rows1)
 
 
 def solution(mesh):

time: 63.3 us -> 59.1 us (0.934)
  waiting for transfers between devices: 10.3 us -> 4.37 us
  Pallas kernels: 24.5 us -> 27.5 us
  local copies, waits for them, and re-layouts: 2.3 us -> 1.09 us
    ppermute x7, waiting for transfers between devices: 5.17 us -> 1.42 us  [to_next(): return lax.ppermute(array, axis, [(i, (i + 1) % size) for i in range(size)])]
    pallas_call x10 -> x11, Pallas kernels: 18.9 us -> 22.5 us  [whole_call(): pl.pallas_call(kernel, in_specs=specs, out_specs=outs, out_shape=out_shap...]
    ppermute x7, waiting for transfers between devices: 5.15 us -> 2.95 us  [to_previous(): return lax.ppermute(array, axis, [((i + 1) % size, i) for i in range(size)])]
    unnamed x36, local copies, waits for them, and re-layouts: 2.3 us -> 1.09 us
  transfers between devices with their start and end apart: 14 -> 14, of which waited for: 6 -> 4; matrix products, arithmetic and copies ran while one was open for 0% -> 0% of each run, Pallas kernels for 28% -> 36%
where the time goes in v4:
time: 59.1 us; the launch traced here: 59 us
  Pallas kernels  27.5 us (47%)
  starting transfers between devices  25.7 us (43%)
  waiting for transfers between devices  4.37 us (7%)
  local copies, waits for them, and re-layouts  1.09 us (2%)
    pallas_call x11, Pallas kernels, whole_call(): pl.pallas_call(kernel, in_specs=specs, out_specs=outs, out_shape=out_shap...  22.5 us
    ppermute x7, starting transfers between devices, to_previous(): return lax.ppermute(array, axis, [((i + 1) % size, i) for i in range(size)])  22.4 us
    pallas_call x1, Pallas kernels, final(): pl.pallas_call(kernel, in_specs=[VMEM] * 9, out_specs=pl.BlockSpec(memory...  3.48 us
    ppermute x7, starting transfers between devices, to_next(): return lax.ppermute(array, axis, [(i, (i + 1) % size) for i in range(size)])  3.29 us
    ppermute x7, waiting for transfers between devices, to_previous(): return lax.ppermute(array, axis, [((i + 1) % size, i) for i in range(size)])  2.95 us
    pallas_call x1, Pallas kernels, first_messages(): pl.pallas_call(kernel, in_specs=[pl.BlockSpec(memory_space=pltpu.HBM)], o...  1.51 us
    ppermute x7, waiting for transfers between devices, to_next(): return lax.ppermute(array, axis, [(i, (i + 1) % size) for i in range(size)])  1.42 us
  transfers between devices with their start and end apart: 14, of which 4 were waited for; matrix products, arithmetic and copies ran while one was open for 0% of the time, Pallas kernels for 36%

profile of v4, /device:TPU:0, one launch (start us, length us, event | category | flops | bytes accessed | tf_op | source)
XLA Modules:
  0.0 59.0 jit_solution(6682732589021559920)
XLA Ops:
  0.0 1.5 %first_messages.1 = (f32[2,128,256]{2,1,0:T(8,128)S(1)}, f32[2,128,256]{2,1,0:T(8,128)S(1)}, f32[32,8,256]{2,1,0:T(8,128)S(1)}, f32[32,8,256]{2,1,0:T(8,128)S(1)}) custom-call(f32[32,128,256]{2,1,0:T(8,128)} %v_ref.3), custom_call_target="tpu_custom_call" | custom-call | flops 1000000 | bytes 3000000 | tf_op jit(solution)/shard_map/first_messages/pallas_call | solution.py:226
  1.5 0.5 collective-permute-start.4
  2.0 2.0 %collective-permute-start.5 = (f32[32,8,256]{2,1,0:T(8,128)S(1)}, f32[32,8,256]{2,1,0:T(8,128)S(1)}, u32[]{:S(2)}, u32[]{:S(2)}) collective-permute-start(f32[32,8,256]{2,1,0:T(8,128)S(1)} %get-tuple-element.40), channel_id=1, source_target_pairs={{1,0},{2,1},{3,2},{0,3},{5,4},{6,5},{7,6},{4,7},{9,8},{10,9},{11,1... | collective-permute-start | bytes 786440 | tf_op jit(solution)/shard_map/ppermute | solution.py:780
  4.0 2.2 %collective-permute-start = (f32[2,128,256]{2,1,0:T(8,128)S(1)}, f32[2,128,256]{2,1,0:T(8,128)S(1)}, u32[]{:S(2)}, u32[]{:S(2)}) collective-permute-start(f32[2,128,256]{2,1,0:T(8,128)S(1)} %get-tuple-element.35), channel_id=1, source_target_pairs={{0,4},{4,8},{8,12},{12,16},{16,20},{20,24},{24,28},{28,0},{1,5},{5... | collective-permute-start | bytes 786440 | tf_op jit(solution)/shard_map/ppermute | solution.py:775
  6.3 3.0 %collective-permute-start.1 = (f32[2,128,256]{2,1,0:T(8,128)S(1)}, f32[2,128,256]{2,1,0:T(8,128)S(1)}, u32[]{:S(2)}, u32[]{:S(2)}) collective-permute-start(f32[2,128,256]{2,1,0:T(8,128)S(1)} %get-tuple-element.36), channel_id=1, source_target_pairs={{4,0},{8,4},{12,8},{16,12},{20,16},{24,20},{28,24},{0,28},{5,1},{9... | collective-permute-start | bytes 786440 | tf_op jit(solution)/shard_map/ppermute | solution.py:780
  9.3 1.0 %copy-done.1 = bf16[768,256]{1,0:T(8,128)(2,1)S(1)} copy-done((bf16[768,256]{1,0:T(8,128)(2,1)S(1)}, bf16[768,256]{1,0:T(8,128)(2,1)}, u32[]{:S(2)}) %copy-start.1) | copy-done | bytes 393240
  10.3 2.0 %depth_analysis.1.zed_ref = f32[32,128,256]{2,1,0:T(8,128)S(1)} custom-call(f32[32,128,256]{2,1,0:T(8,128)S(1)} %copy-done, bf16[768,256]{1,0:T(8,128)(2,1)S(1)} %copy-done.1), custom_call_target="tpu_custom_call" | custom-call | flops 1610612736 | bytes 8388608 | tf_op jit(solution)/shard_map/depth_analysis/pallas_call | solution.py:182
  12.3 0.0 collective-permute-done.4.left
  12.3 2.3 %y_analysis.1.b_ref = f32[32,144,256]{2,1,0:T(8,128)S(1)} custom-call(f32[32,128,256]{2,1,0:T(8,128)S(1)} %depth_analysis.1.zed_ref, f32[32,8,256]{2,1,0:T(8,128)S(1)} %collective-permute-done.4.left, f32[32,8,256]{2,1,0:T(8,128)S(1)} %collective-permute-done.5.right, bf16[768,256]{1,0:T(8,128)(2,1)S(1)} %copy-done.1, bf16[144,432]{1,0:T(8,128)(2,1)S(1)} %copy-done.3), custom_call_target="tpu_custom_call" | custom-call | flops 1019215872 | bytes 9437184 | tf_op jit(solution)/shard_map/y_analysis/pallas_call | solution.py:182
  14.6 0.0 copy-start.10
  14.6 0.0 copy-start.11
  14.7 0.3 own_approx.1
  15.0 0.1 collective-permute-start.6
  15.1 1.7 %collective-permute-start.7 = (f32[16,24,128]{2,1,0:T(8,128)S(1)}, f32[16,24,128]{2,1,0:T(8,128)S(1)}, u32[]{:S(2)}, u32[]{:S(2)}) collective-permute-start(f32[16,24,128]{2,1,0:T(8,128)S(1)} %get-tuple-element.46), channel_id=1, source_target_pairs={{1,0},{2,1},{3,2},{0,3},{5,4},{6,5},{7,6},{4,7},{9,8},{10,9},{11,1... | collective-permute-start | bytes 589832 | tf_op jit(solution)/shard_map/ppermute | solution.py:780
  16.8 0.7 %collective-permute-done.xl = f32[2,128,256]{2,1,0:T(8,128)S(1)} collective-permute-done((f32[2,128,256]{2,1,0:T(8,128)S(1)}, f32[2,128,256]{2,1,0:T(8,128)S(1)}, u32[]{:S(2)}, u32[]{:S(2)}) %collective-permute-start) | collective-permute-done | bytes 262176 | tf_op jit(solution)/shard_map/ppermute | solution.py:775
  17.5 2.2 %collective-permute-done.1.xr = f32[2,128,256]{2,1,0:T(8,128)S(1)} collective-permute-done((f32[2,128,256]{2,1,0:T(8,128)S(1)}, f32[2,128,256]{2,1,0:T(8,128)S(1)}, u32[]{:S(2)}, u32[]{:S(2)}) %collective-permute-start.1) | collective-permute-done | bytes 262176 | tf_op jit(solution)/shard_map/ppermute | solution.py:780
  19.7 0.4 x_halo_messages.1
  20.1 0.0 copy-start.5
  20.1 0.0 copy-start.7
  20.1 0.0 copy-start.8
  20.1 0.1 collective-permute-start.2
  20.2 1.7 %collective-permute-start.3 = (f32[4,56,128]{2,1,0:T(8,128)S(1)}, f32[4,56,128]{2,1,0:T(8,128)S(1)}, u32[]{:S(2)}, u32[]{:S(2)}) collective-permute-start(f32[4,56,128]{2,1,0:T(8,128)S(1)} %get-tuple-element.38), channel_id=1, source_target_pairs={{1,0},{2,1},{3,2},{0,3},{5,4},{6,5},{7,6},{4,7},{9,8},{10,9},{11,1... | collective-permute-start | bytes 344072 | tf_op jit(solution)/shard_map/ppermute | solution.py:780
  21.9 2.2 %inner_bands.1.coeffs = f32[24,144,256]{2,1,0:T(8,128)S(1)} custom-call(f32[16]{0:T(128)S(1)} %copy-done.11, s32[3,7]{1,0:T(4,128)S(1)} %copy-done.10, f32[32,144,256]{2,1,0:T(8,128)S(1)} %y_analysis.1.b_ref), custom_call_target="tpu_custom_call" | custom-call | flops 35389440 | bytes 9437184 | tf_op jit(solution)/shard_map/inner_bands/pallas_call | solution.py:182
  24.1 0.0 copy-start.12
  24.1 0.0 copy-start.13
  24.1 0.7 %collective-permute-done.2.hl = f32[4,56,128]{2,1,0:T(8,128)S(1)} collective-permute-done((f32[4,56,128]{2,1,0:T(8,128)S(1)}, f32[4,56,128]{2,1,0:T(8,128)S(1)}, u32[]{:S(2)}, u32[]{:S(2)}) %collective-permute-start.2) | collective-permute-done | bytes 114720 | tf_op jit(solution)/shard_map/ppermute | solution.py:775
  24.8 0.0 collective-permute-done.3.hr
  24.8 0.0 collective-permute-done.6.l_ref
  24.8 0.0 collective-permute-done.7.r_ref
  24.9 1.3 %second_bands.1 = (f32[16,96,128]{2,1,0:T(8,128)S(1)}, f32[248,128]{1,0:T(8,128)S(1)}, f32[248,128]{1,0:T(8,128)S(1)}) custom-call(f32[16,64,128]{2,1,0:T(8,128)S(1)} %get-tuple-element.44.o_ref, f32[16,24,128]{2,1,0:T(8,128)S(1)} %collective-permute-done.6.l_ref, f32[16,24,128]{2,1,0:T(8,128)S(1)} %collective-permute-done.7.r_ref, ...), custom_call_target="tpu_custom_call" | custom-call | flops 308281344 | bytes 1703936 | tf_op jit(solution)/shard_map/second_bands/pallas_call | solution.py:182
  26.2 0.3 collective-permute-start.8
  26.5 4.4 %collective-permute-start.9 = (f32[248,128]{1,0:T(8,128)S(1)}, f32[248,128]{1,0:T(8,128)S(1)}, u32[]{:S(2)}, u32[]{:S(2)}) collective-permute-start(f32[248,128]{1,0:T(8,128)S(1)} %get-tuple-element.55), channel_id=1, source_target_pairs={{4,0},{8,4},{12,8},{16,12},{20,16},{24,20},{28,24},{0,28},{5,1},{9... | collective-permute-start | bytes 380936 | tf_op jit(solution)/shard_map/ppermute | solution.py:780
  30.9 0.0 copy-start.16
  31.0 0.0 copy-start.17
  31.0 1.6 %edge_bands.1.c_ref = f32[8,144,256]{2,1,0:T(8,128)S(1)} custom-call(f32[16]{0:T(128)S(1)} %copy-done.11, s32[3,7]{1,0:T(4,128)S(1)} %copy-done.10, f32[32,144,256]{2,1,0:T(8,128)S(1)} %y_analysis.1.b_ref, f32[4,128,256]{2,1,0:T(8,128)S(1)} %get-tuple-element.47.x_ref, f32[4,56,128]{2,1,0:T(8,128)S(1)} %collective-permute-done.2.hl, ...), custom_call_target="tpu_custom_call" | custom-call | flops 23592960 | bytes 4718592 | tf_op jit(solution)/shard_map/edge_bands/pallas_call | solution.py:182
  32.6 1.3 %detail_edges.1 = (f32[8,128,256]{2,1,0:T(8,128)S(1)}, f32[2,128,256]{2,1,0:T(8,128)S(1)}, f32[2,128,256]{2,1,0:T(8,128)S(1)}) custom-call(f32[8,144,256]{2,1,0:T(8,128)S(1)} %edge_bands.1.c_ref, bf16[768,256]{1,0:T(8,128)(2,1)S(1)} %copy-done.12, bf16[128,432]{1,0:T(8,128)(2,1)S(1)} %copy-done.13), custom_call_target="tpu_custom_call" | custom-call | flops 679477248 | bytes 2228224 | tf_op jit(solution)/shard_map/detail_edges/pallas_call | solution.py:182
  34.0 0.1 collective-permute-start.12
  34.1 4.7 %collective-permute-start.13 = (f32[2,128,256]{2,1,0:T(8,128)S(1)}, f32[2,128,256]{2,1,0:T(8,128)S(1)}, u32[]{:S(2)}, u32[]{:S(2)}) collective-permute-start(f32[2,128,256]{2,1,0:T(8,128)S(1)} %get-tuple-element.64), channel_id=1, source_target_pairs={{4,0},{8,4},{12,8},{16,12},{20,16},{24,20},{28,24},{0,28},{5,1},{9... | collective-permute-start | bytes 786440 | tf_op jit(solution)/shard_map/ppermute | solution.py:780
  38.8 0.0 collective-permute-done.8.l_ref
  38.8 2.9 %coarse.1 = (f32[20,72,128]{2,1,0:T(8,128)S(1)}, f32[344,128]{1,0:T(8,128)S(1)}, f32[344,128]{1,0:T(8,128)S(1)}) custom-call(f32[16]{0:T(128)S(1)} %copy-done.11, s32[3,7]{1,0:T(4,128)S(1)} %copy-done.10, f32[16,96,128]{2,1,0:T(8,128)S(1)} %get-tuple-element.53.b_ref, f32[248,128]{1,0:T(8,128)S(1)} %collective-permute-done.8.l_ref, ...), custom_call_target="tpu_custom_call" | custom-call | flops 1500000000 | bytes 1572864 | tf_op jit(solution)/shard_map/coarse/pallas_call | solution.py:182
  41.8 0.0 copy-start.2
  41.8 0.0 copy-start.4
  41.8 0.1 collective-permute-start.10
  41.8 4.7 %collective-permute-start.11 = (f32[344,128]{1,0:T(8,128)S(1)}, f32[344,128]{1,0:T(8,128)S(1)}, u32[]{:S(2)}, u32[]{:S(2)}) collective-permute-start(f32[344,128]{1,0:T(8,128)S(1)} %get-tuple-element.57), channel_id=1, source_target_pairs={{4,0},{8,4},{12,8},{16,12},{20,16},{24,20},{28,24},{0,28},{5,1},{9... | collective-permute-start | bytes 528392 | tf_op jit(solution)/shard_map/ppermute | solution.py:780
  46.6 3.3 %detail_rest.1.r_ref = f32[24,128,256]{2,1,0:T(8,128)S(1)} custom-call(f32[24,144,256]{2,1,0:T(8,128)S(1)} %inner_bands.1.coeffs, bf16[768,256]{1,0:T(8,128)(2,1)S(1)} %copy-done.12, bf16[128,432]{1,0:T(8,128)(2,1)S(1)} %copy-done.13), custom_call_target="tpu_custom_call" | custom-call | flops 2038431744 | bytes 6684672 | tf_op jit(solution)/shard_map/detail_rest/pallas_call | solution.py:182
  49.9 4.8 %own_result.1.d_ref = f32[32,128,256]{2,1,0:T(8,128)S(1)} custom-call(f32[8,128,256]{2,1,0:T(8,128)S(1)} %get-tuple-element.58.e_ref, f32[24,128,256]{2,1,0:T(8,128)S(1)} %detail_rest.1.r_ref, f32[20,72,128]{2,1,0:T(8,128)S(1)} %get-tuple-element.62.a_ref, bf16[384,256]{1,0:T(8,128)(2,1)S(1)} %copy-done.2, bf16[128,240]{1,0:T(8,128)(2,1)S(1)} %copy-done.4), custom_call_target="tpu_custom_call" | custom-call | flops 16777216 | bytes 8388608 | tf_op jit(solution)/shard_map/own_result/pallas_call | solution.py:182
  54.8 0.7 %collective-permute-done.11.r_ref = f32[344,128]{1,0:T(8,128)S(1)} collective-permute-done((f32[344,128]{1,0:T(8,128)S(1)}, f32[344,128]{1,0:T(8,128)S(1)}, u32[]{:S(2)}, u32[]{:S(2)}) %collective-permute-start.11) | collective-permute-done | bytes 176160 | tf_op jit(solution)/shard_map/ppermute | solution.py:780
  55.5 3.5 %final.1 = f32[32,128,256]{2,1,0:T(8,128)} custom-call(f32[344,128]{1,0:T(8,128)S(1)} %collective-permute-done.10.l_ref, f32[344,128]{1,0:T(8,128)S(1)} %collective-permute-done.11.r_ref, f32[32,128,256]{2,1,0:T(8,128)S(1)} %own_result.1.d_ref, f32[2,128,256]{2,1,0:T(8,128)S(1)} %collective-permute-done.12.el, ...), custom_call_target="tpu_custom_call" | custom-call | flops 8388608 | bytes 8388608 | tf_op jit(solution)/shard_map/final/pallas_call | solution.py:757
  (29 shorter events, 0.1 us)
Async XLA Ops:
  0.0 9.3 %copy-start = (f32[32,128,256]{2,1,0:T(8,128)S(1)}, f32[32,128,256]{2,1,0:T(8,128)}, u32[]{:S(2)}) copy-start(f32[32,128,256]{2,1,0:T(8,128)} %v_ref.3) | copy-start | bytes 12582916
  1.5 10.8 %collective-permute-start.4 = (f32[32,8,256]{2,1,0:T(8,128)S(1)}, f32[32,8,256]{2,1,0:T(8,128)S(1)}, u32[]{:S(2)}, u32[]{:S(2)}) collective-permute-start(f32[32,8,256]{2,1,0:T(8,128)S(1)} %get-tuple-element.39), channel_id=1, source_target_pairs={{0,1},{1,2},{2,3},{3,0},{4,5},{5,6},{6,7},{7,4},{8,9},{9,10},{10,1... | collective-permute-start | bytes 786440 | tf_op jit(solution)/shard_map/ppermute | solution.py:775
  2.0 10.3 %collective-permute-start.5 = (f32[32,8,256]{2,1,0:T(8,128)S(1)}, f32[32,8,256]{2,1,0:T(8,128)S(1)}, u32[]{:S(2)}, u32[]{:S(2)}) collective-permute-start(f32[32,8,256]{2,1,0:T(8,128)S(1)} %get-tuple-element.40), channel_id=1, source_target_pairs={{1,0},{2,1},{3,2},{0,3},{5,4},{6,5},{7,6},{4,7},{9,8},{10,9},{11,1... | collective-permute-start | bytes 786440 | tf_op jit(solution)/shard_map/ppermute | solution.py:780
  4.0 13.5 %collective-permute-start = (f32[2,128,256]{2,1,0:T(8,128)S(1)}, f32[2,128,256]{2,1,0:T(8,128)S(1)}, u32[]{:S(2)}, u32[]{:S(2)}) collective-permute-start(f32[2,128,256]{2,1,0:T(8,128)S(1)} %get-tuple-element.35), channel_id=1, source_target_pairs={{0,4},{4,8},{8,12},{12,16},{16,20},{20,24},{24,28},{28,0},{1,5},{5... | collective-permute-start | bytes 786440 | tf_op jit(solution)/shard_map/ppermute | solution.py:775
  6.3 13.4 %collective-permute-start.1 = (f32[2,128,256]{2,1,0:T(8,128)S(1)}, f32[2,128,256]{2,1,0:T(8,128)S(1)}, u32[]{:S(2)}, u32[]{:S(2)}) collective-permute-start(f32[2,128,256]{2,1,0:T(8,128)S(1)} %get-tuple-element.36), channel_id=1, source_target_pairs={{4,0},{8,4},{12,8},{16,12},{20,16},{24,20},{28,24},{0,28},{5,1},{9... | collective-permute-start | bytes 786440 | tf_op jit(solution)/shard_map/ppermute | solution.py:780
  9.3 1.0 %copy-start.1 = (bf16[768,256]{1,0:T(8,128)(2,1)S(1)}, bf16[768,256]{1,0:T(8,128)(2,1)}, u32[]{:S(2)}) copy-start(bf16[768,256]{1,0:T(8,128)(2,1)} %constant.30.clone.z) | copy-start | bytes 1179652
  10.3 2.0 %copy-start.3 = (bf16[144,432]{1,0:T(8,128)(2,1)S(1)}, bf16[144,432]{1,0:T(8,128)(2,1)}, u32[]{:S(2)}) copy-start(bf16[144,432]{1,0:T(8,128)(2,1)} %constant.31.clone.y) | copy-start | bytes 373252
  14.6 7.3 %copy-start.10 = (s32[3,7]{1,0:T(4,128)S(1)}, s32[3,7]{1,0:T(4,128)}, u32[]{:S(2)}) copy-start(s32[3,7]{1,0:T(4,128)} %index_ref.5) | copy-start | bytes 256
  14.6 7.3 %copy-start.11 = (f32[16]{0:T(128)S(1)}, f32[16]{0:T(128)}, u32[]{:S(2)}) copy-start(f32[16]{0:T(128)} %table_ref.5) | copy-start | bytes 196
  15.0 9.9 %collective-permute-start.6 = (f32[16,24,128]{2,1,0:T(8,128)S(1)}, f32[16,24,128]{2,1,0:T(8,128)S(1)}, u32[]{:S(2)}, u32[]{:S(2)}) collective-permute-start(f32[16,24,128]{2,1,0:T(8,128)S(1)} %get-tuple-element.45), channel_id=1, source_target_pairs={{0,1},{1,2},{2,3},{3,0},{4,5},{5,6},{6,7},{7,4},{8,9},{9,10},{10,1... | collective-permute-start | bytes 589832 | tf_op jit(solution)/shard_map/ppermute | solution.py:775
  15.1 9.8 %collective-permute-start.7 = (f32[16,24,128]{2,1,0:T(8,128)S(1)}, f32[16,24,128]{2,1,0:T(8,128)S(1)}, u32[]{:S(2)}, u32[]{:S(2)}) collective-permute-start(f32[16,24,128]{2,1,0:T(8,128)S(1)} %get-tuple-element.46), channel_id=1, source_target_pairs={{1,0},{2,1},{3,2},{0,3},{5,4},{6,5},{7,6},{4,7},{9,8},{10,9},{11,1... | collective-permute-start | bytes 589832 | tf_op jit(solution)/shard_map/ppermute | solution.py:780
  20.1 4.8 %copy-start.5 = (bf16[112,672]{1,0:T(8,128)(2,1)S(1)}, bf16[112,672]{1,0:T(8,128)(2,1)}, u32[]{:S(2)}) copy-start(bf16[112,672]{1,0:T(8,128)(2,1)} %constant.33.clone.yx) | copy-start | bytes 451588
  20.1 4.8 %copy-start.7 = (bf16[384,128]{1,0:T(8,128)(2,1)S(1)}, bf16[384,128]{1,0:T(8,128)(2,1)}, u32[]{:S(2)}) copy-start(bf16[384,128]{1,0:T(8,128)(2,1)} %constant.32.clone.z) | copy-start | bytes 294916
  20.1 4.8 %copy-start.8 = (bf16[96,336]{1,0:T(8,128)(2,1)S(1)}, bf16[96,336]{1,0:T(8,128)(2,1)}, u32[]{:S(2)}) copy-start(bf16[96,336]{1,0:T(8,128)(2,1)} %constant.34.clone.y) | copy-start | bytes 193540
  20.1 4.7 %collective-permute-start.2 = (f32[4,56,128]{2,1,0:T(8,128)S(1)}, f32[4,56,128]{2,1,0:T(8,128)S(1)}, u32[]{:S(2)}, u32[]{:S(2)}) collective-permute-start(f32[4,56,128]{2,1,0:T(8,128)S(1)} %get-tuple-element.37), channel_id=1, source_target_pairs={{0,1},{1,2},{2,3},{3,0},{4,5},{5,6},{6,7},{7,4},{8,9},{9,10},{10,1... | collective-permute-start | bytes 344072 | tf_op jit(solution)/shard_map/ppermute | solution.py:775
  20.2 4.7 %collective-permute-start.3 = (f32[4,56,128]{2,1,0:T(8,128)S(1)}, f32[4,56,128]{2,1,0:T(8,128)S(1)}, u32[]{:S(2)}, u32[]{:S(2)}) collective-permute-start(f32[4,56,128]{2,1,0:T(8,128)S(1)} %get-tuple-element.38), channel_id=1, source_target_pairs={{1,0},{2,1},{3,2},{0,3},{5,4},{6,5},{7,6},{4,7},{9,8},{10,9},{11,1... | collective-permute-start | bytes 344072 | tf_op jit(solution)/shard_map/ppermute | solution.py:780
  24.1 8.5 %copy-start.12 = (bf16[768,256]{1,0:T(8,128)(2,1)S(1)}, bf16[768,256]{1,0:T(8,128)(2,1)}, u32[]{:S(2)}) copy-start(bf16[768,256]{1,0:T(8,128)(2,1)} %constant.35.clone.z) | copy-start | bytes 1179652
  24.1 8.5 %copy-start.13 = (bf16[128,432]{1,0:T(8,128)(2,1)S(1)}, bf16[128,432]{1,0:T(8,128)(2,1)}, u32[]{:S(2)}) copy-start(bf16[128,432]{1,0:T(8,128)(2,1)} %constant.36.clone.y) | copy-start | bytes 331780
  26.2 12.6 %collective-permute-start.8 = (f32[248,128]{1,0:T(8,128)S(1)}, f32[248,128]{1,0:T(8,128)S(1)}, u32[]{:S(2)}, u32[]{:S(2)}) collective-permute-start(f32[248,128]{1,0:T(8,128)S(1)} %get-tuple-element.54), channel_id=1, source_target_pairs={{0,4},{4,8},{8,12},{12,16},{16,20},{20,24},{24,28},{28,0},{1,5},{5... | collective-permute-start | bytes 380936 | tf_op jit(solution)/shard_map/ppermute | solution.py:775
  26.5 12.3 %collective-permute-start.9 = (f32[248,128]{1,0:T(8,128)S(1)}, f32[248,128]{1,0:T(8,128)S(1)}, u32[]{:S(2)}, u32[]{:S(2)}) collective-permute-start(f32[248,128]{1,0:T(8,128)S(1)} %get-tuple-element.55), channel_id=1, source_target_pairs={{4,0},{8,4},{12,8},{16,12},{20,16},{24,20},{28,24},{0,28},{5,1},{9... | collective-permute-start | bytes 380936 | tf_op jit(solution)/shard_map/ppermute | solution.py:780
  30.9 7.8 %copy-start.6 = (bf16[384,128]{1,0:T(8,128)(2,1)S(1)}, bf16[384,128]{1,0:T(8,128)(2,1)}, u32[]{:S(2)}) copy-start(bf16[384,128]{1,0:T(8,128)(2,1)} %constant.37.clone.z1) | copy-start | bytes 294916
  30.9 7.8 %copy-start.9 = (bf16[80,288]{1,0:T(8,128)(2,1)S(1)}, bf16[80,288]{1,0:T(8,128)(2,1)}, u32[]{:S(2)}) copy-start(bf16[80,288]{1,0:T(8,128)(2,1)} %constant.42.clone.s1) | copy-start | bytes 138244
  30.9 7.9 %copy-start.14 = (bf16[384,128]{1,0:T(8,128)(2,1)S(1)}, bf16[384,128]{1,0:T(8,128)(2,1)}, u32[]{:S(2)}) copy-start(bf16[384,128]{1,0:T(8,128)(2,1)} %constant.39.clone.z2s) | copy-start | bytes 294916
  30.9 7.9 %copy-start.15 = (bf16[384,128]{1,0:T(8,128)(2,1)S(1)}, bf16[384,128]{1,0:T(8,128)(2,1)}, u32[]{:S(2)}) copy-start(bf16[384,128]{1,0:T(8,128)(2,1)} %constant.38.clone.z2a) | copy-start | bytes 294916
  30.9 7.9 %copy-start.16 = (bf16[64,144]{1,0:T(8,128)(2,1)S(1)}, bf16[64,144]{1,0:T(8,128)(2,1)}, u32[]{:S(2)}) copy-start(bf16[64,144]{1,0:T(8,128)(2,1)} %constant.41.clone.s2) | copy-start | bytes 55300
  31.0 7.9 %copy-start.17 = (bf16[48,192]{1,0:T(8,128)(2,1)S(1)}, bf16[48,192]{1,0:T(8,128)(2,1)}, u32[]{:S(2)}) copy-start(bf16[48,192]{1,0:T(8,128)(2,1)} %constant.40.clone.a2) | copy-start | bytes 55300
  34.0 20.8 %collective-permute-start.12 = (f32[2,128,256]{2,1,0:T(8,128)S(1)}, f32[2,128,256]{2,1,0:T(8,128)S(1)}, u32[]{:S(2)}, u32[]{:S(2)}) collective-permute-start(f32[2,128,256]{2,1,0:T(8,128)S(1)} %get-tuple-element.63), channel_id=1, source_target_pairs={{0,4},{4,8},{8,12},{12,16},{16,20},{20,24},{24,28},{28,0},{1,5},{5... | collective-permute-start | bytes 786440 | tf_op jit(solution)/shard_map/ppermute | solution.py:775
  34.1 20.7 %collective-permute-start.13 = (f32[2,128,256]{2,1,0:T(8,128)S(1)}, f32[2,128,256]{2,1,0:T(8,128)S(1)}, u32[]{:S(2)}, u32[]{:S(2)}) collective-permute-start(f32[2,128,256]{2,1,0:T(8,128)S(1)} %get-tuple-element.64), channel_id=1, source_target_pairs={{4,0},{8,4},{12,8},{16,12},{20,16},{24,20},{28,24},{0,28},{5,1},{9... | collective-permute-start | bytes 786440 | tf_op jit(solution)/shard_map/ppermute | solution.py:780
  41.8 8.1 %copy-start.2 = (bf16[384,256]{1,0:T(8,128)(2,1)S(1)}, bf16[384,256]{1,0:T(8,128)(2,1)}, u32[]{:S(2)}) copy-start(bf16[384,256]{1,0:T(8,128)(2,1)} %constant.43.clone.z) | copy-start | bytes 589828
  41.8 8.1 %copy-start.4 = (bf16[128,240]{1,0:T(8,128)(2,1)S(1)}, bf16[128,240]{1,0:T(8,128)(2,1)}, u32[]{:S(2)}) copy-start(bf16[128,240]{1,0:T(8,128)(2,1)} %constant.44.clone.y) | copy-start | bytes 184324
  41.8 13.0 %collective-permute-start.10 = (f32[344,128]{1,0:T(8,128)S(1)}, f32[344,128]{1,0:T(8,128)S(1)}, u32[]{:S(2)}, u32[]{:S(2)}) collective-permute-start(f32[344,128]{1,0:T(8,128)S(1)} %get-tuple-element.56), channel_id=1, source_target_pairs={{0,4},{4,8},{8,12},{12,16},{16,20},{20,24},{24,28},{28,0},{1,5},{5... | collective-permute-start | bytes 528392 | tf_op jit(solution)/shard_map/ppermute | solution.py:775
  41.8 13.7 %collective-permute-start.11 = (f32[344,128]{1,0:T(8,128)S(1)}, f32[344,128]{1,0:T(8,128)S(1)}, u32[]{:S(2)}, u32[]{:S(2)}) collective-permute-start(f32[344,128]{1,0:T(8,128)S(1)} %get-tuple-element.57), channel_id=1, source_target_pairs={{4,0},{8,4},{12,8},{16,12},{20,16},{24,20},{28,24},{0,28},{5,1},{9... | collective-permute-start | bytes 528392 | tf_op jit(solution)/shard_map/ppermute | solution.py:780

commit v5 on v4

--- a/solution.py
+++ b/solution.py
@@ -158,6 +158,21 @@
     return added(terms)
 
 
+def x_synth_interior(lows, highs, n):
+    first, second, tangents = lattice()
+    a = {k - 1: lows[k] for k in range(n)}
+    b = {k - 1: highs[k] for k in range(n)}
+    for t in reversed(tangents):
+        a, b = {i + 1: a[i] - t * b[i] for i in a}, {i: b[i] + t * a[i] for i in b}
+        both = [i for i in a if i in b]
+        a, b = {i: a[i] for i in both}, {i: b[i] for i in both}
+    cells = {}
+    for i in a:
+        cells[2 * i - 1] = first[0] * a[i] + second[0] * b[i]
+        cells[2 * i] = first[1] * a[i] + second[1] * b[i]
+    return cells
+
+
 def spill_up(low, high, n):
     first = added([(H[5], low[n - 1]), (G[5], high[n - 1]), (H[7], low[n - 2]), (G[7], high[n - 2])])
     return first, added([(H[6], low[n - 1]), (G[6], high[n - 1])])
@@ -202,15 +217,17 @@
 def first_messages(v):
     nx, ny, nz = v.shape
 
-    def kernel(v_ref, up, down, y_up, y_down, last, first, sems):
+    kept = nx - nx // 8
+
+    def kernel(v_ref, up, down, y_up, y_down, last, first, rows_up, rows_down, sems):
         copies = [
             pltpu.make_async_copy(source, target, sems.at[i])
             for i, (source, target) in enumerate(
                 (
                     (v_ref.at[pl.ds(nx - 3, 3)], last),
                     (v_ref.at[pl.ds(0, 3)], first),
-                    (v_ref.at[:, pl.ds(ny - 8, 8)], y_up),
-                    (v_ref.at[:, pl.ds(0, 8)], y_down),
+                    (v_ref.at[:, pl.ds(ny - 8, 8)], rows_up),
+                    (v_ref.at[:, pl.ds(0, 8)], rows_down),
                 )
             )
         ]
@@ -222,13 +239,21 @@
         up[1] = H[0] * last[0] + H[1] * last[1]
         down[0] = first[0]
         down[1] = H[6] * first[1] + H[7] * first[2]
+        y_up[...] = rows_up[:kept]
+        y_down[...] = rows_down[:kept]
+        for i in range(kept):
+            plane, row = kept + i // 7, i % 7
+            y_up[i, 0:1] = rows_up[plane, row + 1 : row + 2]
+            y_down[i, 7:8] = rows_down[plane, row : row + 1]
 
     return pl.pallas_call(
         kernel,
         in_specs=[pl.BlockSpec(memory_space=pltpu.HBM)],
         out_specs=[VMEM] * 4,
-        out_shape=[shape(2, ny, nz)] * 2 + [shape(nx, 8, nz)] * 2,
-        scratch_shapes=[pltpu.VMEM((3, ny, nz), F32)] * 2 + [pltpu.SemaphoreType.DMA((4,))],
+        out_shape=[shape(2, ny, nz)] * 2 + [shape(kept, 8, nz)] * 2,
+        scratch_shapes=[pltpu.VMEM((3, ny, nz), F32)] * 2
+        + [pltpu.VMEM((nx, 8, nz), F32)] * 2
+        + [pltpu.SemaphoreType.DMA((4,))],
         name="first_messages",
         cost_estimate=pl.CostEstimate(flops=1000000, bytes_accessed=3000000, transcendentals=0),
         compiler_params=pltpu.CompilerParams(vmem_limit_bytes=50 * 1024 * 1024),
@@ -261,11 +286,17 @@
 def y_analysis(zed, y_left, y_right, z_matrix, y_matrix):
     nx, ny, nz = zed.shape
     rows = y_matrix.shape[0]
+    kept = y_left.shape[0]
     group = 8
 
     def kernel(zed_ref, left, right, z, y, out, left_z, right_z):
-        left_z[...] = times(left[...].reshape(8 * nx, nz), z).reshape(nx, 8, nz)
-        right_z[...] = times(right[...].reshape(8 * nx, nz), z).reshape(nx, 8, nz)
+        for part, out_z in ((left, left_z), (right, right_z)):
+            out_z[:kept] = times(part[...].reshape(8 * kept, nz), z).reshape(kept, 8, nz)
+            out_z[kept:] = jnp.zeros((nx - kept, 8, nz), F32)
+        for i in range(kept):
+            plane, row = kept + i // 7, i % 7
+            left_z[plane, row + 1 : row + 2] = left_z[i, 0:1]
+            right_z[plane, row : row + 1] = right_z[i, 7:8]
 
         def body(first):
             for j in range(group):
@@ -278,8 +309,8 @@
         kernel,
         shape(nx, rows, nz),
         [zed, y_left, y_right, z_matrix, y_matrix],
-        6 * nx * rows * (ny + 16) * nz,
-        4 * nx * nz * (ny + rows + 16),
+        1000,
+        1000,
         scratch=[pltpu.VMEM((nx, 8, nz), F32)] * 2,
         name="y_analysis",
     )
@@ -296,6 +327,10 @@
             values = {i: b_ref[i, at, :half_z] for i in range(nx)}
             for k in range(n1):
                 approx[k, at] = added([(c, values[i]) for i, c, _ in x_terms(k, nx) if i in values])
+            approx[n1, at] = added([(H[5 + i], values[i]) for i in range(3)])
+            approx[n1 + 1, at] = H[1] * H[7] * values[0]
+            approx[n1 + 2, at] = added([(H[i], values[nx - 3 + i]) for i in range(3)])
+            approx[n1 + 3, at] = H[6] * H[0] * values[nx - 1]
             return carry
 
         lax.fori_loop(0, own // 8, tile, 0)
@@ -304,10 +339,10 @@
 
     return whole_call(
         kernel,
-        [shape(n1, own, half_z), shape(n1, ghost_rows, half_z), shape(n1, ghost_rows, half_z)],
+        [shape(n1 + 4, own, half_z), shape(n1 + 4, ghost_rows, half_z), shape(n1 + 4, ghost_rows, half_z)],
         [bands],
-        16 * n1 * own * half_z,
-        3e6,
+        1000,
+        1000,
         name="own_approx",
     )
 
@@ -417,19 +452,17 @@
     )
 
 
-def yz_synthesis(coeffs, z, y, out, zed):
-    count, rows, nz = coeffs.shape
-
-    def z_body(first):
-        at = pl.ds(first, 8)
-        zed[at] = times(coeffs[at].reshape(8 * rows, nz), z).reshape(8, rows, nz)
+def yz_synthesis(planes, z, y, out, zed):
+    count, rows, nz = zed.shape
+    group = max(g for g in range(1, 13) if count % g == 0)
+    for first in range(0, count, group):
+        zed[first : first + group] = times(planes(first, group), z).reshape(group, rows, nz)
 
     def y_body(first):
-        for j in range(8):
+        for j in range(4):
             out[first + j] = left_times(y, zed[first + j])
 
-    over_planes(count, 8, z_body)
-    over_planes(count, 8, y_body)
+    over_planes(count, 4, y_body)
 
 
 def detail_edges(coeffs, z_matrix, y_matrix):
@@ -437,7 +470,7 @@
     ny = y_matrix.shape[0]
 
     def kernel(c_ref, z, y, out, up, down, zed):
-        yz_synthesis(c_ref, z, y, out, zed)
+        yz_synthesis(lambda first, n: c_ref[first : first + n].reshape(n * rows, nz), z, y, out, zed)
         part = lambda ks, at: {k: out[i] for k, i in zip(ks, at)}
         up[0], up[1] = spill_up(part((0, 1), (2, 3)), part((0, 1), (6, 7)), 2)
         down[0], down[1] = spill_down(part((0, 1), (0, 1)), part((0, 1), (4, 5)))
@@ -453,17 +486,33 @@
     )
 
 
-def detail_rest(coeffs, z_matrix, y_matrix):
+def inner_yz(coeffs, approx, z_matrix, y_matrix):
     count, rows, nz = coeffs.shape
     ny = y_matrix.shape[0]
-    return whole_call(
-        yz_synthesis,
+    _, low_rows, half_z = approx.shape
+    lows = count // 2
+
+    def kernel(c_ref, a_ref, z, y, out, zed):
+        def plane(i):
+            if i >= lows:
+                return c_ref[i]
+            corner = c_ref[i, :low_rows, :half_z] + a_ref[i + 4]
+            top = jnp.concatenate([corner, c_ref[i, :low_rows, half_z:]], axis=1)
+            return jnp.concatenate([top, c_ref[i, low_rows:]], axis=0)
+
+        def planes(first, n):
+            return jnp.concatenate([plane(i) for i in range(first, first + n)], axis=0)
+
+        yz_synthesis(planes, z, y, out, zed)
+
+    return whole_call(
+        kernel,
         shape(count, ny, nz),
-        [coeffs, z_matrix, y_matrix],
+        [coeffs, approx, z_matrix, y_matrix],
         6 * count * rows * nz * (nz + ny),
         4 * count * nz * (rows + ny),
         scratch=[pltpu.VMEM((count, rows, nz), F32)],
-        name="detail_rest",
+        name="inner_yz",
     )
 
 
@@ -475,12 +524,12 @@
     planes, rows, half_z = approx.shape
 
     def kernel(e_ref, r_ref, a_ref, z, y, out, parts):
-        def body(first):
-            zed = times(a_ref[pl.ds(first, 4)].reshape(4 * rows, half_z), z)
+        for first in (0, 4):
+            start = first and n1
+            zed = times(a_ref[start : start + 4].reshape(4 * rows, half_z), z)
             for j, plane in enumerate(cut(zed, rows)):
                 parts[first + j] = left_times(y, plane)
-
-        over_planes(planes, 4, body)
+        place = {k: i for i, k in enumerate([-2, -1, 0, 1, n1 - 2, n1 - 1, n1, n1 + 1])}
 
         def tile(t, carry):
             at = pl.ds(pl.multiple_of(t * 8, 8), 8)
@@ -492,12 +541,14 @@
                         return e_ref[4 * high + ends.index(k), at, lanes]
                     return r_ref[(n1 - 4) * high + k - 2, at, lanes]
 
-                lows = {k: parts[k + 2, at, lanes] for k in range(-2, n1 + 2)}
-                for k in range(n1):
-                    lows[k] = lows[k] + coeff(k, 0)
+                lows = {k: coeff(k, 0) for k in range(n1)}
                 highs = {k: coeff(k, 1) for k in range(n1)}
+                for k, i in place.items():
+                    part = parts[i, at, lanes]
+                    lows[k] = lows[k] + part if k in lows else part
+                cells = x_synth_interior(lows, highs, n1)
                 for m in range(nx):
-                    out[m, at, lanes] = x_synth(m, lows, highs)
+                    out[m, at, lanes] = cells[m] if m in cells else x_synth(m, lows, highs)
             return carry
 
         lax.fori_loop(0, ny // 8, tile, 0)
@@ -508,7 +559,7 @@
         [edge, rest, approx, z_matrix, y_matrix],
         16 * nx * ny * nz,
         8 * nx * ny * nz,
-        scratch=[pltpu.VMEM((planes, ny, nz), F32)],
+        scratch=[pltpu.VMEM((8, ny, nz), F32)],
         name="own_result",
     )
 
@@ -538,27 +589,16 @@
     return [jnp.where(lane < half, part, 0.0) for part in (both, pltpu.roll(both, half, 1))]
 
 
-def second_bands(own, left, right, halo, h_left, h_right, z_matrix, yx_matrix, y_matrix, low_rows):
-    n1, own_rows, nz = own.shape
+def second_bands(own, left, right, z_matrix, y_matrix, low_rows):
+    planes, own_rows, nz = own.shape
+    n1 = planes - 4
     in_rows = own_rows + 2 * left.shape[1]
     rows = y_matrix.shape[0]
 
-    wide = h_left.shape[1] - 8
-
-    def kernel(o_ref, l_ref, r_ref, x_ref, hl, hr, z, yx, y, out, up, down):
-        planes = [jnp.concatenate([hl[i, :wide], x_ref[i, :, :nz], hr[i, :wide]], axis=0) for i in range(4)]
-        l1, l2, r1, r2 = [plane[:in_rows] for plane in in_pairs(yx, planes)]
-        beyond = {
-            0: l2 + H[2] * l1,
-            1: H[0] * l1,
-            n1 - 2: H[7] * r1,
-            n1 - 1: r2 + H[5] * r1,
-        }
-        for i in range(0, n1, 8):
-            stack = []
-            for j in range(i, i + 8):
-                plane = jnp.concatenate([o_ref[j], l_ref[j], r_ref[j]], axis=0)
-                stack.append(plane + beyond[j] if j in beyond else plane)
+
+    def kernel(o_ref, l_ref, r_ref, z, y, out, up, down):
+        for i in range(0, planes, 10):
+            stack = [part[j] for j in range(i, i + 10) for part in (o_ref, l_ref, r_ref)]
             zed = times(jnp.concatenate(stack, axis=0), z)
             for j, plane in enumerate(in_pairs(y, cut(zed, in_rows))):
                 out[i + j] = plane
@@ -579,8 +619,8 @@
     message = 2 * rows + low_rows
     return whole_call(
         kernel,
-        [shape(n1, rows, nz), shape(message, nz), shape(message, nz)],
-        [own, left, right, halo, h_left, h_right, z_matrix, yx_matrix, y_matrix],
+        [shape(planes, rows, nz), shape(message, nz), shape(message, nz)],
+        [own, left, right, z_matrix, y_matrix],
         6 * n1 * in_rows * nz * (nz + rows),
         4 * n1 * nz * (in_rows + rows),
         name="second_bands",
@@ -599,21 +639,37 @@
     return jnp.where(row_high, jnp.where(lane_high, limit(1, 1), limit(1, 0)), low_y)
 
 
-def coarse(bands, left, right, table, index, zs1, za2, zs2, ya2, ys2, ys1, low_rows, out_rows):
-    n1, rows, nz = bands.shape
+def coarse(
+    bands, left, right, halo, h_left, h_right, table, index, za1, yx0, ya1, zs1, za2, zs2, ya2, ys2, ys1, low_rows, out_rows
+):
+    planes_in, rows, nz = bands.shape
+    n1 = planes_in - 4
+    in_rows = yx0.shape[0]
+    wide = h_left.shape[1] - 8
     n2, n3 = n1 // 2, n1 // 4
     rows2 = ya2.shape[0]
     lane_half = nz // 2
 
-    def kernel(table_ref, index_ref, b_ref, l_ref, r_ref, z1, z2a, z2s, a2, s2, s1, approx, up, down, c1, p1):
-        sides = {
-            "l1": lambda: l_ref[0:rows],
-            "l2": lambda: l_ref[rows : 2 * rows],
-            "r1": lambda: r_ref[0:rows],
-            "r2": lambda: r_ref[rows : 2 * rows],
-        }
-        get = lambda key: sides[key]() if isinstance(key, str) else b_ref[key]
-        low_part = lambda c: b_ref[c, :low_rows]
+    def kernel(
+        table_ref, index_ref, b_ref, l_ref, r_ref, x_ref, hl, hr, z1a, yx, a1, z1, z2a, z2s, a2, s2, s1,
+        approx, up, down, c1, p1,
+    ):
+        halo_planes = [jnp.concatenate([hl[i, :wide], x_ref[i, :, :nz], hr[i, :wide]], axis=0) for i in range(4)]
+        halo_planes = jnp.concatenate([plane[:in_rows] for plane in in_pairs(yx, halo_planes)], axis=0)
+        hl1, hl2, hr1, hr2 = in_pairs(a1, cut(times(halo_planes, z1a), in_rows))
+        values = {k: b_ref[k] for k in range(2, n1 - 2)}
+        values[0] = b_ref[0] + (hl2 + H[2] * hl1)
+        values[1] = b_ref[1] + H[0] * hl1
+        values[n1 - 2] = b_ref[n1 - 2] + H[7] * hr1
+        values[n1 - 1] = b_ref[n1 - 1] + (hr2 + H[5] * hr1)
+        xl1, xl2, xr1, xr2 = [b_ref[n1 + i] for i in range(4)]
+        values["l1"] = l_ref[0:rows] + xl1
+        values["l2"] = l_ref[rows : 2 * rows] + xl2
+        values["r1"] = r_ref[0:rows] + xr1
+        values["r2"] = r_ref[rows : 2 * rows] + xr2
+        get = values.get
+        low_part = lambda c: values[c][:low_rows]
+        xl1, xl2, xr1, xr2 = [part[:low_rows] for part in (xl1, xl2, xr1, xr2)]
         dims = (rows, nz)
         quiet = limits_plane(table_ref, index_ref, 1, 0, dims, low_rows, lane_half, NOTHING)
         loud = limits_plane(table_ref, index_ref, 1, 1, dims, low_rows, lane_half, NOTHING)
@@ -624,11 +680,15 @@
             c1[k] = shrink(low, quiet)
             c1[n2 + k] = shrink(x_high(get, k, n1), loud)
         first, second = unpacked(l_ref[2 * rows :])
-        planes.append(first + added([(H[5 + i], low_part(i)) for i in range(3)]))
-        planes.append(second + H[1] * H[7] * low_part(0))
+        own = [(H[5 + i], low_part(i)) for i in range(3)]
+        planes.append(first + added([(H[3] / H[1], xl2), (H[4], xl1)] + own))
+        own = [((H[0] * H[7] + H[1] * H[5]) / H[1], xl2), (H[1] * H[6], xl1), (H[1] * H[7], low_part(0))]
+        planes.append(second + added(own))
         first, second = unpacked(r_ref[2 * rows :])
-        planes.append(first + added([(H[i], low_part(n1 - 3 + i)) for i in range(3)]))
-        planes.append(second + H[6] * H[0] * low_part(n1 - 1))
+        own = [(H[i], low_part(n1 - 3 + i)) for i in range(3)]
+        planes.append(first + added([(H[3], xr1), (H[4] / H[6], xr2)] + own))
+        own = [((H[6] * H[2] + H[7] * H[0]) / H[6], xr2), (H[6] * H[1], xr1), (H[6] * H[0], low_part(n1 - 1))]
+        planes.append(second + added(own))
         third = in_pairs(a2, cut(times(jnp.concatenate(planes, axis=0), z2a), low_rows))
         keys = {"l1": n2, "l2": n2 + 1, "r1": n2 + 2, "r2": n2 + 3}
         get2 = lambda key: third[keys.get(key, key)]
@@ -678,7 +738,7 @@
     return whole_call(
         kernel,
         [shape(n1 + 4, out_rows, nz), shape(message, nz), shape(message, nz)],
-        [table, index, bands, left, right, zs1, za2, zs2, ya2, ys2, ys1],
+        [table, index, bands, left, right, halo, h_left, h_right, za1, yx0, ya1, zs1, za2, zs2, ya2, ys2, ys1],
         1.5e9,
         8 * n1 * rows * nz,
         scratch=[pltpu.VMEM((2 * n2, rows, nz), F32), pltpu.VMEM((2 * n2 + 6, out_rows, nz), F32)],
@@ -818,15 +878,13 @@
     approx, a_up, a_down = own_approx(bands, y1, ghost)
     a_left = to_next(a_up, "gy")
     a_right = to_previous(a_down, "gy")
+    inner = inner_bands(bands, table, index)
+    x_left, x_right, inner = lax.optimization_barrier((x_left, x_right, inner))
     halo, h_up, h_down = x_halo_messages(x_left, x_right, za0, wide)
     h_left = to_next(h_up, "gy")
     h_right = to_previous(h_down, "gy")
-    bands, halo = lax.optimization_barrier((bands, halo))
-    rest = inner_bands(bands, table, index)
-    rest, approx = lax.optimization_barrier((rest, approx))
-    bands1, b_up, b_down = second_bands(
-        approx, a_left, a_right, halo, h_left, h_right, za1, yx0, ya1, rows1
-    )
+    approx, halo = lax.optimization_barrier((approx, halo))
+    bands1, b_up, b_down = second_bands(approx, a_left, a_right, za1, ya1, rows1)
     b_left = to_next(b_up, "gx")
     b_right = to_previous(b_down, "gx")
     h_left, h_right, bands1 = lax.optimization_barrier((h_left, h_right, bands1))
@@ -836,12 +894,13 @@
     e_right = to_previous(e_down, "gx")
     bands1, edge = lax.optimization_barrier((bands1, edge))
     approx1, s_up, s_down = coarse(
-        bands1, b_left, b_right, table, index, zs1, za2, zs2, ya2, ys2, ys1, rows1, rows0
+        bands1, b_left, b_right, halo, h_left, h_right, table, index,
+        za1, yx0, ya1, zs1, za2, zs2, ya2, ys2, ys1, rows1, rows0,
     )
     s_left = to_next(s_up, "gx")
     s_right = to_previous(s_down, "gx")
-    rest, approx1 = lax.optimization_barrier((rest, approx1))
-    own = own_result(edge, detail_rest(rest, zs0, ys0), approx1, zs0_low, ys0_low)
+    rest = inner_yz(inner, approx1, zs0, ys0)
+    own = own_result(edge, rest, approx1, zs0_low, ys0_low)
     return final(s_left, s_right, own, e_left, e_right, zs1, ys1, zs0_low, ys0_low, rows1)
 
 

time: 59.1 us -> 57.3 us (0.970)
  Pallas kernels: 27.5 us -> 25.8 us
    pallas_call x11, Pallas kernels: 22.5 us -> 20.7 us  [whole_call(): pl.pallas_call(kernel, in_specs=specs, out_specs=outs, out_shape=out_shap...]
    ppermute x7, waiting for transfers between devices: 1.42 us -> 0.02 us  [to_next(): return lax.ppermute(array, axis, [(i, (i + 1) % size) for i in range(size)])]
    ppermute x7, waiting for transfers between devices: 2.95 us -> 4.08 us  [to_previous(): return lax.ppermute(array, axis, [((i + 1) % size, i) for i in range(size)])]
  transfers between devices with their start and end apart: 14 -> 14, of which waited for: 4 -> 3; matrix products, arithmetic and copies ran while one was open for 0% -> 0% of each run, Pallas kernels for 36% -> 36%
where the time goes in v5:
time: 57.3 us; the launch traced here: 57.1 us
  Pallas kernels  25.8 us (45%)
  starting transfers between devices  25.6 us (45%)
  waiting for transfers between devices  4.1 us (7%)
  local copies, waits for them, and re-layouts  1.1 us (2%)
    ppermute x7, starting transfers between devices, to_previous(): return lax.ppermute(array, axis, [((i + 1) % size, i) for i in range(size)])  22.6 us
    pallas_call x11, Pallas kernels, whole_call(): pl.pallas_call(kernel, in_specs=specs, out_specs=outs, out_shape=out_shap...  20.7 us
    ppermute x7, waiting for transfers between devices, to_previous(): return lax.ppermute(array, axis, [((i + 1) % size, i) for i in range(size)])  4.08 us
    pallas_call x1, Pallas kernels, final(): pl.pallas_call(kernel, in_specs=[VMEM] * 9, out_specs=pl.BlockSpec(memory...  3.48 us
    ppermute x7, starting transfers between devices, to_next(): return lax.ppermute(array, axis, [(i, (i + 1) % size) for i in range(size)])  3.01 us
    pallas_call x1, Pallas kernels, first_messages(): pl.pallas_call(kernel, in_specs=[pl.BlockSpec(memory_space=pltpu.HBM)], o...  1.57 us
  transfers between devices with their start and end apart: 14, of which 3 were waited for; matrix products, arithmetic and copies ran while one was open for 0% of the time, Pallas kernels for 36%

profile of v5, /device:TPU:0, one launch (start us, length us, event | category | flops | bytes accessed | tf_op | source)
XLA Modules:
  0.0 57.1 jit_solution(17529094949984223094)
XLA Ops:
  0.0 1.6 %first_messages.1 = (f32[2,128,256]{2,1,0:T(8,128)S(1)}, f32[2,128,256]{2,1,0:T(8,128)S(1)}, f32[28,8,256]{2,1,0:T(8,128)S(1)}, f32[28,8,256]{2,1,0:T(8,128)S(1)}) custom-call(f32[32,128,256]{2,1,0:T(8,128)} %v_ref.3), custom_call_target="tpu_custom_call" | custom-call | flops 1000000 | bytes 3000000 | tf_op jit(solution)/shard_map/first_messages/pallas_call | solution.py:249
  1.6 0.5 collective-permute-start.2
  2.1 2.0 %collective-permute-start.3 = (f32[28,8,256]{2,1,0:T(8,128)S(1)}, f32[28,8,256]{2,1,0:T(8,128)S(1)}, u32[]{:S(2)}, u32[]{:S(2)}) collective-permute-start(f32[28,8,256]{2,1,0:T(8,128)S(1)} %get-tuple-element.37), channel_id=1, source_target_pairs={{1,0},{2,1},{3,2},{0,3},{5,4},{6,5},{7,6},{4,7},{9,8},{10,9},{11,1... | collective-permute-start | bytes 688136 | tf_op jit(solution)/shard_map/ppermute | solution.py:840
  4.1 2.2 %collective-permute-start = (f32[2,128,256]{2,1,0:T(8,128)S(1)}, f32[2,128,256]{2,1,0:T(8,128)S(1)}, u32[]{:S(2)}, u32[]{:S(2)}) collective-permute-start(f32[2,128,256]{2,1,0:T(8,128)S(1)} %get-tuple-element.34), channel_id=1, source_target_pairs={{0,4},{4,8},{8,12},{12,16},{16,20},{20,24},{24,28},{28,0},{1,5},{5... | collective-permute-start | bytes 786440 | tf_op jit(solution)/shard_map/ppermute | solution.py:835
  6.3 3.0 %collective-permute-start.1 = (f32[2,128,256]{2,1,0:T(8,128)S(1)}, f32[2,128,256]{2,1,0:T(8,128)S(1)}, u32[]{:S(2)}, u32[]{:S(2)}) collective-permute-start(f32[2,128,256]{2,1,0:T(8,128)S(1)} %get-tuple-element.35), channel_id=1, source_target_pairs={{4,0},{8,4},{12,8},{16,12},{20,16},{24,20},{28,24},{0,28},{5,1},{9... | collective-permute-start | bytes 786440 | tf_op jit(solution)/shard_map/ppermute | solution.py:840
  9.4 1.0 %copy-done.1 = bf16[768,256]{1,0:T(8,128)(2,1)S(1)} copy-done((bf16[768,256]{1,0:T(8,128)(2,1)S(1)}, bf16[768,256]{1,0:T(8,128)(2,1)}, u32[]{:S(2)}) %copy-start.1) | copy-done | bytes 393240
  10.4 2.0 %depth_analysis.1.zed_ref = f32[32,128,256]{2,1,0:T(8,128)S(1)} custom-call(f32[32,128,256]{2,1,0:T(8,128)S(1)} %copy-done, bf16[768,256]{1,0:T(8,128)(2,1)S(1)} %copy-done.1), custom_call_target="tpu_custom_call" | custom-call | flops 1610612736 | bytes 8388608 | tf_op jit(solution)/shard_map/depth_analysis/pallas_call | solution.py:197
  12.3 0.0 collective-permute-done.2.left
  12.4 2.3 %y_analysis.1.b_ref = f32[32,144,256]{2,1,0:T(8,128)S(1)} custom-call(f32[32,128,256]{2,1,0:T(8,128)S(1)} %depth_analysis.1.zed_ref, f32[28,8,256]{2,1,0:T(8,128)S(1)} %collective-permute-done.2.left, f32[28,8,256]{2,1,0:T(8,128)S(1)} %collective-permute-done.3.right, bf16[768,256]{1,0:T(8,128)(2,1)S(1)} %copy-done.1, bf16[144,432]{1,0:T(8,128)(2,1)S(1)} %copy-done.3), custom_call_target="tpu_custom_call" | custom-call | flops 1000 | bytes 1000 | tf_op jit(solution)/shard_map/y_analysis/pallas_call | solution.py:197
  14.7 0.0 copy-start.11
  14.7 0.0 copy-start.12
  14.7 0.3 own_approx.1
  15.0 0.1 collective-permute-start.6
  15.1 0.0 copy-start.8
  15.1 0.0 copy-start.9
  15.1 1.7 %collective-permute-start.7 = (f32[20,24,128]{2,1,0:T(8,128)S(1)}, f32[20,24,128]{2,1,0:T(8,128)S(1)}, u32[]{:S(2)}, u32[]{:S(2)}) collective-permute-start(f32[20,24,128]{2,1,0:T(8,128)S(1)} %get-tuple-element.46), channel_id=1, source_target_pairs={{1,0},{2,1},{3,2},{0,3},{5,4},{6,5},{7,6},{4,7},{9,8},{10,9},{11,1... | collective-permute-start | bytes 737288 | tf_op jit(solution)/shard_map/ppermute | solution.py:840
  16.9 2.2 %inner_bands.1.c_ref = f32[24,144,256]{2,1,0:T(8,128)S(1)} custom-call(f32[16]{0:T(128)S(1)} %copy-done.12, s32[3,7]{1,0:T(4,128)S(1)} %copy-done.11, f32[32,144,256]{2,1,0:T(8,128)S(1)} %y_analysis.1.b_ref), custom_call_target="tpu_custom_call" | custom-call | flops 35389440 | bytes 9437184 | tf_op jit(solution)/shard_map/inner_bands/pallas_call | solution.py:197
  19.0 0.0 collective-permute-done.xl
  19.1 0.7 %collective-permute-done.1.xr = f32[2,128,256]{2,1,0:T(8,128)S(1)} collective-permute-done((f32[2,128,256]{2,1,0:T(8,128)S(1)}, f32[2,128,256]{2,1,0:T(8,128)S(1)}, u32[]{:S(2)}, u32[]{:S(2)}) %collective-permute-start.1) | collective-permute-done | bytes 262176 | tf_op jit(solution)/shard_map/ppermute | solution.py:840
  19.8 0.4 x_halo_messages.1
  20.1 0.0 copy-start.4
  20.1 0.0 copy-start.6
  20.2 0.1 collective-permute-start.4
  20.2 1.7 %collective-permute-start.5 = (f32[4,56,128]{2,1,0:T(8,128)S(1)}, f32[4,56,128]{2,1,0:T(8,128)S(1)}, u32[]{:S(2)}, u32[]{:S(2)}) collective-permute-start(f32[4,56,128]{2,1,0:T(8,128)S(1)} %get-tuple-element.41), channel_id=1, source_target_pairs={{1,0},{2,1},{3,2},{0,3},{5,4},{6,5},{7,6},{4,7},{9,8},{10,9},{11,1... | collective-permute-start | bytes 344072 | tf_op jit(solution)/shard_map/ppermute | solution.py:840
  22.0 0.0 collective-permute-done.6.l_ref
  22.0 1.2 %collective-permute-done.7.r_ref = f32[20,24,128]{2,1,0:T(8,128)S(1)} collective-permute-done((f32[20,24,128]{2,1,0:T(8,128)S(1)}, f32[20,24,128]{2,1,0:T(8,128)S(1)}, u32[]{:S(2)}, u32[]{:S(2)}) %collective-permute-start.7) | collective-permute-done | bytes 245792 | tf_op jit(solution)/shard_map/ppermute | solution.py:840
  23.1 1.1 %second_bands.1 = (f32[20,96,128]{2,1,0:T(8,128)S(1)}, f32[248,128]{1,0:T(8,128)S(1)}, f32[248,128]{1,0:T(8,128)S(1)}) custom-call(f32[20,64,128]{2,1,0:T(8,128)S(1)} %get-tuple-element.44.o_ref, f32[20,24,128]{2,1,0:T(8,128)S(1)} %collective-permute-done.6.l_ref, f32[20,24,128]{2,1,0:T(8,128)S(1)} %collective-permute-done.7.r_ref, ...), custom_call_target="tpu_custom_call" | custom-call | flops 308281344 | bytes 1703936 | tf_op jit(solution)/shard_map/second_bands/pallas_call | solution.py:197
  24.2 0.1 collective-permute-start.8
  24.3 4.7 %collective-permute-start.9 = (f32[248,128]{1,0:T(8,128)S(1)}, f32[248,128]{1,0:T(8,128)S(1)}, u32[]{:S(2)}, u32[]{:S(2)}) collective-permute-start(f32[248,128]{1,0:T(8,128)S(1)} %get-tuple-element.55), channel_id=1, source_target_pairs={{4,0},{8,4},{12,8},{16,12},{20,16},{24,20},{28,24},{0,28},{5,1},{9... | collective-permute-start | bytes 380936 | tf_op jit(solution)/shard_map/ppermute | solution.py:840
  29.0 0.0 copy-start.10
  29.0 0.0 copy-start.13
  29.0 0.0 copy-start.14
  29.1 0.0 copy-start.15
  29.1 0.0 copy-start.16
  29.1 0.0 copy-start.17
  29.1 1.6 %edge_bands.1.c_ref = f32[8,144,256]{2,1,0:T(8,128)S(1)} custom-call(f32[16]{0:T(128)S(1)} %copy-done.12, s32[3,7]{1,0:T(4,128)S(1)} %copy-done.11, f32[32,144,256]{2,1,0:T(8,128)S(1)} %y_analysis.1.b_ref, f32[4,128,256]{2,1,0:T(8,128)S(1)} %get-tuple-element.49.x_ref, f32[4,56,128]{2,1,0:T(8,128)S(1)} %collective-permute-done.4.hl, ...), custom_call_target="tpu_custom_call" | custom-call | flops 23592960 | bytes 4718592 | tf_op jit(solution)/shard_map/edge_bands/pallas_call | solution.py:197
  30.8 1.4 %detail_edges.1 = (f32[8,128,256]{2,1,0:T(8,128)S(1)}, f32[2,128,256]{2,1,0:T(8,128)S(1)}, f32[2,128,256]{2,1,0:T(8,128)S(1)}) custom-call(f32[8,144,256]{2,1,0:T(8,128)S(1)} %edge_bands.1.c_ref, bf16[768,256]{1,0:T(8,128)(2,1)S(1)} %copy-done.4, bf16[128,432]{1,0:T(8,128)(2,1)S(1)} %copy-done.6), custom_call_target="tpu_custom_call" | custom-call | flops 679477248 | bytes 2228224 | tf_op jit(solution)/shard_map/detail_edges/pallas_call | solution.py:197
  32.1 0.1 collective-permute-start.12
  32.2 4.7 %collective-permute-start.13 = (f32[2,128,256]{2,1,0:T(8,128)S(1)}, f32[2,128,256]{2,1,0:T(8,128)S(1)}, u32[]{:S(2)}, u32[]{:S(2)}) collective-permute-start(f32[2,128,256]{2,1,0:T(8,128)S(1)} %get-tuple-element.62), channel_id=1, source_target_pairs={{4,0},{8,4},{12,8},{16,12},{20,16},{24,20},{28,24},{0,28},{5,1},{9... | collective-permute-start | bytes 786440 | tf_op jit(solution)/shard_map/ppermute | solution.py:840
  37.0 3.5 %coarse.1 = (f32[20,72,128]{2,1,0:T(8,128)S(1)}, f32[344,128]{1,0:T(8,128)S(1)}, f32[344,128]{1,0:T(8,128)S(1)}) custom-call(f32[16]{0:T(128)S(1)} %copy-done.12, s32[3,7]{1,0:T(4,128)S(1)} %copy-done.11, f32[20,96,128]{2,1,0:T(8,128)S(1)} %get-tuple-element.53.b_ref, f32[248,128]{1,0:T(8,128)S(1)} %collective-permute-done.8.l_ref, ...), custom_call_target="tpu_custom_call" | custom-call | flops 1500000000 | bytes 1572864 | tf_op jit(solution)/shard_map/coarse/pallas_call | solution.py:197
  40.5 0.0 copy-start.2
  40.6 0.0 copy-start.5
  40.6 0.1 collective-permute-start.10
  40.6 4.7 %collective-permute-start.11 = (f32[344,128]{1,0:T(8,128)S(1)}, f32[344,128]{1,0:T(8,128)S(1)}, u32[]{:S(2)}, u32[]{:S(2)}) collective-permute-start(f32[344,128]{1,0:T(8,128)S(1)} %get-tuple-element.57), channel_id=1, source_target_pairs={{4,0},{8,4},{12,8},{16,12},{20,16},{24,20},{28,24},{0,28},{5,1},{9... | collective-permute-start | bytes 528392 | tf_op jit(solution)/shard_map/ppermute | solution.py:840
  45.3 3.5 %inner_yz.1.r_ref = f32[24,128,256]{2,1,0:T(8,128)S(1)} custom-call(f32[24,144,256]{2,1,0:T(8,128)S(1)} %inner_bands.1.c_ref, f32[20,72,128]{2,1,0:T(8,128)S(1)} %get-tuple-element.60.a_ref, bf16[768,256]{1,0:T(8,128)(2,1)S(1)} %copy-done.4, bf16[128,432]{1,0:T(8,128)(2,1)S(1)} %copy-done.6), custom_call_target="tpu_custom_call" | custom-call | flops 2038431744 | bytes 6684672 | tf_op jit(solution)/shard_map/inner_yz/pallas_call | solution.py:197
  48.8 2.5 %own_result.1.d_ref = f32[32,128,256]{2,1,0:T(8,128)S(1)} custom-call(f32[8,128,256]{2,1,0:T(8,128)S(1)} %get-tuple-element.58.e_ref, f32[24,128,256]{2,1,0:T(8,128)S(1)} %inner_yz.1.r_ref, f32[20,72,128]{2,1,0:T(8,128)S(1)} %get-tuple-element.60.a_ref, bf16[384,256]{1,0:T(8,128)(2,1)S(1)} %copy-done.2, bf16[128,240]{1,0:T(8,128)(2,1)S(1)} %copy-done.5), custom_call_target="tpu_custom_call" | custom-call | flops 16777216 | bytes 8388608 | tf_op jit(solution)/shard_map/own_result/pallas_call | solution.py:197
  51.3 2.2 %collective-permute-done.11.r_ref = f32[344,128]{1,0:T(8,128)S(1)} collective-permute-done((f32[344,128]{1,0:T(8,128)S(1)}, f32[344,128]{1,0:T(8,128)S(1)}, u32[]{:S(2)}, u32[]{:S(2)}) %collective-permute-start.11) | collective-permute-done | bytes 176160 | tf_op jit(solution)/shard_map/ppermute | solution.py:840
  53.5 3.5 %final.1 = f32[32,128,256]{2,1,0:T(8,128)} custom-call(f32[344,128]{1,0:T(8,128)S(1)} %collective-permute-done.10.l_ref, f32[344,128]{1,0:T(8,128)S(1)} %collective-permute-done.11.r_ref, f32[32,128,256]{2,1,0:T(8,128)S(1)} %own_result.1.d_ref, f32[2,128,256]{2,1,0:T(8,128)S(1)} %collective-permute-done.12.el, ...), custom_call_target="tpu_custom_call" | custom-call | flops 8388608 | bytes 8388608 | tf_op jit(solution)/shard_map/final/pallas_call | solution.py:817
  (29 shorter events, 0.1 us)
Async XLA Ops:
  0.0 9.4 %copy-start = (f32[32,128,256]{2,1,0:T(8,128)S(1)}, f32[32,128,256]{2,1,0:T(8,128)}, u32[]{:S(2)}) copy-start(f32[32,128,256]{2,1,0:T(8,128)} %v_ref.3) | copy-start | bytes 12582916
  1.6 10.8 %collective-permute-start.2 = (f32[28,8,256]{2,1,0:T(8,128)S(1)}, f32[28,8,256]{2,1,0:T(8,128)S(1)}, u32[]{:S(2)}, u32[]{:S(2)}) collective-permute-start(f32[28,8,256]{2,1,0:T(8,128)S(1)} %get-tuple-element.36), channel_id=1, source_target_pairs={{0,1},{1,2},{2,3},{3,0},{4,5},{5,6},{6,7},{7,4},{8,9},{9,10},{10,1... | collective-permute-start | bytes 688136 | tf_op jit(solution)/shard_map/ppermute | solution.py:835
  2.1 10.3 %collective-permute-start.3 = (f32[28,8,256]{2,1,0:T(8,128)S(1)}, f32[28,8,256]{2,1,0:T(8,128)S(1)}, u32[]{:S(2)}, u32[]{:S(2)}) collective-permute-start(f32[28,8,256]{2,1,0:T(8,128)S(1)} %get-tuple-element.37), channel_id=1, source_target_pairs={{1,0},{2,1},{3,2},{0,3},{5,4},{6,5},{7,6},{4,7},{9,8},{10,9},{11,1... | collective-permute-start | bytes 688136 | tf_op jit(solution)/shard_map/ppermute | solution.py:840
  4.1 14.9 %collective-permute-start = (f32[2,128,256]{2,1,0:T(8,128)S(1)}, f32[2,128,256]{2,1,0:T(8,128)S(1)}, u32[]{:S(2)}, u32[]{:S(2)}) collective-permute-start(f32[2,128,256]{2,1,0:T(8,128)S(1)} %get-tuple-element.34), channel_id=1, source_target_pairs={{0,4},{4,8},{8,12},{12,16},{16,20},{20,24},{24,28},{28,0},{1,5},{5... | collective-permute-start | bytes 786440 | tf_op jit(solution)/shard_map/ppermute | solution.py:835
  6.3 13.4 %collective-permute-start.1 = (f32[2,128,256]{2,1,0:T(8,128)S(1)}, f32[2,128,256]{2,1,0:T(8,128)S(1)}, u32[]{:S(2)}, u32[]{:S(2)}) collective-permute-start(f32[2,128,256]{2,1,0:T(8,128)S(1)} %get-tuple-element.35), channel_id=1, source_target_pairs={{4,0},{8,4},{12,8},{16,12},{20,16},{24,20},{28,24},{0,28},{5,1},{9... | collective-permute-start | bytes 786440 | tf_op jit(solution)/shard_map/ppermute | solution.py:840
  9.4 1.0 %copy-start.1 = (bf16[768,256]{1,0:T(8,128)(2,1)S(1)}, bf16[768,256]{1,0:T(8,128)(2,1)}, u32[]{:S(2)}) copy-start(bf16[768,256]{1,0:T(8,128)(2,1)} %constant.30.clone.z) | copy-start | bytes 1179652
  10.4 2.0 %copy-start.3 = (bf16[144,432]{1,0:T(8,128)(2,1)S(1)}, bf16[144,432]{1,0:T(8,128)(2,1)}, u32[]{:S(2)}) copy-start(bf16[144,432]{1,0:T(8,128)(2,1)} %constant.31.clone.y) | copy-start | bytes 373252
  14.7 2.2 %copy-start.11 = (s32[3,7]{1,0:T(4,128)S(1)}, s32[3,7]{1,0:T(4,128)}, u32[]{:S(2)}) copy-start(s32[3,7]{1,0:T(4,128)} %index_ref.5) | copy-start | bytes 256
  14.7 2.2 %copy-start.12 = (f32[16]{0:T(128)S(1)}, f32[16]{0:T(128)}, u32[]{:S(2)}) copy-start(f32[16]{0:T(128)} %table_ref.5) | copy-start | bytes 196
  15.0 6.9 %collective-permute-start.6 = (f32[20,24,128]{2,1,0:T(8,128)S(1)}, f32[20,24,128]{2,1,0:T(8,128)S(1)}, u32[]{:S(2)}, u32[]{:S(2)}) collective-permute-start(f32[20,24,128]{2,1,0:T(8,128)S(1)} %get-tuple-element.45), channel_id=1, source_target_pairs={{0,1},{1,2},{2,3},{3,0},{4,5},{5,6},{6,7},{7,4},{8,9},{9,10},{10,1... | collective-permute-start | bytes 737288 | tf_op jit(solution)/shard_map/ppermute | solution.py:835
  15.1 8.0 %copy-start.8 = (bf16[384,128]{1,0:T(8,128)(2,1)S(1)}, bf16[384,128]{1,0:T(8,128)(2,1)}, u32[]{:S(2)}) copy-start(bf16[384,128]{1,0:T(8,128)(2,1)} %constant.32.clone.z.z1a) | copy-start | bytes 294916
  15.1 8.0 %copy-start.9 = (bf16[96,336]{1,0:T(8,128)(2,1)S(1)}, bf16[96,336]{1,0:T(8,128)(2,1)}, u32[]{:S(2)}) copy-start(bf16[96,336]{1,0:T(8,128)(2,1)} %constant.33.clone.y.a1) | copy-start | bytes 193540
  15.1 8.0 %collective-permute-start.7 = (f32[20,24,128]{2,1,0:T(8,128)S(1)}, f32[20,24,128]{2,1,0:T(8,128)S(1)}, u32[]{:S(2)}, u32[]{:S(2)}) collective-permute-start(f32[20,24,128]{2,1,0:T(8,128)S(1)} %get-tuple-element.46), channel_id=1, source_target_pairs={{1,0},{2,1},{3,2},{0,3},{5,4},{6,5},{7,6},{4,7},{9,8},{10,9},{11,1... | collective-permute-start | bytes 737288 | tf_op jit(solution)/shard_map/ppermute | solution.py:840
  20.1 10.6 %copy-start.4 = (bf16[768,256]{1,0:T(8,128)(2,1)S(1)}, bf16[768,256]{1,0:T(8,128)(2,1)}, u32[]{:S(2)}) copy-start(bf16[768,256]{1,0:T(8,128)(2,1)} %constant.34.clone.z) | copy-start | bytes 1179652
  20.1 10.6 %copy-start.6 = (bf16[128,432]{1,0:T(8,128)(2,1)S(1)}, bf16[128,432]{1,0:T(8,128)(2,1)}, u32[]{:S(2)}) copy-start(bf16[128,432]{1,0:T(8,128)(2,1)} %constant.35.clone.y) | copy-start | bytes 331780
  20.2 8.9 %collective-permute-start.4 = (f32[4,56,128]{2,1,0:T(8,128)S(1)}, f32[4,56,128]{2,1,0:T(8,128)S(1)}, u32[]{:S(2)}, u32[]{:S(2)}) collective-permute-start(f32[4,56,128]{2,1,0:T(8,128)S(1)} %get-tuple-element.40), channel_id=1, source_target_pairs={{0,1},{1,2},{2,3},{3,0},{4,5},{5,6},{6,7},{7,4},{8,9},{9,10},{10,1... | collective-permute-start | bytes 344072 | tf_op jit(solution)/shard_map/ppermute | solution.py:835
  20.2 8.8 %collective-permute-start.5 = (f32[4,56,128]{2,1,0:T(8,128)S(1)}, f32[4,56,128]{2,1,0:T(8,128)S(1)}, u32[]{:S(2)}, u32[]{:S(2)}) collective-permute-start(f32[4,56,128]{2,1,0:T(8,128)S(1)} %get-tuple-element.41), channel_id=1, source_target_pairs={{1,0},{2,1},{3,2},{0,3},{5,4},{6,5},{7,6},{4,7},{9,8},{10,9},{11,1... | collective-permute-start | bytes 344072 | tf_op jit(solution)/shard_map/ppermute | solution.py:840
  24.2 12.7 %collective-permute-start.8 = (f32[248,128]{1,0:T(8,128)S(1)}, f32[248,128]{1,0:T(8,128)S(1)}, u32[]{:S(2)}, u32[]{:S(2)}) collective-permute-start(f32[248,128]{1,0:T(8,128)S(1)} %get-tuple-element.54), channel_id=1, source_target_pairs={{0,4},{4,8},{8,12},{12,16},{16,20},{20,24},{24,28},{28,0},{1,5},{5... | collective-permute-start | bytes 380936 | tf_op jit(solution)/shard_map/ppermute | solution.py:835
  24.3 12.6 %collective-permute-start.9 = (f32[248,128]{1,0:T(8,128)S(1)}, f32[248,128]{1,0:T(8,128)S(1)}, u32[]{:S(2)}, u32[]{:S(2)}) collective-permute-start(f32[248,128]{1,0:T(8,128)S(1)} %get-tuple-element.55), channel_id=1, source_target_pairs={{4,0},{8,4},{12,8},{16,12},{20,16},{24,20},{28,24},{0,28},{5,1},{9... | collective-permute-start | bytes 380936 | tf_op jit(solution)/shard_map/ppermute | solution.py:840
  29.0 7.9 %copy-start.7 = (bf16[384,128]{1,0:T(8,128)(2,1)S(1)}, bf16[384,128]{1,0:T(8,128)(2,1)}, u32[]{:S(2)}) copy-start(bf16[384,128]{1,0:T(8,128)(2,1)} %constant.37.clone.z1) | copy-start | bytes 294916
  29.0 7.9 %copy-start.10 = (bf16[80,288]{1,0:T(8,128)(2,1)S(1)}, bf16[80,288]{1,0:T(8,128)(2,1)}, u32[]{:S(2)}) copy-start(bf16[80,288]{1,0:T(8,128)(2,1)} %constant.42.clone.s1) | copy-start | bytes 138244
  29.0 7.9 %copy-start.13 = (bf16[112,672]{1,0:T(8,128)(2,1)S(1)}, bf16[112,672]{1,0:T(8,128)(2,1)}, u32[]{:S(2)}) copy-start(bf16[112,672]{1,0:T(8,128)(2,1)} %constant.36.clone.yx) | copy-start | bytes 451588
  29.0 7.9 %copy-start.14 = (bf16[384,128]{1,0:T(8,128)(2,1)S(1)}, bf16[384,128]{1,0:T(8,128)(2,1)}, u32[]{:S(2)}) copy-start(bf16[384,128]{1,0:T(8,128)(2,1)} %constant.39.clone.z2s) | copy-start | bytes 294916
  29.1 7.9 %copy-start.15 = (bf16[384,128]{1,0:T(8,128)(2,1)S(1)}, bf16[384,128]{1,0:T(8,128)(2,1)}, u32[]{:S(2)}) copy-start(bf16[384,128]{1,0:T(8,128)(2,1)} %constant.38.clone.z2a) | copy-start | bytes 294916
  29.1 7.9 %copy-start.16 = (bf16[64,144]{1,0:T(8,128)(2,1)S(1)}, bf16[64,144]{1,0:T(8,128)(2,1)}, u32[]{:S(2)}) copy-start(bf16[64,144]{1,0:T(8,128)(2,1)} %constant.41.clone.s2) | copy-start | bytes 55300
  29.1 7.9 %copy-start.17 = (bf16[48,192]{1,0:T(8,128)(2,1)S(1)}, bf16[48,192]{1,0:T(8,128)(2,1)}, u32[]{:S(2)}) copy-start(bf16[48,192]{1,0:T(8,128)(2,1)} %constant.40.clone.a2) | copy-start | bytes 55300
  32.1 19.2 %collective-permute-start.12 = (f32[2,128,256]{2,1,0:T(8,128)S(1)}, f32[2,128,256]{2,1,0:T(8,128)S(1)}, u32[]{:S(2)}, u32[]{:S(2)}) collective-permute-start(f32[2,128,256]{2,1,0:T(8,128)S(1)} %get-tuple-element.61), channel_id=1, source_target_pairs={{0,4},{4,8},{8,12},{12,16},{16,20},{20,24},{24,28},{28,0},{1,5},{5... | collective-permute-start | bytes 786440 | tf_op jit(solution)/shard_map/ppermute | solution.py:835
  32.2 19.1 %collective-permute-start.13 = (f32[2,128,256]{2,1,0:T(8,128)S(1)}, f32[2,128,256]{2,1,0:T(8,128)S(1)}, u32[]{:S(2)}, u32[]{:S(2)}) collective-permute-start(f32[2,128,256]{2,1,0:T(8,128)S(1)} %get-tuple-element.62), channel_id=1, source_target_pairs={{4,0},{8,4},{12,8},{16,12},{20,16},{24,20},{28,24},{0,28},{5,1},{9... | collective-permute-start | bytes 786440 | tf_op jit(solution)/shard_map/ppermute | solution.py:840
  40.5 8.3 %copy-start.2 = (bf16[384,256]{1,0:T(8,128)(2,1)S(1)}, bf16[384,256]{1,0:T(8,128)(2,1)}, u32[]{:S(2)}) copy-start(bf16[384,256]{1,0:T(8,128)(2,1)} %constant.43.clone.z) | copy-start | bytes 589828
  40.6 8.3 %copy-start.5 = (bf16[128,240]{1,0:T(8,128)(2,1)S(1)}, bf16[128,240]{1,0:T(8,128)(2,1)}, u32[]{:S(2)}) copy-start(bf16[128,240]{1,0:T(8,128)(2,1)} %constant.44.clone.y) | copy-start | bytes 184324
  40.6 10.7 %collective-permute-start.10 = (f32[344,128]{1,0:T(8,128)S(1)}, f32[344,128]{1,0:T(8,128)S(1)}, u32[]{:S(2)}, u32[]{:S(2)}) collective-permute-start(f32[344,128]{1,0:T(8,128)S(1)} %get-tuple-element.56), channel_id=1, source_target_pairs={{0,4},{4,8},{8,12},{12,16},{16,20},{20,24},{24,28},{28,0},{1,5},{5... | collective-permute-start | bytes 528392 | tf_op jit(solution)/shard_map/ppermute | solution.py:835
  40.6 12.9 %collective-permute-start.11 = (f32[344,128]{1,0:T(8,128)S(1)}, f32[344,128]{1,0:T(8,128)S(1)}, u32[]{:S(2)}, u32[]{:S(2)}) collective-permute-start(f32[344,128]{1,0:T(8,128)S(1)} %get-tuple-element.57), channel_id=1, source_target_pairs={{4,0},{8,4},{12,8},{16,12},{20,16},{24,20},{28,24},{0,28},{5,1},{9... | collective-permute-start | bytes 528392 | tf_op jit(solution)/shard_map/ppermute | solution.py:840

commit v6 on v5

--- a/solution.py
+++ b/solution.py
@@ -316,15 +316,22 @@
     )
 
 
-def own_approx(bands, own, ghost_rows):
-    nx, rows, nz = bands.shape
+def own_approx(zed, y_matrix, own, rows, ghost_rows):
+    nx, ny, nz = zed.shape
     half_z = nz // 2
     n1 = nx // 2
 
-    def kernel(b_ref, approx, up, down):
+    def kernel(zed_ref, y, approx, up, down, low):
+        def y_body(first):
+            planes = [zed_ref[first + i, :, :half_z] for i in range(8)]
+            for i, plane in enumerate(in_pairs(y, planes)):
+                low[first + i] = plane[:rows]
+
+        over_planes(nx, 8, y_body)
+
         def tile(t, carry):
             at = pl.ds(pl.multiple_of(t * 8, 8), 8)
-            values = {i: b_ref[i, at, :half_z] for i in range(nx)}
+            values = {i: low[i, at] for i in range(nx)}
             for k in range(n1):
                 approx[k, at] = added([(c, values[i]) for i, c, _ in x_terms(k, nx) if i in values])
             approx[n1, at] = added([(H[5 + i], values[i]) for i in range(3)])
@@ -333,16 +340,20 @@
             approx[n1 + 3, at] = H[6] * H[0] * values[nx - 1]
             return carry
 
-        lax.fori_loop(0, own // 8, tile, 0)
-        up[...] = approx[:, own - ghost_rows :]
-        down[...] = approx[:, :ghost_rows]
-
-    return whole_call(
-        kernel,
-        [shape(n1 + 4, own, half_z), shape(n1 + 4, ghost_rows, half_z), shape(n1 + 4, ghost_rows, half_z)],
-        [bands],
+        lax.fori_loop(0, rows // 8, tile, 0)
+        inside = ghost_rows - 2
+        up[:, :inside] = approx[:, own - inside : own]
+        up[:, inside:] = approx[:, own + 2 : own + 4]
+        down[:, :2] = approx[:, own : own + 2]
+        down[:, 2:] = approx[:, :inside]
+
+    return whole_call(
+        kernel,
+        [shape(n1 + 4, rows, half_z), shape(n1 + 4, ghost_rows, half_z), shape(n1 + 4, ghost_rows, half_z)],
+        [zed, y_matrix],
         1000,
         1000,
+        scratch=[pltpu.VMEM((nx, rows, half_z), F32)],
         name="own_approx",
     )
 
@@ -389,7 +400,7 @@
                 body(at, pl.ds(bz * half_z, half_z), by, bz)
             return carry
 
-        lax.fori_loop(0, half_tiles, tile, 0)
+        lax.fori_loop(0, half_tiles, tile, 0, unroll=3 if half_tiles % 3 == 0 else 1)
 
 
 def inner_bands(bands, table, index):
@@ -640,11 +651,12 @@
 
 
 def coarse(
-    bands, left, right, halo, h_left, h_right, table, index, za1, yx0, ya1, zs1, za2, zs2, ya2, ys2, ys1, low_rows, out_rows
+    bands, left, right, halo, h_left, h_right, table, index, za1, yx0, ya1, zs1, za2, zs2, ya2, ys2, ys1,
+    in_rows1, low_rows, out_rows,
 ):
     planes_in, rows, nz = bands.shape
     n1 = planes_in - 4
-    in_rows = yx0.shape[0]
+    in_rows = in_rows1
     wide = h_left.shape[1] - 8
     n2, n3 = n1 // 2, n1 // 4
     rows2 = ya2.shape[0]
@@ -847,7 +859,8 @@
     cells0 = list(range(-8, ny + 8))
     rows0 = up_to(y1 + 4, 8)
     ks0 = fill(list(range(y1)) + [-2, -1, y1, y1 + 1], rows0)
-    cells1 = list(range(y1)) + list(range(-ghost, 0)) + list(range(y1, y1 + ghost))
+    cells1 = ks0 + list(range(2 - ghost, 2)) + list(range(y1 - 2, y1 + ghost - 2))
+    once = [c if cells1.index(c) == i else None for i, c in enumerate(cells1)]
     rows1 = up_to(y2 + 18, 8)
     low1 = fill(list(range(-9, y2 + 9)), rows1)
     high1 = fill(list(range(-3, y2 + 3)), up_to(y2 + 6, 8))
@@ -856,7 +869,8 @@
     ys0_matrix = synthesis_rows(list(range(ny)), ks0, ks0)
     ys0 = from_left(ys0_matrix)
     ys0_low = from_left(ys0_matrix[:, :rows0])
-    yx0 = from_left(analysis_rows(list(range(-wide, ny + wide)), cells1, []))
+    yl0 = from_left(analysis_rows(list(range(ny)), ks0, []))
+    yx0 = from_left(analysis_rows(list(range(-wide, ny + wide)), once, []))
     ya1 = from_left(analysis_rows(cells1, low1, high1))
     ys1 = from_left(synthesis_rows(ks0, low1, high1))
     ya2 = from_left(analysis_rows(low1, ks2, ks2))
@@ -874,10 +888,11 @@
     y_left = to_next(y_up, "gy")
     y_right = to_previous(y_down, "gy")
     zed = depth(velocity, za0, 16, "depth_analysis")
-    bands = y_analysis(zed, y_left, y_right, za0, ya0)
-    approx, a_up, a_down = own_approx(bands, y1, ghost)
+    approx, a_up, a_down = own_approx(zed, yl0, y1, rows0, ghost)
     a_left = to_next(a_up, "gy")
     a_right = to_previous(a_down, "gy")
+    zed, a_up = lax.optimization_barrier((zed, a_up))
+    bands = y_analysis(zed, y_left, y_right, za0, ya0)
     inner = inner_bands(bands, table, index)
     x_left, x_right, inner = lax.optimization_barrier((x_left, x_right, inner))
     halo, h_up, h_down = x_halo_messages(x_left, x_right, za0, wide)
@@ -895,7 +910,7 @@
     bands1, edge = lax.optimization_barrier((bands1, edge))
     approx1, s_up, s_down = coarse(
         bands1, b_left, b_right, halo, h_left, h_right, table, index,
-        za1, yx0, ya1, zs1, za2, zs2, ya2, ys2, ys1, rows1, rows0,
+        za1, yx0, ya1, zs1, za2, zs2, ya2, ys2, ys1, len(cells1), rows1, rows0,
     )
     s_left = to_next(s_up, "gx")
     s_right = to_previous(s_down, "gx")

time: 57.3 us -> 56.6 us (0.988)
  Pallas kernels: 25.8 us -> 27.5 us
  waiting for transfers between devices: 4.1 us -> 2.87 us
  starting transfers between devices: 25.6 us -> 24.4 us
    ppermute x7, starting transfers between devices: 22.6 us -> 20.2 us  [to_previous(): return lax.ppermute(array, axis, [((i + 1) % size, i) for i in range(size)])]
    pallas_call x11, Pallas kernels: 20.7 us -> 22.5 us  [whole_call(): pl.pallas_call(kernel, in_specs=specs, out_specs=outs, out_shape=out_shap...]
    ppermute x7, waiting for transfers between devices: 4.08 us -> 2.72 us  [to_previous(): return lax.ppermute(array, axis, [((i + 1) % size, i) for i in range(size)])]
    ppermute x7, starting transfers between devices: 3.01 us -> 4.2 us  [to_next(): return lax.ppermute(array, axis, [(i, (i + 1) % size) for i in range(size)])]
  transfers between devices with their start and end apart: 14 -> 14, of which waited for: 3 -> 3; matrix products, arithmetic and copies ran while one was open for 0% -> 0% of each run, Pallas kernels for 36% -> 40%
where the time goes in v6:
time: 56.6 us; the launch traced here: 56.5 us
  Pallas kernels  27.5 us (49%)
  starting transfers between devices  24.4 us (43%)
  waiting for transfers between devices  2.87 us (5%)
  local copies, waits for them, and re-layouts  1.12 us (2%)
    pallas_call x11, Pallas kernels, whole_call(): pl.pallas_call(kernel, in_specs=specs, out_specs=outs, out_shape=out_shap...  22.5 us
    ppermute x7, starting transfers between devices, to_previous(): return lax.ppermute(array, axis, [((i + 1) % size, i) for i in range(size)])  20.2 us
    ppermute x7, starting transfers between devices, to_next(): return lax.ppermute(array, axis, [(i, (i + 1) % size) for i in range(size)])  4.2 us
    pallas_call x1, Pallas kernels, final(): pl.pallas_call(kernel, in_specs=[VMEM] * 9, out_specs=pl.BlockSpec(memory...  3.49 us
    ppermute x7, waiting for transfers between devices, to_previous(): return lax.ppermute(array, axis, [((i + 1) % size, i) for i in range(size)])  2.72 us
    pallas_call x1, Pallas kernels, first_messages(): pl.pallas_call(kernel, in_specs=[pl.BlockSpec(memory_space=pltpu.HBM)], o...  1.57 us
  transfers between devices with their start and end apart: 14, of which 3 were waited for; matrix products, arithmetic and copies ran while one was open for 0% of the time, Pallas kernels for 40%

profile of v6, /device:TPU:0, one launch (start us, length us, event | category | flops | bytes accessed | tf_op | source)
XLA Modules:
  0.0 56.5 jit_solution(16367393635131103019)
XLA Ops:
  0.0 1.6 %first_messages.1 = (f32[2,128,256]{2,1,0:T(8,128)S(1)}, f32[2,128,256]{2,1,0:T(8,128)S(1)}, f32[28,8,256]{2,1,0:T(8,128)S(1)}, f32[28,8,256]{2,1,0:T(8,128)S(1)}) custom-call(f32[32,128,256]{2,1,0:T(8,128)} %v_ref.3), custom_call_target="tpu_custom_call" | custom-call | flops 1000000 | bytes 3000000 | tf_op jit(solution)/shard_map/first_messages/pallas_call | solution.py:249
  1.6 0.5 collective-permute-start.2
  2.1 2.0 %collective-permute-start.3 = (f32[28,8,256]{2,1,0:T(8,128)S(1)}, f32[28,8,256]{2,1,0:T(8,128)S(1)}, u32[]{:S(2)}, u32[]{:S(2)}) collective-permute-start(f32[28,8,256]{2,1,0:T(8,128)S(1)} %get-tuple-element.40), channel_id=1, source_target_pairs={{1,0},{2,1},{3,2},{0,3},{5,4},{6,5},{7,6},{4,7},{9,8},{10,9},{11,1... | collective-permute-start | bytes 688136 | tf_op jit(solution)/shard_map/ppermute | solution.py:852
  4.1 2.2 %collective-permute-start = (f32[2,128,256]{2,1,0:T(8,128)S(1)}, f32[2,128,256]{2,1,0:T(8,128)S(1)}, u32[]{:S(2)}, u32[]{:S(2)}) collective-permute-start(f32[2,128,256]{2,1,0:T(8,128)S(1)} %get-tuple-element.35), channel_id=1, source_target_pairs={{0,4},{4,8},{8,12},{12,16},{16,20},{20,24},{24,28},{28,0},{1,5},{5... | collective-permute-start | bytes 786440 | tf_op jit(solution)/shard_map/ppermute | solution.py:847
  6.3 3.0 %collective-permute-start.1 = (f32[2,128,256]{2,1,0:T(8,128)S(1)}, f32[2,128,256]{2,1,0:T(8,128)S(1)}, u32[]{:S(2)}, u32[]{:S(2)}) collective-permute-start(f32[2,128,256]{2,1,0:T(8,128)S(1)} %get-tuple-element.36), channel_id=1, source_target_pairs={{4,0},{8,4},{12,8},{16,12},{20,16},{24,20},{28,24},{0,28},{5,1},{9... | collective-permute-start | bytes 786440 | tf_op jit(solution)/shard_map/ppermute | solution.py:852
  9.4 1.0 %copy-done.1 = bf16[768,256]{1,0:T(8,128)(2,1)S(1)} copy-done((bf16[768,256]{1,0:T(8,128)(2,1)S(1)}, bf16[768,256]{1,0:T(8,128)(2,1)}, u32[]{:S(2)}) %copy-start.1) | copy-done | bytes 393240
  10.4 2.0 %depth_analysis.1.zed_ref = f32[32,128,256]{2,1,0:T(8,128)S(1)} custom-call(f32[32,128,256]{2,1,0:T(8,128)S(1)} %copy-done, bf16[768,256]{1,0:T(8,128)(2,1)S(1)} %copy-done.1), custom_call_target="tpu_custom_call" | custom-call | flops 1610612736 | bytes 8388608 | tf_op jit(solution)/shard_map/depth_analysis/pallas_call | solution.py:197
  12.4 0.0 copy-start.4
  12.4 1.5 %own_approx.1 = (f32[20,72,128]{2,1,0:T(8,128)S(1)}, f32[20,24,128]{2,1,0:T(8,128)S(1)}, f32[20,24,128]{2,1,0:T(8,128)S(1)}) custom-call(f32[32,128,256]{2,1,0:T(8,128)S(1)} %depth_analysis.1.zed_ref, bf16[80,384]{1,0:T(8,128)(2,1)S(1)} %copy-done.12), custom_call_target="tpu_custom_call" | custom-call | flops 1000 | bytes 1000 | tf_op jit(solution)/shard_map/own_approx/pallas_call | solution.py:197
  13.9 0.1 collective-permute-start.7
  13.9 0.0 collective-permute-done.2.left
  13.9 0.0 copy-start.13
  13.9 0.0 copy-start.14
  14.0 0.5 collective-permute-start.6
  14.4 2.4 %y_analysis.1.b_ref = f32[32,144,256]{2,1,0:T(8,128)S(1)} custom-call(f32[32,128,256]{2,1,0:T(8,128)S(1)} %depth_analysis.1.zed_ref, f32[28,8,256]{2,1,0:T(8,128)S(1)} %collective-permute-done.2.left, f32[28,8,256]{2,1,0:T(8,128)S(1)} %collective-permute-done.3.right, bf16[768,256]{1,0:T(8,128)(2,1)S(1)} %copy-done.1, bf16[144,432]{1,0:T(8,128)(2,1)S(1)} %copy-done.4), custom_call_target="tpu_custom_call" | custom-call | flops 1000 | bytes 1000 | tf_op jit(solution)/shard_map/y_analysis/pallas_call | solution.py:197
  16.8 0.0 copy-start.2
  16.9 0.0 copy-start.9
  16.9 0.0 copy-start.10
  16.9 2.1 %inner_bands.1.c_ref = f32[24,144,256]{2,1,0:T(8,128)S(1)} custom-call(f32[16]{0:T(128)S(1)} %copy-done.14, s32[3,7]{1,0:T(4,128)S(1)} %copy-done.13, f32[32,144,256]{2,1,0:T(8,128)S(1)} %y_analysis.1.b_ref), custom_call_target="tpu_custom_call" | custom-call | flops 35389440 | bytes 9437184 | tf_op jit(solution)/shard_map/inner_bands/pallas_call | solution.py:197
  19.0 0.8 %collective-permute-done.1.xr = f32[2,128,256]{2,1,0:T(8,128)S(1)} collective-permute-done((f32[2,128,256]{2,1,0:T(8,128)S(1)}, f32[2,128,256]{2,1,0:T(8,128)S(1)}, u32[]{:S(2)}, u32[]{:S(2)}) %collective-permute-start.1) | collective-permute-done | bytes 262176 | tf_op jit(solution)/shard_map/ppermute | solution.py:852
  19.8 0.4 x_halo_messages.1
  20.1 0.0 copy-start.5
  20.2 0.0 copy-start.7
  20.2 0.7 %collective-permute-start.4 = (f32[4,56,128]{2,1,0:T(8,128)S(1)}, f32[4,56,128]{2,1,0:T(8,128)S(1)}, u32[]{:S(2)}, u32[]{:S(2)}) collective-permute-start(f32[4,56,128]{2,1,0:T(8,128)S(1)} %get-tuple-element.43), channel_id=1, source_target_pairs={{0,1},{1,2},{2,3},{3,0},{4,5},{5,6},{6,7},{7,4},{8,9},{9,10},{10,1... | collective-permute-start | bytes 344072 | tf_op jit(solution)/shard_map/ppermute | solution.py:847
  20.8 1.1 %collective-permute-start.5 = (f32[4,56,128]{2,1,0:T(8,128)S(1)}, f32[4,56,128]{2,1,0:T(8,128)S(1)}, u32[]{:S(2)}, u32[]{:S(2)}) collective-permute-start(f32[4,56,128]{2,1,0:T(8,128)S(1)} %get-tuple-element.44), channel_id=1, source_target_pairs={{1,0},{2,1},{3,2},{0,3},{5,4},{6,5},{7,6},{4,7},{9,8},{10,9},{11,1... | collective-permute-start | bytes 344072 | tf_op jit(solution)/shard_map/ppermute | solution.py:852
  22.0 0.1 collective-permute-done.6.l_ref
  22.1 1.8 %second_bands.1 = (f32[20,96,128]{2,1,0:T(8,128)S(1)}, f32[248,128]{1,0:T(8,128)S(1)}, f32[248,128]{1,0:T(8,128)S(1)}) custom-call(f32[20,72,128]{2,1,0:T(8,128)S(1)} %get-tuple-element.47.o_ref, f32[20,24,128]{2,1,0:T(8,128)S(1)} %collective-permute-done.6.l_ref, f32[20,24,128]{2,1,0:T(8,128)S(1)} %collective-permute-done.7.r_ref, ...), custom_call_target="tpu_custom_call" | custom-call | flops 330301440 | bytes 1769472 | tf_op jit(solution)/shard_map/second_bands/pallas_call | solution.py:197
  23.9 0.2 collective-permute-start.8
  24.1 4.6 %collective-permute-start.9 = (f32[248,128]{1,0:T(8,128)S(1)}, f32[248,128]{1,0:T(8,128)S(1)}, u32[]{:S(2)}, u32[]{:S(2)}) collective-permute-start(f32[248,128]{1,0:T(8,128)S(1)} %get-tuple-element.57), channel_id=1, source_target_pairs={{4,0},{8,4},{12,8},{16,12},{20,16},{24,20},{28,24},{0,28},{5,1},{9... | collective-permute-start | bytes 380936 | tf_op jit(solution)/shard_map/ppermute | solution.py:852
  28.7 0.0 copy-start.11
  28.7 0.0 copy-start.15
  28.7 0.0 copy-start.16
  28.7 0.0 copy-start.17
  28.8 0.0 copy-start.18
  28.8 0.0 copy-start.19
  28.8 1.6 %edge_bands.1.c_ref = f32[8,144,256]{2,1,0:T(8,128)S(1)} custom-call(f32[16]{0:T(128)S(1)} %copy-done.14, s32[3,7]{1,0:T(4,128)S(1)} %copy-done.13, f32[32,144,256]{2,1,0:T(8,128)S(1)} %y_analysis.1.b_ref, f32[4,128,256]{2,1,0:T(8,128)S(1)} %get-tuple-element.51.x_ref, f32[4,56,128]{2,1,0:T(8,128)S(1)} %collective-permute-done.4.hl, ...), custom_call_target="tpu_custom_call" | custom-call | flops 23592960 | bytes 4718592 | tf_op jit(solution)/shard_map/edge_bands/pallas_call | solution.py:197
  30.4 1.4 %detail_edges.1 = (f32[8,128,256]{2,1,0:T(8,128)S(1)}, f32[2,128,256]{2,1,0:T(8,128)S(1)}, f32[2,128,256]{2,1,0:T(8,128)S(1)}) custom-call(f32[8,144,256]{2,1,0:T(8,128)S(1)} %edge_bands.1.c_ref, bf16[768,256]{1,0:T(8,128)(2,1)S(1)} %copy-done.5, bf16[128,432]{1,0:T(8,128)(2,1)S(1)} %copy-done.7), custom_call_target="tpu_custom_call" | custom-call | flops 679477248 | bytes 2228224 | tf_op jit(solution)/shard_map/detail_edges/pallas_call | solution.py:197
  31.7 0.1 collective-permute-start.12
  31.8 4.7 %collective-permute-start.13 = (f32[2,128,256]{2,1,0:T(8,128)S(1)}, f32[2,128,256]{2,1,0:T(8,128)S(1)}, u32[]{:S(2)}, u32[]{:S(2)}) collective-permute-start(f32[2,128,256]{2,1,0:T(8,128)S(1)} %get-tuple-element.64), channel_id=1, source_target_pairs={{4,0},{8,4},{12,8},{16,12},{20,16},{24,20},{28,24},{0,28},{5,1},{9... | collective-permute-start | bytes 786440 | tf_op jit(solution)/shard_map/ppermute | solution.py:852
  36.6 3.5 %coarse.1 = (f32[20,72,128]{2,1,0:T(8,128)S(1)}, f32[344,128]{1,0:T(8,128)S(1)}, f32[344,128]{1,0:T(8,128)S(1)}) custom-call(f32[16]{0:T(128)S(1)} %copy-done.14, s32[3,7]{1,0:T(4,128)S(1)} %copy-done.13, f32[20,96,128]{2,1,0:T(8,128)S(1)} %get-tuple-element.55.b_ref, f32[248,128]{1,0:T(8,128)S(1)} %collective-permute-done.8.l_ref, ...), custom_call_target="tpu_custom_call" | custom-call | flops 1500000000 | bytes 1572864 | tf_op jit(solution)/shard_map/coarse/pallas_call | solution.py:197
  40.1 0.0 copy-start.3
  40.1 0.0 copy-start.6
  40.1 0.1 collective-permute-start.10
  40.2 4.7 %collective-permute-start.11 = (f32[344,128]{1,0:T(8,128)S(1)}, f32[344,128]{1,0:T(8,128)S(1)}, u32[]{:S(2)}, u32[]{:S(2)}) collective-permute-start(f32[344,128]{1,0:T(8,128)S(1)} %get-tuple-element.59), channel_id=1, source_target_pairs={{4,0},{8,4},{12,8},{16,12},{20,16},{24,20},{28,24},{0,28},{5,1},{9... | collective-permute-start | bytes 528392 | tf_op jit(solution)/shard_map/ppermute | solution.py:852
  44.9 3.5 %inner_yz.1.r_ref = f32[24,128,256]{2,1,0:T(8,128)S(1)} custom-call(f32[24,144,256]{2,1,0:T(8,128)S(1)} %inner_bands.1.c_ref, f32[20,72,128]{2,1,0:T(8,128)S(1)} %get-tuple-element.62.a_ref, bf16[768,256]{1,0:T(8,128)(2,1)S(1)} %copy-done.5, bf16[128,432]{1,0:T(8,128)(2,1)S(1)} %copy-done.7), custom_call_target="tpu_custom_call" | custom-call | flops 2038431744 | bytes 6684672 | tf_op jit(solution)/shard_map/inner_yz/pallas_call | solution.py:197
  48.4 2.5 %own_result.1.d_ref = f32[32,128,256]{2,1,0:T(8,128)S(1)} custom-call(f32[8,128,256]{2,1,0:T(8,128)S(1)} %get-tuple-element.60.e_ref, f32[24,128,256]{2,1,0:T(8,128)S(1)} %inner_yz.1.r_ref, f32[20,72,128]{2,1,0:T(8,128)S(1)} %get-tuple-element.62.a_ref, bf16[384,256]{1,0:T(8,128)(2,1)S(1)} %copy-done.3, bf16[128,240]{1,0:T(8,128)(2,1)S(1)} %copy-done.6), custom_call_target="tpu_custom_call" | custom-call | flops 16777216 | bytes 8388608 | tf_op jit(solution)/shard_map/own_result/pallas_call | solution.py:197
  50.9 1.9 %collective-permute-done.11.r_ref = f32[344,128]{1,0:T(8,128)S(1)} collective-permute-done((f32[344,128]{1,0:T(8,128)S(1)}, f32[344,128]{1,0:T(8,128)S(1)}, u32[]{:S(2)}, u32[]{:S(2)}) %collective-permute-start.11) | collective-permute-done | bytes 176160 | tf_op jit(solution)/shard_map/ppermute | solution.py:852
  52.8 3.5 %final.1 = f32[32,128,256]{2,1,0:T(8,128)} custom-call(f32[344,128]{1,0:T(8,128)S(1)} %collective-permute-done.10.l_ref, f32[344,128]{1,0:T(8,128)S(1)} %collective-permute-done.11.r_ref, f32[32,128,256]{2,1,0:T(8,128)S(1)} %own_result.1.d_ref, f32[2,128,256]{2,1,0:T(8,128)S(1)} %collective-permute-done.12.el, ...), custom_call_target="tpu_custom_call" | custom-call | flops 8388608 | bytes 8388608 | tf_op jit(solution)/shard_map/final/pallas_call | solution.py:829
  (33 shorter events, 0.1 us)
Async XLA Ops:
  0.0 9.4 %copy-start = (f32[32,128,256]{2,1,0:T(8,128)S(1)}, f32[32,128,256]{2,1,0:T(8,128)}, u32[]{:S(2)}) copy-start(f32[32,128,256]{2,1,0:T(8,128)} %v_ref.3) | copy-start | bytes 12582916
  1.6 12.3 %collective-permute-start.2 = (f32[28,8,256]{2,1,0:T(8,128)S(1)}, f32[28,8,256]{2,1,0:T(8,128)S(1)}, u32[]{:S(2)}, u32[]{:S(2)}) collective-permute-start(f32[28,8,256]{2,1,0:T(8,128)S(1)} %get-tuple-element.39), channel_id=1, source_target_pairs={{0,1},{1,2},{2,3},{3,0},{4,5},{5,6},{6,7},{7,4},{8,9},{9,10},{10,1... | collective-permute-start | bytes 688136 | tf_op jit(solution)/shard_map/ppermute | solution.py:847
  2.1 12.3 %collective-permute-start.3 = (f32[28,8,256]{2,1,0:T(8,128)S(1)}, f32[28,8,256]{2,1,0:T(8,128)S(1)}, u32[]{:S(2)}, u32[]{:S(2)}) collective-permute-start(f32[28,8,256]{2,1,0:T(8,128)S(1)} %get-tuple-element.40), channel_id=1, source_target_pairs={{1,0},{2,1},{3,2},{0,3},{5,4},{6,5},{7,6},{4,7},{9,8},{10,9},{11,1... | collective-permute-start | bytes 688136 | tf_op jit(solution)/shard_map/ppermute | solution.py:852
  4.1 14.8 %collective-permute-start = (f32[2,128,256]{2,1,0:T(8,128)S(1)}, f32[2,128,256]{2,1,0:T(8,128)S(1)}, u32[]{:S(2)}, u32[]{:S(2)}) collective-permute-start(f32[2,128,256]{2,1,0:T(8,128)S(1)} %get-tuple-element.35), channel_id=1, source_target_pairs={{0,4},{4,8},{8,12},{12,16},{16,20},{20,24},{24,28},{28,0},{1,5},{5... | collective-permute-start | bytes 786440 | tf_op jit(solution)/shard_map/ppermute | solution.py:847
  6.3 13.4 %collective-permute-start.1 = (f32[2,128,256]{2,1,0:T(8,128)S(1)}, f32[2,128,256]{2,1,0:T(8,128)S(1)}, u32[]{:S(2)}, u32[]{:S(2)}) collective-permute-start(f32[2,128,256]{2,1,0:T(8,128)S(1)} %get-tuple-element.36), channel_id=1, source_target_pairs={{4,0},{8,4},{12,8},{16,12},{20,16},{24,20},{28,24},{0,28},{5,1},{9... | collective-permute-start | bytes 786440 | tf_op jit(solution)/shard_map/ppermute | solution.py:852
  9.4 1.0 %copy-start.1 = (bf16[768,256]{1,0:T(8,128)(2,1)S(1)}, bf16[768,256]{1,0:T(8,128)(2,1)}, u32[]{:S(2)}) copy-start(bf16[768,256]{1,0:T(8,128)(2,1)} %constant.32.clone.z) | copy-start | bytes 1179652
  10.4 2.0 %copy-start.12 = (bf16[80,384]{1,0:T(8,128)(2,1)S(1)}, bf16[80,384]{1,0:T(8,128)(2,1)}, u32[]{:S(2)}) copy-start(bf16[80,384]{1,0:T(8,128)(2,1)} %constant.33.clone.y) | copy-start | bytes 184324
  12.4 2.1 %copy-start.4 = (bf16[144,432]{1,0:T(8,128)(2,1)S(1)}, bf16[144,432]{1,0:T(8,128)(2,1)}, u32[]{:S(2)}) copy-start(bf16[144,432]{1,0:T(8,128)(2,1)} %constant.34.clone.y) | copy-start | bytes 373252
  13.9 8.1 %collective-permute-start.7 = (f32[20,24,128]{2,1,0:T(8,128)S(1)}, f32[20,24,128]{2,1,0:T(8,128)S(1)}, u32[]{:S(2)}, u32[]{:S(2)}) collective-permute-start(f32[20,24,128]{2,1,0:T(8,128)S(1)} %get-tuple-element.48), channel_id=1, source_target_pairs={{1,0},{2,1},{3,2},{0,3},{5,4},{6,5},{7,6},{4,7},{9,8},{10,9},{11,1... | collective-permute-start | bytes 737288 | tf_op jit(solution)/shard_map/ppermute | solution.py:852
  13.9 2.9 %copy-start.13 = (s32[3,7]{1,0:T(4,128)S(1)}, s32[3,7]{1,0:T(4,128)}, u32[]{:S(2)}) copy-start(s32[3,7]{1,0:T(4,128)} %index_ref.5) | copy-start | bytes 256
  13.9 2.9 %copy-start.14 = (f32[16]{0:T(128)S(1)}, f32[16]{0:T(128)}, u32[]{:S(2)}) copy-start(f32[16]{0:T(128)} %table_ref.5) | copy-start | bytes 196
  14.0 8.1 %collective-permute-start.6 = (f32[20,24,128]{2,1,0:T(8,128)S(1)}, f32[20,24,128]{2,1,0:T(8,128)S(1)}, u32[]{:S(2)}, u32[]{:S(2)}) collective-permute-start(f32[20,24,128]{2,1,0:T(8,128)S(1)} %get-tuple-element.37), channel_id=1, source_target_pairs={{0,1},{1,2},{2,3},{3,0},{4,5},{5,6},{6,7},{7,4},{8,9},{9,10},{10,1... | collective-permute-start | bytes 737288 | tf_op jit(solution)/shard_map/ppermute | solution.py:847
  16.8 2.9 %copy-start.2 = (bf16[768,256]{1,0:T(8,128)(2,1)S(1)}, bf16[768,256]{1,0:T(8,128)(2,1)}, u32[]{:S(2)}) copy-start(bf16[768,256]{1,0:T(8,128)(2,1)} %constant.32.clone.z) | copy-start | bytes 1179652
  16.9 5.2 %copy-start.9 = (bf16[384,128]{1,0:T(8,128)(2,1)S(1)}, bf16[384,128]{1,0:T(8,128)(2,1)}, u32[]{:S(2)}) copy-start(bf16[384,128]{1,0:T(8,128)(2,1)} %constant.35.clone.z.z1a) | copy-start | bytes 294916
  16.9 5.2 %copy-start.10 = (bf16[96,384]{1,0:T(8,128)(2,1)S(1)}, bf16[96,384]{1,0:T(8,128)(2,1)}, u32[]{:S(2)}) copy-start(bf16[96,384]{1,0:T(8,128)(2,1)} %constant.36.clone.y.a1) | copy-start | bytes 221188
  20.1 10.2 %copy-start.5 = (bf16[768,256]{1,0:T(8,128)(2,1)S(1)}, bf16[768,256]{1,0:T(8,128)(2,1)}, u32[]{:S(2)}) copy-start(bf16[768,256]{1,0:T(8,128)(2,1)} %constant.37.clone.z) | copy-start | bytes 1179652
  20.2 10.2 %copy-start.7 = (bf16[128,432]{1,0:T(8,128)(2,1)S(1)}, bf16[128,432]{1,0:T(8,128)(2,1)}, u32[]{:S(2)}) copy-start(bf16[128,432]{1,0:T(8,128)(2,1)} %constant.38.clone.y) | copy-start | bytes 331780
  20.2 8.5 %collective-permute-start.4 = (f32[4,56,128]{2,1,0:T(8,128)S(1)}, f32[4,56,128]{2,1,0:T(8,128)S(1)}, u32[]{:S(2)}, u32[]{:S(2)}) collective-permute-start(f32[4,56,128]{2,1,0:T(8,128)S(1)} %get-tuple-element.43), channel_id=1, source_target_pairs={{0,1},{1,2},{2,3},{3,0},{4,5},{5,6},{6,7},{7,4},{8,9},{9,10},{10,1... | collective-permute-start | bytes 344072 | tf_op jit(solution)/shard_map/ppermute | solution.py:847
  20.8 7.9 %collective-permute-start.5 = (f32[4,56,128]{2,1,0:T(8,128)S(1)}, f32[4,56,128]{2,1,0:T(8,128)S(1)}, u32[]{:S(2)}, u32[]{:S(2)}) collective-permute-start(f32[4,56,128]{2,1,0:T(8,128)S(1)} %get-tuple-element.44), channel_id=1, source_target_pairs={{1,0},{2,1},{3,2},{0,3},{5,4},{6,5},{7,6},{4,7},{9,8},{10,9},{11,1... | collective-permute-start | bytes 344072 | tf_op jit(solution)/shard_map/ppermute | solution.py:852
  23.9 12.6 %collective-permute-start.8 = (f32[248,128]{1,0:T(8,128)S(1)}, f32[248,128]{1,0:T(8,128)S(1)}, u32[]{:S(2)}, u32[]{:S(2)}) collective-permute-start(f32[248,128]{1,0:T(8,128)S(1)} %get-tuple-element.56), channel_id=1, source_target_pairs={{0,4},{4,8},{8,12},{12,16},{16,20},{20,24},{24,28},{28,0},{1,5},{5... | collective-permute-start | bytes 380936 | tf_op jit(solution)/shard_map/ppermute | solution.py:847
  24.1 12.4 %collective-permute-start.9 = (f32[248,128]{1,0:T(8,128)S(1)}, f32[248,128]{1,0:T(8,128)S(1)}, u32[]{:S(2)}, u32[]{:S(2)}) collective-permute-start(f32[248,128]{1,0:T(8,128)S(1)} %get-tuple-element.57), channel_id=1, source_target_pairs={{4,0},{8,4},{12,8},{16,12},{20,16},{24,20},{28,24},{0,28},{5,1},{9... | collective-permute-start | bytes 380936 | tf_op jit(solution)/shard_map/ppermute | solution.py:852
  28.7 7.8 %copy-start.8 = (bf16[384,128]{1,0:T(8,128)(2,1)S(1)}, bf16[384,128]{1,0:T(8,128)(2,1)}, u32[]{:S(2)}) copy-start(bf16[384,128]{1,0:T(8,128)(2,1)} %constant.40.clone.z1) | copy-start | bytes 294916
  28.7 7.8 %copy-start.11 = (bf16[80,288]{1,0:T(8,128)(2,1)S(1)}, bf16[80,288]{1,0:T(8,128)(2,1)}, u32[]{:S(2)}) copy-start(bf16[80,288]{1,0:T(8,128)(2,1)} %constant.45.clone.s1) | copy-start | bytes 138244
  28.7 7.8 %copy-start.15 = (bf16[128,672]{1,0:T(8,128)(2,1)S(1)}, bf16[128,672]{1,0:T(8,128)(2,1)}, u32[]{:S(2)}) copy-start(bf16[128,672]{1,0:T(8,128)(2,1)} %constant.39.clone.yx) | copy-start | bytes 516100
  28.7 7.8 %copy-start.16 = (bf16[384,128]{1,0:T(8,128)(2,1)S(1)}, bf16[384,128]{1,0:T(8,128)(2,1)}, u32[]{:S(2)}) copy-start(bf16[384,128]{1,0:T(8,128)(2,1)} %constant.42.clone.z2s) | copy-start | bytes 294916
  28.7 7.8 %copy-start.17 = (bf16[384,128]{1,0:T(8,128)(2,1)S(1)}, bf16[384,128]{1,0:T(8,128)(2,1)}, u32[]{:S(2)}) copy-start(bf16[384,128]{1,0:T(8,128)(2,1)} %constant.41.clone.z2a) | copy-start | bytes 294916
  28.8 7.8 %copy-start.18 = (bf16[64,144]{1,0:T(8,128)(2,1)S(1)}, bf16[64,144]{1,0:T(8,128)(2,1)}, u32[]{:S(2)}) copy-start(bf16[64,144]{1,0:T(8,128)(2,1)} %constant.44.clone.s2) | copy-start | bytes 55300
  28.8 7.8 %copy-start.19 = (bf16[48,192]{1,0:T(8,128)(2,1)S(1)}, bf16[48,192]{1,0:T(8,128)(2,1)}, u32[]{:S(2)}) copy-start(bf16[48,192]{1,0:T(8,128)(2,1)} %constant.43.clone.a2) | copy-start | bytes 55300
  31.7 21.1 %collective-permute-start.12 = (f32[2,128,256]{2,1,0:T(8,128)S(1)}, f32[2,128,256]{2,1,0:T(8,128)S(1)}, u32[]{:S(2)}, u32[]{:S(2)}) collective-permute-start(f32[2,128,256]{2,1,0:T(8,128)S(1)} %get-tuple-element.63), channel_id=1, source_target_pairs={{0,4},{4,8},{8,12},{12,16},{16,20},{20,24},{24,28},{28,0},{1,5},{5... | collective-permute-start | bytes 786440 | tf_op jit(solution)/shard_map/ppermute | solution.py:847
  31.8 21.0 %collective-permute-start.13 = (f32[2,128,256]{2,1,0:T(8,128)S(1)}, f32[2,128,256]{2,1,0:T(8,128)S(1)}, u32[]{:S(2)}, u32[]{:S(2)}) collective-permute-start(f32[2,128,256]{2,1,0:T(8,128)S(1)} %get-tuple-element.64), channel_id=1, source_target_pairs={{4,0},{8,4},{12,8},{16,12},{20,16},{24,20},{28,24},{0,28},{5,1},{9... | collective-permute-start | bytes 786440 | tf_op jit(solution)/shard_map/ppermute | solution.py:852
  40.1 8.3 %copy-start.3 = (bf16[384,256]{1,0:T(8,128)(2,1)S(1)}, bf16[384,256]{1,0:T(8,128)(2,1)}, u32[]{:S(2)}) copy-start(bf16[384,256]{1,0:T(8,128)(2,1)} %constant.46.clone.z) | copy-start | bytes 589828
  40.1 8.3 %copy-start.6 = (bf16[128,240]{1,0:T(8,128)(2,1)S(1)}, bf16[128,240]{1,0:T(8,128)(2,1)}, u32[]{:S(2)}) copy-start(bf16[128,240]{1,0:T(8,128)(2,1)} %constant.47.clone.y) | copy-start | bytes 184324
  40.1 10.8 %collective-permute-start.10 = (f32[344,128]{1,0:T(8,128)S(1)}, f32[344,128]{1,0:T(8,128)S(1)}, u32[]{:S(2)}, u32[]{:S(2)}) collective-permute-start(f32[344,128]{1,0:T(8,128)S(1)} %get-tuple-element.58), channel_id=1, source_target_pairs={{0,4},{4,8},{8,12},{12,16},{16,20},{20,24},{24,28},{28,0},{1,5},{5... | collective-permute-start | bytes 528392 | tf_op jit(solution)/shard_map/ppermute | solution.py:847
  40.2 12.6 %collective-permute-start.11 = (f32[344,128]{1,0:T(8,128)S(1)}, f32[344,128]{1,0:T(8,128)S(1)}, u32[]{:S(2)}, u32[]{:S(2)}) collective-permute-start(f32[344,128]{1,0:T(8,128)S(1)} %get-tuple-element.59), channel_id=1, source_target_pairs={{4,0},{8,4},{12,8},{16,12},{20,16},{24,20},{28,24},{0,28},{5,1},{9... | collective-permute-start | bytes 528392 | tf_op jit(solution)/shard_map/ppermute | solution.py:852

commit v7 on v6

--- a/solution.py
+++ b/solution.py
@@ -77,6 +77,22 @@
     return pieces(matrix, 0)
 
 
+def wide_right(matrix):
+    rows, cols = matrix.shape
+    both = pieces(matrix, 0)
+    high, low = both[:rows], both[2 * rows :]
+    return np.block([[high, low], [high, np.zeros_like(low)]])
+
+
+def tall_left(matrix):
+    return np.ascontiguousarray(wide_right(np.ascontiguousarray(padded_to_tiles(matrix).T)).T)
+
+
+def padded_to_tiles(matrix):
+    rows, cols = matrix.shape
+    return np.pad(matrix, ((0, up_to(rows, 16) - rows), (0, up_to(cols, 16) - cols)))
+
+
 def halves(values):
     high = values.astype(BF16)
     return high, (values - high.astype(F32)).astype(BF16)
@@ -93,6 +109,19 @@
         values = jnp.concatenate([values, jnp.zeros((missing, values.shape[1]), F32)], axis=0)
     high, low = halves(values)
     return jnp.dot(matrix[...], jnp.concatenate([high, low, high], axis=0), preferred_element_type=F32)
+
+
+def times_wide(values, matrix):
+    both = jnp.dot(jnp.concatenate(halves(values), axis=1), matrix[...], preferred_element_type=F32)
+    return both[:, : both.shape[1] // 2] + both[:, both.shape[1] // 2 :]
+
+
+def left_times_tall(matrix, values):
+    missing = matrix.shape[1] // 2 - values.shape[0]
+    if missing:
+        values = jnp.concatenate([values, jnp.zeros((missing, values.shape[1]), F32)], axis=0)
+    both = jnp.dot(matrix[...], jnp.concatenate(halves(values), axis=0), preferred_element_type=F32)
+    return both[: both.shape[0] // 2] + both[both.shape[0] // 2 :]
 
 
 def added(terms):
@@ -201,7 +230,7 @@
         out_shape=out_shapes,
         scratch_shapes=list(scratch),
         name=name,
-        cost_estimate=pl.CostEstimate(flops=int(flops), bytes_accessed=int(moved), transcendentals=0),
+        cost_estimate=pl.CostEstimate(flops=1000, bytes_accessed=1000, transcendentals=0),
         compiler_params=pltpu.CompilerParams(vmem_limit_bytes=VMEM_BYTES),
     )(*args)
 
@@ -427,18 +456,32 @@
     )
 
 
-def edge_bands(bands, halo, h_left, h_right, table, index, y_matrix):
+def yz_synthesis(planes, z, y, out, zed):
+    count, rows, nz = zed.shape
+    group = max(g for g in range(1, 13) if count % g == 0)
+    for first in range(0, count, group):
+        zed[first : first + group] = times(planes(first, group), z).reshape(group, rows, nz)
+
+    def y_body(first):
+        for j in range(4):
+            out[first + j] = left_times(y, zed[first + j])
+
+    over_planes(count, 4, y_body)
+
+
+def edge_details(bands, halo, h_left, h_right, table, index, ya_matrix, z_matrix, y_matrix):
     nx, rows, nz = bands.shape
+    ny = y_matrix.shape[0]
     n1 = nx // 2
     half_z = nz // 2
     wide = h_left.shape[1] - 8
     ends = edges_of(n1)
 
-    def kernel(table_ref, index_ref, b_ref, x_ref, hl, hr, y, out, h_ref):
+    def kernel(table_ref, index_ref, b_ref, x_ref, hl, hr, ya, z, y, out, up, down, h_ref, coeffs, zed):
         for i in range(4):
             low = jnp.concatenate([hl[i, wide - 8 : wide], x_ref[i, :, :half_z], hr[i, :8]], axis=0)
             high = jnp.concatenate([hl[i, wide:], x_ref[i, :, half_z:], hr[i, wide:]], axis=0)
-            h_ref[i] = left_times(y, jnp.concatenate([low, high], axis=1))
+            h_ref[i] = left_times(ya, jnp.concatenate([low, high], axis=1))
         place = {"l1": 0, "l2": 1, "r1": 2, "r2": 3}
 
         def body(at, lanes, by, bz):
@@ -447,53 +490,23 @@
             values.update({i: b_ref[i, at, lanes] for i in [*range(7), *range(nx - 7, nx)]})
             for i, k in enumerate(ends):
                 low, high = x_low(values.get, k, nx), x_high(values.get, k, nx)
-                out[i, at, lanes] = shrink(low, quiet) if by + bz else jnp.zeros_like(low)
-                out[4 + i, at, lanes] = shrink(high, loud)
+                coeffs[i, at, lanes] = shrink(low, quiet) if by + bz else jnp.zeros_like(low)
+                coeffs[4 + i, at, lanes] = shrink(high, loud)
 
         over_tiles(rows, nz, body)
-
-    return whole_call(
-        kernel,
-        shape(8, rows, nz),
-        [table, index, bands, halo, h_left, h_right, y_matrix],
-        20 * nx * rows * nz,
-        4 * nx * rows * nz,
-        scratch=[pltpu.VMEM((4, rows, nz), F32)],
-        name="edge_bands",
-    )
-
-
-def yz_synthesis(planes, z, y, out, zed):
-    count, rows, nz = zed.shape
-    group = max(g for g in range(1, 13) if count % g == 0)
-    for first in range(0, count, group):
-        zed[first : first + group] = times(planes(first, group), z).reshape(group, rows, nz)
-
-    def y_body(first):
-        for j in range(4):
-            out[first + j] = left_times(y, zed[first + j])
-
-    over_planes(count, 4, y_body)
-
-
-def detail_edges(coeffs, z_matrix, y_matrix):
-    count, rows, nz = coeffs.shape
-    ny = y_matrix.shape[0]
-
-    def kernel(c_ref, z, y, out, up, down, zed):
-        yz_synthesis(lambda first, n: c_ref[first : first + n].reshape(n * rows, nz), z, y, out, zed)
+        yz_synthesis(lambda first, n: coeffs[first : first + n].reshape(n * rows, nz), z, y, out, zed)
         part = lambda ks, at: {k: out[i] for k, i in zip(ks, at)}
         up[0], up[1] = spill_up(part((0, 1), (2, 3)), part((0, 1), (6, 7)), 2)
         down[0], down[1] = spill_down(part((0, 1), (0, 1)), part((0, 1), (4, 5)))
 
     return whole_call(
         kernel,
-        [shape(count, ny, nz), shape(2, ny, nz), shape(2, ny, nz)],
-        [coeffs, z_matrix, y_matrix],
-        6 * count * rows * nz * (nz + ny),
-        4 * count * nz * (rows + ny),
-        scratch=[pltpu.VMEM((count, rows, nz), F32)],
-        name="detail_edges",
+        [shape(8, ny, nz), shape(2, ny, nz), shape(2, ny, nz)],
+        [table, index, bands, halo, h_left, h_right, ya_matrix, z_matrix, y_matrix],
+        48 * rows * nz * (nz + ny),
+        4 * nx * rows * nz,
+        scratch=[pltpu.VMEM((4, rows, nz), F32)] + [pltpu.VMEM((8, rows, nz), F32)] * 2,
+        name="edge_details",
     )
 
 
@@ -610,7 +623,7 @@
     def kernel(o_ref, l_ref, r_ref, z, y, out, up, down):
         for i in range(0, planes, 10):
             stack = [part[j] for j in range(i, i + 10) for part in (o_ref, l_ref, r_ref)]
-            zed = times(jnp.concatenate(stack, axis=0), z)
+            zed = times_wide(jnp.concatenate(stack, axis=0), z)
             for j, plane in enumerate(in_pairs(y, cut(zed, in_rows))):
                 out[i + j] = plane
         low = lambda c: out[c, :low_rows]
@@ -652,7 +665,7 @@
 
 def coarse(
     bands, left, right, halo, h_left, h_right, table, index, za1, yx0, ya1, zs1, za2, zs2, ya2, ys2, ys1,
-    in_rows1, low_rows, out_rows,
+    in_rows1, low_rows, out_rows, own_rows, spill_at, spill_rows,
 ):
     planes_in, rows, nz = bands.shape
     n1 = planes_in - 4
@@ -668,7 +681,7 @@
     ):
         halo_planes = [jnp.concatenate([hl[i, :wide], x_ref[i, :, :nz], hr[i, :wide]], axis=0) for i in range(4)]
         halo_planes = jnp.concatenate([plane[:in_rows] for plane in in_pairs(yx, halo_planes)], axis=0)
-        hl1, hl2, hr1, hr2 = in_pairs(a1, cut(times(halo_planes, z1a), in_rows))
+        hl1, hl2, hr1, hr2 = in_pairs(a1, cut(times_wide(halo_planes, z1a), in_rows))
         values = {k: b_ref[k] for k in range(2, n1 - 2)}
         values[0] = b_ref[0] + (hl2 + H[2] * hl1)
         values[1] = b_ref[1] + H[0] * hl1
@@ -701,7 +714,7 @@
         planes.append(first + added([(H[3], xr1), (H[4] / H[6], xr2)] + own))
         own = [((H[6] * H[2] + H[7] * H[0]) / H[6], xr2), (H[6] * H[1], xr1), (H[6] * H[0], low_part(n1 - 1))]
         planes.append(second + added(own))
-        third = in_pairs(a2, cut(times(jnp.concatenate(planes, axis=0), z2a), low_rows))
+        third = in_pairs(a2, cut(times_wide(jnp.concatenate(planes, axis=0), z2a), low_rows))
         keys = {"l1": n2, "l2": n2 + 1, "r1": n2 + 2, "r2": n2 + 3}
         get2 = lambda key: third[keys.get(key, key)]
         dims = (rows2, nz)
@@ -709,7 +722,7 @@
         loud = limits_plane(table_ref, index_ref, 2, 1, dims, rows2 // 2, lane_half // 2, 0.0)
         kept = [shrink(x_low(get2, k, n2), quiet) for k in range(n3)]
         kept += [shrink(x_high(get2, k, n2), loud) for k in range(n3)]
-        parts = in_pairs(s2, cut(times(jnp.concatenate(kept, axis=0), z2s), rows2))
+        parts = in_pairs(s2, cut(times_wide(jnp.concatenate(kept, axis=0), z2s), rows2))
         parts = [part[:low_rows] for part in parts]
         lows = dict(enumerate(parts[:n3]))
         highs = dict(enumerate(parts[n3:]))
@@ -718,11 +731,11 @@
             c1[k, :low_rows] += x_synth(k, lows, highs)
         stack = [x_synth(k, lows, highs) for k in ghosts]
         beyond = dict(zip(ghosts, stack))
-        zed = times(jnp.concatenate(stack, axis=0), z1)
+        zed = times_wide(jnp.concatenate(stack, axis=0), z1)
         for i, plane in enumerate(in_pairs(s1, cut(zed, low_rows))):
             p1[2 * n2 + i] = plane[:out_rows]
         for i in range(0, 2 * n2, 8):
-            zed = times(c1[i : i + 8].reshape(8 * rows, nz), z1)
+            zed = times_wide(c1[i : i + 8].reshape(8 * rows, nz), z1)
             for j, plane in enumerate(in_pairs(s1, cut(zed, rows))):
                 p1[i + j] = plane[:out_rows]
         lows = {k: p1.at[k] for k in range(n2)}
@@ -738,15 +751,19 @@
             approx[m + 2] = cell(m)
         value = lambda part, ks: {k: part[k][...] for k in ks}
         ends = (n2 - 2, n2 - 1)
-        slot = lambda i: pl.ds(i * out_rows, out_rows)
-        up[slot(0)], up[slot(1)] = approx[n1], approx[n1 + 1]
-        up[slot(2)], up[slot(3)] = spill_up(value(lows, ends), value(highs, ends), n2)
-        up[4 * out_rows :] = packed(beyond[n2], beyond[n2 + 1])
-        down[slot(0)], down[slot(1)] = approx[2], approx[3]
-        down[slot(2)], down[slot(3)] = spill_down(value(lows, (0, 1)), value(highs, (0, 1)))
-        down[4 * out_rows :] = packed(beyond[-1], beyond[-2])
-
-    message = 4 * out_rows + low_rows
+
+        def send(message, four, two):
+            for i, plane in enumerate(four):
+                message[i * own_rows : (i + 1) * own_rows] = plane[:own_rows]
+                message[4 * own_rows + 4 * i : 4 * own_rows + 4 * i + 4] = plane[own_rows : own_rows + 4]
+            message[4 * own_rows + 16 :] = packed(*two)[spill_at : spill_at + spill_rows]
+
+        up_two = spill_up(value(lows, ends), value(highs, ends), n2)
+        send(up, (approx[n1], approx[n1 + 1], *up_two), (beyond[n2], beyond[n2 + 1]))
+        down_two = spill_down(value(lows, (0, 1)), value(highs, (0, 1)))
+        send(down, (approx[2], approx[3], *down_two), (beyond[-1], beyond[-2]))
+
+    message = 4 * own_rows + 16 + spill_rows
     return whole_call(
         kernel,
         [shape(n1 + 4, out_rows, nz), shape(message, nz), shape(message, nz)],
@@ -777,22 +794,27 @@
     return from_approx @ approx
 
 
-def final(left, right, own, e_left, e_right, zs1, ys1, z_matrix, y_matrix, low_rows):
+def final(left, right, own, e_left, e_right, zs1, ys1, z_matrix, y_matrix, rows, spill_rows):
     nx, ny, nz = own.shape
     half_z = nz // 2
-    rows = (left.shape[0] - low_rows) // 4
+    own_rows = ny // 2
     step_rows = 16
     steps = ny // step_rows
     taps = received_taps(nx // 2)
 
-    def kernel(l_ref, r_ref, d_ref, el, er, z1, s1, z, y, out, parts, done, sems):
-        stack = [p for ref in (l_ref, r_ref) for p in unpacked(ref[4 * rows :])]
-        zed = times(jnp.concatenate(stack, axis=0), z1)
-        spilled = [p[:rows] for p in in_pairs(s1, cut(zed, low_rows))]
-        planes = []
+    def kernel(l_ref, r_ref, d_ref, el, er, z1, s1, z, y, out, planes, parts, done, sems):
+        stack = [p for ref in (l_ref, r_ref) for p in unpacked(ref[4 * own_rows + 16 :])]
+        zed = times_wide(jnp.concatenate(stack, axis=0), z1)
+        spilled = [p[:rows] for p in in_pairs(s1, cut(zed, spill_rows))]
         for side, ref in enumerate((l_ref, r_ref)):
-            planes += [ref[pl.ds(i * rows, rows)] for i in range(4)] + spilled[2 * side : 2 * side + 2]
-        for i, plane in enumerate(cut(times(jnp.concatenate(planes, axis=0), z), rows)):
+            for i in range(4):
+                plane = planes.at[6 * side + i]
+                plane[:own_rows] = ref[i * own_rows : (i + 1) * own_rows]
+                plane[own_rows:] = jnp.zeros((rows - own_rows, half_z), F32)
+                plane[own_rows : own_rows + 4] = ref[4 * own_rows + 4 * i : 4 * own_rows + 4 * i + 4]
+            for i in range(2):
+                planes[6 * side + 4 + i] = spilled[2 * side + i]
+        for i, plane in enumerate(cut(times(planes[...].reshape(12 * rows, half_z), z), rows)):
             parts[i] = left_times(y, plane)
 
         def copy(i):
@@ -832,6 +854,7 @@
         out_specs=pl.BlockSpec(memory_space=pl.ANY),
         out_shape=shape(nx, ny, nz),
         scratch_shapes=[
+            pltpu.VMEM((12, rows, half_z), F32),
             pltpu.VMEM((12, ny, nz), F32),
             pltpu.VMEM((nx, ny, nz), F32),
             pltpu.SemaphoreType.DMA((steps,)),
@@ -864,6 +887,7 @@
     rows1 = up_to(y2 + 18, 8)
     low1 = fill(list(range(-9, y2 + 9)), rows1)
     high1 = fill(list(range(-3, y2 + 3)), up_to(y2 + 6, 8))
+    spill_at, spill_rows = 6, up_to(y2 + 6, 8)
     ks2 = fill(list(range(-3, y3 + 3)), up_to(y3 + 6, 8))
     ya0 = from_left(analysis_rows(cells0, ks0, ks0))
     ys0_matrix = synthesis_rows(list(range(ny)), ks0, ks0)
@@ -873,14 +897,15 @@
     yx0 = from_left(analysis_rows(list(range(-wide, ny + wide)), once, []))
     ya1 = from_left(analysis_rows(cells1, low1, high1))
     ys1 = from_left(synthesis_rows(ks0, low1, high1))
+    ys1_spill = from_left(synthesis_rows(ks0, low1[spill_at : spill_at + spill_rows], []))
     ya2 = from_left(analysis_rows(low1, ks2, ks2))
     ys2 = from_left(synthesis_rows(low1, ks2, ks2))
     z0 = periodic(nz, nz)
     z1 = periodic(nz // 2, nz // 2)
     z2 = periodic(nz // 4, nz // 2)
     za0, zs0, zs0_low = from_right(z0), from_right(z0.T), from_right(z0.T[: nz // 2])
-    za1, zs1 = from_right(z1), from_right(z1.T)
-    za2, zs2 = from_right(z2), from_right(z2.T)
+    za1, zs1 = wide_right(z1), wide_right(z1.T)
+    za2, zs2 = wide_right(z2), wide_right(z2.T)
 
     x_up, x_down, y_up, y_down = first_messages(velocity)
     x_left = to_next(x_up, "gx")
@@ -903,20 +928,19 @@
     b_left = to_next(b_up, "gx")
     b_right = to_previous(b_down, "gx")
     h_left, h_right, bands1 = lax.optimization_barrier((h_left, h_right, bands1))
-    edge = edge_bands(bands, halo, h_left, h_right, table, index, ya0)
-    edge, e_up, e_down = detail_edges(edge, zs0, ys0)
+    edge, e_up, e_down = edge_details(bands, halo, h_left, h_right, table, index, ya0, zs0, ys0)
     e_left = to_next(e_up, "gx")
     e_right = to_previous(e_down, "gx")
     bands1, edge = lax.optimization_barrier((bands1, edge))
     approx1, s_up, s_down = coarse(
         bands1, b_left, b_right, halo, h_left, h_right, table, index,
-        za1, yx0, ya1, zs1, za2, zs2, ya2, ys2, ys1, len(cells1), rows1, rows0,
+        za1, yx0, ya1, zs1, za2, zs2, ya2, ys2, ys1, len(cells1), rows1, rows0, y1, spill_at, spill_rows,
     )
     s_left = to_next(s_up, "gx")
     s_right = to_previous(s_down, "gx")
     rest = inner_yz(inner, approx1, zs0, ys0)
     own = own_result(edge, rest, approx1, zs0_low, ys0_low)
-    return final(s_left, s_right, own, e_left, e_right, zs1, ys1, zs0_low, ys0_low, rows1)
+    return final(s_left, s_right, own, e_left, e_right, zs1, ys1_spill, zs0_low, ys0_low, rows0, spill_rows)
 
 
 def solution(mesh):

time: 56.6 us -> 54.7 us (0.966)
  Pallas kernels: 27.5 us -> 26.4 us
  waiting for transfers between devices: 2.87 us -> 2.26 us
    ppermute x7, waiting for transfers between devices: 2.72 us -> 1.59 us  [to_previous(): return lax.ppermute(array, axis, [((i + 1) % size, i) for i in range(size)])]
    pallas_call x11 -> x10, Pallas kernels: 22.5 us -> 21.5 us  [whole_call(): pl.pallas_call(kernel, in_specs=specs, out_specs=outs, out_shape=out_shap...]
  transfers between devices with their start and end apart: 14 -> 14, of which waited for: 3 -> 3; matrix products, arithmetic and copies ran while one was open for 0% -> 0% of each run, Pallas kernels for 40% -> 39%
where the time goes in v7:
time: 54.7 us; the launch traced here: 54.5 us
  Pallas kernels  26.4 us (48%)
  starting transfers between devices  24.2 us (44%)
  waiting for transfers between devices  2.26 us (4%)
  local copies, waits for them, and re-layouts  1.12 us (2%)
    pallas_call x10, Pallas kernels, whole_call(): pl.pallas_call(kernel, in_specs=specs, out_specs=outs, out_shape=out_shap...  21.5 us
    ppermute x7, starting transfers between devices, to_previous(): return lax.ppermute(array, axis, [((i + 1) % size, i) for i in range(size)])  19.9 us
    ppermute x7, starting transfers between devices, to_next(): return lax.ppermute(array, axis, [(i, (i + 1) % size) for i in range(size)])  4.27 us
    pallas_call x1, Pallas kernels, final(): pl.pallas_call(kernel, in_specs=[VMEM] * 9, out_specs=pl.BlockSpec(memory...  3.42 us
    ppermute x7, waiting for transfers between devices, to_previous(): return lax.ppermute(array, axis, [((i + 1) % size, i) for i in range(size)])  1.59 us
    pallas_call x1, Pallas kernels, first_messages(): pl.pallas_call(kernel, in_specs=[pl.BlockSpec(memory_space=pltpu.HBM)], o...  1.57 us
    unnamed x42, local copies, waits for them, and re-layouts  1.12 us
  transfers between devices with their start and end apart: 14, of which 3 were waited for; matrix products, arithmetic and copies ran while one was open for 0% of the time, Pallas kernels for 39%

profile of v7, /device:TPU:0, one launch (start us, length us, event | category | flops | bytes accessed | tf_op | source)
XLA Modules:
  0.0 54.5 jit_solution(11016502739101296743)
XLA Ops:
  0.0 1.6 %first_messages.1 = (f32[2,128,256]{2,1,0:T(8,128)S(1)}, f32[2,128,256]{2,1,0:T(8,128)S(1)}, f32[28,8,256]{2,1,0:T(8,128)S(1)}, f32[28,8,256]{2,1,0:T(8,128)S(1)}) custom-call(f32[32,128,256]{2,1,0:T(8,128)} %v_ref.3), custom_call_target="tpu_custom_call" | custom-call | flops 1000000 | bytes 3000000 | tf_op jit(solution)/shard_map/first_messages/pallas_call | solution.py:278
  1.6 0.5 collective-permute-start.2
  2.1 2.6 %collective-permute-start = (f32[2,128,256]{2,1,0:T(8,128)S(1)}, f32[2,128,256]{2,1,0:T(8,128)S(1)}, u32[]{:S(2)}, u32[]{:S(2)}) collective-permute-start(f32[2,128,256]{2,1,0:T(8,128)S(1)} %get-tuple-element.35), channel_id=1, source_target_pairs={{0,4},{4,8},{8,12},{12,16},{16,20},{20,24},{24,28},{28,0},{1,5},{5... | collective-permute-start | bytes 786440 | tf_op jit(solution)/shard_map/ppermute | solution.py:870
  4.6 3.1 %collective-permute-start.1 = (f32[2,128,256]{2,1,0:T(8,128)S(1)}, f32[2,128,256]{2,1,0:T(8,128)S(1)}, u32[]{:S(2)}, u32[]{:S(2)}) collective-permute-start(f32[2,128,256]{2,1,0:T(8,128)S(1)} %get-tuple-element.36), channel_id=1, source_target_pairs={{4,0},{8,4},{12,8},{16,12},{20,16},{24,20},{28,24},{0,28},{5,1},{9... | collective-permute-start | bytes 786440 | tf_op jit(solution)/shard_map/ppermute | solution.py:875
  7.7 1.3 %collective-permute-start.3 = (f32[28,8,256]{2,1,0:T(8,128)S(1)}, f32[28,8,256]{2,1,0:T(8,128)S(1)}, u32[]{:S(2)}, u32[]{:S(2)}) collective-permute-start(f32[28,8,256]{2,1,0:T(8,128)S(1)} %get-tuple-element.40), channel_id=1, source_target_pairs={{1,0},{2,1},{3,2},{0,3},{5,4},{6,5},{7,6},{4,7},{9,8},{10,9},{11,1... | collective-permute-start | bytes 688136 | tf_op jit(solution)/shard_map/ppermute | solution.py:875
  9.1 1.0 %copy-done.1 = bf16[768,256]{1,0:T(8,128)(2,1)S(1)} copy-done((bf16[768,256]{1,0:T(8,128)(2,1)S(1)}, bf16[768,256]{1,0:T(8,128)(2,1)}, u32[]{:S(2)}) %copy-start.1) | copy-done | bytes 393240
  10.1 2.0 %depth_analysis.1.zed_ref = f32[32,128,256]{2,1,0:T(8,128)S(1)} custom-call(f32[32,128,256]{2,1,0:T(8,128)S(1)} %copy-done, bf16[768,256]{1,0:T(8,128)(2,1)S(1)} %copy-done.1), custom_call_target="tpu_custom_call" | custom-call | flops 1000 | bytes 1000 | tf_op jit(solution)/shard_map/depth_analysis/pallas_call | solution.py:226
  12.1 0.0 copy-start.5
  12.1 1.5 %own_approx.1 = (f32[20,72,128]{2,1,0:T(8,128)S(1)}, f32[20,24,128]{2,1,0:T(8,128)S(1)}, f32[20,24,128]{2,1,0:T(8,128)S(1)}) custom-call(f32[32,128,256]{2,1,0:T(8,128)S(1)} %depth_analysis.1.zed_ref, bf16[80,384]{1,0:T(8,128)(2,1)S(1)} %copy-done.14), custom_call_target="tpu_custom_call" | custom-call | flops 1000 | bytes 1000 | tf_op jit(solution)/shard_map/own_approx/pallas_call | solution.py:226
  13.6 0.5 collective-permute-start.7
  14.1 0.0 collective-permute-done.2.left
  14.1 0.1 collective-permute-start.6
  14.2 2.4 %y_analysis.1.b_ref = f32[32,144,256]{2,1,0:T(8,128)S(1)} custom-call(f32[32,128,256]{2,1,0:T(8,128)S(1)} %depth_analysis.1.zed_ref, f32[28,8,256]{2,1,0:T(8,128)S(1)} %collective-permute-done.2.left, f32[28,8,256]{2,1,0:T(8,128)S(1)} %collective-permute-done.3.right, bf16[768,256]{1,0:T(8,128)(2,1)S(1)} %copy-done.1, bf16[144,432]{1,0:T(8,128)(2,1)S(1)} %copy-done.5), custom_call_target="tpu_custom_call" | custom-call | flops 1000 | bytes 1000 | tf_op jit(solution)/shard_map/y_analysis/pallas_call | solution.py:226
  16.6 0.0 copy-start.2
  16.6 0.0 copy-start.8
  16.6 0.0 copy-start.9
  16.6 0.0 copy-start.3
  16.6 0.0 copy-start.7
  16.6 2.1 %inner_bands.1.c_ref = f32[24,144,256]{2,1,0:T(8,128)S(1)} custom-call(f32[16]{0:T(128)S(1)} %copy-done.20, s32[3,7]{1,0:T(4,128)S(1)} %copy-done.19, f32[32,144,256]{2,1,0:T(8,128)S(1)} %y_analysis.1.b_ref), custom_call_target="tpu_custom_call" | custom-call | flops 1000 | bytes 1000 | tf_op jit(solution)/shard_map/inner_bands/pallas_call | solution.py:226
  18.7 0.0 copy-start.6
  18.7 0.0 copy-start.11
  18.7 0.0 copy-start.12
  18.7 0.0 copy-start.13
  18.7 0.0 copy-start.15
  18.8 0.0 copy-start.17
  18.8 0.0 copy-start.18
  18.8 0.3 collective-permute-done.1.xr
  19.1 0.4 x_halo_messages.1
  19.5 1.0 %collective-permute-start.4 = (f32[4,56,128]{2,1,0:T(8,128)S(1)}, f32[4,56,128]{2,1,0:T(8,128)S(1)}, u32[]{:S(2)}, u32[]{:S(2)}) collective-permute-start(f32[4,56,128]{2,1,0:T(8,128)S(1)} %get-tuple-element.43), channel_id=1, source_target_pairs={{0,1},{1,2},{2,3},{3,0},{4,5},{5,6},{6,7},{7,4},{8,9},{9,10},{10,1... | collective-permute-start | bytes 344072 | tf_op jit(solution)/shard_map/ppermute | solution.py:870
  20.5 0.8 %collective-permute-start.5 = (f32[4,56,128]{2,1,0:T(8,128)S(1)}, f32[4,56,128]{2,1,0:T(8,128)S(1)}, u32[]{:S(2)}, u32[]{:S(2)}) collective-permute-start(f32[4,56,128]{2,1,0:T(8,128)S(1)} %get-tuple-element.44), channel_id=1, source_target_pairs={{1,0},{2,1},{3,2},{0,3},{5,4},{6,5},{7,6},{4,7},{9,8},{10,9},{11,1... | collective-permute-start | bytes 344072 | tf_op jit(solution)/shard_map/ppermute | solution.py:875
  21.3 0.0 collective-permute-done.7.r_ref
  21.3 0.7 %collective-permute-done.6.l_ref = f32[20,24,128]{2,1,0:T(8,128)S(1)} collective-permute-done((f32[20,24,128]{2,1,0:T(8,128)S(1)}, f32[20,24,128]{2,1,0:T(8,128)S(1)}, u32[]{:S(2)}, u32[]{:S(2)}) %collective-permute-start.6) | collective-permute-done | bytes 245792 | tf_op jit(solution)/shard_map/ppermute | solution.py:870
  22.0 1.2 %second_bands.1 = (f32[20,96,128]{2,1,0:T(8,128)S(1)}, f32[248,128]{1,0:T(8,128)S(1)}, f32[248,128]{1,0:T(8,128)S(1)}) custom-call(f32[20,72,128]{2,1,0:T(8,128)S(1)} %get-tuple-element.47.o_ref, f32[20,24,128]{2,1,0:T(8,128)S(1)} %collective-permute-done.6.l_ref, f32[20,24,128]{2,1,0:T(8,128)S(1)} %collective-permute-done.7.r_ref, ...), custom_call_target="tpu_custom_call" | custom-call | flops 1000 | bytes 1000 | tf_op jit(solution)/shard_map/second_bands/pallas_call | solution.py:226
  23.2 0.1 collective-permute-start.8
  23.2 4.7 %collective-permute-start.9 = (f32[248,128]{1,0:T(8,128)S(1)}, f32[248,128]{1,0:T(8,128)S(1)}, u32[]{:S(2)}, u32[]{:S(2)}) collective-permute-start(f32[248,128]{1,0:T(8,128)S(1)} %get-tuple-element.57), channel_id=1, source_target_pairs={{4,0},{8,4},{12,8},{16,12},{20,16},{24,20},{28,24},{0,28},{5,1},{9... | collective-permute-start | bytes 380936 | tf_op jit(solution)/shard_map/ppermute | solution.py:875
  27.9 2.9 %edge_details.1 = (f32[8,128,256]{2,1,0:T(8,128)S(1)}, f32[2,128,256]{2,1,0:T(8,128)S(1)}, f32[2,128,256]{2,1,0:T(8,128)S(1)}) custom-call(f32[16]{0:T(128)S(1)} %copy-done.20, s32[3,7]{1,0:T(4,128)S(1)} %copy-done.19, f32[32,144,256]{2,1,0:T(8,128)S(1)} %y_analysis.1.b_ref, f32[4,128,256]{2,1,0:T(8,128)S(1)} %get-tuple-element.51.x_ref, ...), custom_call_target="tpu_custom_call" | custom-call | flops 1000 | bytes 1000 | tf_op jit(solution)/shard_map/edge_details/pallas_call | solution.py:226
  30.9 0.1 collective-permute-start.12
  30.9 4.7 %collective-permute-start.13 = (f32[2,128,256]{2,1,0:T(8,128)S(1)}, f32[2,128,256]{2,1,0:T(8,128)S(1)}, u32[]{:S(2)}, u32[]{:S(2)}) collective-permute-start(f32[2,128,256]{2,1,0:T(8,128)S(1)} %get-tuple-element.64), channel_id=1, source_target_pairs={{4,0},{8,4},{12,8},{16,12},{20,16},{24,20},{28,24},{0,28},{5,1},{9... | collective-permute-start | bytes 786440 | tf_op jit(solution)/shard_map/ppermute | solution.py:875
  35.7 3.2 %coarse.1 = (f32[20,72,128]{2,1,0:T(8,128)S(1)}, f32[312,128]{1,0:T(8,128)S(1)}, f32[312,128]{1,0:T(8,128)S(1)}) custom-call(f32[16]{0:T(128)S(1)} %copy-done.20, s32[3,7]{1,0:T(4,128)S(1)} %copy-done.19, f32[20,96,128]{2,1,0:T(8,128)S(1)} %get-tuple-element.55.b_ref, f32[248,128]{1,0:T(8,128)S(1)} %collective-permute-done.8.l_ref, ...), custom_call_target="tpu_custom_call" | custom-call | flops 1000 | bytes 1000 | tf_op jit(solution)/shard_map/coarse/pallas_call | solution.py:226
  38.9 0.0 copy-start.4
  38.9 0.0 copy-start.10
  38.9 0.1 collective-permute-start.10
  39.0 4.7 %collective-permute-start.11 = (f32[312,128]{1,0:T(8,128)S(1)}, f32[312,128]{1,0:T(8,128)S(1)}, u32[]{:S(2)}, u32[]{:S(2)}) collective-permute-start(f32[312,128]{1,0:T(8,128)S(1)} %get-tuple-element.59), channel_id=1, source_target_pairs={{4,0},{8,4},{12,8},{16,12},{20,16},{24,20},{28,24},{0,28},{5,1},{9... | collective-permute-start | bytes 479240 | tf_op jit(solution)/shard_map/ppermute | solution.py:875
  43.7 3.4 %inner_yz.1.r_ref = f32[24,128,256]{2,1,0:T(8,128)S(1)} custom-call(f32[24,144,256]{2,1,0:T(8,128)S(1)} %inner_bands.1.c_ref, f32[20,72,128]{2,1,0:T(8,128)S(1)} %get-tuple-element.62.a_ref, bf16[768,256]{1,0:T(8,128)(2,1)S(1)} %copy-done.3, bf16[128,432]{1,0:T(8,128)(2,1)S(1)} %copy-done.7), custom_call_target="tpu_custom_call" | custom-call | flops 1000 | bytes 1000 | tf_op jit(solution)/shard_map/inner_yz/pallas_call | solution.py:226
  47.2 0.0 copy-start.16
  47.2 2.5 %own_result.1.d_ref = f32[32,128,256]{2,1,0:T(8,128)S(1)} custom-call(f32[8,128,256]{2,1,0:T(8,128)S(1)} %get-tuple-element.60.e_ref, f32[24,128,256]{2,1,0:T(8,128)S(1)} %inner_yz.1.r_ref, f32[20,72,128]{2,1,0:T(8,128)S(1)} %get-tuple-element.62.a_ref, bf16[384,256]{1,0:T(8,128)(2,1)S(1)} %copy-done.4, bf16[128,240]{1,0:T(8,128)(2,1)S(1)} %copy-done.10), custom_call_target="tpu_custom_call" | custom-call | flops 1000 | bytes 1000 | tf_op jit(solution)/shard_map/own_result/pallas_call | solution.py:226
  49.7 1.3 %collective-permute-done.11.r_ref = f32[312,128]{1,0:T(8,128)S(1)} collective-permute-done((f32[312,128]{1,0:T(8,128)S(1)}, f32[312,128]{1,0:T(8,128)S(1)}, u32[]{:S(2)}, u32[]{:S(2)}) %collective-permute-start.11) | collective-permute-done | bytes 159776 | tf_op jit(solution)/shard_map/ppermute | solution.py:875
  50.9 3.4 %final.1 = f32[32,128,256]{2,1,0:T(8,128)} custom-call(f32[312,128]{1,0:T(8,128)S(1)} %collective-permute-done.10.l_ref, f32[312,128]{1,0:T(8,128)S(1)} %collective-permute-done.11.r_ref, f32[32,128,256]{2,1,0:T(8,128)S(1)} %own_result.1.d_ref, f32[2,128,256]{2,1,0:T(8,128)S(1)} %collective-permute-done.12.el, ...), custom_call_target="tpu_custom_call" | custom-call | flops 8388608 | bytes 8388608 | tf_op jit(solution)/shard_map/final/pallas_call | solution.py:851
  (34 shorter events, 0.1 us)
Async XLA Ops:
  0.0 9.1 %copy-start = (f32[32,128,256]{2,1,0:T(8,128)S(1)}, f32[32,128,256]{2,1,0:T(8,128)}, u32[]{:S(2)}) copy-start(f32[32,128,256]{2,1,0:T(8,128)} %v_ref.3) | copy-start | bytes 12582916
  1.6 12.5 %collective-permute-start.2 = (f32[28,8,256]{2,1,0:T(8,128)S(1)}, f32[28,8,256]{2,1,0:T(8,128)S(1)}, u32[]{:S(2)}, u32[]{:S(2)}) collective-permute-start(f32[28,8,256]{2,1,0:T(8,128)S(1)} %get-tuple-element.39), channel_id=1, source_target_pairs={{0,1},{1,2},{2,3},{3,0},{4,5},{5,6},{6,7},{7,4},{8,9},{9,10},{10,1... | collective-permute-start | bytes 688136 | tf_op jit(solution)/shard_map/ppermute | solution.py:870
  2.1 16.7 %collective-permute-start = (f32[2,128,256]{2,1,0:T(8,128)S(1)}, f32[2,128,256]{2,1,0:T(8,128)S(1)}, u32[]{:S(2)}, u32[]{:S(2)}) collective-permute-start(f32[2,128,256]{2,1,0:T(8,128)S(1)} %get-tuple-element.35), channel_id=1, source_target_pairs={{0,4},{4,8},{8,12},{12,16},{16,20},{20,24},{24,28},{28,0},{1,5},{5... | collective-permute-start | bytes 786440 | tf_op jit(solution)/shard_map/ppermute | solution.py:870
  4.6 14.5 %collective-permute-start.1 = (f32[2,128,256]{2,1,0:T(8,128)S(1)}, f32[2,128,256]{2,1,0:T(8,128)S(1)}, u32[]{:S(2)}, u32[]{:S(2)}) collective-permute-start(f32[2,128,256]{2,1,0:T(8,128)S(1)} %get-tuple-element.36), channel_id=1, source_target_pairs={{4,0},{8,4},{12,8},{16,12},{20,16},{24,20},{28,24},{0,28},{5,1},{9... | collective-permute-start | bytes 786440 | tf_op jit(solution)/shard_map/ppermute | solution.py:875
  7.7 6.4 %collective-permute-start.3 = (f32[28,8,256]{2,1,0:T(8,128)S(1)}, f32[28,8,256]{2,1,0:T(8,128)S(1)}, u32[]{:S(2)}, u32[]{:S(2)}) collective-permute-start(f32[28,8,256]{2,1,0:T(8,128)S(1)} %get-tuple-element.40), channel_id=1, source_target_pairs={{1,0},{2,1},{3,2},{0,3},{5,4},{6,5},{7,6},{4,7},{9,8},{10,9},{11,1... | collective-permute-start | bytes 688136 | tf_op jit(solution)/shard_map/ppermute | solution.py:875
  9.1 1.0 %copy-start.1 = (bf16[768,256]{1,0:T(8,128)(2,1)S(1)}, bf16[768,256]{1,0:T(8,128)(2,1)}, u32[]{:S(2)}) copy-start(bf16[768,256]{1,0:T(8,128)(2,1)} %constant.34.clone.z) | copy-start | bytes 1179652
  10.1 2.0 %copy-start.14 = (bf16[80,384]{1,0:T(8,128)(2,1)S(1)}, bf16[80,384]{1,0:T(8,128)(2,1)}, u32[]{:S(2)}) copy-start(bf16[80,384]{1,0:T(8,128)(2,1)} %constant.35.clone.y) | copy-start | bytes 184324
  12.1 2.1 %copy-start.5 = (bf16[144,432]{1,0:T(8,128)(2,1)S(1)}, bf16[144,432]{1,0:T(8,128)(2,1)}, u32[]{:S(2)}) copy-start(bf16[144,432]{1,0:T(8,128)(2,1)} %constant.36.clone.y.ya) | copy-start | bytes 373252
  13.6 7.7 %collective-permute-start.7 = (f32[20,24,128]{2,1,0:T(8,128)S(1)}, f32[20,24,128]{2,1,0:T(8,128)S(1)}, u32[]{:S(2)}, u32[]{:S(2)}) collective-permute-start(f32[20,24,128]{2,1,0:T(8,128)S(1)} %get-tuple-element.48), channel_id=1, source_target_pairs={{1,0},{2,1},{3,2},{0,3},{5,4},{6,5},{7,6},{4,7},{9,8},{10,9},{11,1... | collective-permute-start | bytes 737288 | tf_op jit(solution)/shard_map/ppermute | solution.py:875
  14.1 2.5 %copy-start.19 = (s32[3,7]{1,0:T(4,128)S(1)}, s32[3,7]{1,0:T(4,128)}, u32[]{:S(2)}) copy-start(s32[3,7]{1,0:T(4,128)} %index_ref.5) | copy-start | bytes 256
  14.1 2.5 %copy-start.20 = (f32[16]{0:T(128)S(1)}, f32[16]{0:T(128)}, u32[]{:S(2)}) copy-start(f32[16]{0:T(128)} %table_ref.5) | copy-start | bytes 196
  14.1 7.9 %collective-permute-start.6 = (f32[20,24,128]{2,1,0:T(8,128)S(1)}, f32[20,24,128]{2,1,0:T(8,128)S(1)}, u32[]{:S(2)}, u32[]{:S(2)}) collective-permute-start(f32[20,24,128]{2,1,0:T(8,128)S(1)} %get-tuple-element.37), channel_id=1, source_target_pairs={{0,1},{1,2},{2,3},{3,0},{4,5},{5,6},{6,7},{7,4},{8,9},{9,10},{10,1... | collective-permute-start | bytes 737288 | tf_op jit(solution)/shard_map/ppermute | solution.py:870
  16.6 2.6 %copy-start.2 = (bf16[768,256]{1,0:T(8,128)(2,1)S(1)}, bf16[768,256]{1,0:T(8,128)(2,1)}, u32[]{:S(2)}) copy-start(bf16[768,256]{1,0:T(8,128)(2,1)} %constant.34.clone.z) | copy-start | bytes 1179652
  16.6 5.4 %copy-start.8 = (bf16[256,256]{1,0:T(8,128)(2,1)S(1)}, bf16[256,256]{1,0:T(8,128)(2,1)}, u32[]{:S(2)}) copy-start(bf16[256,256]{1,0:T(8,128)(2,1)} %constant.37.clone.z.z1a) | copy-start | bytes 393220
  16.6 5.4 %copy-start.9 = (bf16[96,384]{1,0:T(8,128)(2,1)S(1)}, bf16[96,384]{1,0:T(8,128)(2,1)}, u32[]{:S(2)}) copy-start(bf16[96,384]{1,0:T(8,128)(2,1)} %constant.38.clone.y.a1) | copy-start | bytes 221188
  16.6 11.3 %copy-start.3 = (bf16[768,256]{1,0:T(8,128)(2,1)S(1)}, bf16[768,256]{1,0:T(8,128)(2,1)}, u32[]{:S(2)}) copy-start(bf16[768,256]{1,0:T(8,128)(2,1)} %constant.39.clone.z) | copy-start | bytes 1179652
  16.6 11.3 %copy-start.7 = (bf16[128,432]{1,0:T(8,128)(2,1)S(1)}, bf16[128,432]{1,0:T(8,128)(2,1)}, u32[]{:S(2)}) copy-start(bf16[128,432]{1,0:T(8,128)(2,1)} %constant.40.clone.y) | copy-start | bytes 331780
  18.7 17.0 %copy-start.6 = (bf16[256,256]{1,0:T(8,128)(2,1)S(1)}, bf16[256,256]{1,0:T(8,128)(2,1)}, u32[]{:S(2)}) copy-start(bf16[256,256]{1,0:T(8,128)(2,1)} %constant.42.clone.z1) | copy-start | bytes 393220
  18.7 17.0 %copy-start.11 = (bf16[128,672]{1,0:T(8,128)(2,1)S(1)}, bf16[128,672]{1,0:T(8,128)(2,1)}, u32[]{:S(2)}) copy-start(bf16[128,672]{1,0:T(8,128)(2,1)} %constant.41.clone.yx) | copy-start | bytes 516100
  18.7 17.0 %copy-start.12 = (bf16[256,256]{1,0:T(8,128)(2,1)S(1)}, bf16[256,256]{1,0:T(8,128)(2,1)}, u32[]{:S(2)}) copy-start(bf16[256,256]{1,0:T(8,128)(2,1)} %constant.44.clone.z2s) | copy-start | bytes 393220
  18.7 16.9 %copy-start.13 = (bf16[256,256]{1,0:T(8,128)(2,1)S(1)}, bf16[256,256]{1,0:T(8,128)(2,1)}, u32[]{:S(2)}) copy-start(bf16[256,256]{1,0:T(8,128)(2,1)} %constant.43.clone.z2a) | copy-start | bytes 393220
  18.7 16.9 %copy-start.15 = (bf16[80,288]{1,0:T(8,128)(2,1)S(1)}, bf16[80,288]{1,0:T(8,128)(2,1)}, u32[]{:S(2)}) copy-start(bf16[80,288]{1,0:T(8,128)(2,1)} %constant.47.clone.s1) | copy-start | bytes 138244
  18.8 16.9 %copy-start.17 = (bf16[64,144]{1,0:T(8,128)(2,1)S(1)}, bf16[64,144]{1,0:T(8,128)(2,1)}, u32[]{:S(2)}) copy-start(bf16[64,144]{1,0:T(8,128)(2,1)} %constant.46.clone.s2) | copy-start | bytes 55300
  18.8 16.9 %copy-start.18 = (bf16[48,192]{1,0:T(8,128)(2,1)S(1)}, bf16[48,192]{1,0:T(8,128)(2,1)}, u32[]{:S(2)}) copy-start(bf16[48,192]{1,0:T(8,128)(2,1)} %constant.45.clone.a2) | copy-start | bytes 55300
  19.5 8.4 %collective-permute-start.4 = (f32[4,56,128]{2,1,0:T(8,128)S(1)}, f32[4,56,128]{2,1,0:T(8,128)S(1)}, u32[]{:S(2)}, u32[]{:S(2)}) collective-permute-start(f32[4,56,128]{2,1,0:T(8,128)S(1)} %get-tuple-element.43), channel_id=1, source_target_pairs={{0,1},{1,2},{2,3},{3,0},{4,5},{5,6},{6,7},{7,4},{8,9},{9,10},{10,1... | collective-permute-start | bytes 344072 | tf_op jit(solution)/shard_map/ppermute | solution.py:870
  20.5 7.5 %collective-permute-start.5 = (f32[4,56,128]{2,1,0:T(8,128)S(1)}, f32[4,56,128]{2,1,0:T(8,128)S(1)}, u32[]{:S(2)}, u32[]{:S(2)}) collective-permute-start(f32[4,56,128]{2,1,0:T(8,128)S(1)} %get-tuple-element.44), channel_id=1, source_target_pairs={{1,0},{2,1},{3,2},{0,3},{5,4},{6,5},{7,6},{4,7},{9,8},{10,9},{11,1... | collective-permute-start | bytes 344072 | tf_op jit(solution)/shard_map/ppermute | solution.py:875
  23.2 12.5 %collective-permute-start.8 = (f32[248,128]{1,0:T(8,128)S(1)}, f32[248,128]{1,0:T(8,128)S(1)}, u32[]{:S(2)}, u32[]{:S(2)}) collective-permute-start(f32[248,128]{1,0:T(8,128)S(1)} %get-tuple-element.56), channel_id=1, source_target_pairs={{0,4},{4,8},{8,12},{12,16},{16,20},{20,24},{24,28},{28,0},{1,5},{5... | collective-permute-start | bytes 380936 | tf_op jit(solution)/shard_map/ppermute | solution.py:870
  23.2 12.4 %collective-permute-start.9 = (f32[248,128]{1,0:T(8,128)S(1)}, f32[248,128]{1,0:T(8,128)S(1)}, u32[]{:S(2)}, u32[]{:S(2)}) collective-permute-start(f32[248,128]{1,0:T(8,128)S(1)} %get-tuple-element.57), channel_id=1, source_target_pairs={{4,0},{8,4},{12,8},{16,12},{20,16},{24,20},{28,24},{0,28},{5,1},{9... | collective-permute-start | bytes 380936 | tf_op jit(solution)/shard_map/ppermute | solution.py:875
  30.9 20.1 %collective-permute-start.12 = (f32[2,128,256]{2,1,0:T(8,128)S(1)}, f32[2,128,256]{2,1,0:T(8,128)S(1)}, u32[]{:S(2)}, u32[]{:S(2)}) collective-permute-start(f32[2,128,256]{2,1,0:T(8,128)S(1)} %get-tuple-element.63), channel_id=1, source_target_pairs={{0,4},{4,8},{8,12},{12,16},{16,20},{20,24},{24,28},{28,0},{1,5},{5... | collective-permute-start | bytes 786440 | tf_op jit(solution)/shard_map/ppermute | solution.py:870
  30.9 20.0 %collective-permute-start.13 = (f32[2,128,256]{2,1,0:T(8,128)S(1)}, f32[2,128,256]{2,1,0:T(8,128)S(1)}, u32[]{:S(2)}, u32[]{:S(2)}) collective-permute-start(f32[2,128,256]{2,1,0:T(8,128)S(1)} %get-tuple-element.64), channel_id=1, source_target_pairs={{4,0},{8,4},{12,8},{16,12},{20,16},{24,20},{28,24},{0,28},{5,1},{9... | collective-permute-start | bytes 786440 | tf_op jit(solution)/shard_map/ppermute | solution.py:875
  38.9 8.3 %copy-start.4 = (bf16[384,256]{1,0:T(8,128)(2,1)S(1)}, bf16[384,256]{1,0:T(8,128)(2,1)}, u32[]{:S(2)}) copy-start(bf16[384,256]{1,0:T(8,128)(2,1)} %constant.48.clone.z) | copy-start | bytes 589828
  38.9 8.3 %copy-start.10 = (bf16[128,240]{1,0:T(8,128)(2,1)S(1)}, bf16[128,240]{1,0:T(8,128)(2,1)}, u32[]{:S(2)}) copy-start(bf16[128,240]{1,0:T(8,128)(2,1)} %constant.49.clone.y) | copy-start | bytes 184324
  38.9 10.7 %collective-permute-start.10 = (f32[312,128]{1,0:T(8,128)S(1)}, f32[312,128]{1,0:T(8,128)S(1)}, u32[]{:S(2)}, u32[]{:S(2)}) collective-permute-start(f32[312,128]{1,0:T(8,128)S(1)} %get-tuple-element.58), channel_id=1, source_target_pairs={{0,4},{4,8},{8,12},{12,16},{16,20},{20,24},{24,28},{28,0},{1,5},{5... | collective-permute-start | bytes 479240 | tf_op jit(solution)/shard_map/ppermute | solution.py:870
  39.0 11.9 %collective-permute-start.11 = (f32[312,128]{1,0:T(8,128)S(1)}, f32[312,128]{1,0:T(8,128)S(1)}, u32[]{:S(2)}, u32[]{:S(2)}) collective-permute-start(f32[312,128]{1,0:T(8,128)S(1)} %get-tuple-element.59), channel_id=1, source_target_pairs={{4,0},{8,4},{12,8},{16,12},{20,16},{24,20},{28,24},{0,28},{5,1},{9... | collective-permute-start | bytes 479240 | tf_op jit(solution)/shard_map/ppermute | solution.py:875
  47.2 3.7 %copy-start.16 = (bf16[80,144]{1,0:T(8,128)(2,1)S(1)}, bf16[80,144]{1,0:T(8,128)(2,1)}, u32[]{:S(2)}) copy-start(bf16[80,144]{1,0:T(8,128)(2,1)} %constant.50.clone.s1) | copy-start | bytes 69124

commit v8 on v7

--- a/solution.py
+++ b/solution.py
@@ -220,18 +220,42 @@
     return values - jnp.minimum(jnp.maximum(values, -thresh), thresh)
 
 
-def whole_call(kernel, out_shapes, args, flops, moved, scratch=(), name=None):
+def paired(kernel, args, outs, scratch, received, sent):
+    extra = [pltpu.VMEM((2,) + args[i].shape, F32) for i, _ in received]
+    extra += [pltpu.VMEM((2,) + outs[j].shape, F32) for j, _ in sent]
+
+    def wrapped(*refs):
+        refs, both = list(refs[: len(refs) - len(extra)]), refs[len(refs) - len(extra) :]
+        for (i, axis), pair in zip(received, both):
+            parity = lax.rem(lax.axis_index(axis), 2)
+            pair[0], pair[1] = refs[i][...], refs[i + 1][...]
+            refs[i], refs[i + 1] = pair.at[1 - parity], pair.at[parity]
+        carried = []
+        for (j, axis), pair in zip(sent, both[len(received) :]):
+            parity = lax.rem(lax.axis_index(axis), 2)
+            j += len(args)
+            carried.append((refs[j], refs[j + 1], pair))
+            refs[j], refs[j + 1] = pair.at[parity], pair.at[1 - parity]
+        kernel(*refs)
+        for first, second, pair in carried:
+            first[...], second[...] = pair[0], pair[1]
+
+    return wrapped, list(scratch) + extra
+
+
+def whole_call(kernel, outs, args, scratch=(), received=(), sent=(), name=None, **changes):
+    out_list = outs if isinstance(outs, list) else [outs]
+    kernel, scratch = paired(kernel, args, out_list, scratch, received, sent)
     specs = [SMEM if a.ndim == 1 or a.dtype == jnp.int32 else VMEM for a in args]
-    outs = [VMEM] * len(out_shapes) if isinstance(out_shapes, list) else VMEM
     return pl.pallas_call(
         kernel,
-        in_specs=specs,
-        out_specs=outs,
-        out_shape=out_shapes,
-        scratch_shapes=list(scratch),
+        in_specs=changes.get("in_specs", specs),
+        out_specs=changes.get("out_specs", [VMEM] * len(outs) if outs is out_list else VMEM),
+        out_shape=outs,
+        scratch_shapes=scratch,
         name=name,
         cost_estimate=pl.CostEstimate(flops=1000, bytes_accessed=1000, transcendentals=0),
-        compiler_params=pltpu.CompilerParams(vmem_limit_bytes=VMEM_BYTES),
+        compiler_params=pltpu.CompilerParams(vmem_limit_bytes=changes.get("vmem", VMEM_BYTES)),
     )(*args)
 
 
@@ -275,18 +299,18 @@
             y_up[i, 0:1] = rows_up[plane, row + 1 : row + 2]
             y_down[i, 7:8] = rows_down[plane, row : row + 1]
 
-    return pl.pallas_call(
-        kernel,
-        in_specs=[pl.BlockSpec(memory_space=pltpu.HBM)],
-        out_specs=[VMEM] * 4,
-        out_shape=[shape(2, ny, nz)] * 2 + [shape(kept, 8, nz)] * 2,
-        scratch_shapes=[pltpu.VMEM((3, ny, nz), F32)] * 2
+    return whole_call(
+        kernel,
+        [shape(2, ny, nz)] * 2 + [shape(kept, 8, nz)] * 2,
+        [v],
+        scratch=[pltpu.VMEM((3, ny, nz), F32)] * 2
         + [pltpu.VMEM((nx, 8, nz), F32)] * 2
         + [pltpu.SemaphoreType.DMA((4,))],
+        sent=[(0, "gx"), (2, "gy")],
         name="first_messages",
-        cost_estimate=pl.CostEstimate(flops=1000000, bytes_accessed=3000000, transcendentals=0),
-        compiler_params=pltpu.CompilerParams(vmem_limit_bytes=50 * 1024 * 1024),
-    )(v)
+        in_specs=[pl.BlockSpec(memory_space=pltpu.HBM)],
+        vmem=50 * 1024 * 1024,
+    )
 
 
 def over_planes(count, group, body):
@@ -307,9 +331,7 @@
 
         over_planes(nx, group, body)
 
-    return whole_call(
-        kernel, shape(nx, rows, nz), [v, z_matrix], 6 * nx * rows * nz * nz, 8 * nx * rows * nz, name=name
-    )
+    return whole_call(kernel, shape(nx, rows, nz), [v, z_matrix], name=name)
 
 
 def y_analysis(zed, y_left, y_right, z_matrix, y_matrix):
@@ -338,9 +360,8 @@
         kernel,
         shape(nx, rows, nz),
         [zed, y_left, y_right, z_matrix, y_matrix],
-        1000,
-        1000,
         scratch=[pltpu.VMEM((nx, 8, nz), F32)] * 2,
+        received=[(1, "gy")],
         name="y_analysis",
     )
 
@@ -380,9 +401,8 @@
         kernel,
         [shape(n1 + 4, rows, half_z), shape(n1 + 4, ghost_rows, half_z), shape(n1 + 4, ghost_rows, half_z)],
         [zed, y_matrix],
-        1000,
-        1000,
         scratch=[pltpu.VMEM((nx, rows, half_z), F32)],
+        sent=[(1, "gy")],
         name="own_approx",
     )
 
@@ -403,8 +423,8 @@
         kernel,
         [shape(4, ny, nz), shape(4, wide + 8, half_z), shape(4, wide + 8, half_z)],
         [x_left, x_right, z_matrix],
-        24 * ny * nz * nz,
-        3e6,
+        received=[(0, "gx")],
+        sent=[(1, "gy")],
         name="x_halo_messages",
     )
 
@@ -450,8 +470,6 @@
         kernel,
         shape(2 * count, rows, nz),
         [table, index, bands],
-        30 * nx * rows * nz,
-        8 * nx * rows * nz,
         name="inner_bands",
     )
 
@@ -503,9 +521,9 @@
         kernel,
         [shape(8, ny, nz), shape(2, ny, nz), shape(2, ny, nz)],
         [table, index, bands, halo, h_left, h_right, ya_matrix, z_matrix, y_matrix],
-        48 * rows * nz * (nz + ny),
-        4 * nx * rows * nz,
         scratch=[pltpu.VMEM((4, rows, nz), F32)] + [pltpu.VMEM((8, rows, nz), F32)] * 2,
+        received=[(4, "gy")],
+        sent=[(1, "gx")],
         name="edge_details",
     )
 
@@ -533,8 +551,6 @@
         kernel,
         shape(count, ny, nz),
         [coeffs, approx, z_matrix, y_matrix],
-        6 * count * rows * nz * (nz + ny),
-        4 * count * nz * (rows + ny),
         scratch=[pltpu.VMEM((count, rows, nz), F32)],
         name="inner_yz",
     )
@@ -581,8 +597,6 @@
         kernel,
         shape(nx, ny, nz),
         [edge, rest, approx, z_matrix, y_matrix],
-        16 * nx * ny * nz,
-        8 * nx * ny * nz,
         scratch=[pltpu.VMEM((8, ny, nz), F32)],
         name="own_result",
     )
@@ -645,8 +659,8 @@
         kernel,
         [shape(planes, rows, nz), shape(message, nz), shape(message, nz)],
         [own, left, right, z_matrix, y_matrix],
-        6 * n1 * in_rows * nz * (nz + rows),
-        4 * n1 * nz * (in_rows + rows),
+        received=[(1, "gy")],
+        sent=[(1, "gx")],
         name="second_bands",
     )
 
@@ -768,9 +782,9 @@
         kernel,
         [shape(n1 + 4, out_rows, nz), shape(message, nz), shape(message, nz)],
         [table, index, bands, left, right, halo, h_left, h_right, za1, yx0, ya1, zs1, za2, zs2, ya2, ys2, ys1],
-        1.5e9,
-        8 * n1 * rows * nz,
         scratch=[pltpu.VMEM((2 * n2, rows, nz), F32), pltpu.VMEM((2 * n2 + 6, out_rows, nz), F32)],
+        received=[(3, "gx"), (6, "gy")],
+        sent=[(1, "gx")],
         name="coarse",
     )
 
@@ -848,31 +862,28 @@
 
         lax.fori_loop(0, steps, finish, 0)
 
-    return pl.pallas_call(
-        kernel,
-        in_specs=[VMEM] * 9,
-        out_specs=pl.BlockSpec(memory_space=pl.ANY),
-        out_shape=shape(nx, ny, nz),
-        scratch_shapes=[
+    return whole_call(
+        kernel,
+        shape(nx, ny, nz),
+        [left, right, own, e_left, e_right, zs1, ys1, z_matrix, y_matrix],
+        scratch=[
             pltpu.VMEM((12, rows, half_z), F32),
             pltpu.VMEM((12, ny, nz), F32),
             pltpu.VMEM((nx, ny, nz), F32),
             pltpu.SemaphoreType.DMA((steps,)),
         ],
+        received=[(0, "gx"), (3, "gx")],
         name="final",
-        cost_estimate=pl.CostEstimate(flops=8 * nx * ny * nz, bytes_accessed=8 * nx * ny * nz, transcendentals=0),
-        compiler_params=pltpu.CompilerParams(vmem_limit_bytes=VMEM_BYTES),
-    )(left, right, own, e_left, e_right, zs1, ys1, z_matrix, y_matrix)
-
-
-def to_next(array, axis):
+        out_specs=pl.BlockSpec(memory_space=pl.ANY),
+    )
+
+
+def exchange(first, second, axis):
     size = lax.axis_size(axis)
-    return lax.ppermute(array, axis, [(i, (i + 1) % size) for i in range(size)])
-
-
-def to_previous(array, axis):
-    size = lax.axis_size(axis)
-    return lax.ppermute(array, axis, [((i + 1) % size, i) for i in range(size)])
+    assert size % 2 == 0
+    here = [(i, i ^ 1) for i in range(size)]
+    across = [(i, (i + 1) % size if i % 2 else (i - 1) % size) for i in range(size)]
+    return lax.ppermute(first, axis, here), lax.ppermute(second, axis, across)
 
 
 def local(velocity, table, index):
@@ -908,37 +919,30 @@
     za2, zs2 = wide_right(z2), wide_right(z2.T)
 
     x_up, x_down, y_up, y_down = first_messages(velocity)
-    x_left = to_next(x_up, "gx")
-    x_right = to_previous(x_down, "gx")
-    y_left = to_next(y_up, "gy")
-    y_right = to_previous(y_down, "gy")
+    x_left, x_right = exchange(x_up, x_down, "gx")
+    y_left, y_right = exchange(y_up, y_down, "gy")
     zed = depth(velocity, za0, 16, "depth_analysis")
     approx, a_up, a_down = own_approx(zed, yl0, y1, rows0, ghost)
-    a_left = to_next(a_up, "gy")
-    a_right = to_previous(a_down, "gy")
+    a_left, a_right = exchange(a_up, a_down, "gy")
     zed, a_up = lax.optimization_barrier((zed, a_up))
     bands = y_analysis(zed, y_left, y_right, za0, ya0)
-    inner = inner_bands(bands, table, index)
-    x_left, x_right, inner = lax.optimization_barrier((x_left, x_right, inner))
+    x_left, x_right, bands = lax.optimization_barrier((x_left, x_right, bands))
     halo, h_up, h_down = x_halo_messages(x_left, x_right, za0, wide)
-    h_left = to_next(h_up, "gy")
-    h_right = to_previous(h_down, "gy")
+    h_left, h_right = exchange(h_up, h_down, "gy")
     approx, halo = lax.optimization_barrier((approx, halo))
     bands1, b_up, b_down = second_bands(approx, a_left, a_right, za1, ya1, rows1)
-    b_left = to_next(b_up, "gx")
-    b_right = to_previous(b_down, "gx")
+    b_left, b_right = exchange(b_up, b_down, "gx")
     h_left, h_right, bands1 = lax.optimization_barrier((h_left, h_right, bands1))
     edge, e_up, e_down = edge_details(bands, halo, h_left, h_right, table, index, ya0, zs0, ys0)
-    e_left = to_next(e_up, "gx")
-    e_right = to_previous(e_down, "gx")
+    e_left, e_right = exchange(e_up, e_down, "gx")
     bands1, edge = lax.optimization_barrier((bands1, edge))
     approx1, s_up, s_down = coarse(
         bands1, b_left, b_right, halo, h_left, h_right, table, index,
         za1, yx0, ya1, zs1, za2, zs2, ya2, ys2, ys1, len(cells1), rows1, rows0, y1, spill_at, spill_rows,
     )
-    s_left = to_next(s_up, "gx")
-    s_right = to_previous(s_down, "gx")
-    rest = inner_yz(inner, approx1, zs0, ys0)
+    s_left, s_right = exchange(s_up, s_down, "gx")
+    bands, approx1 = lax.optimization_barrier((bands, approx1))
+    rest = inner_yz(inner_bands(bands, table, index), approx1, zs0, ys0)
     own = own_result(edge, rest, approx1, zs0_low, ys0_low)
     return final(s_left, s_right, own, e_left, e_right, zs1, ys1_spill, zs0_low, ys0_low, rows0, spill_rows)
 

time: 54.7 us -> 53.1 us (0.971)
  starting transfers between devices: 24.2 us -> 18.5 us
  waiting for transfers between devices: 2.26 us -> 6.13 us
    ppermute x14, starting transfers between devices: 24.2 us -> 18.5 us  [exchange(): return (lax.ppermute(first, axis, here), lax.ppermute(second, axis, across))]
    ppermute x14, waiting for transfers between devices: 2.26 us -> 6.13 us  [exchange(): return (lax.ppermute(first, axis, here), lax.ppermute(second, axis, across))]
    unnamed x42 -> x40, local copies, waits for them, and re-layouts: 1.12 us -> 1.11 us
  transfers between devices with their start and end apart: 14 -> 14, of which waited for: 3 -> 4; matrix products, arithmetic and copies ran while one was open for 0% -> 0% of each run, Pallas kernels for 39% -> 41%
where the time goes in v8:
time: 53.1 us; the launch traced here: 52.9 us
  Pallas kernels  26.9 us (51%)
  starting transfers between devices  18.5 us (35%)
  waiting for transfers between devices  6.13 us (12%)
  local copies, waits for them, and re-layouts  1.11 us (2%)
    pallas_call x12, Pallas kernels, whole_call(): pl.pallas_call(kernel, in_specs=changes.get('in_specs', specs), out_specs...  26.9 us
    ppermute x14, starting transfers between devices, exchange(): return (lax.ppermute(first, axis, here), lax.ppermute(second, axis, across))  18.5 us
    ppermute x14, waiting for transfers between devices, exchange(): return (lax.ppermute(first, axis, here), lax.ppermute(second, axis, across))  6.13 us
    unnamed x40, local copies, waits for them, and re-layouts  1.11 us
  transfers between devices with their start and end apart: 14, of which 4 were waited for; matrix products, arithmetic and copies ran while one was open for 0% of the time, Pallas kernels for 41%

profile of v8, /device:TPU:0, one launch (start us, length us, event | category | flops | bytes accessed | tf_op | source)
XLA Modules:
  0.0 52.9 jit_solution(13728103255887152383)
XLA Ops:
  0.0 1.6 %first_messages.1 = (f32[2,128,256]{2,1,0:T(8,128)S(1)}, f32[2,128,256]{2,1,0:T(8,128)S(1)}, f32[28,8,256]{2,1,0:T(8,128)S(1)}, f32[28,8,256]{2,1,0:T(8,128)S(1)}) custom-call(f32[32,128,256]{2,1,0:T(8,128)} %refs_0_.6), custom_call_target="tpu_custom_call" | custom-call | flops 1000 | bytes 1000 | tf_op jit(solution)/shard_map/first_messages/pallas_call | solution.py:250
  1.6 0.5 collective-permute-start.2
  2.2 2.6 %collective-permute-start = (f32[2,128,256]{2,1,0:T(8,128)S(1)}, f32[2,128,256]{2,1,0:T(8,128)S(1)}, u32[]{:S(2)}, u32[]{:S(2)}) collective-permute-start(f32[2,128,256]{2,1,0:T(8,128)S(1)} %get-tuple-element.37), channel_id=1, source_target_pairs={{0,4},{4,0},{8,12},{12,8},{16,20},{20,16},{24,28},{28,24},{1,5},{5... | collective-permute-start | bytes 786440 | tf_op jit(solution)/shard_map/ppermute | solution.py:886
  4.7 3.6 %collective-permute-start.1 = (f32[2,128,256]{2,1,0:T(8,128)S(1)}, f32[2,128,256]{2,1,0:T(8,128)S(1)}, u32[]{:S(2)}, u32[]{:S(2)}) collective-permute-start(f32[2,128,256]{2,1,0:T(8,128)S(1)} %get-tuple-element.38), channel_id=1, source_target_pairs={{0,28},{4,8},{8,4},{12,16},{16,12},{20,24},{24,20},{28,0},{1,29},{... | collective-permute-start | bytes 786440 | tf_op jit(solution)/shard_map/ppermute | solution.py:886
  8.3 1.0 %collective-permute-start.3 = (f32[28,8,256]{2,1,0:T(8,128)S(1)}, f32[28,8,256]{2,1,0:T(8,128)S(1)}, u32[]{:S(2)}, u32[]{:S(2)}) collective-permute-start(f32[28,8,256]{2,1,0:T(8,128)S(1)} %get-tuple-element.42), channel_id=1, source_target_pairs={{0,3},{1,2},{2,1},{3,0},{4,7},{5,6},{6,5},{7,4},{8,11},{9,10},{10,... | collective-permute-start | bytes 688136 | tf_op jit(solution)/shard_map/ppermute | solution.py:886
  9.3 1.0 %copy-done.1 = bf16[768,256]{1,0:T(8,128)(2,1)S(1)} copy-done((bf16[768,256]{1,0:T(8,128)(2,1)S(1)}, bf16[768,256]{1,0:T(8,128)(2,1)}, u32[]{:S(2)}) %copy-start.1) | copy-done | bytes 393240
  10.3 2.0 %depth_analysis.1.refs_0_ = f32[32,128,256]{2,1,0:T(8,128)S(1)} custom-call(f32[32,128,256]{2,1,0:T(8,128)S(1)} %copy-done, bf16[768,256]{1,0:T(8,128)(2,1)S(1)} %copy-done.1), custom_call_target="tpu_custom_call" | custom-call | flops 1000 | bytes 1000 | tf_op jit(solution)/shard_map/depth_analysis/pallas_call | solution.py:250
  12.3 0.0 copy-start.4
  12.3 1.5 %own_approx.1 = (f32[20,72,128]{2,1,0:T(8,128)S(1)}, f32[20,24,128]{2,1,0:T(8,128)S(1)}, f32[20,24,128]{2,1,0:T(8,128)S(1)}) custom-call(f32[32,128,256]{2,1,0:T(8,128)S(1)} %depth_analysis.1.refs_0_, bf16[80,384]{1,0:T(8,128)(2,1)S(1)} %copy-done.13), custom_call_target="tpu_custom_call" | custom-call | flops 1000 | bytes 1000 | tf_op jit(solution)/shard_map/own_approx/pallas_call | solution.py:250
  13.9 0.8 %collective-permute-start.7 = (f32[20,24,128]{2,1,0:T(8,128)S(1)}, f32[20,24,128]{2,1,0:T(8,128)S(1)}, u32[]{:S(2)}, u32[]{:S(2)}) collective-permute-start(f32[20,24,128]{2,1,0:T(8,128)S(1)} %get-tuple-element.50), channel_id=1, source_target_pairs={{0,3},{1,2},{2,1},{3,0},{4,7},{5,6},{6,5},{7,4},{8,11},{9,10},{10,... | collective-permute-start | bytes 737288 | tf_op jit(solution)/shard_map/ppermute | solution.py:886
  14.7 0.0 collective-permute-done.2.refs_1_
  14.7 0.0 copy-start.6
  14.7 0.0 copy-start.18
  14.7 0.0 copy-start.19
  14.7 0.1 collective-permute-start.6
  14.8 1.3 %collective-permute-done.3.refs_2_ = f32[28,8,256]{2,1,0:T(8,128)S(1)} collective-permute-done((f32[28,8,256]{2,1,0:T(8,128)S(1)}, f32[28,8,256]{2,1,0:T(8,128)S(1)}, u32[]{:S(2)}, u32[]{:S(2)}) %collective-permute-start.3) | collective-permute-done | bytes 229408 | tf_op jit(solution)/shard_map/ppermute | solution.py:886
  16.1 2.5 %y_analysis.1.refs_2_ = f32[32,144,256]{2,1,0:T(8,128)S(1)} custom-call(f32[32,128,256]{2,1,0:T(8,128)S(1)} %depth_analysis.1.refs_0_, f32[28,8,256]{2,1,0:T(8,128)S(1)} %collective-permute-done.2.refs_1_, f32[28,8,256]{2,1,0:T(8,128)S(1)} %collective-permute-done.3.refs_2_, bf16[768,256]{1,0:T(8,128)(2,1)S(1)} %copy-done.1, bf16[144,432]{1,0:T(8,128)(2,1)S(1)} %copy-done.4), custom_call_target="tpu_custom_call" | custom-call | flops 1000 | bytes 1000 | tf_op jit(solution)/shard_map/y_analysis/pallas_call | solution.py:250
  18.6 0.0 copy-start.5
  18.6 0.0 copy-start.10
  18.6 0.0 copy-start.11
  18.6 0.0 copy-start.12
  18.7 0.0 copy-start.14
  18.7 0.0 copy-start.16
  18.7 0.0 copy-start.17
  18.7 0.0 collective-permute-done.1.refs_1_
  18.7 0.4 x_halo_messages.1
  19.1 0.2 collective-permute-start.4
  19.4 1.5 %collective-permute-start.5 = (f32[4,56,128]{2,1,0:T(8,128)S(1)}, f32[4,56,128]{2,1,0:T(8,128)S(1)}, u32[]{:S(2)}, u32[]{:S(2)}) collective-permute-start(f32[4,56,128]{2,1,0:T(8,128)S(1)} %get-tuple-element.46), channel_id=1, source_target_pairs={{0,3},{1,2},{2,1},{3,0},{4,7},{5,6},{6,5},{7,4},{8,11},{9,10},{10,... | collective-permute-start | bytes 344072 | tf_op jit(solution)/shard_map/ppermute | solution.py:886
  20.8 0.6 %collective-permute-done.7.refs_2_ = f32[20,24,128]{2,1,0:T(8,128)S(1)} collective-permute-done((f32[20,24,128]{2,1,0:T(8,128)S(1)}, f32[20,24,128]{2,1,0:T(8,128)S(1)}, u32[]{:S(2)}, u32[]{:S(2)}) %collective-permute-start.7) | collective-permute-done | bytes 245792 | tf_op jit(solution)/shard_map/ppermute | solution.py:886
  21.4 1.2 %second_bands.1 = (f32[20,96,128]{2,1,0:T(8,128)S(1)}, f32[248,128]{1,0:T(8,128)S(1)}, f32[248,128]{1,0:T(8,128)S(1)}) custom-call(f32[20,72,128]{2,1,0:T(8,128)S(1)} %get-tuple-element.49.refs_0_, f32[20,24,128]{2,1,0:T(8,128)S(1)} %collective-permute-done.6.refs_1_, f32[20,24,128]{2,1,0:T(8,128)S(1)} %collective-permute-done.7.refs_2_, ...), custom_call_target="tpu_custom_call" | custom-call | flops 1000 | bytes 1000 | tf_op jit(solution)/shard_map/second_bands/pallas_call | solution.py:250
  22.6 0.1 collective-permute-start.8
  22.7 3.3 %collective-permute-start.9 = (f32[248,128]{1,0:T(8,128)S(1)}, f32[248,128]{1,0:T(8,128)S(1)}, u32[]{:S(2)}, u32[]{:S(2)}) collective-permute-start(f32[248,128]{1,0:T(8,128)S(1)} %get-tuple-element.60), channel_id=1, source_target_pairs={{0,28},{4,8},{8,4},{12,16},{16,12},{20,24},{24,20},{28,0},{1,29},{... | collective-permute-start | bytes 380936 | tf_op jit(solution)/shard_map/ppermute | solution.py:886
  26.1 3.0 %edge_details.1 = (f32[8,128,256]{2,1,0:T(8,128)S(1)}, f32[2,128,256]{2,1,0:T(8,128)S(1)}, f32[2,128,256]{2,1,0:T(8,128)S(1)}) custom-call(f32[16]{0:T(128)S(1)} %copy-done.19, s32[3,7]{1,0:T(4,128)S(1)} %copy-done.18, f32[32,144,256]{2,1,0:T(8,128)S(1)} %y_analysis.1.refs_2_, f32[4,128,256]{2,1,0:T(8,128)S(1)} %get-tuple-element.54.refs_3_.refs_5_, ...), custom_call_target="tpu_custom_call" | custom-call | flops 1000 | bytes 1000 | tf_op jit(solution)/shard_map/edge_details/pallas_call | solution.py:250
  29.1 0.1 collective-permute-start.12
  29.1 2.0 %collective-permute-start.13 = (f32[2,128,256]{2,1,0:T(8,128)S(1)}, f32[2,128,256]{2,1,0:T(8,128)S(1)}, u32[]{:S(2)}, u32[]{:S(2)}) collective-permute-start(f32[2,128,256]{2,1,0:T(8,128)S(1)} %get-tuple-element.68), channel_id=1, source_target_pairs={{0,28},{4,8},{8,4},{12,16},{16,12},{20,24},{24,20},{28,0},{1,29},{... | collective-permute-start | bytes 786440 | tf_op jit(solution)/shard_map/ppermute | solution.py:886
  31.1 0.2 collective-permute-done.9.refs_4_
  31.4 3.3 %coarse.1 = (f32[20,72,128]{2,1,0:T(8,128)S(1)}, f32[312,128]{1,0:T(8,128)S(1)}, f32[312,128]{1,0:T(8,128)S(1)}) custom-call(f32[16]{0:T(128)S(1)} %copy-done.19, s32[3,7]{1,0:T(4,128)S(1)} %copy-done.18, f32[20,96,128]{2,1,0:T(8,128)S(1)} %get-tuple-element.58.refs_2_, f32[248,128]{1,0:T(8,128)S(1)} %collective-permute-done.8.refs_3_, ...), custom_call_target="tpu_custom_call" | custom-call | flops 1000 | bytes 1000 | tf_op jit(solution)/shard_map/coarse/pallas_call | solution.py:250
  34.7 0.3 collective-permute-start.10
  35.1 2.5 %collective-permute-start.11 = (f32[312,128]{1,0:T(8,128)S(1)}, f32[312,128]{1,0:T(8,128)S(1)}, u32[]{:S(2)}, u32[]{:S(2)}) collective-permute-start(f32[312,128]{1,0:T(8,128)S(1)} %get-tuple-element.62), channel_id=1, source_target_pairs={{0,28},{4,8},{8,4},{12,16},{16,12},{20,24},{24,20},{28,0},{1,29},{... | collective-permute-start | bytes 479240 | tf_op jit(solution)/shard_map/ppermute | solution.py:886
  37.5 2.1 %inner_bands.1.refs_0_ = f32[24,144,256]{2,1,0:T(8,128)S(1)} custom-call(f32[16]{0:T(128)S(1)} %copy-done.19, s32[3,7]{1,0:T(4,128)S(1)} %copy-done.18, f32[32,144,256]{2,1,0:T(8,128)S(1)} %y_analysis.1.refs_2_), custom_call_target="tpu_custom_call" | custom-call | flops 1000 | bytes 1000 | tf_op jit(solution)/shard_map/inner_bands/pallas_call | solution.py:250
  39.6 0.0 copy-start.3
  39.6 0.0 copy-start.9
  39.6 3.4 %inner_yz.1.refs_1_ = f32[24,128,256]{2,1,0:T(8,128)S(1)} custom-call(f32[24,144,256]{2,1,0:T(8,128)S(1)} %inner_bands.1.refs_0_, f32[20,72,128]{2,1,0:T(8,128)S(1)} %get-tuple-element.66.refs_1_.refs_2_, bf16[768,256]{1,0:T(8,128)(2,1)S(1)} %copy-done.2, bf16[128,432]{1,0:T(8,128)(2,1)S(1)} %copy-done.6), custom_call_target="tpu_custom_call" | custom-call | flops 1000 | bytes 1000 | tf_op jit(solution)/shard_map/inner_yz/pallas_call | solution.py:250
  43.0 0.0 copy-start.15
  43.0 2.5 %own_result.1.refs_2_ = f32[32,128,256]{2,1,0:T(8,128)S(1)} custom-call(f32[8,128,256]{2,1,0:T(8,128)S(1)} %get-tuple-element.63.refs_0_, f32[24,128,256]{2,1,0:T(8,128)S(1)} %inner_yz.1.refs_1_, f32[20,72,128]{2,1,0:T(8,128)S(1)} %get-tuple-element.66.refs_1_.refs_2_, bf16[384,256]{1,0:T(8,128)(2,1)S(1)} %copy-done.3, bf16[128,240]{1,0:T(8,128)(2,1)S(1)} %copy-done.9), custom_call_target="tpu_custom_call" | custom-call | flops 1000 | bytes 1000 | tf_op jit(solution)/shard_map/own_result/pallas_call | solution.py:250
  45.5 4.0 %collective-permute-done.10.refs_0_ = f32[312,128]{1,0:T(8,128)S(1)} collective-permute-done((f32[312,128]{1,0:T(8,128)S(1)}, f32[312,128]{1,0:T(8,128)S(1)}, u32[]{:S(2)}, u32[]{:S(2)}) %collective-permute-start.10) | collective-permute-done | bytes 159776 | tf_op jit(solution)/shard_map/ppermute | solution.py:886
  49.5 0.0 collective-permute-done.11.refs_1_
  49.5 3.5 %final.1 = f32[32,128,256]{2,1,0:T(8,128)} custom-call(f32[312,128]{1,0:T(8,128)S(1)} %collective-permute-done.10.refs_0_, f32[312,128]{1,0:T(8,128)S(1)} %collective-permute-done.11.refs_1_, f32[32,128,256]{2,1,0:T(8,128)S(1)} %own_result.1.refs_2_, f32[2,128,256]{2,1,0:T(8,128)S(1)} %collective-permute-done.12.refs_3_, ...), custom_call_target="tpu_custom_call" | custom-call | flops 1000 | bytes 1000 | tf_op jit(solution)/shard_map/final/pallas_call | solution.py:250
  (32 shorter events, 0.1 us)
Async XLA Ops:
  0.0 9.3 %copy-start = (f32[32,128,256]{2,1,0:T(8,128)S(1)}, f32[32,128,256]{2,1,0:T(8,128)}, u32[]{:S(2)}) copy-start(f32[32,128,256]{2,1,0:T(8,128)} %refs_0_.6) | copy-start | bytes 12582916
  1.6 13.0 %collective-permute-start.2 = (f32[28,8,256]{2,1,0:T(8,128)S(1)}, f32[28,8,256]{2,1,0:T(8,128)S(1)}, u32[]{:S(2)}, u32[]{:S(2)}) collective-permute-start(f32[28,8,256]{2,1,0:T(8,128)S(1)} %get-tuple-element.41), channel_id=1, source_target_pairs={{0,1},{1,0},{2,3},{3,2},{4,5},{5,4},{6,7},{7,6},{8,9},{9,8},{10,11... | collective-permute-start | bytes 688136 | tf_op jit(solution)/shard_map/ppermute | solution.py:886
  2.2 16.5 %collective-permute-start = (f32[2,128,256]{2,1,0:T(8,128)S(1)}, f32[2,128,256]{2,1,0:T(8,128)S(1)}, u32[]{:S(2)}, u32[]{:S(2)}) collective-permute-start(f32[2,128,256]{2,1,0:T(8,128)S(1)} %get-tuple-element.37), channel_id=1, source_target_pairs={{0,4},{4,0},{8,12},{12,8},{16,20},{20,16},{24,28},{28,24},{1,5},{5... | collective-permute-start | bytes 786440 | tf_op jit(solution)/shard_map/ppermute | solution.py:886
  4.7 14.0 %collective-permute-start.1 = (f32[2,128,256]{2,1,0:T(8,128)S(1)}, f32[2,128,256]{2,1,0:T(8,128)S(1)}, u32[]{:S(2)}, u32[]{:S(2)}) collective-permute-start(f32[2,128,256]{2,1,0:T(8,128)S(1)} %get-tuple-element.38), channel_id=1, source_target_pairs={{0,28},{4,8},{8,4},{12,16},{16,12},{20,24},{24,20},{28,0},{1,29},{... | collective-permute-start | bytes 786440 | tf_op jit(solution)/shard_map/ppermute | solution.py:886
  8.3 7.8 %collective-permute-start.3 = (f32[28,8,256]{2,1,0:T(8,128)S(1)}, f32[28,8,256]{2,1,0:T(8,128)S(1)}, u32[]{:S(2)}, u32[]{:S(2)}) collective-permute-start(f32[28,8,256]{2,1,0:T(8,128)S(1)} %get-tuple-element.42), channel_id=1, source_target_pairs={{0,3},{1,2},{2,1},{3,0},{4,7},{5,6},{6,5},{7,4},{8,11},{9,10},{10,... | collective-permute-start | bytes 688136 | tf_op jit(solution)/shard_map/ppermute | solution.py:886
  9.3 1.0 %copy-start.1 = (bf16[768,256]{1,0:T(8,128)(2,1)S(1)}, bf16[768,256]{1,0:T(8,128)(2,1)}, u32[]{:S(2)}) copy-start(bf16[768,256]{1,0:T(8,128)(2,1)} %constant.34.clone.refs_1_.refs_3_.refs_2_) | copy-start | bytes 1179652
  10.3 2.0 %copy-start.13 = (bf16[80,384]{1,0:T(8,128)(2,1)S(1)}, bf16[80,384]{1,0:T(8,128)(2,1)}, u32[]{:S(2)}) copy-start(bf16[80,384]{1,0:T(8,128)(2,1)} %constant.35.clone.refs_1_) | copy-start | bytes 184324
  12.3 3.8 %copy-start.4 = (bf16[144,432]{1,0:T(8,128)(2,1)S(1)}, bf16[144,432]{1,0:T(8,128)(2,1)}, u32[]{:S(2)}) copy-start(bf16[144,432]{1,0:T(8,128)(2,1)} %constant.36.clone.refs_4_.refs_6_) | copy-start | bytes 373252
  13.9 7.5 %collective-permute-start.7 = (f32[20,24,128]{2,1,0:T(8,128)S(1)}, f32[20,24,128]{2,1,0:T(8,128)S(1)}, u32[]{:S(2)}, u32[]{:S(2)}) collective-permute-start(f32[20,24,128]{2,1,0:T(8,128)S(1)} %get-tuple-element.50), channel_id=1, source_target_pairs={{0,3},{1,2},{2,1},{3,0},{4,7},{5,6},{6,5},{7,4},{8,11},{9,10},{10,... | collective-permute-start | bytes 737288 | tf_op jit(solution)/shard_map/ppermute | solution.py:886
  14.7 6.7 %copy-start.7 = (bf16[256,256]{1,0:T(8,128)(2,1)S(1)}, bf16[256,256]{1,0:T(8,128)(2,1)}, u32[]{:S(2)}) copy-start(bf16[256,256]{1,0:T(8,128)(2,1)} %constant.37.clone.refs_3_.refs_8_) | copy-start | bytes 393220
  14.7 6.7 %copy-start.8 = (bf16[96,384]{1,0:T(8,128)(2,1)S(1)}, bf16[96,384]{1,0:T(8,128)(2,1)}, u32[]{:S(2)}) copy-start(bf16[96,384]{1,0:T(8,128)(2,1)} %constant.38.clone.refs_4_.refs_10_) | copy-start | bytes 221188
  14.7 11.4 %copy-start.2 = (bf16[768,256]{1,0:T(8,128)(2,1)S(1)}, bf16[768,256]{1,0:T(8,128)(2,1)}, u32[]{:S(2)}) copy-start(bf16[768,256]{1,0:T(8,128)(2,1)} %constant.39.clone.refs_7_.refs_2_) | copy-start | bytes 1179652
  14.7 11.4 %copy-start.6 = (bf16[128,432]{1,0:T(8,128)(2,1)S(1)}, bf16[128,432]{1,0:T(8,128)(2,1)}, u32[]{:S(2)}) copy-start(bf16[128,432]{1,0:T(8,128)(2,1)} %constant.40.clone.refs_8_.refs_3_) | copy-start | bytes 331780
  14.7 11.4 %copy-start.18 = (s32[3,7]{1,0:T(4,128)S(1)}, s32[3,7]{1,0:T(4,128)}, u32[]{:S(2)}) copy-start(s32[3,7]{1,0:T(4,128)} %refs_1_.7) | copy-start | bytes 256
  14.7 11.4 %copy-start.19 = (f32[16]{0:T(128)S(1)}, f32[16]{0:T(128)}, u32[]{:S(2)}) copy-start(f32[16]{0:T(128)} %refs_0_.9) | copy-start | bytes 196
  14.7 6.7 %collective-permute-start.6 = (f32[20,24,128]{2,1,0:T(8,128)S(1)}, f32[20,24,128]{2,1,0:T(8,128)S(1)}, u32[]{:S(2)}, u32[]{:S(2)}) collective-permute-start(f32[20,24,128]{2,1,0:T(8,128)S(1)} %get-tuple-element.39), channel_id=1, source_target_pairs={{0,1},{1,0},{2,3},{3,2},{4,5},{5,4},{6,7},{7,6},{8,9},{9,8},{10,11... | collective-permute-start | bytes 737288 | tf_op jit(solution)/shard_map/ppermute | solution.py:886
  18.6 12.8 %copy-start.5 = (bf16[256,256]{1,0:T(8,128)(2,1)S(1)}, bf16[256,256]{1,0:T(8,128)(2,1)}, u32[]{:S(2)}) copy-start(bf16[256,256]{1,0:T(8,128)(2,1)} %constant.42.clone.refs_11_.refs_5_) | copy-start | bytes 393220
  18.6 12.8 %copy-start.10 = (bf16[128,672]{1,0:T(8,128)(2,1)S(1)}, bf16[128,672]{1,0:T(8,128)(2,1)}, u32[]{:S(2)}) copy-start(bf16[128,672]{1,0:T(8,128)(2,1)} %constant.41.clone.refs_9_) | copy-start | bytes 516100
  18.6 12.8 %copy-start.11 = (bf16[256,256]{1,0:T(8,128)(2,1)S(1)}, bf16[256,256]{1,0:T(8,128)(2,1)}, u32[]{:S(2)}) copy-start(bf16[256,256]{1,0:T(8,128)(2,1)} %constant.44.clone.refs_13_) | copy-start | bytes 393220
  18.6 12.8 %copy-start.12 = (bf16[256,256]{1,0:T(8,128)(2,1)S(1)}, bf16[256,256]{1,0:T(8,128)(2,1)}, u32[]{:S(2)}) copy-start(bf16[256,256]{1,0:T(8,128)(2,1)} %constant.43.clone.refs_12_) | copy-start | bytes 393220
  18.7 12.8 %copy-start.14 = (bf16[80,288]{1,0:T(8,128)(2,1)S(1)}, bf16[80,288]{1,0:T(8,128)(2,1)}, u32[]{:S(2)}) copy-start(bf16[80,288]{1,0:T(8,128)(2,1)} %constant.47.clone.refs_16_) | copy-start | bytes 138244
  18.7 12.8 %copy-start.16 = (bf16[64,144]{1,0:T(8,128)(2,1)S(1)}, bf16[64,144]{1,0:T(8,128)(2,1)}, u32[]{:S(2)}) copy-start(bf16[64,144]{1,0:T(8,128)(2,1)} %constant.46.clone.refs_15_) | copy-start | bytes 55300
  18.7 12.8 %copy-start.17 = (bf16[48,192]{1,0:T(8,128)(2,1)S(1)}, bf16[48,192]{1,0:T(8,128)(2,1)}, u32[]{:S(2)}) copy-start(bf16[48,192]{1,0:T(8,128)(2,1)} %constant.45.clone.refs_14_) | copy-start | bytes 55300
  19.1 6.9 %collective-permute-start.4 = (f32[4,56,128]{2,1,0:T(8,128)S(1)}, f32[4,56,128]{2,1,0:T(8,128)S(1)}, u32[]{:S(2)}, u32[]{:S(2)}) collective-permute-start(f32[4,56,128]{2,1,0:T(8,128)S(1)} %get-tuple-element.45), channel_id=1, source_target_pairs={{0,1},{1,0},{2,3},{3,2},{4,5},{5,4},{6,7},{7,6},{8,9},{9,8},{10,11... | collective-permute-start | bytes 344072 | tf_op jit(solution)/shard_map/ppermute | solution.py:886
  19.4 6.6 %collective-permute-start.5 = (f32[4,56,128]{2,1,0:T(8,128)S(1)}, f32[4,56,128]{2,1,0:T(8,128)S(1)}, u32[]{:S(2)}, u32[]{:S(2)}) collective-permute-start(f32[4,56,128]{2,1,0:T(8,128)S(1)} %get-tuple-element.46), channel_id=1, source_target_pairs={{0,3},{1,2},{2,1},{3,0},{4,7},{5,6},{6,5},{7,4},{8,11},{9,10},{10,... | collective-permute-start | bytes 344072 | tf_op jit(solution)/shard_map/ppermute | solution.py:886
  22.6 8.5 %collective-permute-start.8 = (f32[248,128]{1,0:T(8,128)S(1)}, f32[248,128]{1,0:T(8,128)S(1)}, u32[]{:S(2)}, u32[]{:S(2)}) collective-permute-start(f32[248,128]{1,0:T(8,128)S(1)} %get-tuple-element.59), channel_id=1, source_target_pairs={{0,4},{4,0},{8,12},{12,8},{16,20},{20,16},{24,28},{28,24},{1,5},{5... | collective-permute-start | bytes 380936 | tf_op jit(solution)/shard_map/ppermute | solution.py:886
  22.7 8.7 %collective-permute-start.9 = (f32[248,128]{1,0:T(8,128)S(1)}, f32[248,128]{1,0:T(8,128)S(1)}, u32[]{:S(2)}, u32[]{:S(2)}) collective-permute-start(f32[248,128]{1,0:T(8,128)S(1)} %get-tuple-element.60), channel_id=1, source_target_pairs={{0,28},{4,8},{8,4},{12,16},{16,12},{20,24},{24,20},{28,0},{1,29},{... | collective-permute-start | bytes 380936 | tf_op jit(solution)/shard_map/ppermute | solution.py:886
  29.1 20.4 %collective-permute-start.12 = (f32[2,128,256]{2,1,0:T(8,128)S(1)}, f32[2,128,256]{2,1,0:T(8,128)S(1)}, u32[]{:S(2)}, u32[]{:S(2)}) collective-permute-start(f32[2,128,256]{2,1,0:T(8,128)S(1)} %get-tuple-element.67), channel_id=1, source_target_pairs={{0,4},{4,0},{8,12},{12,8},{16,20},{20,16},{24,28},{28,24},{1,5},{5... | collective-permute-start | bytes 786440 | tf_op jit(solution)/shard_map/ppermute | solution.py:886
  29.1 20.3 %collective-permute-start.13 = (f32[2,128,256]{2,1,0:T(8,128)S(1)}, f32[2,128,256]{2,1,0:T(8,128)S(1)}, u32[]{:S(2)}, u32[]{:S(2)}) collective-permute-start(f32[2,128,256]{2,1,0:T(8,128)S(1)} %get-tuple-element.68), channel_id=1, source_target_pairs={{0,28},{4,8},{8,4},{12,16},{16,12},{20,24},{24,20},{28,0},{1,29},{... | collective-permute-start | bytes 786440 | tf_op jit(solution)/shard_map/ppermute | solution.py:886
  34.7 14.7 %collective-permute-start.10 = (f32[312,128]{1,0:T(8,128)S(1)}, f32[312,128]{1,0:T(8,128)S(1)}, u32[]{:S(2)}, u32[]{:S(2)}) collective-permute-start(f32[312,128]{1,0:T(8,128)S(1)} %get-tuple-element.61), channel_id=1, source_target_pairs={{0,4},{4,0},{8,12},{12,8},{16,20},{20,16},{24,28},{28,24},{1,5},{5... | collective-permute-start | bytes 479240 | tf_op jit(solution)/shard_map/ppermute | solution.py:886
  35.1 14.4 %collective-permute-start.11 = (f32[312,128]{1,0:T(8,128)S(1)}, f32[312,128]{1,0:T(8,128)S(1)}, u32[]{:S(2)}, u32[]{:S(2)}) collective-permute-start(f32[312,128]{1,0:T(8,128)S(1)} %get-tuple-element.62), channel_id=1, source_target_pairs={{0,28},{4,8},{8,4},{12,16},{16,12},{20,24},{24,20},{28,0},{1,29},{... | collective-permute-start | bytes 479240 | tf_op jit(solution)/shard_map/ppermute | solution.py:886
  39.6 3.4 %copy-start.3 = (bf16[384,256]{1,0:T(8,128)(2,1)S(1)}, bf16[384,256]{1,0:T(8,128)(2,1)}, u32[]{:S(2)}) copy-start(bf16[384,256]{1,0:T(8,128)(2,1)} %constant.48.clone.refs_3_.refs_7_) | copy-start | bytes 589828
  39.6 3.4 %copy-start.9 = (bf16[128,240]{1,0:T(8,128)(2,1)S(1)}, bf16[128,240]{1,0:T(8,128)(2,1)}, u32[]{:S(2)}) copy-start(bf16[128,240]{1,0:T(8,128)(2,1)} %constant.49.clone.refs_4_.refs_8_) | copy-start | bytes 184324
  43.0 6.5 %copy-start.15 = (bf16[80,144]{1,0:T(8,128)(2,1)S(1)}, bf16[80,144]{1,0:T(8,128)(2,1)}, u32[]{:S(2)}) copy-start(bf16[80,144]{1,0:T(8,128)(2,1)} %constant.50.clone.refs_6_) | copy-start | bytes 69124

commit v9 on v8

--- a/solution.py
+++ b/solution.py
@@ -334,13 +334,13 @@
     return whole_call(kernel, shape(nx, rows, nz), [v, z_matrix], name=name)
 
 
-def y_analysis(zed, y_left, y_right, z_matrix, y_matrix):
+def y_analysis(zed, y_across, y_here, z_matrix, y_matrix):
     nx, ny, nz = zed.shape
     rows = y_matrix.shape[0]
-    kept = y_left.shape[0]
+    kept = y_here.shape[0]
     group = 8
 
-    def kernel(zed_ref, left, right, z, y, out, left_z, right_z):
+    def kernel(zed_ref, right, left, z, y, out, left_z, right_z):
         for part, out_z in ((left, left_z), (right, right_z)):
             out_z[:kept] = times(part[...].reshape(8 * kept, nz), z).reshape(kept, 8, nz)
             out_z[kept:] = jnp.zeros((nx - kept, 8, nz), F32)
@@ -359,7 +359,7 @@
     return whole_call(
         kernel,
         shape(nx, rows, nz),
-        [zed, y_left, y_right, z_matrix, y_matrix],
+        [zed, y_across, y_here, z_matrix, y_matrix],
         scratch=[pltpu.VMEM((nx, 8, nz), F32)] * 2,
         received=[(1, "gy")],
         name="y_analysis",
@@ -392,14 +392,14 @@
 
         lax.fori_loop(0, rows // 8, tile, 0)
         inside = ghost_rows - 2
-        up[:, :inside] = approx[:, own - inside : own]
-        up[:, inside:] = approx[:, own + 2 : own + 4]
-        down[:, :2] = approx[:, own : own + 2]
-        down[:, 2:] = approx[:, :inside]
-
-    return whole_call(
-        kernel,
-        [shape(n1 + 4, rows, half_z), shape(n1 + 4, ghost_rows, half_z), shape(n1 + 4, ghost_rows, half_z)],
+        up[:, :inside] = approx[:n1, own - inside : own]
+        up[:, inside:] = approx[:n1, own + 2 : own + 4]
+        down[:, :2] = approx[:n1, own : own + 2]
+        down[:, 2:] = approx[:n1, :inside]
+
+    return whole_call(
+        kernel,
+        [shape(n1 + 4, rows, half_z), shape(n1, ghost_rows, half_z), shape(n1, ghost_rows, half_z)],
         [zed, y_matrix],
         scratch=[pltpu.VMEM((nx, rows, half_z), F32)],
         sent=[(1, "gy")],
@@ -407,22 +407,29 @@
     )
 
 
-def x_halo_messages(x_left, x_right, z_matrix, wide):
+def x_halo_messages(x_left, x_right, approx, z_matrix, wide, ghost_rows):
     _, ny, nz = x_left.shape
     half_z = nz // 2
-
-    def kernel(xl, xr, z, out, up, down):
+    n1 = approx.shape[0] - 4
+    own, inside = ny // 2, ghost_rows - 2
+    message = wide + 8 + ghost_rows
+
+    def kernel(xl, xr, a_ref, z, out, up, down):
         planes = jnp.concatenate([xl[0], xl[1], xr[0], xr[1]], axis=0)
         out[...] = times(planes, z).reshape(4, ny, nz)
         up[:, :wide] = out[:, ny - wide :, :half_z]
-        up[:, wide:] = out[:, ny - 8 :, half_z:]
+        up[:, wide : wide + 8] = out[:, ny - 8 :, half_z:]
         down[:, :wide] = out[:, :wide, :half_z]
-        down[:, wide:] = out[:, :8, half_z:]
-
-    return whole_call(
-        kernel,
-        [shape(4, ny, nz), shape(4, wide + 8, half_z), shape(4, wide + 8, half_z)],
-        [x_left, x_right, z_matrix],
+        down[:, wide : wide + 8] = out[:, :8, half_z:]
+        up[:, wide + 8 : wide + 8 + inside] = a_ref[n1:, own - inside : own]
+        up[:, wide + 8 + inside :] = a_ref[n1:, own + 2 : own + 4]
+        down[:, wide + 8 : wide + 10] = a_ref[n1:, own : own + 2]
+        down[:, wide + 10 :] = a_ref[n1:, :inside]
+
+    return whole_call(
+        kernel,
+        [shape(4, ny, nz), shape(4, message, half_z), shape(4, message, half_z)],
+        [x_left, x_right, approx, z_matrix],
         received=[(0, "gx")],
         sent=[(1, "gy")],
         name="x_halo_messages",
@@ -476,7 +483,7 @@
 
 def yz_synthesis(planes, z, y, out, zed):
     count, rows, nz = zed.shape
-    group = max(g for g in range(1, 13) if count % g == 0)
+    group = max(g for g in range(1, 17) if count % g == 0)
     for first in range(0, count, group):
         zed[first : first + group] = times(planes(first, group), z).reshape(group, rows, nz)
 
@@ -487,18 +494,19 @@
     over_planes(count, 4, y_body)
 
 
-def edge_details(bands, halo, h_left, h_right, table, index, ya_matrix, z_matrix, y_matrix):
+def edge_details(bands, halo, h_left, h_right, table, index, ya_matrix, z_matrix, y_matrix, wide):
     nx, rows, nz = bands.shape
     ny = y_matrix.shape[0]
     n1 = nx // 2
     half_z = nz // 2
-    wide = h_left.shape[1] - 8
     ends = edges_of(n1)
 
-    def kernel(table_ref, index_ref, b_ref, x_ref, hl, hr, ya, z, y, out, up, down, h_ref, coeffs, zed):
+    def kernel(table_ref, index_ref, b_ref, x_ref, hl, hr, ya, z, y, coeffs, up, down, h_ref, beyond, zed):
         for i in range(4):
             low = jnp.concatenate([hl[i, wide - 8 : wide], x_ref[i, :, :half_z], hr[i, :8]], axis=0)
-            high = jnp.concatenate([hl[i, wide:], x_ref[i, :, half_z:], hr[i, wide:]], axis=0)
+            high = jnp.concatenate(
+                [hl[i, wide : wide + 8], x_ref[i, :, half_z:], hr[i, wide : wide + 8]], axis=0
+            )
             h_ref[i] = left_times(ya, jnp.concatenate([low, high], axis=1))
         place = {"l1": 0, "l2": 1, "r1": 2, "r2": 3}
 
@@ -506,41 +514,53 @@
             quiet, loud = band_limits(table_ref, index_ref, by, bz)
             values = {key: h_ref[i, at, lanes] for key, i in place.items()}
             values.update({i: b_ref[i, at, lanes] for i in [*range(7), *range(nx - 7, nx)]})
+            lows, highs = {}, {}
             for i, k in enumerate(ends):
                 low, high = x_low(values.get, k, nx), x_high(values.get, k, nx)
-                coeffs[i, at, lanes] = shrink(low, quiet) if by + bz else jnp.zeros_like(low)
-                coeffs[4 + i, at, lanes] = shrink(high, loud)
+                lows[k] = shrink(low, quiet) if by + bz else jnp.zeros_like(low)
+                highs[k] = shrink(high, loud)
+                coeffs[i, at, lanes] = lows[k]
+                coeffs[4 + i, at, lanes] = highs[k]
+            spilled = spill_up(lows, highs, n1) + spill_down(lows, highs)
+            for i, part in enumerate(spilled):
+                beyond[i, at, lanes] = part
 
         over_tiles(rows, nz, body)
-        yz_synthesis(lambda first, n: coeffs[first : first + n].reshape(n * rows, nz), z, y, out, zed)
-        part = lambda ks, at: {k: out[i] for k, i in zip(ks, at)}
-        up[0], up[1] = spill_up(part((0, 1), (2, 3)), part((0, 1), (6, 7)), 2)
-        down[0], down[1] = spill_down(part((0, 1), (0, 1)), part((0, 1), (4, 5)))
-
-    return whole_call(
-        kernel,
-        [shape(8, ny, nz), shape(2, ny, nz), shape(2, ny, nz)],
+        zed[...] = times(beyond[...].reshape(4 * rows, nz), z).reshape(4, rows, nz)
+        for i, target in enumerate((up.at[0], up.at[1], down.at[0], down.at[1])):
+            target[...] = left_times(y, zed[i])
+
+    return whole_call(
+        kernel,
+        [shape(8, rows, nz), shape(2, ny, nz), shape(2, ny, nz)],
         [table, index, bands, halo, h_left, h_right, ya_matrix, z_matrix, y_matrix],
-        scratch=[pltpu.VMEM((4, rows, nz), F32)] + [pltpu.VMEM((8, rows, nz), F32)] * 2,
+        scratch=[pltpu.VMEM((4, rows, nz), F32)] * 3,
         received=[(4, "gy")],
         sent=[(1, "gx")],
         name="edge_details",
     )
 
 
-def inner_yz(coeffs, approx, z_matrix, y_matrix):
-    count, rows, nz = coeffs.shape
+def detail_yz(edge, inner, approx, z_matrix, y_matrix):
+    count, rows, nz = inner.shape
     ny = y_matrix.shape[0]
     _, low_rows, half_z = approx.shape
-    lows = count // 2
-
-    def kernel(c_ref, a_ref, z, y, out, zed):
+    n1 = count // 2 + 4
+    ends = edges_of(n1)
+
+    def kernel(e_ref, i_ref, a_ref, z, y, out, zed):
+        def coeff(k, high):
+            if k in ends:
+                return e_ref.at[4 * high + ends.index(k)]
+            return i_ref.at[(n1 - 4) * high + k - 2]
+
         def plane(i):
-            if i >= lows:
-                return c_ref[i]
-            corner = c_ref[i, :low_rows, :half_z] + a_ref[i + 4]
-            top = jnp.concatenate([corner, c_ref[i, :low_rows, half_z:]], axis=1)
-            return jnp.concatenate([top, c_ref[i, low_rows:]], axis=0)
+            ref = coeff(i % n1, i // n1)
+            if i >= n1:
+                return ref[...]
+            corner = ref[:low_rows, :half_z] + a_ref[i + 2]
+            top = jnp.concatenate([corner, ref[:low_rows, half_z:]], axis=1)
+            return jnp.concatenate([top, ref[low_rows:]], axis=0)
 
         def planes(first, n):
             return jnp.concatenate([plane(i) for i in range(first, first + n)], axis=0)
@@ -549,46 +569,41 @@
 
     return whole_call(
         kernel,
-        shape(count, ny, nz),
-        [coeffs, approx, z_matrix, y_matrix],
-        scratch=[pltpu.VMEM((count, rows, nz), F32)],
-        name="inner_yz",
-    )
-
-
-def own_result(edge, rest, approx, z_matrix, y_matrix):
-    count, ny, nz = rest.shape
-    n1 = (count + 8) // 2
-    nx = 2 * n1
-    ends = edges_of(n1)
+        shape(2 * n1, ny, nz),
+        [edge, inner, approx, z_matrix, y_matrix],
+        scratch=[pltpu.VMEM((2 * n1, rows, nz), F32)],
+        name="detail_yz",
+    )
+
+
+def own_result(parts, approx, left, right, z_matrix, y_matrix):
+    nx, ny, nz = parts.shape
+    n1 = nx // 2
     planes, rows, half_z = approx.shape
 
-    def kernel(e_ref, r_ref, a_ref, z, y, out, parts):
-        for first in (0, 4):
-            start = first and n1
-            zed = times(a_ref[start : start + 4].reshape(4 * rows, half_z), z)
-            for j, plane in enumerate(cut(zed, rows)):
-                parts[first + j] = left_times(y, plane)
-        place = {k: i for i, k in enumerate([-2, -1, 0, 1, n1 - 2, n1 - 1, n1, n1 + 1])}
+    def kernel(p_ref, a_ref, el, er, z, y, out, ghosts):
+        stack = jnp.concatenate([a_ref[i] for i in (0, 1, n1 + 2, n1 + 3)], axis=0)
+        for i, plane in enumerate(cut(times(stack, z), rows)):
+            ghosts[i] = left_times(y, plane)
 
         def tile(t, carry):
             at = pl.ds(pl.multiple_of(t * 8, 8), 8)
             for lane in range(0, nz, 128):
                 lanes = pl.ds(lane, 128)
-
-                def coeff(k, high):
-                    if k in ends:
-                        return e_ref[4 * high + ends.index(k), at, lanes]
-                    return r_ref[(n1 - 4) * high + k - 2, at, lanes]
-
-                lows = {k: coeff(k, 0) for k in range(n1)}
-                highs = {k: coeff(k, 1) for k in range(n1)}
-                for k, i in place.items():
-                    part = parts[i, at, lanes]
-                    lows[k] = lows[k] + part if k in lows else part
+                lows = {k: p_ref[k, at, lanes] for k in range(n1)}
+                highs = {k: p_ref[n1 + k, at, lanes] for k in range(n1)}
+                for i, k in enumerate((-2, -1, n1, n1 + 1)):
+                    lows[k] = ghosts[i, at, lanes]
                 cells = x_synth_interior(lows, highs, n1)
                 for m in range(nx):
-                    out[m, at, lanes] = cells[m] if m in cells else x_synth(m, lows, highs)
+                    value = cells[m] if m in cells else x_synth(m, lows, highs)
+                    if m < 3:
+                        extra = el[(0, 1, 1)[m], at, lanes]
+                        value += extra if m < 2 else THIRD_UP * extra
+                    if m >= nx - 3:
+                        extra = er[(0, 1, 1)[nx - 1 - m], at, lanes]
+                        value += extra if m > nx - 3 else THIRD_DOWN * extra
+                    out[m, at, lanes] = value
             return carry
 
         lax.fori_loop(0, ny // 8, tile, 0)
@@ -596,8 +611,9 @@
     return whole_call(
         kernel,
         shape(nx, ny, nz),
-        [edge, rest, approx, z_matrix, y_matrix],
-        scratch=[pltpu.VMEM((8, ny, nz), F32)],
+        [parts, approx, left, right, z_matrix, y_matrix],
+        scratch=[pltpu.VMEM((4, ny, nz), F32)],
+        received=[(2, "gx")],
         name="own_result",
     )
 
@@ -628,15 +644,15 @@
 
 
 def second_bands(own, left, right, z_matrix, y_matrix, low_rows):
-    planes, own_rows, nz = own.shape
-    n1 = planes - 4
+    _, own_rows, nz = own.shape
+    n1 = left.shape[0]
     in_rows = own_rows + 2 * left.shape[1]
     rows = y_matrix.shape[0]
 
 
     def kernel(o_ref, l_ref, r_ref, z, y, out, up, down):
-        for i in range(0, planes, 10):
-            stack = [part[j] for j in range(i, i + 10) for part in (o_ref, l_ref, r_ref)]
+        for i in range(0, n1, 8):
+            stack = [part[j] for j in range(i, i + 8) for part in (o_ref, l_ref, r_ref)]
             zed = times_wide(jnp.concatenate(stack, axis=0), z)
             for j, plane in enumerate(in_pairs(y, cut(zed, in_rows))):
                 out[i + j] = plane
@@ -657,7 +673,7 @@
     message = 2 * rows + low_rows
     return whole_call(
         kernel,
-        [shape(planes, rows, nz), shape(message, nz), shape(message, nz)],
+        [shape(n1, rows, nz), shape(message, nz), shape(message, nz)],
         [own, left, right, z_matrix, y_matrix],
         received=[(1, "gy")],
         sent=[(1, "gx")],
@@ -678,30 +694,31 @@
 
 
 def coarse(
-    bands, left, right, halo, h_left, h_right, table, index, za1, yx0, ya1, zs1, za2, zs2, ya2, ys2, ys1,
-    in_rows1, low_rows, out_rows, own_rows, spill_at, spill_rows,
+    bands, left, right, halo, h_left, h_right, approx_in, table, index, za1, yx0, ya1, zs1, za2, zs2, ya2, ys2, ys1,
+    in_rows1, low_rows, out_rows, own_rows, spill_at, spill_rows, wide,
 ):
-    planes_in, rows, nz = bands.shape
-    n1 = planes_in - 4
+    n1, rows, nz = bands.shape
     in_rows = in_rows1
-    wide = h_left.shape[1] - 8
     n2, n3 = n1 // 2, n1 // 4
     rows2 = ya2.shape[0]
     lane_half = nz // 2
 
     def kernel(
-        table_ref, index_ref, b_ref, l_ref, r_ref, x_ref, hl, hr, z1a, yx, a1, z1, z2a, z2s, a2, s2, s1,
+        table_ref, index_ref, b_ref, l_ref, r_ref, x_ref, hl, hr, a_ref, z1a, yx, a1, z1, z2a, z2s, a2, s2, s1,
         approx, up, down, c1, p1,
     ):
         halo_planes = [jnp.concatenate([hl[i, :wide], x_ref[i, :, :nz], hr[i, :wide]], axis=0) for i in range(4)]
-        halo_planes = jnp.concatenate([plane[:in_rows] for plane in in_pairs(yx, halo_planes)], axis=0)
-        hl1, hl2, hr1, hr2 = in_pairs(a1, cut(times_wide(halo_planes, z1a), in_rows))
+        halo_planes = [plane[:in_rows] for plane in in_pairs(yx, halo_planes)]
+        own_planes = [
+            jnp.concatenate([a_ref[n1 + i], hl[i, wide + 8 :], hr[i, wide + 8 :]], axis=0) for i in range(4)
+        ]
+        both = times_wide(jnp.concatenate(halo_planes + own_planes, axis=0), z1a)
+        hl1, hl2, hr1, hr2, xl1, xl2, xr1, xr2 = in_pairs(a1, cut(both, in_rows))
         values = {k: b_ref[k] for k in range(2, n1 - 2)}
         values[0] = b_ref[0] + (hl2 + H[2] * hl1)
         values[1] = b_ref[1] + H[0] * hl1
         values[n1 - 2] = b_ref[n1 - 2] + H[7] * hr1
         values[n1 - 1] = b_ref[n1 - 1] + (hr2 + H[5] * hr1)
-        xl1, xl2, xr1, xr2 = [b_ref[n1 + i] for i in range(4)]
         values["l1"] = l_ref[0:rows] + xl1
         values["l2"] = l_ref[rows : 2 * rows] + xl2
         values["r1"] = r_ref[0:rows] + xr1
@@ -781,7 +798,7 @@
     return whole_call(
         kernel,
         [shape(n1 + 4, out_rows, nz), shape(message, nz), shape(message, nz)],
-        [table, index, bands, left, right, halo, h_left, h_right, za1, yx0, ya1, zs1, za2, zs2, ya2, ys2, ys1],
+        [table, index, bands, left, right, halo, h_left, h_right, approx_in, za1, yx0, ya1, zs1, za2, zs2, ya2, ys2, ys1],
         scratch=[pltpu.VMEM((2 * n2, rows, nz), F32), pltpu.VMEM((2 * n2 + 6, out_rows, nz), F32)],
         received=[(3, "gx"), (6, "gy")],
         sent=[(1, "gx")],
@@ -808,7 +825,7 @@
     return from_approx @ approx
 
 
-def final(left, right, own, e_left, e_right, zs1, ys1, z_matrix, y_matrix, rows, spill_rows):
+def final(left, right, own, zs1, ys1, z_matrix, y_matrix, rows, spill_rows):
     nx, ny, nz = own.shape
     half_z = nz // 2
     own_rows = ny // 2
@@ -816,20 +833,19 @@
     steps = ny // step_rows
     taps = received_taps(nx // 2)
 
-    def kernel(l_ref, r_ref, d_ref, el, er, z1, s1, z, y, out, planes, parts, done, sems):
+    def kernel(l_ref, r_ref, d_ref, z1, s1, z, y, out, planes, parts, done, sems):
         stack = [p for ref in (l_ref, r_ref) for p in unpacked(ref[4 * own_rows + 16 :])]
-        zed = times_wide(jnp.concatenate(stack, axis=0), z1)
-        spilled = [p[:rows] for p in in_pairs(s1, cut(zed, spill_rows))]
+        spilled = cut(times(jnp.concatenate(stack, axis=0), z1), spill_rows)
         for side, ref in enumerate((l_ref, r_ref)):
             for i in range(4):
-                plane = planes.at[6 * side + i]
+                plane = planes.at[4 * side + i]
                 plane[:own_rows] = ref[i * own_rows : (i + 1) * own_rows]
                 plane[own_rows:] = jnp.zeros((rows - own_rows, half_z), F32)
                 plane[own_rows : own_rows + 4] = ref[4 * own_rows + 4 * i : 4 * own_rows + 4 * i + 4]
-            for i in range(2):
-                planes[6 * side + 4 + i] = spilled[2 * side + i]
-        for i, plane in enumerate(cut(times(planes[...].reshape(12 * rows, half_z), z), rows)):
-            parts[i] = left_times(y, plane)
+        for i, plane in enumerate(cut(times(planes[...].reshape(8 * rows, half_z), z), rows)):
+            parts[6 * (i // 4) + i % 4] = left_times(y, plane)
+        for i, plane in enumerate(spilled):
+            parts[6 * (i // 2) + 4 + i % 2] = left_times(s1, plane)
 
         def copy(i):
             at = pl.ds(pl.multiple_of(i * step_rows, step_rows), step_rows)
@@ -844,12 +860,6 @@
                     for m in range(nx):
                         value = d_ref[m, at, lanes]
                         value += added([(float(c), v) for c, v in zip(taps[m], values) if c != 0.0])
-                        if m < 3:
-                            extra = el[(0, 1, 1)[m], at, lanes]
-                            value += extra if m < 2 else THIRD_UP * extra
-                        if m >= nx - 3:
-                            extra = er[(0, 1, 1)[nx - 1 - m], at, lanes]
-                            value += extra if m > nx - 3 else THIRD_DOWN * extra
                         done[m, at, lanes] = value
             copy(i).start()
             return carry
@@ -865,14 +875,14 @@
     return whole_call(
         kernel,
         shape(nx, ny, nz),
-        [left, right, own, e_left, e_right, zs1, ys1, z_matrix, y_matrix],
+        [left, right, own, zs1, ys1, z_matrix, y_matrix],
         scratch=[
-            pltpu.VMEM((12, rows, half_z), F32),
+            pltpu.VMEM((8, rows, half_z), F32),
             pltpu.VMEM((12, ny, nz), F32),
             pltpu.VMEM((nx, ny, nz), F32),
             pltpu.SemaphoreType.DMA((steps,)),
         ],
-        received=[(0, "gx"), (3, "gx")],
+        received=[(0, "gx")],
         name="final",
         out_specs=pl.BlockSpec(memory_space=pl.ANY),
     )
@@ -908,7 +918,8 @@
     yx0 = from_left(analysis_rows(list(range(-wide, ny + wide)), once, []))
     ya1 = from_left(analysis_rows(cells1, low1, high1))
     ys1 = from_left(synthesis_rows(ks0, low1, high1))
-    ys1_spill = from_left(synthesis_rows(ks0, low1[spill_at : spill_at + spill_rows], []))
+    spill_matrix = synthesis_rows(ks0, low1[spill_at : spill_at + spill_rows], [])
+    ys_spill = from_left(ys0_matrix[:, :rows0] @ spill_matrix)
     ya2 = from_left(analysis_rows(low1, ks2, ks2))
     ys2 = from_left(synthesis_rows(low1, ks2, ks2))
     z0 = periodic(nz, nz)
@@ -917,34 +928,35 @@
     za0, zs0, zs0_low = from_right(z0), from_right(z0.T), from_right(z0.T[: nz // 2])
     za1, zs1 = wide_right(z1), wide_right(z1.T)
     za2, zs2 = wide_right(z2), wide_right(z2.T)
+    zs_spill = from_right(z1.T @ z0.T[: nz // 2])
 
     x_up, x_down, y_up, y_down = first_messages(velocity)
     x_left, x_right = exchange(x_up, x_down, "gx")
-    y_left, y_right = exchange(y_up, y_down, "gy")
+    y_here, y_across = exchange(y_up, y_down, "gy")
     zed = depth(velocity, za0, 16, "depth_analysis")
     approx, a_up, a_down = own_approx(zed, yl0, y1, rows0, ghost)
     a_left, a_right = exchange(a_up, a_down, "gy")
     zed, a_up = lax.optimization_barrier((zed, a_up))
-    bands = y_analysis(zed, y_left, y_right, za0, ya0)
+    bands = y_analysis(zed, y_across, y_here, za0, ya0)
     x_left, x_right, bands = lax.optimization_barrier((x_left, x_right, bands))
-    halo, h_up, h_down = x_halo_messages(x_left, x_right, za0, wide)
+    halo, h_up, h_down = x_halo_messages(x_left, x_right, approx, za0, wide, ghost)
     h_left, h_right = exchange(h_up, h_down, "gy")
     approx, halo = lax.optimization_barrier((approx, halo))
     bands1, b_up, b_down = second_bands(approx, a_left, a_right, za1, ya1, rows1)
     b_left, b_right = exchange(b_up, b_down, "gx")
     h_left, h_right, bands1 = lax.optimization_barrier((h_left, h_right, bands1))
-    edge, e_up, e_down = edge_details(bands, halo, h_left, h_right, table, index, ya0, zs0, ys0)
+    edge, e_up, e_down = edge_details(bands, halo, h_left, h_right, table, index, ya0, zs0, ys0, wide)
     e_left, e_right = exchange(e_up, e_down, "gx")
     bands1, edge = lax.optimization_barrier((bands1, edge))
     approx1, s_up, s_down = coarse(
-        bands1, b_left, b_right, halo, h_left, h_right, table, index,
-        za1, yx0, ya1, zs1, za2, zs2, ya2, ys2, ys1, len(cells1), rows1, rows0, y1, spill_at, spill_rows,
+        bands1, b_left, b_right, halo, h_left, h_right, approx, table, index,
+        za1, yx0, ya1, zs1, za2, zs2, ya2, ys2, ys1, len(cells1), rows1, rows0, y1, spill_at, spill_rows, wide,
     )
     s_left, s_right = exchange(s_up, s_down, "gx")
     bands, approx1 = lax.optimization_barrier((bands, approx1))
-    rest = inner_yz(inner_bands(bands, table, index), approx1, zs0, ys0)
-    own = own_result(edge, rest, approx1, zs0_low, ys0_low)
-    return final(s_left, s_right, own, e_left, e_right, zs1, ys1_spill, zs0_low, ys0_low, rows0, spill_rows)
+    parts = detail_yz(edge, inner_bands(bands, table, index), approx1, zs0, ys0)
+    own = own_result(parts, approx1, e_left, e_right, zs0_low, ys0_low)
+    return final(s_left, s_right, own, zs_spill, ys_spill, zs0_low, ys0_low, rows0, spill_rows)
 
 
 def solution(mesh):

time: 53.1 us -> 52.4 us (0.987)
  waiting for transfers between devices: 6.13 us -> 4.69 us
  starting transfers between devices: 18.5 us -> 19.3 us
    ppermute x14, waiting for transfers between devices: 6.13 us -> 4.69 us  [exchange(): return (lax.ppermute(first, axis, here), lax.ppermute(second, axis, across))]
    ppermute x14, starting transfers between devices: 18.5 us -> 19.3 us  [exchange(): return (lax.ppermute(first, axis, here), lax.ppermute(second, axis, across))]
    unnamed x40 -> x42, local copies, waits for them, and re-layouts: 1.11 us -> 1.12 us
  transfers between devices with their start and end apart: 14 -> 14, of which waited for: 4 -> 3; matrix products, arithmetic and copies ran while one was open for 0% -> 0% of each run, Pallas kernels for 41% -> 42%
where the time goes in v9:
time: 52.4 us; the launch traced here: 52.3 us
  Pallas kernels  26.8 us (51%)
  starting transfers between devices  19.3 us (37%)
  waiting for transfers between devices  4.69 us (9%)
  local copies, waits for them, and re-layouts  1.12 us (2%)
    pallas_call x12, Pallas kernels, whole_call(): pl.pallas_call(kernel, in_specs=changes.get('in_specs', specs), out_specs...  26.8 us
    ppermute x14, starting transfers between devices, exchange(): return (lax.ppermute(first, axis, here), lax.ppermute(second, axis, across))  19.3 us
    ppermute x14, waiting for transfers between devices, exchange(): return (lax.ppermute(first, axis, here), lax.ppermute(second, axis, across))  4.69 us
    unnamed x42, local copies, waits for them, and re-layouts  1.12 us
  transfers between devices with their start and end apart: 14, of which 3 were waited for; matrix products, arithmetic and copies ran while one was open for 0% of the time, Pallas kernels for 42%

profile of v9, /device:TPU:0, one launch (start us, length us, event | category | flops | bytes accessed | tf_op | source)
XLA Modules:
  0.0 52.3 jit_solution(12574899634683900609)
XLA Ops:
  0.0 1.6 %first_messages.1 = (f32[2,128,256]{2,1,0:T(8,128)S(1)}, f32[2,128,256]{2,1,0:T(8,128)S(1)}, f32[28,8,256]{2,1,0:T(8,128)S(1)}, f32[28,8,256]{2,1,0:T(8,128)S(1)}) custom-call(f32[32,128,256]{2,1,0:T(8,128)} %refs_0_.6), custom_call_target="tpu_custom_call" | custom-call | flops 1000 | bytes 1000 | tf_op jit(solution)/shard_map/first_messages/pallas_call | solution.py:250
  1.6 2.5 %collective-permute-start.2 = (f32[28,8,256]{2,1,0:T(8,128)S(1)}, f32[28,8,256]{2,1,0:T(8,128)S(1)}, u32[]{:S(2)}, u32[]{:S(2)}) collective-permute-start(f32[28,8,256]{2,1,0:T(8,128)S(1)} %get-tuple-element.41), channel_id=1, source_target_pairs={{0,3},{1,2},{2,1},{3,0},{4,7},{5,6},{6,5},{7,4},{8,11},{9,10},{10,... | collective-permute-start | bytes 688136 | tf_op jit(solution)/shard_map/ppermute | solution.py:896
  4.1 1.5 %collective-permute-start = (f32[2,128,256]{2,1,0:T(8,128)S(1)}, f32[2,128,256]{2,1,0:T(8,128)S(1)}, u32[]{:S(2)}, u32[]{:S(2)}) collective-permute-start(f32[2,128,256]{2,1,0:T(8,128)S(1)} %get-tuple-element.37), channel_id=1, source_target_pairs={{0,4},{4,0},{8,12},{12,8},{16,20},{20,16},{24,28},{28,24},{1,5},{5... | collective-permute-start | bytes 786440 | tf_op jit(solution)/shard_map/ppermute | solution.py:896
  5.6 3.6 %collective-permute-start.1 = (f32[2,128,256]{2,1,0:T(8,128)S(1)}, f32[2,128,256]{2,1,0:T(8,128)S(1)}, u32[]{:S(2)}, u32[]{:S(2)}) collective-permute-start(f32[2,128,256]{2,1,0:T(8,128)S(1)} %get-tuple-element.38), channel_id=1, source_target_pairs={{0,28},{4,8},{8,4},{12,16},{16,12},{20,24},{24,20},{28,0},{1,29},{... | collective-permute-start | bytes 786440 | tf_op jit(solution)/shard_map/ppermute | solution.py:896
  9.2 0.1 collective-permute-start.3
  9.3 1.0 %copy-done.1 = bf16[768,256]{1,0:T(8,128)(2,1)S(1)} copy-done((bf16[768,256]{1,0:T(8,128)(2,1)S(1)}, bf16[768,256]{1,0:T(8,128)(2,1)}, u32[]{:S(2)}) %copy-start.1) | copy-done | bytes 393240
  10.3 2.0 %depth_analysis.1.refs_0_ = f32[32,128,256]{2,1,0:T(8,128)S(1)} custom-call(f32[32,128,256]{2,1,0:T(8,128)S(1)} %copy-done, bf16[768,256]{1,0:T(8,128)(2,1)S(1)} %copy-done.1), custom_call_target="tpu_custom_call" | custom-call | flops 1000 | bytes 1000 | tf_op jit(solution)/shard_map/depth_analysis/pallas_call | solution.py:250
  12.3 0.0 copy-start.4
  12.3 1.5 %own_approx.1 = (f32[20,72,128]{2,1,0:T(8,128)S(1)}, f32[16,24,128]{2,1,0:T(8,128)S(1)}, f32[16,24,128]{2,1,0:T(8,128)S(1)}) custom-call(f32[32,128,256]{2,1,0:T(8,128)S(1)} %depth_analysis.1.refs_0_, bf16[80,384]{1,0:T(8,128)(2,1)S(1)} %copy-done.15), custom_call_target="tpu_custom_call" | custom-call | flops 1000 | bytes 1000 | tf_op jit(solution)/shard_map/own_approx/pallas_call | solution.py:250
  13.9 0.7 %collective-permute-start.7 = (f32[16,24,128]{2,1,0:T(8,128)S(1)}, f32[16,24,128]{2,1,0:T(8,128)S(1)}, u32[]{:S(2)}, u32[]{:S(2)}) collective-permute-start(f32[16,24,128]{2,1,0:T(8,128)S(1)} %get-tuple-element.50), channel_id=1, source_target_pairs={{0,3},{1,2},{2,1},{3,0},{4,7},{5,6},{6,5},{7,4},{8,11},{9,10},{10,... | collective-permute-start | bytes 589832 | tf_op jit(solution)/shard_map/ppermute | solution.py:896
  14.5 0.0 collective-permute-done.2.refs_1_
  14.6 0.0 copy-start.5
  14.6 0.0 copy-start.19
  14.6 0.0 copy-start.20
  14.6 0.1 collective-permute-start.6
  14.7 0.0 collective-permute-done.3.refs_2_
  14.7 2.4 %y_analysis.1.refs_2_ = f32[32,144,256]{2,1,0:T(8,128)S(1)} custom-call(f32[32,128,256]{2,1,0:T(8,128)S(1)} %depth_analysis.1.refs_0_, f32[28,8,256]{2,1,0:T(8,128)S(1)} %collective-permute-done.2.refs_1_, f32[28,8,256]{2,1,0:T(8,128)S(1)} %collective-permute-done.3.refs_2_, bf16[768,256]{1,0:T(8,128)(2,1)S(1)} %copy-done.1, bf16[144,432]{1,0:T(8,128)(2,1)S(1)} %copy-done.4), custom_call_target="tpu_custom_call" | custom-call | flops 1000 | bytes 1000 | tf_op jit(solution)/shard_map/y_analysis/pallas_call | solution.py:250
  17.1 1.5 %collective-permute-done.refs_0_ = f32[2,128,256]{2,1,0:T(8,128)S(1)} collective-permute-done((f32[2,128,256]{2,1,0:T(8,128)S(1)}, f32[2,128,256]{2,1,0:T(8,128)S(1)}, u32[]{:S(2)}, u32[]{:S(2)}) %collective-permute-start) | collective-permute-done | bytes 262176 | tf_op jit(solution)/shard_map/ppermute | solution.py:896
  18.6 0.4 x_halo_messages.1
  19.0 0.0 copy-start.9
  19.1 0.0 copy-start.11
  19.1 0.0 copy-start.12
  19.1 0.0 copy-start.13
  19.1 0.0 copy-start.16
  19.1 0.0 copy-start.17
  19.1 0.0 copy-start.18
  19.1 0.1 collective-permute-start.4
  19.2 0.4 collective-permute-start.5
  19.6 1.1 %collective-permute-done.7.refs_2_ = f32[16,24,128]{2,1,0:T(8,128)S(1)} collective-permute-done((f32[16,24,128]{2,1,0:T(8,128)S(1)}, f32[16,24,128]{2,1,0:T(8,128)S(1)}, u32[]{:S(2)}, u32[]{:S(2)}) %collective-permute-start.7) | collective-permute-done | bytes 196640 | tf_op jit(solution)/shard_map/ppermute | solution.py:896
  20.7 1.2 %second_bands.1 = (f32[16,96,128]{2,1,0:T(8,128)S(1)}, f32[248,128]{1,0:T(8,128)S(1)}, f32[248,128]{1,0:T(8,128)S(1)}) custom-call(f32[20,72,128]{2,1,0:T(8,128)S(1)} %get-tuple-element.49.refs_2_.refs_0_.refs_8_, f32[16,24,128]{2,1,0:T(8,128)S(1)} %collective-permute-done.6.refs_1_, f32[16,24,128]{2,1,0:T(8,128)S(1)} %collective-permute-done.7.refs_2_, ...), custom_call_target="tpu_custom_call" | custom-call | flops 1000 | bytes 1000 | tf_op jit(solution)/shard_map/second_bands/pallas_call | solution.py:250
  21.9 0.7 %collective-permute-start.8 = (f32[248,128]{1,0:T(8,128)S(1)}, f32[248,128]{1,0:T(8,128)S(1)}, u32[]{:S(2)}, u32[]{:S(2)}) collective-permute-start(f32[248,128]{1,0:T(8,128)S(1)} %get-tuple-element.59), channel_id=1, source_target_pairs={{0,4},{4,0},{8,12},{12,8},{16,20},{20,16},{24,28},{28,24},{1,5},{5... | collective-permute-start | bytes 380936 | tf_op jit(solution)/shard_map/ppermute | solution.py:896
  22.6 3.6 %collective-permute-start.9 = (f32[248,128]{1,0:T(8,128)S(1)}, f32[248,128]{1,0:T(8,128)S(1)}, u32[]{:S(2)}, u32[]{:S(2)}) collective-permute-start(f32[248,128]{1,0:T(8,128)S(1)} %get-tuple-element.60), channel_id=1, source_target_pairs={{0,28},{4,8},{8,4},{12,16},{16,12},{20,24},{24,20},{28,0},{1,29},{... | collective-permute-start | bytes 380936 | tf_op jit(solution)/shard_map/ppermute | solution.py:896
  26.2 0.0 collective-permute-done.4.refs_4_.refs_6_
  26.2 2.5 %edge_details.1 = (f32[8,144,256]{2,1,0:T(8,128)S(1)}, f32[2,128,256]{2,1,0:T(8,128)S(1)}, f32[2,128,256]{2,1,0:T(8,128)S(1)}) custom-call(f32[16]{0:T(128)S(1)} %copy-done.20, s32[3,7]{1,0:T(4,128)S(1)} %copy-done.19, f32[32,144,256]{2,1,0:T(8,128)S(1)} %y_analysis.1.refs_2_, f32[4,128,256]{2,1,0:T(8,128)S(1)} %get-tuple-element.54.refs_3_.refs_5_, ...), custom_call_target="tpu_custom_call" | custom-call | flops 1000 | bytes 1000 | tf_op jit(solution)/shard_map/edge_details/pallas_call | solution.py:250
  28.7 0.6 %collective-permute-start.12 = (f32[2,128,256]{2,1,0:T(8,128)S(1)}, f32[2,128,256]{2,1,0:T(8,128)S(1)}, u32[]{:S(2)}, u32[]{:S(2)}) collective-permute-start(f32[2,128,256]{2,1,0:T(8,128)S(1)} %get-tuple-element.67), channel_id=1, source_target_pairs={{0,4},{4,0},{8,12},{12,8},{16,20},{20,16},{24,28},{28,24},{1,5},{5... | collective-permute-start | bytes 786440 | tf_op jit(solution)/shard_map/ppermute | solution.py:896
  29.3 3.6 %collective-permute-start.13 = (f32[2,128,256]{2,1,0:T(8,128)S(1)}, f32[2,128,256]{2,1,0:T(8,128)S(1)}, u32[]{:S(2)}, u32[]{:S(2)}) collective-permute-start(f32[2,128,256]{2,1,0:T(8,128)S(1)} %get-tuple-element.68), channel_id=1, source_target_pairs={{0,28},{4,8},{8,4},{12,16},{16,12},{20,24},{24,20},{28,0},{1,29},{... | collective-permute-start | bytes 786440 | tf_op jit(solution)/shard_map/ppermute | solution.py:896
  33.0 3.5 %coarse.1 = (f32[20,72,128]{2,1,0:T(8,128)S(1)}, f32[312,128]{1,0:T(8,128)S(1)}, f32[312,128]{1,0:T(8,128)S(1)}) custom-call(f32[16]{0:T(128)S(1)} %copy-done.20, s32[3,7]{1,0:T(4,128)S(1)} %copy-done.19, f32[16,96,128]{2,1,0:T(8,128)S(1)} %get-tuple-element.58.refs_2_, f32[248,128]{1,0:T(8,128)S(1)} %collective-permute-done.8.refs_3_, ...), custom_call_target="tpu_custom_call" | custom-call | flops 1000 | bytes 1000 | tf_op jit(solution)/shard_map/coarse/pallas_call | solution.py:250
  36.4 0.1 collective-permute-start.10
  36.5 1.9 %collective-permute-start.11 = (f32[312,128]{1,0:T(8,128)S(1)}, f32[312,128]{1,0:T(8,128)S(1)}, u32[]{:S(2)}, u32[]{:S(2)}) collective-permute-start(f32[312,128]{1,0:T(8,128)S(1)} %get-tuple-element.62), channel_id=1, source_target_pairs={{0,28},{4,8},{8,4},{12,16},{16,12},{20,24},{24,20},{28,0},{1,29},{... | collective-permute-start | bytes 479240 | tf_op jit(solution)/shard_map/ppermute | solution.py:896
  38.4 2.1 %inner_bands.1.refs_1_ = f32[24,144,256]{2,1,0:T(8,128)S(1)} custom-call(f32[16]{0:T(128)S(1)} %copy-done.20, s32[3,7]{1,0:T(4,128)S(1)} %copy-done.19, f32[32,144,256]{2,1,0:T(8,128)S(1)} %y_analysis.1.refs_2_), custom_call_target="tpu_custom_call" | custom-call | flops 1000 | bytes 1000 | tf_op jit(solution)/shard_map/inner_bands/pallas_call | solution.py:250
  40.5 0.0 copy-start.3
  40.5 0.0 copy-start.8
  40.5 4.5 %detail_yz.1.refs_0_ = f32[32,128,256]{2,1,0:T(8,128)S(1)} custom-call(f32[8,144,256]{2,1,0:T(8,128)S(1)} %get-tuple-element.63.refs_0_, f32[24,144,256]{2,1,0:T(8,128)S(1)} %inner_bands.1.refs_1_, f32[20,72,128]{2,1,0:T(8,128)S(1)} %get-tuple-element.66.refs_2_.refs_1_, bf16[768,256]{1,0:T(8,128)(2,1)S(1)} %copy-done.2, bf16[128,432]{1,0:T(8,128)(2,1)S(1)} %copy-done.5), custom_call_target="tpu_custom_call" | custom-call | flops 1000 | bytes 1000 | tf_op jit(solution)/shard_map/detail_yz/pallas_call | solution.py:250
  45.0 0.0 copy-start.10
  45.0 0.0 copy-start.14
  45.0 2.0 %collective-permute-done.12.refs_2_ = f32[2,128,256]{2,1,0:T(8,128)S(1)} collective-permute-done((f32[2,128,256]{2,1,0:T(8,128)S(1)}, f32[2,128,256]{2,1,0:T(8,128)S(1)}, u32[]{:S(2)}, u32[]{:S(2)}) %collective-permute-start.12) | collective-permute-done | bytes 262176 | tf_op jit(solution)/shard_map/ppermute | solution.py:896
  47.1 2.1 %own_result.1.refs_2_ = f32[32,128,256]{2,1,0:T(8,128)S(1)} custom-call(f32[32,128,256]{2,1,0:T(8,128)S(1)} %detail_yz.1.refs_0_, f32[20,72,128]{2,1,0:T(8,128)S(1)} %get-tuple-element.66.refs_2_.refs_1_, f32[2,128,256]{2,1,0:T(8,128)S(1)} %collective-permute-done.12.refs_2_, f32[2,128,256]{2,1,0:T(8,128)S(1)} %collective-permute-done.13.refs_3_, ...), custom_call_target="tpu_custom_call" | custom-call | flops 1000 | bytes 1000 | tf_op jit(solution)/shard_map/own_result/pallas_call | solution.py:250
  49.2 3.0 %final.1 = f32[32,128,256]{2,1,0:T(8,128)} custom-call(f32[312,128]{1,0:T(8,128)S(1)} %collective-permute-done.10.refs_0_, f32[312,128]{1,0:T(8,128)S(1)} %collective-permute-done.11.refs_1_, f32[32,128,256]{2,1,0:T(8,128)S(1)} %own_result.1.refs_2_, bf16[384,256]{1,0:T(8,128)(2,1)S(1)} %copy-done.10, bf16[128,144]{1,0:T(8,128)(2,1)S(1)} %copy-done.14, ...), custom_call_target="tpu_custom_call" | custom-call | flops 1000 | bytes 1000 | tf_op jit(solution)/shard_map/final/pallas_call | solution.py:250
  (34 shorter events, 0.1 us)
Async XLA Ops:
  0.0 9.3 %copy-start = (f32[32,128,256]{2,1,0:T(8,128)S(1)}, f32[32,128,256]{2,1,0:T(8,128)}, u32[]{:S(2)}) copy-start(f32[32,128,256]{2,1,0:T(8,128)} %refs_0_.6) | copy-start | bytes 12582916
  1.6 12.9 %collective-permute-start.2 = (f32[28,8,256]{2,1,0:T(8,128)S(1)}, f32[28,8,256]{2,1,0:T(8,128)S(1)}, u32[]{:S(2)}, u32[]{:S(2)}) collective-permute-start(f32[28,8,256]{2,1,0:T(8,128)S(1)} %get-tuple-element.41), channel_id=1, source_target_pairs={{0,3},{1,2},{2,1},{3,0},{4,7},{5,6},{6,5},{7,4},{8,11},{9,10},{10,... | collective-permute-start | bytes 688136 | tf_op jit(solution)/shard_map/ppermute | solution.py:896
  4.1 14.5 %collective-permute-start = (f32[2,128,256]{2,1,0:T(8,128)S(1)}, f32[2,128,256]{2,1,0:T(8,128)S(1)}, u32[]{:S(2)}, u32[]{:S(2)}) collective-permute-start(f32[2,128,256]{2,1,0:T(8,128)S(1)} %get-tuple-element.37), channel_id=1, source_target_pairs={{0,4},{4,0},{8,12},{12,8},{16,20},{20,16},{24,28},{28,24},{1,5},{5... | collective-permute-start | bytes 786440 | tf_op jit(solution)/shard_map/ppermute | solution.py:896
  5.6 13.0 %collective-permute-start.1 = (f32[2,128,256]{2,1,0:T(8,128)S(1)}, f32[2,128,256]{2,1,0:T(8,128)S(1)}, u32[]{:S(2)}, u32[]{:S(2)}) collective-permute-start(f32[2,128,256]{2,1,0:T(8,128)S(1)} %get-tuple-element.38), channel_id=1, source_target_pairs={{0,28},{4,8},{8,4},{12,16},{16,12},{20,24},{24,20},{28,0},{1,29},{... | collective-permute-start | bytes 786440 | tf_op jit(solution)/shard_map/ppermute | solution.py:896
  9.2 5.5 %collective-permute-start.3 = (f32[28,8,256]{2,1,0:T(8,128)S(1)}, f32[28,8,256]{2,1,0:T(8,128)S(1)}, u32[]{:S(2)}, u32[]{:S(2)}) collective-permute-start(f32[28,8,256]{2,1,0:T(8,128)S(1)} %get-tuple-element.42), channel_id=1, source_target_pairs={{0,1},{1,0},{2,3},{3,2},{4,5},{5,4},{6,7},{7,6},{8,9},{9,8},{10,11... | collective-permute-start | bytes 688136 | tf_op jit(solution)/shard_map/ppermute | solution.py:896
  9.3 1.0 %copy-start.1 = (bf16[768,256]{1,0:T(8,128)(2,1)S(1)}, bf16[768,256]{1,0:T(8,128)(2,1)}, u32[]{:S(2)}) copy-start(bf16[768,256]{1,0:T(8,128)(2,1)} %constant.36.clone.refs_1_.refs_3_) | copy-start | bytes 1179652
  10.3 2.0 %copy-start.15 = (bf16[80,384]{1,0:T(8,128)(2,1)S(1)}, bf16[80,384]{1,0:T(8,128)(2,1)}, u32[]{:S(2)}) copy-start(bf16[80,384]{1,0:T(8,128)(2,1)} %constant.37.clone.refs_1_) | copy-start | bytes 184324
  12.3 2.4 %copy-start.4 = (bf16[144,432]{1,0:T(8,128)(2,1)S(1)}, bf16[144,432]{1,0:T(8,128)(2,1)}, u32[]{:S(2)}) copy-start(bf16[144,432]{1,0:T(8,128)(2,1)} %constant.38.clone.refs_4_.refs_6_) | copy-start | bytes 373252
  13.9 6.8 %collective-permute-start.7 = (f32[16,24,128]{2,1,0:T(8,128)S(1)}, f32[16,24,128]{2,1,0:T(8,128)S(1)}, u32[]{:S(2)}, u32[]{:S(2)}) collective-permute-start(f32[16,24,128]{2,1,0:T(8,128)S(1)} %get-tuple-element.50), channel_id=1, source_target_pairs={{0,3},{1,2},{2,1},{3,0},{4,7},{5,6},{6,5},{7,4},{8,11},{9,10},{10,... | collective-permute-start | bytes 589832 | tf_op jit(solution)/shard_map/ppermute | solution.py:896
  14.5 6.2 %copy-start.6 = (bf16[256,256]{1,0:T(8,128)(2,1)S(1)}, bf16[256,256]{1,0:T(8,128)(2,1)}, u32[]{:S(2)}) copy-start(bf16[256,256]{1,0:T(8,128)(2,1)} %constant.39.clone.refs_3_.refs_9_) | copy-start | bytes 393220
  14.5 6.2 %copy-start.7 = (bf16[96,384]{1,0:T(8,128)(2,1)S(1)}, bf16[96,384]{1,0:T(8,128)(2,1)}, u32[]{:S(2)}) copy-start(bf16[96,384]{1,0:T(8,128)(2,1)} %constant.40.clone.refs_4_.refs_11_) | copy-start | bytes 221188
  14.5 11.6 %copy-start.2 = (bf16[768,256]{1,0:T(8,128)(2,1)S(1)}, bf16[768,256]{1,0:T(8,128)(2,1)}, u32[]{:S(2)}) copy-start(bf16[768,256]{1,0:T(8,128)(2,1)} %constant.41.clone.refs_7_.refs_3_) | copy-start | bytes 1179652
  14.6 11.6 %copy-start.5 = (bf16[128,432]{1,0:T(8,128)(2,1)S(1)}, bf16[128,432]{1,0:T(8,128)(2,1)}, u32[]{:S(2)}) copy-start(bf16[128,432]{1,0:T(8,128)(2,1)} %constant.42.clone.refs_8_.refs_4_) | copy-start | bytes 331780
  14.6 11.6 %copy-start.19 = (s32[3,7]{1,0:T(4,128)S(1)}, s32[3,7]{1,0:T(4,128)}, u32[]{:S(2)}) copy-start(s32[3,7]{1,0:T(4,128)} %refs_1_.7) | copy-start | bytes 256
  14.6 11.6 %copy-start.20 = (f32[16]{0:T(128)S(1)}, f32[16]{0:T(128)}, u32[]{:S(2)}) copy-start(f32[16]{0:T(128)} %refs_0_.9) | copy-start | bytes 196
  14.6 6.1 %collective-permute-start.6 = (f32[16,24,128]{2,1,0:T(8,128)S(1)}, f32[16,24,128]{2,1,0:T(8,128)S(1)}, u32[]{:S(2)}, u32[]{:S(2)}) collective-permute-start(f32[16,24,128]{2,1,0:T(8,128)S(1)} %get-tuple-element.39), channel_id=1, source_target_pairs={{0,1},{1,0},{2,3},{3,2},{4,5},{5,4},{6,7},{7,6},{8,9},{9,8},{10,11... | collective-permute-start | bytes 589832 | tf_op jit(solution)/shard_map/ppermute | solution.py:896
  19.0 13.9 %copy-start.9 = (bf16[128,672]{1,0:T(8,128)(2,1)S(1)}, bf16[128,672]{1,0:T(8,128)(2,1)}, u32[]{:S(2)}) copy-start(bf16[128,672]{1,0:T(8,128)(2,1)} %constant.43.clone.refs_10_) | copy-start | bytes 516100
  19.1 13.8 %copy-start.11 = (bf16[256,256]{1,0:T(8,128)(2,1)S(1)}, bf16[256,256]{1,0:T(8,128)(2,1)}, u32[]{:S(2)}) copy-start(bf16[256,256]{1,0:T(8,128)(2,1)} %constant.46.clone.refs_14_) | copy-start | bytes 393220
  19.1 13.8 %copy-start.12 = (bf16[256,256]{1,0:T(8,128)(2,1)S(1)}, bf16[256,256]{1,0:T(8,128)(2,1)}, u32[]{:S(2)}) copy-start(bf16[256,256]{1,0:T(8,128)(2,1)} %constant.45.clone.refs_13_) | copy-start | bytes 393220
  19.1 13.8 %copy-start.13 = (bf16[256,256]{1,0:T(8,128)(2,1)S(1)}, bf16[256,256]{1,0:T(8,128)(2,1)}, u32[]{:S(2)}) copy-start(bf16[256,256]{1,0:T(8,128)(2,1)} %constant.44.clone.refs_12_) | copy-start | bytes 393220
  19.1 13.8 %copy-start.16 = (bf16[80,288]{1,0:T(8,128)(2,1)S(1)}, bf16[80,288]{1,0:T(8,128)(2,1)}, u32[]{:S(2)}) copy-start(bf16[80,288]{1,0:T(8,128)(2,1)} %constant.49.clone.refs_17_) | copy-start | bytes 138244
  19.1 13.8 %copy-start.17 = (bf16[64,144]{1,0:T(8,128)(2,1)S(1)}, bf16[64,144]{1,0:T(8,128)(2,1)}, u32[]{:S(2)}) copy-start(bf16[64,144]{1,0:T(8,128)(2,1)} %constant.48.clone.refs_16_) | copy-start | bytes 55300
  19.1 13.8 %copy-start.18 = (bf16[48,192]{1,0:T(8,128)(2,1)S(1)}, bf16[48,192]{1,0:T(8,128)(2,1)}, u32[]{:S(2)}) copy-start(bf16[48,192]{1,0:T(8,128)(2,1)} %constant.47.clone.refs_15_) | copy-start | bytes 55300
  19.1 7.0 %collective-permute-start.4 = (f32[4,80,128]{2,1,0:T(8,128)S(1)}, f32[4,80,128]{2,1,0:T(8,128)S(1)}, u32[]{:S(2)}, u32[]{:S(2)}) collective-permute-start(f32[4,80,128]{2,1,0:T(8,128)S(1)} %get-tuple-element.46), channel_id=1, source_target_pairs={{0,1},{1,0},{2,3},{3,2},{4,5},{5,4},{6,7},{7,6},{8,9},{9,8},{10,11... | collective-permute-start | bytes 491528 | tf_op jit(solution)/shard_map/ppermute | solution.py:896
  19.2 6.9 %collective-permute-start.5 = (f32[4,80,128]{2,1,0:T(8,128)S(1)}, f32[4,80,128]{2,1,0:T(8,128)S(1)}, u32[]{:S(2)}, u32[]{:S(2)}) collective-permute-start(f32[4,80,128]{2,1,0:T(8,128)S(1)} %get-tuple-element.47), channel_id=1, source_target_pairs={{0,3},{1,2},{2,1},{3,0},{4,7},{5,6},{6,5},{7,4},{8,11},{9,10},{10,... | collective-permute-start | bytes 491528 | tf_op jit(solution)/shard_map/ppermute | solution.py:896
  21.9 11.0 %collective-permute-start.8 = (f32[248,128]{1,0:T(8,128)S(1)}, f32[248,128]{1,0:T(8,128)S(1)}, u32[]{:S(2)}, u32[]{:S(2)}) collective-permute-start(f32[248,128]{1,0:T(8,128)S(1)} %get-tuple-element.59), channel_id=1, source_target_pairs={{0,4},{4,0},{8,12},{12,8},{16,20},{20,16},{24,28},{28,24},{1,5},{5... | collective-permute-start | bytes 380936 | tf_op jit(solution)/shard_map/ppermute | solution.py:896
  22.6 10.3 %collective-permute-start.9 = (f32[248,128]{1,0:T(8,128)S(1)}, f32[248,128]{1,0:T(8,128)S(1)}, u32[]{:S(2)}, u32[]{:S(2)}) collective-permute-start(f32[248,128]{1,0:T(8,128)S(1)} %get-tuple-element.60), channel_id=1, source_target_pairs={{0,28},{4,8},{8,4},{12,16},{16,12},{20,24},{24,20},{28,0},{1,29},{... | collective-permute-start | bytes 380936 | tf_op jit(solution)/shard_map/ppermute | solution.py:896
  28.7 18.3 %collective-permute-start.12 = (f32[2,128,256]{2,1,0:T(8,128)S(1)}, f32[2,128,256]{2,1,0:T(8,128)S(1)}, u32[]{:S(2)}, u32[]{:S(2)}) collective-permute-start(f32[2,128,256]{2,1,0:T(8,128)S(1)} %get-tuple-element.67), channel_id=1, source_target_pairs={{0,4},{4,0},{8,12},{12,8},{16,20},{20,16},{24,28},{28,24},{1,5},{5... | collective-permute-start | bytes 786440 | tf_op jit(solution)/shard_map/ppermute | solution.py:896
  29.3 17.7 %collective-permute-start.13 = (f32[2,128,256]{2,1,0:T(8,128)S(1)}, f32[2,128,256]{2,1,0:T(8,128)S(1)}, u32[]{:S(2)}, u32[]{:S(2)}) collective-permute-start(f32[2,128,256]{2,1,0:T(8,128)S(1)} %get-tuple-element.68), channel_id=1, source_target_pairs={{0,28},{4,8},{8,4},{12,16},{16,12},{20,24},{24,20},{28,0},{1,29},{... | collective-permute-start | bytes 786440 | tf_op jit(solution)/shard_map/ppermute | solution.py:896
  36.4 12.7 %collective-permute-start.10 = (f32[312,128]{1,0:T(8,128)S(1)}, f32[312,128]{1,0:T(8,128)S(1)}, u32[]{:S(2)}, u32[]{:S(2)}) collective-permute-start(f32[312,128]{1,0:T(8,128)S(1)} %get-tuple-element.61), channel_id=1, source_target_pairs={{0,4},{4,0},{8,12},{12,8},{16,20},{20,16},{24,28},{28,24},{1,5},{5... | collective-permute-start | bytes 479240 | tf_op jit(solution)/shard_map/ppermute | solution.py:896
  36.5 12.7 %collective-permute-start.11 = (f32[312,128]{1,0:T(8,128)S(1)}, f32[312,128]{1,0:T(8,128)S(1)}, u32[]{:S(2)}, u32[]{:S(2)}) collective-permute-start(f32[312,128]{1,0:T(8,128)S(1)} %get-tuple-element.62), channel_id=1, source_target_pairs={{0,28},{4,8},{8,4},{12,16},{16,12},{20,24},{24,20},{28,0},{1,29},{... | collective-permute-start | bytes 479240 | tf_op jit(solution)/shard_map/ppermute | solution.py:896
  40.5 6.6 %copy-start.3 = (bf16[384,256]{1,0:T(8,128)(2,1)S(1)}, bf16[384,256]{1,0:T(8,128)(2,1)}, u32[]{:S(2)}) copy-start(bf16[384,256]{1,0:T(8,128)(2,1)} %constant.50.clone.refs_4_.refs_5_) | copy-start | bytes 589828
  40.5 6.6 %copy-start.8 = (bf16[128,240]{1,0:T(8,128)(2,1)S(1)}, bf16[128,240]{1,0:T(8,128)(2,1)}, u32[]{:S(2)}) copy-start(bf16[128,240]{1,0:T(8,128)(2,1)} %constant.51.clone.refs_5_.refs_6_) | copy-start | bytes 184324
  45.0 4.2 %copy-start.10 = (bf16[384,256]{1,0:T(8,128)(2,1)S(1)}, bf16[384,256]{1,0:T(8,128)(2,1)}, u32[]{:S(2)}) copy-start(bf16[384,256]{1,0:T(8,128)(2,1)} %constant.52.clone.refs_3_) | copy-start | bytes 589828
  45.0 4.2 %copy-start.14 = (bf16[128,144]{1,0:T(8,128)(2,1)S(1)}, bf16[128,144]{1,0:T(8,128)(2,1)}, u32[]{:S(2)}) copy-start(bf16[128,144]{1,0:T(8,128)(2,1)} %constant.53.clone.refs_4_) | copy-start | bytes 110596

commit v10 on v9

--- a/solution.py
+++ b/solution.py
@@ -494,8 +494,24 @@
     over_planes(count, 4, y_body)
 
 
-def edge_details(bands, halo, h_left, h_right, table, index, ya_matrix, z_matrix, y_matrix, wide):
+def edge_own(bands):
     nx, rows, nz = bands.shape
+
+    def kernel(b_ref, out):
+        def body(at, lanes, by, bz):
+            values = {i: b_ref[i, at, lanes] for i in [*range(7), *range(nx - 7, nx)]}
+            for i, k in enumerate(edges_of(nx // 2)):
+                terms = [t for t in x_terms(k, nx) if t[0] in values]
+                out[i, at, lanes] = added([(low, values[key]) for key, low, _ in terms])
+                out[4 + i, at, lanes] = added([(high, values[key]) for key, _, high in terms])
+
+        over_tiles(rows, nz, body)
+
+    return whole_call(kernel, shape(8, rows, nz), [bands], name="edge_own")
+
+
+def edge_details(nx, own, halo, h_left, h_right, table, index, ya_matrix, z_matrix, y_matrix, wide):
+    _, rows, nz = own.shape
     ny = y_matrix.shape[0]
     n1 = nx // 2
     half_z = nz // 2
@@ -513,10 +529,11 @@
         def body(at, lanes, by, bz):
             quiet, loud = band_limits(table_ref, index_ref, by, bz)
             values = {key: h_ref[i, at, lanes] for key, i in place.items()}
-            values.update({i: b_ref[i, at, lanes] for i in [*range(7), *range(nx - 7, nx)]})
             lows, highs = {}, {}
             for i, k in enumerate(ends):
-                low, high = x_low(values.get, k, nx), x_high(values.get, k, nx)
+                terms = [t for t in x_terms(k, nx) if t[0] in values]
+                low = b_ref[i, at, lanes] + added([(c, values[key]) for key, c, _ in terms])
+                high = b_ref[4 + i, at, lanes] + added([(c, values[key]) for key, _, c in terms])
                 lows[k] = shrink(low, quiet) if by + bz else jnp.zeros_like(low)
                 highs[k] = shrink(high, loud)
                 coeffs[i, at, lanes] = lows[k]
@@ -533,7 +550,7 @@
     return whole_call(
         kernel,
         [shape(8, rows, nz), shape(2, ny, nz), shape(2, ny, nz)],
-        [table, index, bands, halo, h_left, h_right, ya_matrix, z_matrix, y_matrix],
+        [table, index, own, halo, h_left, h_right, ya_matrix, z_matrix, y_matrix],
         scratch=[pltpu.VMEM((4, rows, nz), F32)] * 3,
         received=[(4, "gy")],
         sent=[(1, "gx")],
@@ -938,14 +955,15 @@
     a_left, a_right = exchange(a_up, a_down, "gy")
     zed, a_up = lax.optimization_barrier((zed, a_up))
     bands = y_analysis(zed, y_across, y_here, za0, ya0)
-    x_left, x_right, bands = lax.optimization_barrier((x_left, x_right, bands))
+    ends = edge_own(bands)
+    x_left, x_right, ends = lax.optimization_barrier((x_left, x_right, ends))
     halo, h_up, h_down = x_halo_messages(x_left, x_right, approx, za0, wide, ghost)
     h_left, h_right = exchange(h_up, h_down, "gy")
     approx, halo = lax.optimization_barrier((approx, halo))
     bands1, b_up, b_down = second_bands(approx, a_left, a_right, za1, ya1, rows1)
     b_left, b_right = exchange(b_up, b_down, "gx")
     h_left, h_right, bands1 = lax.optimization_barrier((h_left, h_right, bands1))
-    edge, e_up, e_down = edge_details(bands, halo, h_left, h_right, table, index, ya0, zs0, ys0, wide)
+    edge, e_up, e_down = edge_details(nx, ends, halo, h_left, h_right, table, index, ya0, zs0, ys0, wide)
     e_left, e_right = exchange(e_up, e_down, "gx")
     bands1, edge = lax.optimization_barrier((bands1, edge))
     approx1, s_up, s_down = coarse(

time: 52.4 us -> 51.9 us (level)
  waiting for transfers between devices: 4.69 us -> 4.02 us
    ppermute x14, waiting for transfers between devices: 4.69 us -> 4.02 us  [exchange(): return (lax.ppermute(first, axis, here), lax.ppermute(second, axis, across))]
    pallas_call x12 -> x13, Pallas kernels: 26.8 us -> 26.9 us  [whole_call(): pl.pallas_call(kernel, in_specs=changes.get('in_specs', specs), out_specs...]
  transfers between devices with their start and end apart: 14 -> 14, of which waited for: 3 -> 3; matrix products, arithmetic and copies ran while one was open for 0% -> 0% of each run, Pallas kernels for 42% -> 43%
where the time goes in v10:
time: 51.9 us; the launch traced here: 51.8 us
  Pallas kernels  26.9 us (52%)
  starting transfers between devices  19.4 us (37%)
  waiting for transfers between devices  4.02 us (8%)
  local copies, waits for them, and re-layouts  1.13 us (2%)
    pallas_call x13, Pallas kernels, whole_call(): pl.pallas_call(kernel, in_specs=changes.get('in_specs', specs), out_specs...  26.9 us
    ppermute x14, starting transfers between devices, exchange(): return (lax.ppermute(first, axis, here), lax.ppermute(second, axis, across))  19.4 us
    ppermute x14, waiting for transfers between devices, exchange(): return (lax.ppermute(first, axis, here), lax.ppermute(second, axis, across))  4.02 us
    unnamed x42, local copies, waits for them, and re-layouts  1.13 us
  transfers between devices with their start and end apart: 14, of which 3 were waited for; matrix products, arithmetic and copies ran while one was open for 0% of the time, Pallas kernels for 43%

profile of v10, /device:TPU:0, one launch (start us, length us, event | category | flops | bytes accessed | tf_op | source)
XLA Modules:
  0.0 51.8 jit_solution(15322606527171906875)
XLA Ops:
  0.0 1.6 %first_messages.1 = (f32[2,128,256]{2,1,0:T(8,128)S(1)}, f32[2,128,256]{2,1,0:T(8,128)S(1)}, f32[28,8,256]{2,1,0:T(8,128)S(1)}, f32[28,8,256]{2,1,0:T(8,128)S(1)}) custom-call(f32[32,128,256]{2,1,0:T(8,128)} %refs_0_.6), custom_call_target="tpu_custom_call" | custom-call | flops 1000 | bytes 1000 | tf_op jit(solution)/shard_map/first_messages/pallas_call | solution.py:250
  1.6 2.5 %collective-permute-start.2 = (f32[28,8,256]{2,1,0:T(8,128)S(1)}, f32[28,8,256]{2,1,0:T(8,128)S(1)}, u32[]{:S(2)}, u32[]{:S(2)}) collective-permute-start(f32[28,8,256]{2,1,0:T(8,128)S(1)} %get-tuple-element.41), channel_id=1, source_target_pairs={{0,3},{1,2},{2,1},{3,0},{4,7},{5,6},{6,5},{7,4},{8,11},{9,10},{10,... | collective-permute-start | bytes 688136 | tf_op jit(solution)/shard_map/ppermute | solution.py:913
  4.1 1.5 %collective-permute-start = (f32[2,128,256]{2,1,0:T(8,128)S(1)}, f32[2,128,256]{2,1,0:T(8,128)S(1)}, u32[]{:S(2)}, u32[]{:S(2)}) collective-permute-start(f32[2,128,256]{2,1,0:T(8,128)S(1)} %get-tuple-element.37), channel_id=1, source_target_pairs={{0,4},{4,0},{8,12},{12,8},{16,20},{20,16},{24,28},{28,24},{1,5},{5... | collective-permute-start | bytes 786440 | tf_op jit(solution)/shard_map/ppermute | solution.py:913
  5.6 3.6 %collective-permute-start.1 = (f32[2,128,256]{2,1,0:T(8,128)S(1)}, f32[2,128,256]{2,1,0:T(8,128)S(1)}, u32[]{:S(2)}, u32[]{:S(2)}) collective-permute-start(f32[2,128,256]{2,1,0:T(8,128)S(1)} %get-tuple-element.38), channel_id=1, source_target_pairs={{0,28},{4,8},{8,4},{12,16},{16,12},{20,24},{24,20},{28,0},{1,29},{... | collective-permute-start | bytes 786440 | tf_op jit(solution)/shard_map/ppermute | solution.py:913
  9.2 0.1 collective-permute-start.3
  9.3 1.0 %copy-done.1 = bf16[768,256]{1,0:T(8,128)(2,1)S(1)} copy-done((bf16[768,256]{1,0:T(8,128)(2,1)S(1)}, bf16[768,256]{1,0:T(8,128)(2,1)}, u32[]{:S(2)}) %copy-start.1) | copy-done | bytes 393240
  10.3 2.0 %depth_analysis.1.refs_0_ = f32[32,128,256]{2,1,0:T(8,128)S(1)} custom-call(f32[32,128,256]{2,1,0:T(8,128)S(1)} %copy-done, bf16[768,256]{1,0:T(8,128)(2,1)S(1)} %copy-done.1), custom_call_target="tpu_custom_call" | custom-call | flops 1000 | bytes 1000 | tf_op jit(solution)/shard_map/depth_analysis/pallas_call | solution.py:250
  12.3 0.0 copy-start.4
  12.3 1.5 %own_approx.1 = (f32[20,72,128]{2,1,0:T(8,128)S(1)}, f32[16,24,128]{2,1,0:T(8,128)S(1)}, f32[16,24,128]{2,1,0:T(8,128)S(1)}) custom-call(f32[32,128,256]{2,1,0:T(8,128)S(1)} %depth_analysis.1.refs_0_, bf16[80,384]{1,0:T(8,128)(2,1)S(1)} %copy-done.15), custom_call_target="tpu_custom_call" | custom-call | flops 1000 | bytes 1000 | tf_op jit(solution)/shard_map/own_approx/pallas_call | solution.py:250
  13.9 0.7 %collective-permute-start.7 = (f32[16,24,128]{2,1,0:T(8,128)S(1)}, f32[16,24,128]{2,1,0:T(8,128)S(1)}, u32[]{:S(2)}, u32[]{:S(2)}) collective-permute-start(f32[16,24,128]{2,1,0:T(8,128)S(1)} %get-tuple-element.50), channel_id=1, source_target_pairs={{0,3},{1,2},{2,1},{3,0},{4,7},{5,6},{6,5},{7,4},{8,11},{9,10},{10,... | collective-permute-start | bytes 589832 | tf_op jit(solution)/shard_map/ppermute | solution.py:913
  14.6 2.4 %y_analysis.1.refs_0_.refs_2_ = f32[32,144,256]{2,1,0:T(8,128)S(1)} custom-call(f32[32,128,256]{2,1,0:T(8,128)S(1)} %depth_analysis.1.refs_0_, f32[28,8,256]{2,1,0:T(8,128)S(1)} %collective-permute-done.2.refs_1_, f32[28,8,256]{2,1,0:T(8,128)S(1)} %collective-permute-done.3.refs_2_, bf16[768,256]{1,0:T(8,128)(2,1)S(1)} %copy-done.1, ...), custom_call_target="tpu_custom_call" | custom-call | flops 1000 | bytes 1000 | tf_op jit(solution)/shard_map/y_analysis/pallas_call | solution.py:250
  16.9 0.0 copy-start.6
  17.0 0.0 copy-start.7
  17.0 0.0 copy-start.2
  17.0 0.0 copy-start.5
  17.0 0.0 copy-start.19
  17.0 0.5 edge_own.1.refs_2_
  17.5 0.0 copy-start.9
  17.5 0.0 copy-start.11
  17.5 0.0 copy-start.12
  17.6 0.0 copy-start.13
  17.6 0.0 copy-start.16
  17.6 0.0 copy-start.17
  17.6 0.0 copy-start.18
  17.6 1.0 %collective-permute-done.refs_0_ = f32[2,128,256]{2,1,0:T(8,128)S(1)} collective-permute-done((f32[2,128,256]{2,1,0:T(8,128)S(1)}, f32[2,128,256]{2,1,0:T(8,128)S(1)}, u32[]{:S(2)}, u32[]{:S(2)}) %collective-permute-start) | collective-permute-done | bytes 262176 | tf_op jit(solution)/shard_map/ppermute | solution.py:913
  18.6 0.4 x_halo_messages.1
  19.0 0.1 collective-permute-start.4
  19.1 0.6 %collective-permute-start.5 = (f32[4,80,128]{2,1,0:T(8,128)S(1)}, f32[4,80,128]{2,1,0:T(8,128)S(1)}, u32[]{:S(2)}, u32[]{:S(2)}) collective-permute-start(f32[4,80,128]{2,1,0:T(8,128)S(1)} %get-tuple-element.47), channel_id=1, source_target_pairs={{0,3},{1,2},{2,1},{3,0},{4,7},{5,6},{6,5},{7,4},{8,11},{9,10},{10,... | collective-permute-start | bytes 491528 | tf_op jit(solution)/shard_map/ppermute | solution.py:913
  19.8 0.9 %collective-permute-done.7.refs_2_ = f32[16,24,128]{2,1,0:T(8,128)S(1)} collective-permute-done((f32[16,24,128]{2,1,0:T(8,128)S(1)}, f32[16,24,128]{2,1,0:T(8,128)S(1)}, u32[]{:S(2)}, u32[]{:S(2)}) %collective-permute-start.7) | collective-permute-done | bytes 196640 | tf_op jit(solution)/shard_map/ppermute | solution.py:913
  20.7 1.2 %second_bands.1 = (f32[16,96,128]{2,1,0:T(8,128)S(1)}, f32[248,128]{1,0:T(8,128)S(1)}, f32[248,128]{1,0:T(8,128)S(1)}) custom-call(f32[20,72,128]{2,1,0:T(8,128)S(1)} %get-tuple-element.49.refs_2_.refs_0_.refs_8_, f32[16,24,128]{2,1,0:T(8,128)S(1)} %collective-permute-done.6.refs_1_, f32[16,24,128]{2,1,0:T(8,128)S(1)} %collective-permute-done.7.refs_2_, ...), custom_call_target="tpu_custom_call" | custom-call | flops 1000 | bytes 1000 | tf_op jit(solution)/shard_map/second_bands/pallas_call | solution.py:250
  21.9 0.6 %collective-permute-start.8 = (f32[248,128]{1,0:T(8,128)S(1)}, f32[248,128]{1,0:T(8,128)S(1)}, u32[]{:S(2)}, u32[]{:S(2)}) collective-permute-start(f32[248,128]{1,0:T(8,128)S(1)} %get-tuple-element.59), channel_id=1, source_target_pairs={{0,4},{4,0},{8,12},{12,8},{16,20},{20,16},{24,28},{28,24},{1,5},{5... | collective-permute-start | bytes 380936 | tf_op jit(solution)/shard_map/ppermute | solution.py:913
  22.5 3.6 %collective-permute-start.9 = (f32[248,128]{1,0:T(8,128)S(1)}, f32[248,128]{1,0:T(8,128)S(1)}, u32[]{:S(2)}, u32[]{:S(2)}) collective-permute-start(f32[248,128]{1,0:T(8,128)S(1)} %get-tuple-element.60), channel_id=1, source_target_pairs={{0,28},{4,8},{8,4},{12,16},{16,12},{20,24},{24,20},{28,0},{1,29},{... | collective-permute-start | bytes 380936 | tf_op jit(solution)/shard_map/ppermute | solution.py:913
  26.1 2.2 %edge_details.1 = (f32[8,144,256]{2,1,0:T(8,128)S(1)}, f32[2,128,256]{2,1,0:T(8,128)S(1)}, f32[2,128,256]{2,1,0:T(8,128)S(1)}) custom-call(f32[16]{0:T(128)S(1)} %copy-done.20, s32[3,7]{1,0:T(4,128)S(1)} %copy-done.19, f32[8,144,256]{2,1,0:T(8,128)S(1)} %edge_own.1.refs_2_, f32[4,128,256]{2,1,0:T(8,128)S(1)} %get-tuple-element.54.refs_3_.refs_5_, ...), custom_call_target="tpu_custom_call" | custom-call | flops 1000 | bytes 1000 | tf_op jit(solution)/shard_map/edge_details/pallas_call | solution.py:250
  28.3 0.6 %collective-permute-start.12 = (f32[2,128,256]{2,1,0:T(8,128)S(1)}, f32[2,128,256]{2,1,0:T(8,128)S(1)}, u32[]{:S(2)}, u32[]{:S(2)}) collective-permute-start(f32[2,128,256]{2,1,0:T(8,128)S(1)} %get-tuple-element.67), channel_id=1, source_target_pairs={{0,4},{4,0},{8,12},{12,8},{16,20},{20,16},{24,28},{28,24},{1,5},{5... | collective-permute-start | bytes 786440 | tf_op jit(solution)/shard_map/ppermute | solution.py:913
  28.9 3.6 %collective-permute-start.13 = (f32[2,128,256]{2,1,0:T(8,128)S(1)}, f32[2,128,256]{2,1,0:T(8,128)S(1)}, u32[]{:S(2)}, u32[]{:S(2)}) collective-permute-start(f32[2,128,256]{2,1,0:T(8,128)S(1)} %get-tuple-element.68), channel_id=1, source_target_pairs={{0,28},{4,8},{8,4},{12,16},{16,12},{20,24},{24,20},{28,0},{1,29},{... | collective-permute-start | bytes 786440 | tf_op jit(solution)/shard_map/ppermute | solution.py:913
  32.5 3.5 %coarse.1 = (f32[20,72,128]{2,1,0:T(8,128)S(1)}, f32[312,128]{1,0:T(8,128)S(1)}, f32[312,128]{1,0:T(8,128)S(1)}) custom-call(f32[16]{0:T(128)S(1)} %copy-done.20, s32[3,7]{1,0:T(4,128)S(1)} %copy-done.19, f32[16,96,128]{2,1,0:T(8,128)S(1)} %get-tuple-element.58.refs_2_, f32[248,128]{1,0:T(8,128)S(1)} %collective-permute-done.8.refs_3_, ...), custom_call_target="tpu_custom_call" | custom-call | flops 1000 | bytes 1000 | tf_op jit(solution)/shard_map/coarse/pallas_call | solution.py:250
  36.0 0.1 collective-permute-start.10
  36.1 1.9 %collective-permute-start.11 = (f32[312,128]{1,0:T(8,128)S(1)}, f32[312,128]{1,0:T(8,128)S(1)}, u32[]{:S(2)}, u32[]{:S(2)}) collective-permute-start(f32[312,128]{1,0:T(8,128)S(1)} %get-tuple-element.62), channel_id=1, source_target_pairs={{0,28},{4,8},{8,4},{12,16},{16,12},{20,24},{24,20},{28,0},{1,29},{... | collective-permute-start | bytes 479240 | tf_op jit(solution)/shard_map/ppermute | solution.py:913
  38.0 2.1 %inner_bands.1.refs_1_ = f32[24,144,256]{2,1,0:T(8,128)S(1)} custom-call(f32[16]{0:T(128)S(1)} %copy-done.20, s32[3,7]{1,0:T(4,128)S(1)} %copy-done.19, f32[32,144,256]{2,1,0:T(8,128)S(1)} %y_analysis.1.refs_0_.refs_2_), custom_call_target="tpu_custom_call" | custom-call | flops 1000 | bytes 1000 | tf_op jit(solution)/shard_map/inner_bands/pallas_call | solution.py:250
  40.0 0.0 copy-start.3
  40.0 0.0 copy-start.8
  40.1 4.5 %detail_yz.1.refs_0_ = f32[32,128,256]{2,1,0:T(8,128)S(1)} custom-call(f32[8,144,256]{2,1,0:T(8,128)S(1)} %get-tuple-element.63.refs_0_, f32[24,144,256]{2,1,0:T(8,128)S(1)} %inner_bands.1.refs_1_, f32[20,72,128]{2,1,0:T(8,128)S(1)} %get-tuple-element.66.refs_2_.refs_1_, bf16[768,256]{1,0:T(8,128)(2,1)S(1)} %copy-done.2, bf16[128,432]{1,0:T(8,128)(2,1)S(1)} %copy-done.5), custom_call_target="tpu_custom_call" | custom-call | flops 1000 | bytes 1000 | tf_op jit(solution)/shard_map/detail_yz/pallas_call | solution.py:250
  44.5 0.0 copy-start.10
  44.5 0.0 copy-start.14
  44.5 2.0 %collective-permute-done.12.refs_2_ = f32[2,128,256]{2,1,0:T(8,128)S(1)} collective-permute-done((f32[2,128,256]{2,1,0:T(8,128)S(1)}, f32[2,128,256]{2,1,0:T(8,128)S(1)}, u32[]{:S(2)}, u32[]{:S(2)}) %collective-permute-start.12) | collective-permute-done | bytes 262176 | tf_op jit(solution)/shard_map/ppermute | solution.py:913
  46.6 2.1 %own_result.1.refs_2_ = f32[32,128,256]{2,1,0:T(8,128)S(1)} custom-call(f32[32,128,256]{2,1,0:T(8,128)S(1)} %detail_yz.1.refs_0_, f32[20,72,128]{2,1,0:T(8,128)S(1)} %get-tuple-element.66.refs_2_.refs_1_, f32[2,128,256]{2,1,0:T(8,128)S(1)} %collective-permute-done.12.refs_2_, f32[2,128,256]{2,1,0:T(8,128)S(1)} %collective-permute-done.13.refs_3_, ...), custom_call_target="tpu_custom_call" | custom-call | flops 1000 | bytes 1000 | tf_op jit(solution)/shard_map/own_result/pallas_call | solution.py:250
  48.7 0.0 collective-permute-done.10.refs_0_
  48.8 3.0 %final.1 = f32[32,128,256]{2,1,0:T(8,128)} custom-call(f32[312,128]{1,0:T(8,128)S(1)} %collective-permute-done.10.refs_0_, f32[312,128]{1,0:T(8,128)S(1)} %collective-permute-done.11.refs_1_, f32[32,128,256]{2,1,0:T(8,128)S(1)} %own_result.1.refs_2_, bf16[384,256]{1,0:T(8,128)(2,1)S(1)} %copy-done.10, bf16[128,144]{1,0:T(8,128)(2,1)S(1)} %copy-done.14, ...), custom_call_target="tpu_custom_call" | custom-call | flops 1000 | bytes 1000 | tf_op jit(solution)/shard_map/final/pallas_call | solution.py:250
  (35 shorter events, 0.1 us)
Async XLA Ops:
  0.0 9.3 %copy-start = (f32[32,128,256]{2,1,0:T(8,128)S(1)}, f32[32,128,256]{2,1,0:T(8,128)}, u32[]{:S(2)}) copy-start(f32[32,128,256]{2,1,0:T(8,128)} %refs_0_.6) | copy-start | bytes 12582916
  1.6 12.9 %collective-permute-start.2 = (f32[28,8,256]{2,1,0:T(8,128)S(1)}, f32[28,8,256]{2,1,0:T(8,128)S(1)}, u32[]{:S(2)}, u32[]{:S(2)}) collective-permute-start(f32[28,8,256]{2,1,0:T(8,128)S(1)} %get-tuple-element.41), channel_id=1, source_target_pairs={{0,3},{1,2},{2,1},{3,0},{4,7},{5,6},{6,5},{7,4},{8,11},{9,10},{10,... | collective-permute-start | bytes 688136 | tf_op jit(solution)/shard_map/ppermute | solution.py:913
  4.1 14.5 %collective-permute-start = (f32[2,128,256]{2,1,0:T(8,128)S(1)}, f32[2,128,256]{2,1,0:T(8,128)S(1)}, u32[]{:S(2)}, u32[]{:S(2)}) collective-permute-start(f32[2,128,256]{2,1,0:T(8,128)S(1)} %get-tuple-element.37), channel_id=1, source_target_pairs={{0,4},{4,0},{8,12},{12,8},{16,20},{20,16},{24,28},{28,24},{1,5},{5... | collective-permute-start | bytes 786440 | tf_op jit(solution)/shard_map/ppermute | solution.py:913
  5.6 13.0 %collective-permute-start.1 = (f32[2,128,256]{2,1,0:T(8,128)S(1)}, f32[2,128,256]{2,1,0:T(8,128)S(1)}, u32[]{:S(2)}, u32[]{:S(2)}) collective-permute-start(f32[2,128,256]{2,1,0:T(8,128)S(1)} %get-tuple-element.38), channel_id=1, source_target_pairs={{0,28},{4,8},{8,4},{12,16},{16,12},{20,24},{24,20},{28,0},{1,29},{... | collective-permute-start | bytes 786440 | tf_op jit(solution)/shard_map/ppermute | solution.py:913
  9.2 5.4 %collective-permute-start.3 = (f32[28,8,256]{2,1,0:T(8,128)S(1)}, f32[28,8,256]{2,1,0:T(8,128)S(1)}, u32[]{:S(2)}, u32[]{:S(2)}) collective-permute-start(f32[28,8,256]{2,1,0:T(8,128)S(1)} %get-tuple-element.42), channel_id=1, source_target_pairs={{0,1},{1,0},{2,3},{3,2},{4,5},{5,4},{6,7},{7,6},{8,9},{9,8},{10,11... | collective-permute-start | bytes 688136 | tf_op jit(solution)/shard_map/ppermute | solution.py:913
  9.3 1.0 %copy-start.1 = (bf16[768,256]{1,0:T(8,128)(2,1)S(1)}, bf16[768,256]{1,0:T(8,128)(2,1)}, u32[]{:S(2)}) copy-start(bf16[768,256]{1,0:T(8,128)(2,1)} %constant.36.clone.refs_1_.refs_3_) | copy-start | bytes 1179652
  10.3 2.0 %copy-start.15 = (bf16[80,384]{1,0:T(8,128)(2,1)S(1)}, bf16[80,384]{1,0:T(8,128)(2,1)}, u32[]{:S(2)}) copy-start(bf16[80,384]{1,0:T(8,128)(2,1)} %constant.37.clone.refs_1_) | copy-start | bytes 184324
  12.3 2.2 %copy-start.4 = (bf16[144,432]{1,0:T(8,128)(2,1)S(1)}, bf16[144,432]{1,0:T(8,128)(2,1)}, u32[]{:S(2)}) copy-start(bf16[144,432]{1,0:T(8,128)(2,1)} %constant.38.clone.refs_4_.refs_6_) | copy-start | bytes 373252
  13.9 6.8 %collective-permute-start.7 = (f32[16,24,128]{2,1,0:T(8,128)S(1)}, f32[16,24,128]{2,1,0:T(8,128)S(1)}, u32[]{:S(2)}, u32[]{:S(2)}) collective-permute-start(f32[16,24,128]{2,1,0:T(8,128)S(1)} %get-tuple-element.50), channel_id=1, source_target_pairs={{0,3},{1,2},{2,1},{3,0},{4,7},{5,6},{6,5},{7,4},{8,11},{9,10},{10,... | collective-permute-start | bytes 589832 | tf_op jit(solution)/shard_map/ppermute | solution.py:913
  14.5 6.2 %collective-permute-start.6 = (f32[16,24,128]{2,1,0:T(8,128)S(1)}, f32[16,24,128]{2,1,0:T(8,128)S(1)}, u32[]{:S(2)}, u32[]{:S(2)}) collective-permute-start(f32[16,24,128]{2,1,0:T(8,128)S(1)} %get-tuple-element.39), channel_id=1, source_target_pairs={{0,1},{1,0},{2,3},{3,2},{4,5},{5,4},{6,7},{7,6},{8,9},{9,8},{10,11... | collective-permute-start | bytes 589832 | tf_op jit(solution)/shard_map/ppermute | solution.py:913
  16.9 3.8 %copy-start.6 = (bf16[256,256]{1,0:T(8,128)(2,1)S(1)}, bf16[256,256]{1,0:T(8,128)(2,1)}, u32[]{:S(2)}) copy-start(bf16[256,256]{1,0:T(8,128)(2,1)} %constant.39.clone.refs_3_.refs_9_) | copy-start | bytes 393220
  17.0 3.7 %copy-start.7 = (bf16[96,384]{1,0:T(8,128)(2,1)S(1)}, bf16[96,384]{1,0:T(8,128)(2,1)}, u32[]{:S(2)}) copy-start(bf16[96,384]{1,0:T(8,128)(2,1)} %constant.40.clone.refs_4_.refs_11_) | copy-start | bytes 221188
  17.0 9.1 %copy-start.2 = (bf16[768,256]{1,0:T(8,128)(2,1)S(1)}, bf16[768,256]{1,0:T(8,128)(2,1)}, u32[]{:S(2)}) copy-start(bf16[768,256]{1,0:T(8,128)(2,1)} %constant.41.clone.refs_7_.refs_3_) | copy-start | bytes 1179652
  17.0 9.1 %copy-start.5 = (bf16[128,432]{1,0:T(8,128)(2,1)S(1)}, bf16[128,432]{1,0:T(8,128)(2,1)}, u32[]{:S(2)}) copy-start(bf16[128,432]{1,0:T(8,128)(2,1)} %constant.42.clone.refs_8_.refs_4_) | copy-start | bytes 331780
  17.0 9.1 %copy-start.19 = (s32[3,7]{1,0:T(4,128)S(1)}, s32[3,7]{1,0:T(4,128)}, u32[]{:S(2)}) copy-start(s32[3,7]{1,0:T(4,128)} %refs_1_.7) | copy-start | bytes 256
  17.0 9.1 %copy-start.20 = (f32[16]{0:T(128)S(1)}, f32[16]{0:T(128)}, u32[]{:S(2)}) copy-start(f32[16]{0:T(128)} %refs_0_.9) | copy-start | bytes 196
  17.5 14.9 %copy-start.9 = (bf16[128,672]{1,0:T(8,128)(2,1)S(1)}, bf16[128,672]{1,0:T(8,128)(2,1)}, u32[]{:S(2)}) copy-start(bf16[128,672]{1,0:T(8,128)(2,1)} %constant.43.clone.refs_10_) | copy-start | bytes 516100
  17.5 14.9 %copy-start.11 = (bf16[256,256]{1,0:T(8,128)(2,1)S(1)}, bf16[256,256]{1,0:T(8,128)(2,1)}, u32[]{:S(2)}) copy-start(bf16[256,256]{1,0:T(8,128)(2,1)} %constant.46.clone.refs_14_) | copy-start | bytes 393220
  17.5 14.9 %copy-start.12 = (bf16[256,256]{1,0:T(8,128)(2,1)S(1)}, bf16[256,256]{1,0:T(8,128)(2,1)}, u32[]{:S(2)}) copy-start(bf16[256,256]{1,0:T(8,128)(2,1)} %constant.45.clone.refs_13_) | copy-start | bytes 393220
  17.6 14.9 %copy-start.13 = (bf16[256,256]{1,0:T(8,128)(2,1)S(1)}, bf16[256,256]{1,0:T(8,128)(2,1)}, u32[]{:S(2)}) copy-start(bf16[256,256]{1,0:T(8,128)(2,1)} %constant.44.clone.refs_12_) | copy-start | bytes 393220
  17.6 14.9 %copy-start.16 = (bf16[80,288]{1,0:T(8,128)(2,1)S(1)}, bf16[80,288]{1,0:T(8,128)(2,1)}, u32[]{:S(2)}) copy-start(bf16[80,288]{1,0:T(8,128)(2,1)} %constant.49.clone.refs_17_) | copy-start | bytes 138244
  17.6 14.9 %copy-start.17 = (bf16[64,144]{1,0:T(8,128)(2,1)S(1)}, bf16[64,144]{1,0:T(8,128)(2,1)}, u32[]{:S(2)}) copy-start(bf16[64,144]{1,0:T(8,128)(2,1)} %constant.48.clone.refs_16_) | copy-start | bytes 55300
  17.6 14.9 %copy-start.18 = (bf16[48,192]{1,0:T(8,128)(2,1)S(1)}, bf16[48,192]{1,0:T(8,128)(2,1)}, u32[]{:S(2)}) copy-start(bf16[48,192]{1,0:T(8,128)(2,1)} %constant.47.clone.refs_15_) | copy-start | bytes 55300
  19.0 7.0 %collective-permute-start.4 = (f32[4,80,128]{2,1,0:T(8,128)S(1)}, f32[4,80,128]{2,1,0:T(8,128)S(1)}, u32[]{:S(2)}, u32[]{:S(2)}) collective-permute-start(f32[4,80,128]{2,1,0:T(8,128)S(1)} %get-tuple-element.46), channel_id=1, source_target_pairs={{0,1},{1,0},{2,3},{3,2},{4,5},{5,4},{6,7},{7,6},{8,9},{9,8},{10,11... | collective-permute-start | bytes 491528 | tf_op jit(solution)/shard_map/ppermute | solution.py:913
  19.1 6.9 %collective-permute-start.5 = (f32[4,80,128]{2,1,0:T(8,128)S(1)}, f32[4,80,128]{2,1,0:T(8,128)S(1)}, u32[]{:S(2)}, u32[]{:S(2)}) collective-permute-start(f32[4,80,128]{2,1,0:T(8,128)S(1)} %get-tuple-element.47), channel_id=1, source_target_pairs={{0,3},{1,2},{2,1},{3,0},{4,7},{5,6},{6,5},{7,4},{8,11},{9,10},{10,... | collective-permute-start | bytes 491528 | tf_op jit(solution)/shard_map/ppermute | solution.py:913
  21.9 10.6 %collective-permute-start.8 = (f32[248,128]{1,0:T(8,128)S(1)}, f32[248,128]{1,0:T(8,128)S(1)}, u32[]{:S(2)}, u32[]{:S(2)}) collective-permute-start(f32[248,128]{1,0:T(8,128)S(1)} %get-tuple-element.59), channel_id=1, source_target_pairs={{0,4},{4,0},{8,12},{12,8},{16,20},{20,16},{24,28},{28,24},{1,5},{5... | collective-permute-start | bytes 380936 | tf_op jit(solution)/shard_map/ppermute | solution.py:913
  22.5 9.9 %collective-permute-start.9 = (f32[248,128]{1,0:T(8,128)S(1)}, f32[248,128]{1,0:T(8,128)S(1)}, u32[]{:S(2)}, u32[]{:S(2)}) collective-permute-start(f32[248,128]{1,0:T(8,128)S(1)} %get-tuple-element.60), channel_id=1, source_target_pairs={{0,28},{4,8},{8,4},{12,16},{16,12},{20,24},{24,20},{28,0},{1,29},{... | collective-permute-start | bytes 380936 | tf_op jit(solution)/shard_map/ppermute | solution.py:913
  28.3 18.3 %collective-permute-start.12 = (f32[2,128,256]{2,1,0:T(8,128)S(1)}, f32[2,128,256]{2,1,0:T(8,128)S(1)}, u32[]{:S(2)}, u32[]{:S(2)}) collective-permute-start(f32[2,128,256]{2,1,0:T(8,128)S(1)} %get-tuple-element.67), channel_id=1, source_target_pairs={{0,4},{4,0},{8,12},{12,8},{16,20},{20,16},{24,28},{28,24},{1,5},{5... | collective-permute-start | bytes 786440 | tf_op jit(solution)/shard_map/ppermute | solution.py:913
  28.9 17.7 %collective-permute-start.13 = (f32[2,128,256]{2,1,0:T(8,128)S(1)}, f32[2,128,256]{2,1,0:T(8,128)S(1)}, u32[]{:S(2)}, u32[]{:S(2)}) collective-permute-start(f32[2,128,256]{2,1,0:T(8,128)S(1)} %get-tuple-element.68), channel_id=1, source_target_pairs={{0,28},{4,8},{8,4},{12,16},{16,12},{20,24},{24,20},{28,0},{1,29},{... | collective-permute-start | bytes 786440 | tf_op jit(solution)/shard_map/ppermute | solution.py:913
  36.0 12.7 %collective-permute-start.10 = (f32[312,128]{1,0:T(8,128)S(1)}, f32[312,128]{1,0:T(8,128)S(1)}, u32[]{:S(2)}, u32[]{:S(2)}) collective-permute-start(f32[312,128]{1,0:T(8,128)S(1)} %get-tuple-element.61), channel_id=1, source_target_pairs={{0,4},{4,0},{8,12},{12,8},{16,20},{20,16},{24,28},{28,24},{1,5},{5... | collective-permute-start | bytes 479240 | tf_op jit(solution)/shard_map/ppermute | solution.py:913
  36.1 12.7 %collective-permute-start.11 = (f32[312,128]{1,0:T(8,128)S(1)}, f32[312,128]{1,0:T(8,128)S(1)}, u32[]{:S(2)}, u32[]{:S(2)}) collective-permute-start(f32[312,128]{1,0:T(8,128)S(1)} %get-tuple-element.62), channel_id=1, source_target_pairs={{0,28},{4,8},{8,4},{12,16},{16,12},{20,24},{24,20},{28,0},{1,29},{... | collective-permute-start | bytes 479240 | tf_op jit(solution)/shard_map/ppermute | solution.py:913
  40.0 6.6 %copy-start.3 = (bf16[384,256]{1,0:T(8,128)(2,1)S(1)}, bf16[384,256]{1,0:T(8,128)(2,1)}, u32[]{:S(2)}) copy-start(bf16[384,256]{1,0:T(8,128)(2,1)} %constant.50.clone.refs_4_.refs_5_) | copy-start | bytes 589828
  40.0 6.5 %copy-start.8 = (bf16[128,240]{1,0:T(8,128)(2,1)S(1)}, bf16[128,240]{1,0:T(8,128)(2,1)}, u32[]{:S(2)}) copy-start(bf16[128,240]{1,0:T(8,128)(2,1)} %constant.51.clone.refs_5_.refs_6_) | copy-start | bytes 184324
  44.5 4.2 %copy-start.10 = (bf16[384,256]{1,0:T(8,128)(2,1)S(1)}, bf16[384,256]{1,0:T(8,128)(2,1)}, u32[]{:S(2)}) copy-start(bf16[384,256]{1,0:T(8,128)(2,1)} %constant.52.clone.refs_3_) | copy-start | bytes 589828
  44.5 4.2 %copy-start.14 = (bf16[128,144]{1,0:T(8,128)(2,1)S(1)}, bf16[128,144]{1,0:T(8,128)(2,1)}, u32[]{:S(2)}) copy-start(bf16[128,144]{1,0:T(8,128)(2,1)} %constant.53.clone.refs_4_) | copy-start | bytes 110596

commit v11 on v10

--- a/solution.py
+++ b/solution.py
@@ -446,7 +446,7 @@
     return quiet, table_ref[index_ref[0, band + 3]]
 
 
-def over_tiles(rows, nz, body):
+def over_tiles(rows, nz, body, unroll=3):
     half_z, half_tiles = nz // 2, rows // 16
     for by in range(2):
 
@@ -456,7 +456,7 @@
                 body(at, pl.ds(bz * half_z, half_z), by, bz)
             return carry
 
-        lax.fori_loop(0, half_tiles, tile, 0, unroll=3 if half_tiles % 3 == 0 else 1)
+        lax.fori_loop(0, half_tiles, tile, 0, unroll=unroll if half_tiles % unroll == 0 else 1)
 
 
 def inner_bands(bands, table, index):
@@ -542,7 +542,7 @@
             for i, part in enumerate(spilled):
                 beyond[i, at, lanes] = part
 
-        over_tiles(rows, nz, body)
+        over_tiles(rows, nz, body, 9)
         zed[...] = times(beyond[...].reshape(4 * rows, nz), z).reshape(4, rows, nz)
         for i, target in enumerate((up.at[0], up.at[1], down.at[0], down.at[1])):
             target[...] = left_times(y, zed[i])

time: 51.9 us -> 51.7 us (level)
  no operation moved by 1% of the time
where the time goes in v11:
time: 51.7 us; the launch traced here: 51.6 us
  Pallas kernels  26.7 us (52%)
  starting transfers between devices  19.4 us (38%)
  waiting for transfers between devices  3.98 us (8%)
  local copies, waits for them, and re-layouts  1.13 us (2%)
    pallas_call x13, Pallas kernels, whole_call(): pl.pallas_call(kernel, in_specs=changes.get('in_specs', specs), out_specs...  26.7 us
    ppermute x14, starting transfers between devices, exchange(): return (lax.ppermute(first, axis, here), lax.ppermute(second, axis, across))  19.4 us
    ppermute x14, waiting for transfers between devices, exchange(): return (lax.ppermute(first, axis, here), lax.ppermute(second, axis, across))  3.98 us
    unnamed x42, local copies, waits for them, and re-layouts  1.13 us
  transfers between devices with their start and end apart: 14, of which 3 were waited for; matrix products, arithmetic and copies ran while one was open for 0% of the time, Pallas kernels for 43%

profile of v11, /device:TPU:0, one launch (start us, length us, event | category | flops | bytes accessed | tf_op | source)
XLA Modules:
  0.0 51.6 jit_solution(13870477517089678698)
XLA Ops:
  0.0 1.6 %first_messages.1 = (f32[2,128,256]{2,1,0:T(8,128)S(1)}, f32[2,128,256]{2,1,0:T(8,128)S(1)}, f32[28,8,256]{2,1,0:T(8,128)S(1)}, f32[28,8,256]{2,1,0:T(8,128)S(1)}) custom-call(f32[32,128,256]{2,1,0:T(8,128)} %refs_0_.6), custom_call_target="tpu_custom_call" | custom-call | flops 1000 | bytes 1000 | tf_op jit(solution)/shard_map/first_messages/pallas_call | solution.py:250
  1.6 2.5 %collective-permute-start.2 = (f32[28,8,256]{2,1,0:T(8,128)S(1)}, f32[28,8,256]{2,1,0:T(8,128)S(1)}, u32[]{:S(2)}, u32[]{:S(2)}) collective-permute-start(f32[28,8,256]{2,1,0:T(8,128)S(1)} %get-tuple-element.41), channel_id=1, source_target_pairs={{0,3},{1,2},{2,1},{3,0},{4,7},{5,6},{6,5},{7,4},{8,11},{9,10},{10,... | collective-permute-start | bytes 688136 | tf_op jit(solution)/shard_map/ppermute | solution.py:913
  4.1 1.5 %collective-permute-start = (f32[2,128,256]{2,1,0:T(8,128)S(1)}, f32[2,128,256]{2,1,0:T(8,128)S(1)}, u32[]{:S(2)}, u32[]{:S(2)}) collective-permute-start(f32[2,128,256]{2,1,0:T(8,128)S(1)} %get-tuple-element.37), channel_id=1, source_target_pairs={{0,4},{4,0},{8,12},{12,8},{16,20},{20,16},{24,28},{28,24},{1,5},{5... | collective-permute-start | bytes 786440 | tf_op jit(solution)/shard_map/ppermute | solution.py:913
  5.6 3.6 %collective-permute-start.1 = (f32[2,128,256]{2,1,0:T(8,128)S(1)}, f32[2,128,256]{2,1,0:T(8,128)S(1)}, u32[]{:S(2)}, u32[]{:S(2)}) collective-permute-start(f32[2,128,256]{2,1,0:T(8,128)S(1)} %get-tuple-element.38), channel_id=1, source_target_pairs={{0,28},{4,8},{8,4},{12,16},{16,12},{20,24},{24,20},{28,0},{1,29},{... | collective-permute-start | bytes 786440 | tf_op jit(solution)/shard_map/ppermute | solution.py:913
  9.2 0.1 collective-permute-start.3
  9.3 1.0 %copy-done.1 = bf16[768,256]{1,0:T(8,128)(2,1)S(1)} copy-done((bf16[768,256]{1,0:T(8,128)(2,1)S(1)}, bf16[768,256]{1,0:T(8,128)(2,1)}, u32[]{:S(2)}) %copy-start.1) | copy-done | bytes 393240
  10.3 2.0 %depth_analysis.1.refs_0_ = f32[32,128,256]{2,1,0:T(8,128)S(1)} custom-call(f32[32,128,256]{2,1,0:T(8,128)S(1)} %copy-done, bf16[768,256]{1,0:T(8,128)(2,1)S(1)} %copy-done.1), custom_call_target="tpu_custom_call" | custom-call | flops 1000 | bytes 1000 | tf_op jit(solution)/shard_map/depth_analysis/pallas_call | solution.py:250
  12.3 0.0 copy-start.4
  12.3 1.5 %own_approx.1 = (f32[20,72,128]{2,1,0:T(8,128)S(1)}, f32[16,24,128]{2,1,0:T(8,128)S(1)}, f32[16,24,128]{2,1,0:T(8,128)S(1)}) custom-call(f32[32,128,256]{2,1,0:T(8,128)S(1)} %depth_analysis.1.refs_0_, bf16[80,384]{1,0:T(8,128)(2,1)S(1)} %copy-done.15), custom_call_target="tpu_custom_call" | custom-call | flops 1000 | bytes 1000 | tf_op jit(solution)/shard_map/own_approx/pallas_call | solution.py:250
  13.9 0.7 %collective-permute-start.7 = (f32[16,24,128]{2,1,0:T(8,128)S(1)}, f32[16,24,128]{2,1,0:T(8,128)S(1)}, u32[]{:S(2)}, u32[]{:S(2)}) collective-permute-start(f32[16,24,128]{2,1,0:T(8,128)S(1)} %get-tuple-element.50), channel_id=1, source_target_pairs={{0,3},{1,2},{2,1},{3,0},{4,7},{5,6},{6,5},{7,4},{8,11},{9,10},{10,... | collective-permute-start | bytes 589832 | tf_op jit(solution)/shard_map/ppermute | solution.py:913
  14.6 2.4 %y_analysis.1.refs_0_.refs_2_ = f32[32,144,256]{2,1,0:T(8,128)S(1)} custom-call(f32[32,128,256]{2,1,0:T(8,128)S(1)} %depth_analysis.1.refs_0_, f32[28,8,256]{2,1,0:T(8,128)S(1)} %collective-permute-done.2.refs_1_, f32[28,8,256]{2,1,0:T(8,128)S(1)} %collective-permute-done.3.refs_2_, bf16[768,256]{1,0:T(8,128)(2,1)S(1)} %copy-done.1, ...), custom_call_target="tpu_custom_call" | custom-call | flops 1000 | bytes 1000 | tf_op jit(solution)/shard_map/y_analysis/pallas_call | solution.py:250
  16.9 0.0 copy-start.6
  17.0 0.0 copy-start.7
  17.0 0.0 copy-start.2
  17.0 0.0 copy-start.5
  17.0 0.0 copy-start.19
  17.0 0.0 copy-start.20
  17.0 0.5 edge_own.1.refs_2_
  17.5 0.0 copy-start.9
  17.5 0.0 copy-start.11
  17.5 0.0 copy-start.12
  17.6 0.0 copy-start.13
  17.6 0.0 copy-start.16
  17.6 0.0 copy-start.17
  17.6 0.0 copy-start.18
  17.6 1.0 %collective-permute-done.refs_0_ = f32[2,128,256]{2,1,0:T(8,128)S(1)} collective-permute-done((f32[2,128,256]{2,1,0:T(8,128)S(1)}, f32[2,128,256]{2,1,0:T(8,128)S(1)}, u32[]{:S(2)}, u32[]{:S(2)}) %collective-permute-start) | collective-permute-done | bytes 262176 | tf_op jit(solution)/shard_map/ppermute | solution.py:913
  18.6 0.4 x_halo_messages.1
  19.0 0.1 collective-permute-start.4
  19.1 0.6 %collective-permute-start.5 = (f32[4,80,128]{2,1,0:T(8,128)S(1)}, f32[4,80,128]{2,1,0:T(8,128)S(1)}, u32[]{:S(2)}, u32[]{:S(2)}) collective-permute-start(f32[4,80,128]{2,1,0:T(8,128)S(1)} %get-tuple-element.47), channel_id=1, source_target_pairs={{0,3},{1,2},{2,1},{3,0},{4,7},{5,6},{6,5},{7,4},{8,11},{9,10},{10,... | collective-permute-start | bytes 491528 | tf_op jit(solution)/shard_map/ppermute | solution.py:913
  19.8 0.9 %collective-permute-done.7.refs_2_ = f32[16,24,128]{2,1,0:T(8,128)S(1)} collective-permute-done((f32[16,24,128]{2,1,0:T(8,128)S(1)}, f32[16,24,128]{2,1,0:T(8,128)S(1)}, u32[]{:S(2)}, u32[]{:S(2)}) %collective-permute-start.7) | collective-permute-done | bytes 196640 | tf_op jit(solution)/shard_map/ppermute | solution.py:913
  20.7 1.2 %second_bands.1 = (f32[16,96,128]{2,1,0:T(8,128)S(1)}, f32[248,128]{1,0:T(8,128)S(1)}, f32[248,128]{1,0:T(8,128)S(1)}) custom-call(f32[20,72,128]{2,1,0:T(8,128)S(1)} %get-tuple-element.49.refs_2_.refs_0_.refs_8_, f32[16,24,128]{2,1,0:T(8,128)S(1)} %collective-permute-done.6.refs_1_, f32[16,24,128]{2,1,0:T(8,128)S(1)} %collective-permute-done.7.refs_2_, ...), custom_call_target="tpu_custom_call" | custom-call | flops 1000 | bytes 1000 | tf_op jit(solution)/shard_map/second_bands/pallas_call | solution.py:250
  21.9 0.6 %collective-permute-start.8 = (f32[248,128]{1,0:T(8,128)S(1)}, f32[248,128]{1,0:T(8,128)S(1)}, u32[]{:S(2)}, u32[]{:S(2)}) collective-permute-start(f32[248,128]{1,0:T(8,128)S(1)} %get-tuple-element.59), channel_id=1, source_target_pairs={{0,4},{4,0},{8,12},{12,8},{16,20},{20,16},{24,28},{28,24},{1,5},{5... | collective-permute-start | bytes 380936 | tf_op jit(solution)/shard_map/ppermute | solution.py:913
  22.5 3.6 %collective-permute-start.9 = (f32[248,128]{1,0:T(8,128)S(1)}, f32[248,128]{1,0:T(8,128)S(1)}, u32[]{:S(2)}, u32[]{:S(2)}) collective-permute-start(f32[248,128]{1,0:T(8,128)S(1)} %get-tuple-element.60), channel_id=1, source_target_pairs={{0,28},{4,8},{8,4},{12,16},{16,12},{20,24},{24,20},{28,0},{1,29},{... | collective-permute-start | bytes 380936 | tf_op jit(solution)/shard_map/ppermute | solution.py:913
  26.1 1.9 %edge_details.1 = (f32[8,144,256]{2,1,0:T(8,128)S(1)}, f32[2,128,256]{2,1,0:T(8,128)S(1)}, f32[2,128,256]{2,1,0:T(8,128)S(1)}) custom-call(f32[16]{0:T(128)S(1)} %copy-done.20, s32[3,7]{1,0:T(4,128)S(1)} %copy-done.19, f32[8,144,256]{2,1,0:T(8,128)S(1)} %edge_own.1.refs_2_, f32[4,128,256]{2,1,0:T(8,128)S(1)} %get-tuple-element.54.refs_3_.refs_5_, ...), custom_call_target="tpu_custom_call" | custom-call | flops 1000 | bytes 1000 | tf_op jit(solution)/shard_map/edge_details/pallas_call | solution.py:250
  28.0 0.6 %collective-permute-start.12 = (f32[2,128,256]{2,1,0:T(8,128)S(1)}, f32[2,128,256]{2,1,0:T(8,128)S(1)}, u32[]{:S(2)}, u32[]{:S(2)}) collective-permute-start(f32[2,128,256]{2,1,0:T(8,128)S(1)} %get-tuple-element.67), channel_id=1, source_target_pairs={{0,4},{4,0},{8,12},{12,8},{16,20},{20,16},{24,28},{28,24},{1,5},{5... | collective-permute-start | bytes 786440 | tf_op jit(solution)/shard_map/ppermute | solution.py:913
  28.6 3.6 %collective-permute-start.13 = (f32[2,128,256]{2,1,0:T(8,128)S(1)}, f32[2,128,256]{2,1,0:T(8,128)S(1)}, u32[]{:S(2)}, u32[]{:S(2)}) collective-permute-start(f32[2,128,256]{2,1,0:T(8,128)S(1)} %get-tuple-element.68), channel_id=1, source_target_pairs={{0,28},{4,8},{8,4},{12,16},{16,12},{20,24},{24,20},{28,0},{1,29},{... | collective-permute-start | bytes 786440 | tf_op jit(solution)/shard_map/ppermute | solution.py:913
  32.3 3.5 %coarse.1 = (f32[20,72,128]{2,1,0:T(8,128)S(1)}, f32[312,128]{1,0:T(8,128)S(1)}, f32[312,128]{1,0:T(8,128)S(1)}) custom-call(f32[16]{0:T(128)S(1)} %copy-done.20, s32[3,7]{1,0:T(4,128)S(1)} %copy-done.19, f32[16,96,128]{2,1,0:T(8,128)S(1)} %get-tuple-element.58.refs_2_, f32[248,128]{1,0:T(8,128)S(1)} %collective-permute-done.8.refs_3_, ...), custom_call_target="tpu_custom_call" | custom-call | flops 1000 | bytes 1000 | tf_op jit(solution)/shard_map/coarse/pallas_call | solution.py:250
  35.8 0.1 collective-permute-start.10
  35.8 1.9 %collective-permute-start.11 = (f32[312,128]{1,0:T(8,128)S(1)}, f32[312,128]{1,0:T(8,128)S(1)}, u32[]{:S(2)}, u32[]{:S(2)}) collective-permute-start(f32[312,128]{1,0:T(8,128)S(1)} %get-tuple-element.62), channel_id=1, source_target_pairs={{0,28},{4,8},{8,4},{12,16},{16,12},{20,24},{24,20},{28,0},{1,29},{... | collective-permute-start | bytes 479240 | tf_op jit(solution)/shard_map/ppermute | solution.py:913
  37.8 2.1 %inner_bands.1.refs_1_ = f32[24,144,256]{2,1,0:T(8,128)S(1)} custom-call(f32[16]{0:T(128)S(1)} %copy-done.20, s32[3,7]{1,0:T(4,128)S(1)} %copy-done.19, f32[32,144,256]{2,1,0:T(8,128)S(1)} %y_analysis.1.refs_0_.refs_2_), custom_call_target="tpu_custom_call" | custom-call | flops 1000 | bytes 1000 | tf_op jit(solution)/shard_map/inner_bands/pallas_call | solution.py:250
  39.8 0.0 copy-start.3
  39.9 0.0 copy-start.8
  39.9 4.4 %detail_yz.1.refs_0_ = f32[32,128,256]{2,1,0:T(8,128)S(1)} custom-call(f32[8,144,256]{2,1,0:T(8,128)S(1)} %get-tuple-element.63.refs_0_, f32[24,144,256]{2,1,0:T(8,128)S(1)} %inner_bands.1.refs_1_, f32[20,72,128]{2,1,0:T(8,128)S(1)} %get-tuple-element.66.refs_2_.refs_1_, bf16[768,256]{1,0:T(8,128)(2,1)S(1)} %copy-done.2, bf16[128,432]{1,0:T(8,128)(2,1)S(1)} %copy-done.5), custom_call_target="tpu_custom_call" | custom-call | flops 1000 | bytes 1000 | tf_op jit(solution)/shard_map/detail_yz/pallas_call | solution.py:250
  44.3 0.0 copy-start.10
  44.3 0.0 copy-start.14
  44.3 2.0 %collective-permute-done.12.refs_2_ = f32[2,128,256]{2,1,0:T(8,128)S(1)} collective-permute-done((f32[2,128,256]{2,1,0:T(8,128)S(1)}, f32[2,128,256]{2,1,0:T(8,128)S(1)}, u32[]{:S(2)}, u32[]{:S(2)}) %collective-permute-start.12) | collective-permute-done | bytes 262176 | tf_op jit(solution)/shard_map/ppermute | solution.py:913
  46.4 2.1 %own_result.1.refs_2_ = f32[32,128,256]{2,1,0:T(8,128)S(1)} custom-call(f32[32,128,256]{2,1,0:T(8,128)S(1)} %detail_yz.1.refs_0_, f32[20,72,128]{2,1,0:T(8,128)S(1)} %get-tuple-element.66.refs_2_.refs_1_, f32[2,128,256]{2,1,0:T(8,128)S(1)} %collective-permute-done.12.refs_2_, f32[2,128,256]{2,1,0:T(8,128)S(1)} %collective-permute-done.13.refs_3_, ...), custom_call_target="tpu_custom_call" | custom-call | flops 1000 | bytes 1000 | tf_op jit(solution)/shard_map/own_result/pallas_call | solution.py:250
  48.5 3.0 %final.1 = f32[32,128,256]{2,1,0:T(8,128)} custom-call(f32[312,128]{1,0:T(8,128)S(1)} %collective-permute-done.10.refs_0_, f32[312,128]{1,0:T(8,128)S(1)} %collective-permute-done.11.refs_1_, f32[32,128,256]{2,1,0:T(8,128)S(1)} %own_result.1.refs_2_, bf16[384,256]{1,0:T(8,128)(2,1)S(1)} %copy-done.10, bf16[128,144]{1,0:T(8,128)(2,1)S(1)} %copy-done.14, ...), custom_call_target="tpu_custom_call" | custom-call | flops 1000 | bytes 1000 | tf_op jit(solution)/shard_map/final/pallas_call | solution.py:250
  (35 shorter events, 0.1 us)
Async XLA Ops:
  0.0 9.3 %copy-start = (f32[32,128,256]{2,1,0:T(8,128)S(1)}, f32[32,128,256]{2,1,0:T(8,128)}, u32[]{:S(2)}) copy-start(f32[32,128,256]{2,1,0:T(8,128)} %refs_0_.6) | copy-start | bytes 12582916
  1.6 12.9 %collective-permute-start.2 = (f32[28,8,256]{2,1,0:T(8,128)S(1)}, f32[28,8,256]{2,1,0:T(8,128)S(1)}, u32[]{:S(2)}, u32[]{:S(2)}) collective-permute-start(f32[28,8,256]{2,1,0:T(8,128)S(1)} %get-tuple-element.41), channel_id=1, source_target_pairs={{0,3},{1,2},{2,1},{3,0},{4,7},{5,6},{6,5},{7,4},{8,11},{9,10},{10,... | collective-permute-start | bytes 688136 | tf_op jit(solution)/shard_map/ppermute | solution.py:913
  4.1 14.5 %collective-permute-start = (f32[2,128,256]{2,1,0:T(8,128)S(1)}, f32[2,128,256]{2,1,0:T(8,128)S(1)}, u32[]{:S(2)}, u32[]{:S(2)}) collective-permute-start(f32[2,128,256]{2,1,0:T(8,128)S(1)} %get-tuple-element.37), channel_id=1, source_target_pairs={{0,4},{4,0},{8,12},{12,8},{16,20},{20,16},{24,28},{28,24},{1,5},{5... | collective-permute-start | bytes 786440 | tf_op jit(solution)/shard_map/ppermute | solution.py:913
  5.6 13.0 %collective-permute-start.1 = (f32[2,128,256]{2,1,0:T(8,128)S(1)}, f32[2,128,256]{2,1,0:T(8,128)S(1)}, u32[]{:S(2)}, u32[]{:S(2)}) collective-permute-start(f32[2,128,256]{2,1,0:T(8,128)S(1)} %get-tuple-element.38), channel_id=1, source_target_pairs={{0,28},{4,8},{8,4},{12,16},{16,12},{20,24},{24,20},{28,0},{1,29},{... | collective-permute-start | bytes 786440 | tf_op jit(solution)/shard_map/ppermute | solution.py:913
  9.2 5.4 %collective-permute-start.3 = (f32[28,8,256]{2,1,0:T(8,128)S(1)}, f32[28,8,256]{2,1,0:T(8,128)S(1)}, u32[]{:S(2)}, u32[]{:S(2)}) collective-permute-start(f32[28,8,256]{2,1,0:T(8,128)S(1)} %get-tuple-element.42), channel_id=1, source_target_pairs={{0,1},{1,0},{2,3},{3,2},{4,5},{5,4},{6,7},{7,6},{8,9},{9,8},{10,11... | collective-permute-start | bytes 688136 | tf_op jit(solution)/shard_map/ppermute | solution.py:913
  9.3 1.0 %copy-start.1 = (bf16[768,256]{1,0:T(8,128)(2,1)S(1)}, bf16[768,256]{1,0:T(8,128)(2,1)}, u32[]{:S(2)}) copy-start(bf16[768,256]{1,0:T(8,128)(2,1)} %constant.36.clone.refs_1_.refs_3_) | copy-start | bytes 1179652
  10.3 2.0 %copy-start.15 = (bf16[80,384]{1,0:T(8,128)(2,1)S(1)}, bf16[80,384]{1,0:T(8,128)(2,1)}, u32[]{:S(2)}) copy-start(bf16[80,384]{1,0:T(8,128)(2,1)} %constant.37.clone.refs_1_) | copy-start | bytes 184324
  12.3 2.2 %copy-start.4 = (bf16[144,432]{1,0:T(8,128)(2,1)S(1)}, bf16[144,432]{1,0:T(8,128)(2,1)}, u32[]{:S(2)}) copy-start(bf16[144,432]{1,0:T(8,128)(2,1)} %constant.38.clone.refs_4_.refs_6_) | copy-start | bytes 373252
  13.9 6.8 %collective-permute-start.7 = (f32[16,24,128]{2,1,0:T(8,128)S(1)}, f32[16,24,128]{2,1,0:T(8,128)S(1)}, u32[]{:S(2)}, u32[]{:S(2)}) collective-permute-start(f32[16,24,128]{2,1,0:T(8,128)S(1)} %get-tuple-element.50), channel_id=1, source_target_pairs={{0,3},{1,2},{2,1},{3,0},{4,7},{5,6},{6,5},{7,4},{8,11},{9,10},{10,... | collective-permute-start | bytes 589832 | tf_op jit(solution)/shard_map/ppermute | solution.py:913
  14.5 6.2 %collective-permute-start.6 = (f32[16,24,128]{2,1,0:T(8,128)S(1)}, f32[16,24,128]{2,1,0:T(8,128)S(1)}, u32[]{:S(2)}, u32[]{:S(2)}) collective-permute-start(f32[16,24,128]{2,1,0:T(8,128)S(1)} %get-tuple-element.39), channel_id=1, source_target_pairs={{0,1},{1,0},{2,3},{3,2},{4,5},{5,4},{6,7},{7,6},{8,9},{9,8},{10,11... | collective-permute-start | bytes 589832 | tf_op jit(solution)/shard_map/ppermute | solution.py:913
  16.9 3.8 %copy-start.6 = (bf16[256,256]{1,0:T(8,128)(2,1)S(1)}, bf16[256,256]{1,0:T(8,128)(2,1)}, u32[]{:S(2)}) copy-start(bf16[256,256]{1,0:T(8,128)(2,1)} %constant.39.clone.refs_3_.refs_9_) | copy-start | bytes 393220
  17.0 3.7 %copy-start.7 = (bf16[96,384]{1,0:T(8,128)(2,1)S(1)}, bf16[96,384]{1,0:T(8,128)(2,1)}, u32[]{:S(2)}) copy-start(bf16[96,384]{1,0:T(8,128)(2,1)} %constant.40.clone.refs_4_.refs_11_) | copy-start | bytes 221188
  17.0 9.1 %copy-start.2 = (bf16[768,256]{1,0:T(8,128)(2,1)S(1)}, bf16[768,256]{1,0:T(8,128)(2,1)}, u32[]{:S(2)}) copy-start(bf16[768,256]{1,0:T(8,128)(2,1)} %constant.41.clone.refs_7_.refs_3_) | copy-start | bytes 1179652
  17.0 9.1 %copy-start.5 = (bf16[128,432]{1,0:T(8,128)(2,1)S(1)}, bf16[128,432]{1,0:T(8,128)(2,1)}, u32[]{:S(2)}) copy-start(bf16[128,432]{1,0:T(8,128)(2,1)} %constant.42.clone.refs_8_.refs_4_) | copy-start | bytes 331780
  17.0 9.1 %copy-start.19 = (s32[3,7]{1,0:T(4,128)S(1)}, s32[3,7]{1,0:T(4,128)}, u32[]{:S(2)}) copy-start(s32[3,7]{1,0:T(4,128)} %refs_1_.7) | copy-start | bytes 256
  17.0 9.1 %copy-start.20 = (f32[16]{0:T(128)S(1)}, f32[16]{0:T(128)}, u32[]{:S(2)}) copy-start(f32[16]{0:T(128)} %refs_0_.9) | copy-start | bytes 196
  17.5 14.7 %copy-start.9 = (bf16[128,672]{1,0:T(8,128)(2,1)S(1)}, bf16[128,672]{1,0:T(8,128)(2,1)}, u32[]{:S(2)}) copy-start(bf16[128,672]{1,0:T(8,128)(2,1)} %constant.43.clone.refs_10_) | copy-start | bytes 516100
  17.5 14.7 %copy-start.11 = (bf16[256,256]{1,0:T(8,128)(2,1)S(1)}, bf16[256,256]{1,0:T(8,128)(2,1)}, u32[]{:S(2)}) copy-start(bf16[256,256]{1,0:T(8,128)(2,1)} %constant.46.clone.refs_14_) | copy-start | bytes 393220
  17.5 14.7 %copy-start.12 = (bf16[256,256]{1,0:T(8,128)(2,1)S(1)}, bf16[256,256]{1,0:T(8,128)(2,1)}, u32[]{:S(2)}) copy-start(bf16[256,256]{1,0:T(8,128)(2,1)} %constant.45.clone.refs_13_) | copy-start | bytes 393220
  17.6 14.7 %copy-start.13 = (bf16[256,256]{1,0:T(8,128)(2,1)S(1)}, bf16[256,256]{1,0:T(8,128)(2,1)}, u32[]{:S(2)}) copy-start(bf16[256,256]{1,0:T(8,128)(2,1)} %constant.44.clone.refs_12_) | copy-start | bytes 393220
  17.6 14.7 %copy-start.16 = (bf16[80,288]{1,0:T(8,128)(2,1)S(1)}, bf16[80,288]{1,0:T(8,128)(2,1)}, u32[]{:S(2)}) copy-start(bf16[80,288]{1,0:T(8,128)(2,1)} %constant.49.clone.refs_17_) | copy-start | bytes 138244
  17.6 14.7 %copy-start.17 = (bf16[64,144]{1,0:T(8,128)(2,1)S(1)}, bf16[64,144]{1,0:T(8,128)(2,1)}, u32[]{:S(2)}) copy-start(bf16[64,144]{1,0:T(8,128)(2,1)} %constant.48.clone.refs_16_) | copy-start | bytes 55300
  17.6 14.7 %copy-start.18 = (bf16[48,192]{1,0:T(8,128)(2,1)S(1)}, bf16[48,192]{1,0:T(8,128)(2,1)}, u32[]{:S(2)}) copy-start(bf16[48,192]{1,0:T(8,128)(2,1)} %constant.47.clone.refs_15_) | copy-start | bytes 55300
  19.0 7.0 %collective-permute-start.4 = (f32[4,80,128]{2,1,0:T(8,128)S(1)}, f32[4,80,128]{2,1,0:T(8,128)S(1)}, u32[]{:S(2)}, u32[]{:S(2)}) collective-permute-start(f32[4,80,128]{2,1,0:T(8,128)S(1)} %get-tuple-element.46), channel_id=1, source_target_pairs={{0,1},{1,0},{2,3},{3,2},{4,5},{5,4},{6,7},{7,6},{8,9},{9,8},{10,11... | collective-permute-start | bytes 491528 | tf_op jit(solution)/shard_map/ppermute | solution.py:913
  19.1 6.9 %collective-permute-start.5 = (f32[4,80,128]{2,1,0:T(8,128)S(1)}, f32[4,80,128]{2,1,0:T(8,128)S(1)}, u32[]{:S(2)}, u32[]{:S(2)}) collective-permute-start(f32[4,80,128]{2,1,0:T(8,128)S(1)} %get-tuple-element.47), channel_id=1, source_target_pairs={{0,3},{1,2},{2,1},{3,0},{4,7},{5,6},{6,5},{7,4},{8,11},{9,10},{10,... | collective-permute-start | bytes 491528 | tf_op jit(solution)/shard_map/ppermute | solution.py:913
  21.9 10.3 %collective-permute-start.8 = (f32[248,128]{1,0:T(8,128)S(1)}, f32[248,128]{1,0:T(8,128)S(1)}, u32[]{:S(2)}, u32[]{:S(2)}) collective-permute-start(f32[248,128]{1,0:T(8,128)S(1)} %get-tuple-element.59), channel_id=1, source_target_pairs={{0,4},{4,0},{8,12},{12,8},{16,20},{20,16},{24,28},{28,24},{1,5},{5... | collective-permute-start | bytes 380936 | tf_op jit(solution)/shard_map/ppermute | solution.py:913
  22.5 9.7 %collective-permute-start.9 = (f32[248,128]{1,0:T(8,128)S(1)}, f32[248,128]{1,0:T(8,128)S(1)}, u32[]{:S(2)}, u32[]{:S(2)}) collective-permute-start(f32[248,128]{1,0:T(8,128)S(1)} %get-tuple-element.60), channel_id=1, source_target_pairs={{0,28},{4,8},{8,4},{12,16},{16,12},{20,24},{24,20},{28,0},{1,29},{... | collective-permute-start | bytes 380936 | tf_op jit(solution)/shard_map/ppermute | solution.py:913
  28.0 18.3 %collective-permute-start.12 = (f32[2,128,256]{2,1,0:T(8,128)S(1)}, f32[2,128,256]{2,1,0:T(8,128)S(1)}, u32[]{:S(2)}, u32[]{:S(2)}) collective-permute-start(f32[2,128,256]{2,1,0:T(8,128)S(1)} %get-tuple-element.67), channel_id=1, source_target_pairs={{0,4},{4,0},{8,12},{12,8},{16,20},{20,16},{24,28},{28,24},{1,5},{5... | collective-permute-start | bytes 786440 | tf_op jit(solution)/shard_map/ppermute | solution.py:913
  28.6 17.7 %collective-permute-start.13 = (f32[2,128,256]{2,1,0:T(8,128)S(1)}, f32[2,128,256]{2,1,0:T(8,128)S(1)}, u32[]{:S(2)}, u32[]{:S(2)}) collective-permute-start(f32[2,128,256]{2,1,0:T(8,128)S(1)} %get-tuple-element.68), channel_id=1, source_target_pairs={{0,28},{4,8},{8,4},{12,16},{16,12},{20,24},{24,20},{28,0},{1,29},{... | collective-permute-start | bytes 786440 | tf_op jit(solution)/shard_map/ppermute | solution.py:913
  35.8 12.7 %collective-permute-start.10 = (f32[312,128]{1,0:T(8,128)S(1)}, f32[312,128]{1,0:T(8,128)S(1)}, u32[]{:S(2)}, u32[]{:S(2)}) collective-permute-start(f32[312,128]{1,0:T(8,128)S(1)} %get-tuple-element.61), channel_id=1, source_target_pairs={{0,4},{4,0},{8,12},{12,8},{16,20},{20,16},{24,28},{28,24},{1,5},{5... | collective-permute-start | bytes 479240 | tf_op jit(solution)/shard_map/ppermute | solution.py:913
  35.8 12.7 %collective-permute-start.11 = (f32[312,128]{1,0:T(8,128)S(1)}, f32[312,128]{1,0:T(8,128)S(1)}, u32[]{:S(2)}, u32[]{:S(2)}) collective-permute-start(f32[312,128]{1,0:T(8,128)S(1)} %get-tuple-element.62), channel_id=1, source_target_pairs={{0,28},{4,8},{8,4},{12,16},{16,12},{20,24},{24,20},{28,0},{1,29},{... | collective-permute-start | bytes 479240 | tf_op jit(solution)/shard_map/ppermute | solution.py:913
  39.8 6.5 %copy-start.3 = (bf16[384,256]{1,0:T(8,128)(2,1)S(1)}, bf16[384,256]{1,0:T(8,128)(2,1)}, u32[]{:S(2)}) copy-start(bf16[384,256]{1,0:T(8,128)(2,1)} %constant.50.clone.refs_4_.refs_5_) | copy-start | bytes 589828
  39.9 6.5 %copy-start.8 = (bf16[128,240]{1,0:T(8,128)(2,1)S(1)}, bf16[128,240]{1,0:T(8,128)(2,1)}, u32[]{:S(2)}) copy-start(bf16[128,240]{1,0:T(8,128)(2,1)} %constant.51.clone.refs_5_.refs_6_) | copy-start | bytes 184324
  44.3 4.2 %copy-start.10 = (bf16[384,256]{1,0:T(8,128)(2,1)S(1)}, bf16[384,256]{1,0:T(8,128)(2,1)}, u32[]{:S(2)}) copy-start(bf16[384,256]{1,0:T(8,128)(2,1)} %constant.52.clone.refs_3_) | copy-start | bytes 589828
  44.3 4.2 %copy-start.14 = (bf16[128,144]{1,0:T(8,128)(2,1)S(1)}, bf16[128,144]{1,0:T(8,128)(2,1)}, u32[]{:S(2)}) copy-start(bf16[128,144]{1,0:T(8,128)(2,1)} %constant.53.clone.refs_4_) | copy-start | bytes 110596

commit v12 on v11

--- a/solution.py
+++ b/solution.py
@@ -668,8 +668,8 @@
 
 
     def kernel(o_ref, l_ref, r_ref, z, y, out, up, down):
-        for i in range(0, n1, 8):
-            stack = [part[j] for j in range(i, i + 8) for part in (o_ref, l_ref, r_ref)]
+        for i in range(0, n1, 16):
+            stack = [part[j] for j in range(i, min(i + 16, n1)) for part in (o_ref, l_ref, r_ref)]
             zed = times_wide(jnp.concatenate(stack, axis=0), z)
             for j, plane in enumerate(in_pairs(y, cut(zed, in_rows))):
                 out[i + j] = plane
@@ -782,8 +782,8 @@
         zed = times_wide(jnp.concatenate(stack, axis=0), z1)
         for i, plane in enumerate(in_pairs(s1, cut(zed, low_rows))):
             p1[2 * n2 + i] = plane[:out_rows]
-        for i in range(0, 2 * n2, 8):
-            zed = times_wide(c1[i : i + 8].reshape(8 * rows, nz), z1)
+        for i in range(0, 2 * n2, 16):
+            zed = times_wide(c1[i : i + 16].reshape(16 * rows, nz), z1)
             for j, plane in enumerate(in_pairs(s1, cut(zed, rows))):
                 p1[i + j] = plane[:out_rows]
         lows = {k: p1.at[k] for k in range(n2)}

time: 51.7 us -> 51.7 us (level)
  transfers between devices with their start and end apart: 14 -> 14, of which waited for: 3 -> 4; matrix products, arithmetic and copies ran while one was open for 0% -> 0% of each run, Pallas kernels for 43% -> 42%
where the time goes in v12:
time: 51.7 us; the launch traced here: 51.5 us
  Pallas kernels  26.4 us (51%)
  starting transfers between devices  19.6 us (38%)
  waiting for transfers between devices  4.03 us (8%)
  local copies, waits for them, and re-layouts  1.13 us (2%)
    pallas_call x13, Pallas kernels, whole_call(): pl.pallas_call(kernel, in_specs=changes.get('in_specs', specs), out_specs...  26.4 us
    ppermute x14, starting transfers between devices, exchange(): return (lax.ppermute(first, axis, here), lax.ppermute(second, axis, across))  19.6 us
    ppermute x14, waiting for transfers between devices, exchange(): return (lax.ppermute(first, axis, here), lax.ppermute(second, axis, across))  4.03 us
    unnamed x42, local copies, waits for them, and re-layouts  1.13 us
  transfers between devices with their start and end apart: 14, of which 4 were waited for; matrix products, arithmetic and copies ran while one was open for 0% of the time, Pallas kernels for 42%

profile of v12, /device:TPU:0, one launch (start us, length us, event | category | flops | bytes accessed | tf_op | source)
XLA Modules:
  0.0 51.5 jit_solution(8871972672822662752)
XLA Ops:
  0.0 1.6 %first_messages.1 = (f32[2,128,256]{2,1,0:T(8,128)S(1)}, f32[2,128,256]{2,1,0:T(8,128)S(1)}, f32[28,8,256]{2,1,0:T(8,128)S(1)}, f32[28,8,256]{2,1,0:T(8,128)S(1)}) custom-call(f32[32,128,256]{2,1,0:T(8,128)} %refs_0_.6), custom_call_target="tpu_custom_call" | custom-call | flops 1000 | bytes 1000 | tf_op jit(solution)/shard_map/first_messages/pallas_call | solution.py:250
  1.6 2.5 %collective-permute-start.2 = (f32[28,8,256]{2,1,0:T(8,128)S(1)}, f32[28,8,256]{2,1,0:T(8,128)S(1)}, u32[]{:S(2)}, u32[]{:S(2)}) collective-permute-start(f32[28,8,256]{2,1,0:T(8,128)S(1)} %get-tuple-element.41), channel_id=1, source_target_pairs={{0,3},{1,2},{2,1},{3,0},{4,7},{5,6},{6,5},{7,4},{8,11},{9,10},{10,... | collective-permute-start | bytes 688136 | tf_op jit(solution)/shard_map/ppermute | solution.py:913
  4.1 1.5 %collective-permute-start = (f32[2,128,256]{2,1,0:T(8,128)S(1)}, f32[2,128,256]{2,1,0:T(8,128)S(1)}, u32[]{:S(2)}, u32[]{:S(2)}) collective-permute-start(f32[2,128,256]{2,1,0:T(8,128)S(1)} %get-tuple-element.37), channel_id=1, source_target_pairs={{0,4},{4,0},{8,12},{12,8},{16,20},{20,16},{24,28},{28,24},{1,5},{5... | collective-permute-start | bytes 786440 | tf_op jit(solution)/shard_map/ppermute | solution.py:913
  5.6 3.6 %collective-permute-start.1 = (f32[2,128,256]{2,1,0:T(8,128)S(1)}, f32[2,128,256]{2,1,0:T(8,128)S(1)}, u32[]{:S(2)}, u32[]{:S(2)}) collective-permute-start(f32[2,128,256]{2,1,0:T(8,128)S(1)} %get-tuple-element.38), channel_id=1, source_target_pairs={{0,28},{4,8},{8,4},{12,16},{16,12},{20,24},{24,20},{28,0},{1,29},{... | collective-permute-start | bytes 786440 | tf_op jit(solution)/shard_map/ppermute | solution.py:913
  9.2 0.1 collective-permute-start.3
  9.3 1.0 %copy-done.1 = bf16[768,256]{1,0:T(8,128)(2,1)S(1)} copy-done((bf16[768,256]{1,0:T(8,128)(2,1)S(1)}, bf16[768,256]{1,0:T(8,128)(2,1)}, u32[]{:S(2)}) %copy-start.1) | copy-done | bytes 393240
  10.3 2.0 %depth_analysis.1.refs_0_ = f32[32,128,256]{2,1,0:T(8,128)S(1)} custom-call(f32[32,128,256]{2,1,0:T(8,128)S(1)} %copy-done, bf16[768,256]{1,0:T(8,128)(2,1)S(1)} %copy-done.1), custom_call_target="tpu_custom_call" | custom-call | flops 1000 | bytes 1000 | tf_op jit(solution)/shard_map/depth_analysis/pallas_call | solution.py:250
  12.3 0.0 copy-start.4
  12.3 1.5 %own_approx.1 = (f32[20,72,128]{2,1,0:T(8,128)S(1)}, f32[16,24,128]{2,1,0:T(8,128)S(1)}, f32[16,24,128]{2,1,0:T(8,128)S(1)}) custom-call(f32[32,128,256]{2,1,0:T(8,128)S(1)} %depth_analysis.1.refs_0_, bf16[80,384]{1,0:T(8,128)(2,1)S(1)} %copy-done.15), custom_call_target="tpu_custom_call" | custom-call | flops 1000 | bytes 1000 | tf_op jit(solution)/shard_map/own_approx/pallas_call | solution.py:250
  13.9 0.7 %collective-permute-start.7 = (f32[16,24,128]{2,1,0:T(8,128)S(1)}, f32[16,24,128]{2,1,0:T(8,128)S(1)}, u32[]{:S(2)}, u32[]{:S(2)}) collective-permute-start(f32[16,24,128]{2,1,0:T(8,128)S(1)} %get-tuple-element.50), channel_id=1, source_target_pairs={{0,3},{1,2},{2,1},{3,0},{4,7},{5,6},{6,5},{7,4},{8,11},{9,10},{10,... | collective-permute-start | bytes 589832 | tf_op jit(solution)/shard_map/ppermute | solution.py:913
  14.6 2.4 %y_analysis.1.refs_0_.refs_2_ = f32[32,144,256]{2,1,0:T(8,128)S(1)} custom-call(f32[32,128,256]{2,1,0:T(8,128)S(1)} %depth_analysis.1.refs_0_, f32[28,8,256]{2,1,0:T(8,128)S(1)} %collective-permute-done.2.refs_1_, f32[28,8,256]{2,1,0:T(8,128)S(1)} %collective-permute-done.3.refs_2_, bf16[768,256]{1,0:T(8,128)(2,1)S(1)} %copy-done.1, ...), custom_call_target="tpu_custom_call" | custom-call | flops 1000 | bytes 1000 | tf_op jit(solution)/shard_map/y_analysis/pallas_call | solution.py:250
  16.9 0.0 copy-start.6
  17.0 0.0 copy-start.7
  17.0 0.0 copy-start.2
  17.0 0.0 copy-start.5
  17.0 0.0 copy-start.19
  17.0 0.5 edge_own.1.refs_2_
  17.5 0.0 copy-start.9
  17.5 0.0 copy-start.11
  17.5 0.0 copy-start.12
  17.6 0.0 copy-start.13
  17.6 0.0 copy-start.16
  17.6 0.0 copy-start.17
  17.6 0.0 copy-start.18
  17.6 1.0 %collective-permute-done.refs_0_ = f32[2,128,256]{2,1,0:T(8,128)S(1)} collective-permute-done((f32[2,128,256]{2,1,0:T(8,128)S(1)}, f32[2,128,256]{2,1,0:T(8,128)S(1)}, u32[]{:S(2)}, u32[]{:S(2)}) %collective-permute-start) | collective-permute-done | bytes 262176 | tf_op jit(solution)/shard_map/ppermute | solution.py:913
  18.6 0.4 x_halo_messages.1
  19.0 0.1 collective-permute-start.4
  19.1 0.6 %collective-permute-start.5 = (f32[4,80,128]{2,1,0:T(8,128)S(1)}, f32[4,80,128]{2,1,0:T(8,128)S(1)}, u32[]{:S(2)}, u32[]{:S(2)}) collective-permute-start(f32[4,80,128]{2,1,0:T(8,128)S(1)} %get-tuple-element.47), channel_id=1, source_target_pairs={{0,3},{1,2},{2,1},{3,0},{4,7},{5,6},{6,5},{7,4},{8,11},{9,10},{10,... | collective-permute-start | bytes 491528 | tf_op jit(solution)/shard_map/ppermute | solution.py:913
  19.8 0.9 %collective-permute-done.7.refs_2_ = f32[16,24,128]{2,1,0:T(8,128)S(1)} collective-permute-done((f32[16,24,128]{2,1,0:T(8,128)S(1)}, f32[16,24,128]{2,1,0:T(8,128)S(1)}, u32[]{:S(2)}, u32[]{:S(2)}) %collective-permute-start.7) | collective-permute-done | bytes 196640 | tf_op jit(solution)/shard_map/ppermute | solution.py:913
  20.7 1.0 %second_bands.1 = (f32[16,96,128]{2,1,0:T(8,128)S(1)}, f32[248,128]{1,0:T(8,128)S(1)}, f32[248,128]{1,0:T(8,128)S(1)}) custom-call(f32[20,72,128]{2,1,0:T(8,128)S(1)} %get-tuple-element.49.refs_2_.refs_0_.refs_8_, f32[16,24,128]{2,1,0:T(8,128)S(1)} %collective-permute-done.6.refs_1_, f32[16,24,128]{2,1,0:T(8,128)S(1)} %collective-permute-done.7.refs_2_, ...), custom_call_target="tpu_custom_call" | custom-call | flops 1000 | bytes 1000 | tf_op jit(solution)/shard_map/second_bands/pallas_call | solution.py:250
  21.7 0.6 %collective-permute-start.8 = (f32[248,128]{1,0:T(8,128)S(1)}, f32[248,128]{1,0:T(8,128)S(1)}, u32[]{:S(2)}, u32[]{:S(2)}) collective-permute-start(f32[248,128]{1,0:T(8,128)S(1)} %get-tuple-element.59), channel_id=1, source_target_pairs={{0,4},{4,0},{8,12},{12,8},{16,20},{20,16},{24,28},{28,24},{1,5},{5... | collective-permute-start | bytes 380936 | tf_op jit(solution)/shard_map/ppermute | solution.py:913
  22.3 3.6 %collective-permute-start.9 = (f32[248,128]{1,0:T(8,128)S(1)}, f32[248,128]{1,0:T(8,128)S(1)}, u32[]{:S(2)}, u32[]{:S(2)}) collective-permute-start(f32[248,128]{1,0:T(8,128)S(1)} %get-tuple-element.60), channel_id=1, source_target_pairs={{0,28},{4,8},{8,4},{12,16},{16,12},{20,24},{24,20},{28,0},{1,29},{... | collective-permute-start | bytes 380936 | tf_op jit(solution)/shard_map/ppermute | solution.py:913
  25.9 1.9 %edge_details.1 = (f32[8,144,256]{2,1,0:T(8,128)S(1)}, f32[2,128,256]{2,1,0:T(8,128)S(1)}, f32[2,128,256]{2,1,0:T(8,128)S(1)}) custom-call(f32[16]{0:T(128)S(1)} %copy-done.20, s32[3,7]{1,0:T(4,128)S(1)} %copy-done.19, f32[8,144,256]{2,1,0:T(8,128)S(1)} %edge_own.1.refs_2_, f32[4,128,256]{2,1,0:T(8,128)S(1)} %get-tuple-element.54.refs_3_.refs_5_, ...), custom_call_target="tpu_custom_call" | custom-call | flops 1000 | bytes 1000 | tf_op jit(solution)/shard_map/edge_details/pallas_call | solution.py:250
  27.8 0.8 %collective-permute-start.12 = (f32[2,128,256]{2,1,0:T(8,128)S(1)}, f32[2,128,256]{2,1,0:T(8,128)S(1)}, u32[]{:S(2)}, u32[]{:S(2)}) collective-permute-start(f32[2,128,256]{2,1,0:T(8,128)S(1)} %get-tuple-element.67), channel_id=1, source_target_pairs={{0,4},{4,0},{8,12},{12,8},{16,20},{20,16},{24,28},{28,24},{1,5},{5... | collective-permute-start | bytes 786440 | tf_op jit(solution)/shard_map/ppermute | solution.py:913
  28.6 3.6 %collective-permute-start.13 = (f32[2,128,256]{2,1,0:T(8,128)S(1)}, f32[2,128,256]{2,1,0:T(8,128)S(1)}, u32[]{:S(2)}, u32[]{:S(2)}) collective-permute-start(f32[2,128,256]{2,1,0:T(8,128)S(1)} %get-tuple-element.68), channel_id=1, source_target_pairs={{0,28},{4,8},{8,4},{12,16},{16,12},{20,24},{24,20},{28,0},{1,29},{... | collective-permute-start | bytes 786440 | tf_op jit(solution)/shard_map/ppermute | solution.py:913
  32.3 3.5 %coarse.1 = (f32[20,72,128]{2,1,0:T(8,128)S(1)}, f32[312,128]{1,0:T(8,128)S(1)}, f32[312,128]{1,0:T(8,128)S(1)}) custom-call(f32[16]{0:T(128)S(1)} %copy-done.20, s32[3,7]{1,0:T(4,128)S(1)} %copy-done.19, f32[16,96,128]{2,1,0:T(8,128)S(1)} %get-tuple-element.58.refs_2_, f32[248,128]{1,0:T(8,128)S(1)} %collective-permute-done.8.refs_3_, ...), custom_call_target="tpu_custom_call" | custom-call | flops 1000 | bytes 1000 | tf_op jit(solution)/shard_map/coarse/pallas_call | solution.py:250
  35.8 0.1 collective-permute-start.10
  35.8 1.9 %collective-permute-start.11 = (f32[312,128]{1,0:T(8,128)S(1)}, f32[312,128]{1,0:T(8,128)S(1)}, u32[]{:S(2)}, u32[]{:S(2)}) collective-permute-start(f32[312,128]{1,0:T(8,128)S(1)} %get-tuple-element.62), channel_id=1, source_target_pairs={{0,28},{4,8},{8,4},{12,16},{16,12},{20,24},{24,20},{28,0},{1,29},{... | collective-permute-start | bytes 479240 | tf_op jit(solution)/shard_map/ppermute | solution.py:913
  37.7 2.1 %inner_bands.1.refs_1_ = f32[24,144,256]{2,1,0:T(8,128)S(1)} custom-call(f32[16]{0:T(128)S(1)} %copy-done.20, s32[3,7]{1,0:T(4,128)S(1)} %copy-done.19, f32[32,144,256]{2,1,0:T(8,128)S(1)} %y_analysis.1.refs_0_.refs_2_), custom_call_target="tpu_custom_call" | custom-call | flops 1000 | bytes 1000 | tf_op jit(solution)/shard_map/inner_bands/pallas_call | solution.py:250
  39.8 0.0 copy-start.3
  39.8 0.0 copy-start.8
  39.8 4.4 %detail_yz.1.refs_0_ = f32[32,128,256]{2,1,0:T(8,128)S(1)} custom-call(f32[8,144,256]{2,1,0:T(8,128)S(1)} %get-tuple-element.63.refs_0_, f32[24,144,256]{2,1,0:T(8,128)S(1)} %inner_bands.1.refs_1_, f32[20,72,128]{2,1,0:T(8,128)S(1)} %get-tuple-element.66.refs_2_.refs_1_, bf16[768,256]{1,0:T(8,128)(2,1)S(1)} %copy-done.2, bf16[128,432]{1,0:T(8,128)(2,1)S(1)} %copy-done.5), custom_call_target="tpu_custom_call" | custom-call | flops 1000 | bytes 1000 | tf_op jit(solution)/shard_map/detail_yz/pallas_call | solution.py:250
  44.3 0.0 copy-start.10
  44.3 0.0 copy-start.14
  44.3 1.8 %collective-permute-done.12.refs_2_ = f32[2,128,256]{2,1,0:T(8,128)S(1)} collective-permute-done((f32[2,128,256]{2,1,0:T(8,128)S(1)}, f32[2,128,256]{2,1,0:T(8,128)S(1)}, u32[]{:S(2)}, u32[]{:S(2)}) %collective-permute-start.12) | collective-permute-done | bytes 262176 | tf_op jit(solution)/shard_map/ppermute | solution.py:913
  46.1 2.1 %own_result.1.refs_2_ = f32[32,128,256]{2,1,0:T(8,128)S(1)} custom-call(f32[32,128,256]{2,1,0:T(8,128)S(1)} %detail_yz.1.refs_0_, f32[20,72,128]{2,1,0:T(8,128)S(1)} %get-tuple-element.66.refs_2_.refs_1_, f32[2,128,256]{2,1,0:T(8,128)S(1)} %collective-permute-done.12.refs_2_, f32[2,128,256]{2,1,0:T(8,128)S(1)} %collective-permute-done.13.refs_3_, ...), custom_call_target="tpu_custom_call" | custom-call | flops 1000 | bytes 1000 | tf_op jit(solution)/shard_map/own_result/pallas_call | solution.py:250
  48.3 0.2 collective-permute-done.10.refs_0_
  48.5 3.0 %final.1 = f32[32,128,256]{2,1,0:T(8,128)} custom-call(f32[312,128]{1,0:T(8,128)S(1)} %collective-permute-done.10.refs_0_, f32[312,128]{1,0:T(8,128)S(1)} %collective-permute-done.11.refs_1_, f32[32,128,256]{2,1,0:T(8,128)S(1)} %own_result.1.refs_2_, bf16[384,256]{1,0:T(8,128)(2,1)S(1)} %copy-done.10, bf16[128,144]{1,0:T(8,128)(2,1)S(1)} %copy-done.14, ...), custom_call_target="tpu_custom_call" | custom-call | flops 1000 | bytes 1000 | tf_op jit(solution)/shard_map/final/pallas_call | solution.py:250
  (35 shorter events, 0.1 us)
Async XLA Ops:
  0.0 9.3 %copy-start = (f32[32,128,256]{2,1,0:T(8,128)S(1)}, f32[32,128,256]{2,1,0:T(8,128)}, u32[]{:S(2)}) copy-start(f32[32,128,256]{2,1,0:T(8,128)} %refs_0_.6) | copy-start | bytes 12582916
  1.6 12.9 %collective-permute-start.2 = (f32[28,8,256]{2,1,0:T(8,128)S(1)}, f32[28,8,256]{2,1,0:T(8,128)S(1)}, u32[]{:S(2)}, u32[]{:S(2)}) collective-permute-start(f32[28,8,256]{2,1,0:T(8,128)S(1)} %get-tuple-element.41), channel_id=1, source_target_pairs={{0,3},{1,2},{2,1},{3,0},{4,7},{5,6},{6,5},{7,4},{8,11},{9,10},{10,... | collective-permute-start | bytes 688136 | tf_op jit(solution)/shard_map/ppermute | solution.py:913
  4.1 14.5 %collective-permute-start = (f32[2,128,256]{2,1,0:T(8,128)S(1)}, f32[2,128,256]{2,1,0:T(8,128)S(1)}, u32[]{:S(2)}, u32[]{:S(2)}) collective-permute-start(f32[2,128,256]{2,1,0:T(8,128)S(1)} %get-tuple-element.37), channel_id=1, source_target_pairs={{0,4},{4,0},{8,12},{12,8},{16,20},{20,16},{24,28},{28,24},{1,5},{5... | collective-permute-start | bytes 786440 | tf_op jit(solution)/shard_map/ppermute | solution.py:913
  5.6 13.0 %collective-permute-start.1 = (f32[2,128,256]{2,1,0:T(8,128)S(1)}, f32[2,128,256]{2,1,0:T(8,128)S(1)}, u32[]{:S(2)}, u32[]{:S(2)}) collective-permute-start(f32[2,128,256]{2,1,0:T(8,128)S(1)} %get-tuple-element.38), channel_id=1, source_target_pairs={{0,28},{4,8},{8,4},{12,16},{16,12},{20,24},{24,20},{28,0},{1,29},{... | collective-permute-start | bytes 786440 | tf_op jit(solution)/shard_map/ppermute | solution.py:913
  9.2 5.4 %collective-permute-start.3 = (f32[28,8,256]{2,1,0:T(8,128)S(1)}, f32[28,8,256]{2,1,0:T(8,128)S(1)}, u32[]{:S(2)}, u32[]{:S(2)}) collective-permute-start(f32[28,8,256]{2,1,0:T(8,128)S(1)} %get-tuple-element.42), channel_id=1, source_target_pairs={{0,1},{1,0},{2,3},{3,2},{4,5},{5,4},{6,7},{7,6},{8,9},{9,8},{10,11... | collective-permute-start | bytes 688136 | tf_op jit(solution)/shard_map/ppermute | solution.py:913
  9.3 1.0 %copy-start.1 = (bf16[768,256]{1,0:T(8,128)(2,1)S(1)}, bf16[768,256]{1,0:T(8,128)(2,1)}, u32[]{:S(2)}) copy-start(bf16[768,256]{1,0:T(8,128)(2,1)} %constant.36.clone.refs_1_.refs_3_) | copy-start | bytes 1179652
  10.3 2.0 %copy-start.15 = (bf16[80,384]{1,0:T(8,128)(2,1)S(1)}, bf16[80,384]{1,0:T(8,128)(2,1)}, u32[]{:S(2)}) copy-start(bf16[80,384]{1,0:T(8,128)(2,1)} %constant.37.clone.refs_1_) | copy-start | bytes 184324
  12.3 2.2 %copy-start.4 = (bf16[144,432]{1,0:T(8,128)(2,1)S(1)}, bf16[144,432]{1,0:T(8,128)(2,1)}, u32[]{:S(2)}) copy-start(bf16[144,432]{1,0:T(8,128)(2,1)} %constant.38.clone.refs_4_.refs_6_) | copy-start | bytes 373252
  13.9 6.8 %collective-permute-start.7 = (f32[16,24,128]{2,1,0:T(8,128)S(1)}, f32[16,24,128]{2,1,0:T(8,128)S(1)}, u32[]{:S(2)}, u32[]{:S(2)}) collective-permute-start(f32[16,24,128]{2,1,0:T(8,128)S(1)} %get-tuple-element.50), channel_id=1, source_target_pairs={{0,3},{1,2},{2,1},{3,0},{4,7},{5,6},{6,5},{7,4},{8,11},{9,10},{10,... | collective-permute-start | bytes 589832 | tf_op jit(solution)/shard_map/ppermute | solution.py:913
  14.5 6.2 %collective-permute-start.6 = (f32[16,24,128]{2,1,0:T(8,128)S(1)}, f32[16,24,128]{2,1,0:T(8,128)S(1)}, u32[]{:S(2)}, u32[]{:S(2)}) collective-permute-start(f32[16,24,128]{2,1,0:T(8,128)S(1)} %get-tuple-element.39), channel_id=1, source_target_pairs={{0,1},{1,0},{2,3},{3,2},{4,5},{5,4},{6,7},{7,6},{8,9},{9,8},{10,11... | collective-permute-start | bytes 589832 | tf_op jit(solution)/shard_map/ppermute | solution.py:913
  16.9 3.8 %copy-start.6 = (bf16[256,256]{1,0:T(8,128)(2,1)S(1)}, bf16[256,256]{1,0:T(8,128)(2,1)}, u32[]{:S(2)}) copy-start(bf16[256,256]{1,0:T(8,128)(2,1)} %constant.39.clone.refs_3_.refs_9_) | copy-start | bytes 393220
  17.0 3.7 %copy-start.7 = (bf16[96,384]{1,0:T(8,128)(2,1)S(1)}, bf16[96,384]{1,0:T(8,128)(2,1)}, u32[]{:S(2)}) copy-start(bf16[96,384]{1,0:T(8,128)(2,1)} %constant.40.clone.refs_4_.refs_11_) | copy-start | bytes 221188
  17.0 8.9 %copy-start.2 = (bf16[768,256]{1,0:T(8,128)(2,1)S(1)}, bf16[768,256]{1,0:T(8,128)(2,1)}, u32[]{:S(2)}) copy-start(bf16[768,256]{1,0:T(8,128)(2,1)} %constant.41.clone.refs_7_.refs_3_) | copy-start | bytes 1179652
  17.0 8.9 %copy-start.5 = (bf16[128,432]{1,0:T(8,128)(2,1)S(1)}, bf16[128,432]{1,0:T(8,128)(2,1)}, u32[]{:S(2)}) copy-start(bf16[128,432]{1,0:T(8,128)(2,1)} %constant.42.clone.refs_8_.refs_4_) | copy-start | bytes 331780
  17.0 8.9 %copy-start.19 = (s32[3,7]{1,0:T(4,128)S(1)}, s32[3,7]{1,0:T(4,128)}, u32[]{:S(2)}) copy-start(s32[3,7]{1,0:T(4,128)} %refs_1_.7) | copy-start | bytes 256
  17.0 8.9 %copy-start.20 = (f32[16]{0:T(128)S(1)}, f32[16]{0:T(128)}, u32[]{:S(2)}) copy-start(f32[16]{0:T(128)} %refs_0_.9) | copy-start | bytes 196
  17.5 14.7 %copy-start.9 = (bf16[128,672]{1,0:T(8,128)(2,1)S(1)}, bf16[128,672]{1,0:T(8,128)(2,1)}, u32[]{:S(2)}) copy-start(bf16[128,672]{1,0:T(8,128)(2,1)} %constant.43.clone.refs_10_) | copy-start | bytes 516100
  17.5 14.7 %copy-start.11 = (bf16[256,256]{1,0:T(8,128)(2,1)S(1)}, bf16[256,256]{1,0:T(8,128)(2,1)}, u32[]{:S(2)}) copy-start(bf16[256,256]{1,0:T(8,128)(2,1)} %constant.46.clone.refs_14_) | copy-start | bytes 393220
  17.5 14.7 %copy-start.12 = (bf16[256,256]{1,0:T(8,128)(2,1)S(1)}, bf16[256,256]{1,0:T(8,128)(2,1)}, u32[]{:S(2)}) copy-start(bf16[256,256]{1,0:T(8,128)(2,1)} %constant.45.clone.refs_13_) | copy-start | bytes 393220
  17.6 14.7 %copy-start.13 = (bf16[256,256]{1,0:T(8,128)(2,1)S(1)}, bf16[256,256]{1,0:T(8,128)(2,1)}, u32[]{:S(2)}) copy-start(bf16[256,256]{1,0:T(8,128)(2,1)} %constant.44.clone.refs_12_) | copy-start | bytes 393220
  17.6 14.7 %copy-start.16 = (bf16[80,288]{1,0:T(8,128)(2,1)S(1)}, bf16[80,288]{1,0:T(8,128)(2,1)}, u32[]{:S(2)}) copy-start(bf16[80,288]{1,0:T(8,128)(2,1)} %constant.49.clone.refs_17_) | copy-start | bytes 138244
  17.6 14.7 %copy-start.17 = (bf16[64,144]{1,0:T(8,128)(2,1)S(1)}, bf16[64,144]{1,0:T(8,128)(2,1)}, u32[]{:S(2)}) copy-start(bf16[64,144]{1,0:T(8,128)(2,1)} %constant.48.clone.refs_16_) | copy-start | bytes 55300
  17.6 14.7 %copy-start.18 = (bf16[48,192]{1,0:T(8,128)(2,1)S(1)}, bf16[48,192]{1,0:T(8,128)(2,1)}, u32[]{:S(2)}) copy-start(bf16[48,192]{1,0:T(8,128)(2,1)} %constant.47.clone.refs_15_) | copy-start | bytes 55300
  19.0 6.8 %collective-permute-start.4 = (f32[4,80,128]{2,1,0:T(8,128)S(1)}, f32[4,80,128]{2,1,0:T(8,128)S(1)}, u32[]{:S(2)}, u32[]{:S(2)}) collective-permute-start(f32[4,80,128]{2,1,0:T(8,128)S(1)} %get-tuple-element.46), channel_id=1, source_target_pairs={{0,1},{1,0},{2,3},{3,2},{4,5},{5,4},{6,7},{7,6},{8,9},{9,8},{10,11... | collective-permute-start | bytes 491528 | tf_op jit(solution)/shard_map/ppermute | solution.py:913
  19.1 6.7 %collective-permute-start.5 = (f32[4,80,128]{2,1,0:T(8,128)S(1)}, f32[4,80,128]{2,1,0:T(8,128)S(1)}, u32[]{:S(2)}, u32[]{:S(2)}) collective-permute-start(f32[4,80,128]{2,1,0:T(8,128)S(1)} %get-tuple-element.47), channel_id=1, source_target_pairs={{0,3},{1,2},{2,1},{3,0},{4,7},{5,6},{6,5},{7,4},{8,11},{9,10},{10,... | collective-permute-start | bytes 491528 | tf_op jit(solution)/shard_map/ppermute | solution.py:913
  21.7 10.5 %collective-permute-start.8 = (f32[248,128]{1,0:T(8,128)S(1)}, f32[248,128]{1,0:T(8,128)S(1)}, u32[]{:S(2)}, u32[]{:S(2)}) collective-permute-start(f32[248,128]{1,0:T(8,128)S(1)} %get-tuple-element.59), channel_id=1, source_target_pairs={{0,4},{4,0},{8,12},{12,8},{16,20},{20,16},{24,28},{28,24},{1,5},{5... | collective-permute-start | bytes 380936 | tf_op jit(solution)/shard_map/ppermute | solution.py:913
  22.3 9.9 %collective-permute-start.9 = (f32[248,128]{1,0:T(8,128)S(1)}, f32[248,128]{1,0:T(8,128)S(1)}, u32[]{:S(2)}, u32[]{:S(2)}) collective-permute-start(f32[248,128]{1,0:T(8,128)S(1)} %get-tuple-element.60), channel_id=1, source_target_pairs={{0,28},{4,8},{8,4},{12,16},{16,12},{20,24},{24,20},{28,0},{1,29},{... | collective-permute-start | bytes 380936 | tf_op jit(solution)/shard_map/ppermute | solution.py:913
  27.8 18.3 %collective-permute-start.12 = (f32[2,128,256]{2,1,0:T(8,128)S(1)}, f32[2,128,256]{2,1,0:T(8,128)S(1)}, u32[]{:S(2)}, u32[]{:S(2)}) collective-permute-start(f32[2,128,256]{2,1,0:T(8,128)S(1)} %get-tuple-element.67), channel_id=1, source_target_pairs={{0,4},{4,0},{8,12},{12,8},{16,20},{20,16},{24,28},{28,24},{1,5},{5... | collective-permute-start | bytes 786440 | tf_op jit(solution)/shard_map/ppermute | solution.py:913
  28.6 17.5 %collective-permute-start.13 = (f32[2,128,256]{2,1,0:T(8,128)S(1)}, f32[2,128,256]{2,1,0:T(8,128)S(1)}, u32[]{:S(2)}, u32[]{:S(2)}) collective-permute-start(f32[2,128,256]{2,1,0:T(8,128)S(1)} %get-tuple-element.68), channel_id=1, source_target_pairs={{0,28},{4,8},{8,4},{12,16},{16,12},{20,24},{24,20},{28,0},{1,29},{... | collective-permute-start | bytes 786440 | tf_op jit(solution)/shard_map/ppermute | solution.py:913
  35.8 12.7 %collective-permute-start.10 = (f32[312,128]{1,0:T(8,128)S(1)}, f32[312,128]{1,0:T(8,128)S(1)}, u32[]{:S(2)}, u32[]{:S(2)}) collective-permute-start(f32[312,128]{1,0:T(8,128)S(1)} %get-tuple-element.61), channel_id=1, source_target_pairs={{0,4},{4,0},{8,12},{12,8},{16,20},{20,16},{24,28},{28,24},{1,5},{5... | collective-permute-start | bytes 479240 | tf_op jit(solution)/shard_map/ppermute | solution.py:913
  35.8 12.7 %collective-permute-start.11 = (f32[312,128]{1,0:T(8,128)S(1)}, f32[312,128]{1,0:T(8,128)S(1)}, u32[]{:S(2)}, u32[]{:S(2)}) collective-permute-start(f32[312,128]{1,0:T(8,128)S(1)} %get-tuple-element.62), channel_id=1, source_target_pairs={{0,28},{4,8},{8,4},{12,16},{16,12},{20,24},{24,20},{28,0},{1,29},{... | collective-permute-start | bytes 479240 | tf_op jit(solution)/shard_map/ppermute | solution.py:913
  39.8 6.3 %copy-start.3 = (bf16[384,256]{1,0:T(8,128)(2,1)S(1)}, bf16[384,256]{1,0:T(8,128)(2,1)}, u32[]{:S(2)}) copy-start(bf16[384,256]{1,0:T(8,128)(2,1)} %constant.50.clone.refs_4_.refs_5_) | copy-start | bytes 589828
  39.8 6.3 %copy-start.8 = (bf16[128,240]{1,0:T(8,128)(2,1)S(1)}, bf16[128,240]{1,0:T(8,128)(2,1)}, u32[]{:S(2)}) copy-start(bf16[128,240]{1,0:T(8,128)(2,1)} %constant.51.clone.refs_5_.refs_6_) | copy-start | bytes 184324
  44.3 4.2 %copy-start.10 = (bf16[384,256]{1,0:T(8,128)(2,1)S(1)}, bf16[384,256]{1,0:T(8,128)(2,1)}, u32[]{:S(2)}) copy-start(bf16[384,256]{1,0:T(8,128)(2,1)} %constant.52.clone.refs_3_) | copy-start | bytes 589828
  44.3 4.2 %copy-start.14 = (bf16[128,144]{1,0:T(8,128)(2,1)S(1)}, bf16[128,144]{1,0:T(8,128)(2,1)}, u32[]{:S(2)}) copy-start(bf16[128,144]{1,0:T(8,128)(2,1)} %constant.53.clone.refs_4_) | copy-start | bytes 110596

commit v13 on v12

--- a/solution.py
+++ b/solution.py
@@ -593,12 +593,12 @@
     )
 
 
-def own_result(parts, approx, left, right, z_matrix, y_matrix):
+def own_result(parts, approx, z_matrix, y_matrix):
     nx, ny, nz = parts.shape
     n1 = nx // 2
     planes, rows, half_z = approx.shape
 
-    def kernel(p_ref, a_ref, el, er, z, y, out, ghosts):
+    def kernel(p_ref, a_ref, z, y, out, ghosts):
         stack = jnp.concatenate([a_ref[i] for i in (0, 1, n1 + 2, n1 + 3)], axis=0)
         for i, plane in enumerate(cut(times(stack, z), rows)):
             ghosts[i] = left_times(y, plane)
@@ -613,14 +613,7 @@
                     lows[k] = ghosts[i, at, lanes]
                 cells = x_synth_interior(lows, highs, n1)
                 for m in range(nx):
-                    value = cells[m] if m in cells else x_synth(m, lows, highs)
-                    if m < 3:
-                        extra = el[(0, 1, 1)[m], at, lanes]
-                        value += extra if m < 2 else THIRD_UP * extra
-                    if m >= nx - 3:
-                        extra = er[(0, 1, 1)[nx - 1 - m], at, lanes]
-                        value += extra if m > nx - 3 else THIRD_DOWN * extra
-                    out[m, at, lanes] = value
+                    out[m, at, lanes] = cells[m] if m in cells else x_synth(m, lows, highs)
             return carry
 
         lax.fori_loop(0, ny // 8, tile, 0)
@@ -628,9 +621,8 @@
     return whole_call(
         kernel,
         shape(nx, ny, nz),
-        [parts, approx, left, right, z_matrix, y_matrix],
+        [parts, approx, z_matrix, y_matrix],
         scratch=[pltpu.VMEM((4, ny, nz), F32)],
-        received=[(2, "gx")],
         name="own_result",
     )
 
@@ -842,7 +834,7 @@
     return from_approx @ approx
 
 
-def final(left, right, own, zs1, ys1, z_matrix, y_matrix, rows, spill_rows):
+def final(left, right, own, e_left, e_right, zs1, ys1, z_matrix, y_matrix, rows, spill_rows):
     nx, ny, nz = own.shape
     half_z = nz // 2
     own_rows = ny // 2
@@ -850,7 +842,7 @@
     steps = ny // step_rows
     taps = received_taps(nx // 2)
 
-    def kernel(l_ref, r_ref, d_ref, z1, s1, z, y, out, planes, parts, done, sems):
+    def kernel(l_ref, r_ref, d_ref, el, er, z1, s1, z, y, out, planes, parts, done, sems):
         stack = [p for ref in (l_ref, r_ref) for p in unpacked(ref[4 * own_rows + 16 :])]
         spilled = cut(times(jnp.concatenate(stack, axis=0), z1), spill_rows)
         for side, ref in enumerate((l_ref, r_ref)):
@@ -877,6 +869,12 @@
                     for m in range(nx):
                         value = d_ref[m, at, lanes]
                         value += added([(float(c), v) for c, v in zip(taps[m], values) if c != 0.0])
+                        if m < 3:
+                            extra = el[(0, 1, 1)[m], at, lanes]
+                            value += extra if m < 2 else THIRD_UP * extra
+                        if m >= nx - 3:
+                            extra = er[(0, 1, 1)[nx - 1 - m], at, lanes]
+                            value += extra if m > nx - 3 else THIRD_DOWN * extra
                         done[m, at, lanes] = value
             copy(i).start()
             return carry
@@ -892,14 +890,14 @@
     return whole_call(
         kernel,
         shape(nx, ny, nz),
-        [left, right, own, zs1, ys1, z_matrix, y_matrix],
+        [left, right, own, e_left, e_right, zs1, ys1, z_matrix, y_matrix],
         scratch=[
             pltpu.VMEM((8, rows, half_z), F32),
             pltpu.VMEM((12, ny, nz), F32),
             pltpu.VMEM((nx, ny, nz), F32),
             pltpu.SemaphoreType.DMA((steps,)),
         ],
-        received=[(0, "gx")],
+        received=[(0, "gx"), (3, "gx")],
         name="final",
         out_specs=pl.BlockSpec(memory_space=pl.ANY),
     )
@@ -973,8 +971,8 @@
     s_left, s_right = exchange(s_up, s_down, "gx")
     bands, approx1 = lax.optimization_barrier((bands, approx1))
     parts = detail_yz(edge, inner_bands(bands, table, index), approx1, zs0, ys0)
-    own = own_result(parts, approx1, e_left, e_right, zs0_low, ys0_low)
-    return final(s_left, s_right, own, zs_spill, ys_spill, zs0_low, ys0_low, rows0, spill_rows)
+    own = own_result(parts, approx1, zs0_low, ys0_low)
+    return final(s_left, s_right, own, e_left, e_right, zs_spill, ys_spill, zs0_low, ys0_low, rows0, spill_rows)
 
 
 def solution(mesh):

time: 51.7 us -> 51.7 us (level)
  transfers between devices with their start and end apart: 14 -> 14, of which waited for: 4 -> 3; matrix products, arithmetic and copies ran while one was open for 0% -> 0% of each run, Pallas kernels for 42% -> 42%
where the time goes in v13:
time: 51.7 us; the launch traced here: 51.6 us
  Pallas kernels  26.4 us (51%)
  starting transfers between devices  19.6 us (38%)
  waiting for transfers between devices  4.09 us (8%)
  local copies, waits for them, and re-layouts  1.13 us (2%)
    pallas_call x13, Pallas kernels, whole_call(): pl.pallas_call(kernel, in_specs=changes.get('in_specs', specs), out_specs...  26.4 us
    ppermute x14, starting transfers between devices, exchange(): return (lax.ppermute(first, axis, here), lax.ppermute(second, axis, across))  19.6 us
    ppermute x14, waiting for transfers between devices, exchange(): return (lax.ppermute(first, axis, here), lax.ppermute(second, axis, across))  4.09 us
    unnamed x42, local copies, waits for them, and re-layouts  1.13 us
  transfers between devices with their start and end apart: 14, of which 3 were waited for; matrix products, arithmetic and copies ran while one was open for 0% of the time, Pallas kernels for 42%

profile of v13, /device:TPU:0, one launch (start us, length us, event | category | flops | bytes accessed | tf_op | source)
XLA Modules:
  0.0 51.6 jit_solution(7011256452528022483)
XLA Ops:
  0.0 1.6 %first_messages.1 = (f32[2,128,256]{2,1,0:T(8,128)S(1)}, f32[2,128,256]{2,1,0:T(8,128)S(1)}, f32[28,8,256]{2,1,0:T(8,128)S(1)}, f32[28,8,256]{2,1,0:T(8,128)S(1)}) custom-call(f32[32,128,256]{2,1,0:T(8,128)} %refs_0_.6), custom_call_target="tpu_custom_call" | custom-call | flops 1000 | bytes 1000 | tf_op jit(solution)/shard_map/first_messages/pallas_call | solution.py:250
  1.6 2.5 %collective-permute-start.2 = (f32[28,8,256]{2,1,0:T(8,128)S(1)}, f32[28,8,256]{2,1,0:T(8,128)S(1)}, u32[]{:S(2)}, u32[]{:S(2)}) collective-permute-start(f32[28,8,256]{2,1,0:T(8,128)S(1)} %get-tuple-element.41), channel_id=1, source_target_pairs={{0,3},{1,2},{2,1},{3,0},{4,7},{5,6},{6,5},{7,4},{8,11},{9,10},{10,... | collective-permute-start | bytes 688136 | tf_op jit(solution)/shard_map/ppermute | solution.py:911
  4.1 1.5 %collective-permute-start = (f32[2,128,256]{2,1,0:T(8,128)S(1)}, f32[2,128,256]{2,1,0:T(8,128)S(1)}, u32[]{:S(2)}, u32[]{:S(2)}) collective-permute-start(f32[2,128,256]{2,1,0:T(8,128)S(1)} %get-tuple-element.37), channel_id=1, source_target_pairs={{0,4},{4,0},{8,12},{12,8},{16,20},{20,16},{24,28},{28,24},{1,5},{5... | collective-permute-start | bytes 786440 | tf_op jit(solution)/shard_map/ppermute | solution.py:911
  5.6 3.6 %collective-permute-start.1 = (f32[2,128,256]{2,1,0:T(8,128)S(1)}, f32[2,128,256]{2,1,0:T(8,128)S(1)}, u32[]{:S(2)}, u32[]{:S(2)}) collective-permute-start(f32[2,128,256]{2,1,0:T(8,128)S(1)} %get-tuple-element.38), channel_id=1, source_target_pairs={{0,28},{4,8},{8,4},{12,16},{16,12},{20,24},{24,20},{28,0},{1,29},{... | collective-permute-start | bytes 786440 | tf_op jit(solution)/shard_map/ppermute | solution.py:911
  9.2 0.1 collective-permute-start.3
  9.3 1.0 %copy-done.1 = bf16[768,256]{1,0:T(8,128)(2,1)S(1)} copy-done((bf16[768,256]{1,0:T(8,128)(2,1)S(1)}, bf16[768,256]{1,0:T(8,128)(2,1)}, u32[]{:S(2)}) %copy-start.1) | copy-done | bytes 393240
  10.3 2.0 %depth_analysis.1.refs_0_ = f32[32,128,256]{2,1,0:T(8,128)S(1)} custom-call(f32[32,128,256]{2,1,0:T(8,128)S(1)} %copy-done, bf16[768,256]{1,0:T(8,128)(2,1)S(1)} %copy-done.1), custom_call_target="tpu_custom_call" | custom-call | flops 1000 | bytes 1000 | tf_op jit(solution)/shard_map/depth_analysis/pallas_call | solution.py:250
  12.3 0.0 copy-start.4
  12.3 1.5 %own_approx.1 = (f32[20,72,128]{2,1,0:T(8,128)S(1)}, f32[16,24,128]{2,1,0:T(8,128)S(1)}, f32[16,24,128]{2,1,0:T(8,128)S(1)}) custom-call(f32[32,128,256]{2,1,0:T(8,128)S(1)} %depth_analysis.1.refs_0_, bf16[80,384]{1,0:T(8,128)(2,1)S(1)} %copy-done.15), custom_call_target="tpu_custom_call" | custom-call | flops 1000 | bytes 1000 | tf_op jit(solution)/shard_map/own_approx/pallas_call | solution.py:250
  13.9 0.7 %collective-permute-start.7 = (f32[16,24,128]{2,1,0:T(8,128)S(1)}, f32[16,24,128]{2,1,0:T(8,128)S(1)}, u32[]{:S(2)}, u32[]{:S(2)}) collective-permute-start(f32[16,24,128]{2,1,0:T(8,128)S(1)} %get-tuple-element.50), channel_id=1, source_target_pairs={{0,3},{1,2},{2,1},{3,0},{4,7},{5,6},{6,5},{7,4},{8,11},{9,10},{10,... | collective-permute-start | bytes 589832 | tf_op jit(solution)/shard_map/ppermute | solution.py:911
  14.6 2.4 %y_analysis.1.refs_0_.refs_2_ = f32[32,144,256]{2,1,0:T(8,128)S(1)} custom-call(f32[32,128,256]{2,1,0:T(8,128)S(1)} %depth_analysis.1.refs_0_, f32[28,8,256]{2,1,0:T(8,128)S(1)} %collective-permute-done.2.refs_1_, f32[28,8,256]{2,1,0:T(8,128)S(1)} %collective-permute-done.3.refs_2_, bf16[768,256]{1,0:T(8,128)(2,1)S(1)} %copy-done.1, ...), custom_call_target="tpu_custom_call" | custom-call | flops 1000 | bytes 1000 | tf_op jit(solution)/shard_map/y_analysis/pallas_call | solution.py:250
  16.9 0.0 copy-start.6
  17.0 0.0 copy-start.7
  17.0 0.0 copy-start.2
  17.0 0.0 copy-start.5
  17.0 0.0 copy-start.19
  17.0 0.0 copy-start.20
  17.0 0.5 edge_own.1.refs_2_
  17.5 0.0 copy-start.10
  17.5 0.0 copy-start.11
  17.5 0.0 copy-start.12
  17.6 0.0 copy-start.13
  17.6 0.0 copy-start.16
  17.6 0.0 copy-start.17
  17.6 0.0 copy-start.18
  17.6 1.0 %collective-permute-done.refs_0_ = f32[2,128,256]{2,1,0:T(8,128)S(1)} collective-permute-done((f32[2,128,256]{2,1,0:T(8,128)S(1)}, f32[2,128,256]{2,1,0:T(8,128)S(1)}, u32[]{:S(2)}, u32[]{:S(2)}) %collective-permute-start) | collective-permute-done | bytes 262176 | tf_op jit(solution)/shard_map/ppermute | solution.py:911
  18.6 0.4 x_halo_messages.1
  19.0 0.1 collective-permute-start.4
  19.1 0.6 %collective-permute-start.5 = (f32[4,80,128]{2,1,0:T(8,128)S(1)}, f32[4,80,128]{2,1,0:T(8,128)S(1)}, u32[]{:S(2)}, u32[]{:S(2)}) collective-permute-start(f32[4,80,128]{2,1,0:T(8,128)S(1)} %get-tuple-element.47), channel_id=1, source_target_pairs={{0,3},{1,2},{2,1},{3,0},{4,7},{5,6},{6,5},{7,4},{8,11},{9,10},{10,... | collective-permute-start | bytes 491528 | tf_op jit(solution)/shard_map/ppermute | solution.py:911
  19.8 0.9 %collective-permute-done.7.refs_2_ = f32[16,24,128]{2,1,0:T(8,128)S(1)} collective-permute-done((f32[16,24,128]{2,1,0:T(8,128)S(1)}, f32[16,24,128]{2,1,0:T(8,128)S(1)}, u32[]{:S(2)}, u32[]{:S(2)}) %collective-permute-start.7) | collective-permute-done | bytes 196640 | tf_op jit(solution)/shard_map/ppermute | solution.py:911
  20.7 1.0 %second_bands.1 = (f32[16,96,128]{2,1,0:T(8,128)S(1)}, f32[248,128]{1,0:T(8,128)S(1)}, f32[248,128]{1,0:T(8,128)S(1)}) custom-call(f32[20,72,128]{2,1,0:T(8,128)S(1)} %get-tuple-element.49.refs_2_.refs_0_.refs_8_, f32[16,24,128]{2,1,0:T(8,128)S(1)} %collective-permute-done.6.refs_1_, f32[16,24,128]{2,1,0:T(8,128)S(1)} %collective-permute-done.7.refs_2_, ...), custom_call_target="tpu_custom_call" | custom-call | flops 1000 | bytes 1000 | tf_op jit(solution)/shard_map/second_bands/pallas_call | solution.py:250
  21.7 0.6 %collective-permute-start.8 = (f32[248,128]{1,0:T(8,128)S(1)}, f32[248,128]{1,0:T(8,128)S(1)}, u32[]{:S(2)}, u32[]{:S(2)}) collective-permute-start(f32[248,128]{1,0:T(8,128)S(1)} %get-tuple-element.59), channel_id=1, source_target_pairs={{0,4},{4,0},{8,12},{12,8},{16,20},{20,16},{24,28},{28,24},{1,5},{5... | collective-permute-start | bytes 380936 | tf_op jit(solution)/shard_map/ppermute | solution.py:911
  22.3 3.6 %collective-permute-start.9 = (f32[248,128]{1,0:T(8,128)S(1)}, f32[248,128]{1,0:T(8,128)S(1)}, u32[]{:S(2)}, u32[]{:S(2)}) collective-permute-start(f32[248,128]{1,0:T(8,128)S(1)} %get-tuple-element.60), channel_id=1, source_target_pairs={{0,28},{4,8},{8,4},{12,16},{16,12},{20,24},{24,20},{28,0},{1,29},{... | collective-permute-start | bytes 380936 | tf_op jit(solution)/shard_map/ppermute | solution.py:911
  25.9 1.9 %edge_details.1 = (f32[8,144,256]{2,1,0:T(8,128)S(1)}, f32[2,128,256]{2,1,0:T(8,128)S(1)}, f32[2,128,256]{2,1,0:T(8,128)S(1)}) custom-call(f32[16]{0:T(128)S(1)} %copy-done.20, s32[3,7]{1,0:T(4,128)S(1)} %copy-done.19, f32[8,144,256]{2,1,0:T(8,128)S(1)} %edge_own.1.refs_2_, f32[4,128,256]{2,1,0:T(8,128)S(1)} %get-tuple-element.54.refs_3_.refs_5_, ...), custom_call_target="tpu_custom_call" | custom-call | flops 1000 | bytes 1000 | tf_op jit(solution)/shard_map/edge_details/pallas_call | solution.py:250
  27.8 0.8 %collective-permute-start.12 = (f32[2,128,256]{2,1,0:T(8,128)S(1)}, f32[2,128,256]{2,1,0:T(8,128)S(1)}, u32[]{:S(2)}, u32[]{:S(2)}) collective-permute-start(f32[2,128,256]{2,1,0:T(8,128)S(1)} %get-tuple-element.67), channel_id=1, source_target_pairs={{0,4},{4,0},{8,12},{12,8},{16,20},{20,16},{24,28},{28,24},{1,5},{5... | collective-permute-start | bytes 786440 | tf_op jit(solution)/shard_map/ppermute | solution.py:911
  28.6 3.6 %collective-permute-start.13 = (f32[2,128,256]{2,1,0:T(8,128)S(1)}, f32[2,128,256]{2,1,0:T(8,128)S(1)}, u32[]{:S(2)}, u32[]{:S(2)}) collective-permute-start(f32[2,128,256]{2,1,0:T(8,128)S(1)} %get-tuple-element.68), channel_id=1, source_target_pairs={{0,28},{4,8},{8,4},{12,16},{16,12},{20,24},{24,20},{28,0},{1,29},{... | collective-permute-start | bytes 786440 | tf_op jit(solution)/shard_map/ppermute | solution.py:911
  32.3 3.5 %coarse.1 = (f32[20,72,128]{2,1,0:T(8,128)S(1)}, f32[312,128]{1,0:T(8,128)S(1)}, f32[312,128]{1,0:T(8,128)S(1)}) custom-call(f32[16]{0:T(128)S(1)} %copy-done.20, s32[3,7]{1,0:T(4,128)S(1)} %copy-done.19, f32[16,96,128]{2,1,0:T(8,128)S(1)} %get-tuple-element.58.refs_2_, f32[248,128]{1,0:T(8,128)S(1)} %collective-permute-done.8.refs_3_, ...), custom_call_target="tpu_custom_call" | custom-call | flops 1000 | bytes 1000 | tf_op jit(solution)/shard_map/coarse/pallas_call | solution.py:250
  35.8 0.1 collective-permute-start.10
  35.8 1.9 %collective-permute-start.11 = (f32[312,128]{1,0:T(8,128)S(1)}, f32[312,128]{1,0:T(8,128)S(1)}, u32[]{:S(2)}, u32[]{:S(2)}) collective-permute-start(f32[312,128]{1,0:T(8,128)S(1)} %get-tuple-element.62), channel_id=1, source_target_pairs={{0,28},{4,8},{8,4},{12,16},{16,12},{20,24},{24,20},{28,0},{1,29},{... | collective-permute-start | bytes 479240 | tf_op jit(solution)/shard_map/ppermute | solution.py:911
  37.7 2.1 %inner_bands.1.refs_1_ = f32[24,144,256]{2,1,0:T(8,128)S(1)} custom-call(f32[16]{0:T(128)S(1)} %copy-done.20, s32[3,7]{1,0:T(4,128)S(1)} %copy-done.19, f32[32,144,256]{2,1,0:T(8,128)S(1)} %y_analysis.1.refs_0_.refs_2_), custom_call_target="tpu_custom_call" | custom-call | flops 1000 | bytes 1000 | tf_op jit(solution)/shard_map/inner_bands/pallas_call | solution.py:250
  39.8 0.0 copy-start.3
  39.8 0.0 copy-start.8
  39.8 4.4 %detail_yz.1.refs_0_ = f32[32,128,256]{2,1,0:T(8,128)S(1)} custom-call(f32[8,144,256]{2,1,0:T(8,128)S(1)} %get-tuple-element.63.refs_0_, f32[24,144,256]{2,1,0:T(8,128)S(1)} %inner_bands.1.refs_1_, f32[20,72,128]{2,1,0:T(8,128)S(1)} %get-tuple-element.66.refs_2_.refs_1_, bf16[768,256]{1,0:T(8,128)(2,1)S(1)} %copy-done.2, bf16[128,432]{1,0:T(8,128)(2,1)S(1)} %copy-done.5), custom_call_target="tpu_custom_call" | custom-call | flops 1000 | bytes 1000 | tf_op jit(solution)/shard_map/detail_yz/pallas_call | solution.py:250
  44.3 0.0 copy-start.9
  44.3 0.0 copy-start.14
  44.3 2.0 %own_result.1.refs_2_ = f32[32,128,256]{2,1,0:T(8,128)S(1)} custom-call(f32[32,128,256]{2,1,0:T(8,128)S(1)} %detail_yz.1.refs_0_, f32[20,72,128]{2,1,0:T(8,128)S(1)} %get-tuple-element.66.refs_2_.refs_1_, bf16[384,256]{1,0:T(8,128)(2,1)S(1)} %copy-done.3, bf16[128,240]{1,0:T(8,128)(2,1)S(1)} %copy-done.8), custom_call_target="tpu_custom_call" | custom-call | flops 1000 | bytes 1000 | tf_op jit(solution)/shard_map/own_result/pallas_call | solution.py:250
  46.4 2.1 %collective-permute-done.10.refs_0_ = f32[312,128]{1,0:T(8,128)S(1)} collective-permute-done((f32[312,128]{1,0:T(8,128)S(1)}, f32[312,128]{1,0:T(8,128)S(1)}, u32[]{:S(2)}, u32[]{:S(2)}) %collective-permute-start.10) | collective-permute-done | bytes 159776 | tf_op jit(solution)/shard_map/ppermute | solution.py:911
  48.5 3.0 %final.1 = f32[32,128,256]{2,1,0:T(8,128)} custom-call(f32[312,128]{1,0:T(8,128)S(1)} %collective-permute-done.10.refs_0_, f32[312,128]{1,0:T(8,128)S(1)} %collective-permute-done.11.refs_1_, f32[32,128,256]{2,1,0:T(8,128)S(1)} %own_result.1.refs_2_, f32[2,128,256]{2,1,0:T(8,128)S(1)} %collective-permute-done.12.refs_3_, ...), custom_call_target="tpu_custom_call" | custom-call | flops 1000 | bytes 1000 | tf_op jit(solution)/shard_map/final/pallas_call | solution.py:250
  (35 shorter events, 0.1 us)
Async XLA Ops:
  0.0 9.3 %copy-start = (f32[32,128,256]{2,1,0:T(8,128)S(1)}, f32[32,128,256]{2,1,0:T(8,128)}, u32[]{:S(2)}) copy-start(f32[32,128,256]{2,1,0:T(8,128)} %refs_0_.6) | copy-start | bytes 12582916
  1.6 12.9 %collective-permute-start.2 = (f32[28,8,256]{2,1,0:T(8,128)S(1)}, f32[28,8,256]{2,1,0:T(8,128)S(1)}, u32[]{:S(2)}, u32[]{:S(2)}) collective-permute-start(f32[28,8,256]{2,1,0:T(8,128)S(1)} %get-tuple-element.41), channel_id=1, source_target_pairs={{0,3},{1,2},{2,1},{3,0},{4,7},{5,6},{6,5},{7,4},{8,11},{9,10},{10,... | collective-permute-start | bytes 688136 | tf_op jit(solution)/shard_map/ppermute | solution.py:911
  4.1 14.5 %collective-permute-start = (f32[2,128,256]{2,1,0:T(8,128)S(1)}, f32[2,128,256]{2,1,0:T(8,128)S(1)}, u32[]{:S(2)}, u32[]{:S(2)}) collective-permute-start(f32[2,128,256]{2,1,0:T(8,128)S(1)} %get-tuple-element.37), channel_id=1, source_target_pairs={{0,4},{4,0},{8,12},{12,8},{16,20},{20,16},{24,28},{28,24},{1,5},{5... | collective-permute-start | bytes 786440 | tf_op jit(solution)/shard_map/ppermute | solution.py:911
  5.6 13.0 %collective-permute-start.1 = (f32[2,128,256]{2,1,0:T(8,128)S(1)}, f32[2,128,256]{2,1,0:T(8,128)S(1)}, u32[]{:S(2)}, u32[]{:S(2)}) collective-permute-start(f32[2,128,256]{2,1,0:T(8,128)S(1)} %get-tuple-element.38), channel_id=1, source_target_pairs={{0,28},{4,8},{8,4},{12,16},{16,12},{20,24},{24,20},{28,0},{1,29},{... | collective-permute-start | bytes 786440 | tf_op jit(solution)/shard_map/ppermute | solution.py:911
  9.2 5.4 %collective-permute-start.3 = (f32[28,8,256]{2,1,0:T(8,128)S(1)}, f32[28,8,256]{2,1,0:T(8,128)S(1)}, u32[]{:S(2)}, u32[]{:S(2)}) collective-permute-start(f32[28,8,256]{2,1,0:T(8,128)S(1)} %get-tuple-element.42), channel_id=1, source_target_pairs={{0,1},{1,0},{2,3},{3,2},{4,5},{5,4},{6,7},{7,6},{8,9},{9,8},{10,11... | collective-permute-start | bytes 688136 | tf_op jit(solution)/shard_map/ppermute | solution.py:911
  9.3 1.0 %copy-start.1 = (bf16[768,256]{1,0:T(8,128)(2,1)S(1)}, bf16[768,256]{1,0:T(8,128)(2,1)}, u32[]{:S(2)}) copy-start(bf16[768,256]{1,0:T(8,128)(2,1)} %constant.36.clone.refs_1_.refs_3_) | copy-start | bytes 1179652
  10.3 2.0 %copy-start.15 = (bf16[80,384]{1,0:T(8,128)(2,1)S(1)}, bf16[80,384]{1,0:T(8,128)(2,1)}, u32[]{:S(2)}) copy-start(bf16[80,384]{1,0:T(8,128)(2,1)} %constant.37.clone.refs_1_) | copy-start | bytes 184324
  12.3 2.2 %copy-start.4 = (bf16[144,432]{1,0:T(8,128)(2,1)S(1)}, bf16[144,432]{1,0:T(8,128)(2,1)}, u32[]{:S(2)}) copy-start(bf16[144,432]{1,0:T(8,128)(2,1)} %constant.38.clone.refs_4_.refs_6_) | copy-start | bytes 373252
  13.9 6.8 %collective-permute-start.7 = (f32[16,24,128]{2,1,0:T(8,128)S(1)}, f32[16,24,128]{2,1,0:T(8,128)S(1)}, u32[]{:S(2)}, u32[]{:S(2)}) collective-permute-start(f32[16,24,128]{2,1,0:T(8,128)S(1)} %get-tuple-element.50), channel_id=1, source_target_pairs={{0,3},{1,2},{2,1},{3,0},{4,7},{5,6},{6,5},{7,4},{8,11},{9,10},{10,... | collective-permute-start | bytes 589832 | tf_op jit(solution)/shard_map/ppermute | solution.py:911
  14.5 6.2 %collective-permute-start.6 = (f32[16,24,128]{2,1,0:T(8,128)S(1)}, f32[16,24,128]{2,1,0:T(8,128)S(1)}, u32[]{:S(2)}, u32[]{:S(2)}) collective-permute-start(f32[16,24,128]{2,1,0:T(8,128)S(1)} %get-tuple-element.39), channel_id=1, source_target_pairs={{0,1},{1,0},{2,3},{3,2},{4,5},{5,4},{6,7},{7,6},{8,9},{9,8},{10,11... | collective-permute-start | bytes 589832 | tf_op jit(solution)/shard_map/ppermute | solution.py:911
  16.9 3.8 %copy-start.6 = (bf16[256,256]{1,0:T(8,128)(2,1)S(1)}, bf16[256,256]{1,0:T(8,128)(2,1)}, u32[]{:S(2)}) copy-start(bf16[256,256]{1,0:T(8,128)(2,1)} %constant.39.clone.refs_3_.refs_9_) | copy-start | bytes 393220
  17.0 3.7 %copy-start.7 = (bf16[96,384]{1,0:T(8,128)(2,1)S(1)}, bf16[96,384]{1,0:T(8,128)(2,1)}, u32[]{:S(2)}) copy-start(bf16[96,384]{1,0:T(8,128)(2,1)} %constant.40.clone.refs_4_.refs_11_) | copy-start | bytes 221188
  17.0 8.9 %copy-start.2 = (bf16[768,256]{1,0:T(8,128)(2,1)S(1)}, bf16[768,256]{1,0:T(8,128)(2,1)}, u32[]{:S(2)}) copy-start(bf16[768,256]{1,0:T(8,128)(2,1)} %constant.41.clone.refs_7_.refs_3_) | copy-start | bytes 1179652
  17.0 8.9 %copy-start.5 = (bf16[128,432]{1,0:T(8,128)(2,1)S(1)}, bf16[128,432]{1,0:T(8,128)(2,1)}, u32[]{:S(2)}) copy-start(bf16[128,432]{1,0:T(8,128)(2,1)} %constant.42.clone.refs_8_.refs_4_) | copy-start | bytes 331780
  17.0 8.9 %copy-start.19 = (s32[3,7]{1,0:T(4,128)S(1)}, s32[3,7]{1,0:T(4,128)}, u32[]{:S(2)}) copy-start(s32[3,7]{1,0:T(4,128)} %refs_1_.7) | copy-start | bytes 256
  17.0 8.9 %copy-start.20 = (f32[16]{0:T(128)S(1)}, f32[16]{0:T(128)}, u32[]{:S(2)}) copy-start(f32[16]{0:T(128)} %refs_0_.9) | copy-start | bytes 196
  17.5 14.7 %copy-start.10 = (bf16[128,672]{1,0:T(8,128)(2,1)S(1)}, bf16[128,672]{1,0:T(8,128)(2,1)}, u32[]{:S(2)}) copy-start(bf16[128,672]{1,0:T(8,128)(2,1)} %constant.43.clone.refs_10_) | copy-start | bytes 516100
  17.5 14.7 %copy-start.11 = (bf16[256,256]{1,0:T(8,128)(2,1)S(1)}, bf16[256,256]{1,0:T(8,128)(2,1)}, u32[]{:S(2)}) copy-start(bf16[256,256]{1,0:T(8,128)(2,1)} %constant.46.clone.refs_14_) | copy-start | bytes 393220
  17.5 14.7 %copy-start.12 = (bf16[256,256]{1,0:T(8,128)(2,1)S(1)}, bf16[256,256]{1,0:T(8,128)(2,1)}, u32[]{:S(2)}) copy-start(bf16[256,256]{1,0:T(8,128)(2,1)} %constant.45.clone.refs_13_) | copy-start | bytes 393220
  17.6 14.7 %copy-start.13 = (bf16[256,256]{1,0:T(8,128)(2,1)S(1)}, bf16[256,256]{1,0:T(8,128)(2,1)}, u32[]{:S(2)}) copy-start(bf16[256,256]{1,0:T(8,128)(2,1)} %constant.44.clone.refs_12_) | copy-start | bytes 393220
  17.6 14.7 %copy-start.16 = (bf16[80,288]{1,0:T(8,128)(2,1)S(1)}, bf16[80,288]{1,0:T(8,128)(2,1)}, u32[]{:S(2)}) copy-start(bf16[80,288]{1,0:T(8,128)(2,1)} %constant.49.clone.refs_17_) | copy-start | bytes 138244
  17.6 14.7 %copy-start.17 = (bf16[64,144]{1,0:T(8,128)(2,1)S(1)}, bf16[64,144]{1,0:T(8,128)(2,1)}, u32[]{:S(2)}) copy-start(bf16[64,144]{1,0:T(8,128)(2,1)} %constant.48.clone.refs_16_) | copy-start | bytes 55300
  17.6 14.7 %copy-start.18 = (bf16[48,192]{1,0:T(8,128)(2,1)S(1)}, bf16[48,192]{1,0:T(8,128)(2,1)}, u32[]{:S(2)}) copy-start(bf16[48,192]{1,0:T(8,128)(2,1)} %constant.47.clone.refs_15_) | copy-start | bytes 55300
  19.0 6.8 %collective-permute-start.4 = (f32[4,80,128]{2,1,0:T(8,128)S(1)}, f32[4,80,128]{2,1,0:T(8,128)S(1)}, u32[]{:S(2)}, u32[]{:S(2)}) collective-permute-start(f32[4,80,128]{2,1,0:T(8,128)S(1)} %get-tuple-element.46), channel_id=1, source_target_pairs={{0,1},{1,0},{2,3},{3,2},{4,5},{5,4},{6,7},{7,6},{8,9},{9,8},{10,11... | collective-permute-start | bytes 491528 | tf_op jit(solution)/shard_map/ppermute | solution.py:911
  19.1 6.7 %collective-permute-start.5 = (f32[4,80,128]{2,1,0:T(8,128)S(1)}, f32[4,80,128]{2,1,0:T(8,128)S(1)}, u32[]{:S(2)}, u32[]{:S(2)}) collective-permute-start(f32[4,80,128]{2,1,0:T(8,128)S(1)} %get-tuple-element.47), channel_id=1, source_target_pairs={{0,3},{1,2},{2,1},{3,0},{4,7},{5,6},{6,5},{7,4},{8,11},{9,10},{10,... | collective-permute-start | bytes 491528 | tf_op jit(solution)/shard_map/ppermute | solution.py:911
  21.7 10.5 %collective-permute-start.8 = (f32[248,128]{1,0:T(8,128)S(1)}, f32[248,128]{1,0:T(8,128)S(1)}, u32[]{:S(2)}, u32[]{:S(2)}) collective-permute-start(f32[248,128]{1,0:T(8,128)S(1)} %get-tuple-element.59), channel_id=1, source_target_pairs={{0,4},{4,0},{8,12},{12,8},{16,20},{20,16},{24,28},{28,24},{1,5},{5... | collective-permute-start | bytes 380936 | tf_op jit(solution)/shard_map/ppermute | solution.py:911
  22.3 9.9 %collective-permute-start.9 = (f32[248,128]{1,0:T(8,128)S(1)}, f32[248,128]{1,0:T(8,128)S(1)}, u32[]{:S(2)}, u32[]{:S(2)}) collective-permute-start(f32[248,128]{1,0:T(8,128)S(1)} %get-tuple-element.60), channel_id=1, source_target_pairs={{0,28},{4,8},{8,4},{12,16},{16,12},{20,24},{24,20},{28,0},{1,29},{... | collective-permute-start | bytes 380936 | tf_op jit(solution)/shard_map/ppermute | solution.py:911
  27.8 20.7 %collective-permute-start.12 = (f32[2,128,256]{2,1,0:T(8,128)S(1)}, f32[2,128,256]{2,1,0:T(8,128)S(1)}, u32[]{:S(2)}, u32[]{:S(2)}) collective-permute-start(f32[2,128,256]{2,1,0:T(8,128)S(1)} %get-tuple-element.67), channel_id=1, source_target_pairs={{0,4},{4,0},{8,12},{12,8},{16,20},{20,16},{24,28},{28,24},{1,5},{5... | collective-permute-start | bytes 786440 | tf_op jit(solution)/shard_map/ppermute | solution.py:911
  28.6 19.9 %collective-permute-start.13 = (f32[2,128,256]{2,1,0:T(8,128)S(1)}, f32[2,128,256]{2,1,0:T(8,128)S(1)}, u32[]{:S(2)}, u32[]{:S(2)}) collective-permute-start(f32[2,128,256]{2,1,0:T(8,128)S(1)} %get-tuple-element.68), channel_id=1, source_target_pairs={{0,28},{4,8},{8,4},{12,16},{16,12},{20,24},{24,20},{28,0},{1,29},{... | collective-permute-start | bytes 786440 | tf_op jit(solution)/shard_map/ppermute | solution.py:911
  35.8 12.7 %collective-permute-start.10 = (f32[312,128]{1,0:T(8,128)S(1)}, f32[312,128]{1,0:T(8,128)S(1)}, u32[]{:S(2)}, u32[]{:S(2)}) collective-permute-start(f32[312,128]{1,0:T(8,128)S(1)} %get-tuple-element.61), channel_id=1, source_target_pairs={{0,4},{4,0},{8,12},{12,8},{16,20},{20,16},{24,28},{28,24},{1,5},{5... | collective-permute-start | bytes 479240 | tf_op jit(solution)/shard_map/ppermute | solution.py:911
  35.8 12.7 %collective-permute-start.11 = (f32[312,128]{1,0:T(8,128)S(1)}, f32[312,128]{1,0:T(8,128)S(1)}, u32[]{:S(2)}, u32[]{:S(2)}) collective-permute-start(f32[312,128]{1,0:T(8,128)S(1)} %get-tuple-element.62), channel_id=1, source_target_pairs={{0,28},{4,8},{8,4},{12,16},{16,12},{20,24},{24,20},{28,0},{1,29},{... | collective-permute-start | bytes 479240 | tf_op jit(solution)/shard_map/ppermute | solution.py:911
  39.8 4.5 %copy-start.3 = (bf16[384,256]{1,0:T(8,128)(2,1)S(1)}, bf16[384,256]{1,0:T(8,128)(2,1)}, u32[]{:S(2)}) copy-start(bf16[384,256]{1,0:T(8,128)(2,1)} %constant.50.clone.refs_2_.refs_7_) | copy-start | bytes 589828
  39.8 4.5 %copy-start.8 = (bf16[128,240]{1,0:T(8,128)(2,1)S(1)}, bf16[128,240]{1,0:T(8,128)(2,1)}, u32[]{:S(2)}) copy-start(bf16[128,240]{1,0:T(8,128)(2,1)} %constant.51.clone.refs_3_.refs_8_) | copy-start | bytes 184324
  44.3 4.2 %copy-start.9 = (bf16[384,256]{1,0:T(8,128)(2,1)S(1)}, bf16[384,256]{1,0:T(8,128)(2,1)}, u32[]{:S(2)}) copy-start(bf16[384,256]{1,0:T(8,128)(2,1)} %constant.52.clone.refs_5_) | copy-start | bytes 589828
  44.3 4.2 %copy-start.14 = (bf16[128,144]{1,0:T(8,128)(2,1)S(1)}, bf16[128,144]{1,0:T(8,128)(2,1)}, u32[]{:S(2)}) copy-start(bf16[128,144]{1,0:T(8,128)(2,1)} %constant.53.clone.refs_6_) | copy-start | bytes 110596
